TPU v7x, 32 devices: a whole 2x2x4 slice. The times are simulated.
32 devices in a mesh: ty: 2 (over x), tx: 16 (over z, y, core).
Axes of the slice: x: 2, y: 2, z: 4, core: 2. Of those that a mesh axis runs over, the one named last changes fastest.
Arguments:
- object_field: float32 [2, 256, 2048], P(None, 'ty', 'tx'), may hold values from -40 to 40
- probe: float32 [2, 4, 128, 128], replicated, may hold values from -3 to 3
- intensities: float32 [2, 16, 3, 128, 128], P('ty', 'tx'), may hold values from 0.25 to 16
- positions: int32 [2, 16, 3, 2], P('ty', 'tx'), may hold values from 0 to 128
Outputs:
- object_out: float32 [2, 256, 2048], P(None, 'ty', 'tx')
- probe_out: float32 [2, 4, 128, 128], replicated
All inputs are finite; a program needn't handle non-finite values.
Results may differ from a plain program's by a relative error of at most 0.0003.
Values sent between devices are 32-bit elements; how exact they have to be, the bound alone decides.
No kernel may reach another device: no remote copies, remote signals or barrier semaphores. Data moves between devices by JAX's collectives and lax.ppermute only.
A program may use at most 64 MiB of HBM per device.

v0:
```python
import functools

import jax
import jax.numpy as jnp
import numpy as np
from jax import lax
from jax.experimental import pallas as pl
from jax.experimental.pallas import tpu as pltpu
from jax.sharding import PartitionSpec as P

ROUNDS = 2
OBJECT_STEP = 0.1
PROBE_RELAX = 0.5
AXES = ("ty", "tx")
SUBLANES = 8
WEIGHT_ROWS = SUBLANES
F32 = jnp.float32
BF16 = jnp.bfloat16


def dft_blocks(win):
    line = np.arange(win, dtype=np.int64)
    angle = (line[:, None] * line[None, :] % win) * (2.0 * np.pi / win)
    c, s = np.cos(angle) / np.sqrt(win), np.sin(angle) / np.sqrt(win)
    full = np.block([[c, -s], [s, c]]).astype(np.float32)
    high = full.astype(jnp.bfloat16)
    low = (full - high.astype(np.float32)).astype(jnp.bfloat16)
    return np.stack([high, low]), np.stack([high.T, low.T])


def pairings(size):
    found = []
    for first in (0, 1):
        pairs = {}
        for low in range(first, size - 1, 2):
            pairs[low], pairs[low + 1] = low + 1, low
        if pairs:
            found.append(pairs)
    return found


def flat_pairs(pairs_y, pairs_x, n_ty, n_tx):
    out = []
    for y in range(n_ty):
        for x in range(n_tx):
            to_y = y if pairs_y is None else pairs_y.get(y)
            to_x = x if pairs_x is None else pairs_x.get(x)
            if to_y is not None and to_x is not None:
                out.append((y * n_tx + x, to_y * n_tx + to_x))
    return out


def xor_permute(x, mask, total):
    return lax.ppermute(x, AXES, [(i, i ^ mask) for i in range(total)])


def split(x):
    high = x.astype(BF16)
    return high, (x - high.astype(F32)).astype(BF16)


def product(a, b):
    (a_high, a_low), (b_high, b_low) = a, b
    dot = functools.partial(jnp.dot, preferred_element_type=F32)
    return dot(a_high, b_high) + (dot(a_low, b_high) + dot(a_high, b_low))


def lane_pick(width, margin, flag):
    lane = lax.broadcasted_iota(jnp.int32, (8, width), 1)
    below = jnp.where(lane < margin, 0, 1)
    return below == flag


def rowwise(mask, rows):
    return jnp.broadcast_to(mask[:1], (rows, mask.shape[1]))


def by_parity(odd, even_value, odd_value):
    return jnp.where(odd == 1, odd_value, even_value)


def compute(
    ext_ref, probe_ref, meas_ref, pos_ref, right_ref, left_ref, grid_ref, grad_ref, *, margin
):
    scans, win = meas_ref.shape[0], meas_ref.shape[1]
    modes = probe_ref.shape[1]
    width = 2 * win
    w_fwd = (right_ref[0], right_ref[1])
    l_fwd = (left_ref[0], left_ref[1])
    grid_ref[...] = jnp.zeros_like(grid_ref)
    weight = jnp.zeros((WEIGHT_ROWS, win), F32)
    for s in range(scans):
        r, c = pos_ref[s, 0], pos_ref[s, 1]
        turn = jnp.where(c <= margin, margin - c, margin + width - c)
        back = jnp.where(c >= margin, c - margin, c + width - margin)
        q = r % SUBLANES
        base = pl.multiple_of(r - q, SUBLANES)
        tall = win + SUBLANES
        lift = jnp.where(q == 0, 0, tall - q)

        def window(part):
            band = pltpu.roll(ext_ref[part, pl.ds(base, tall), :], turn, 1)[:, :win]
            return pltpu.roll(band, lift, 0)[:win]

        o_re, o_im = window(0), window(1)
        power = o_re * o_re + o_im * o_im
        weight = weight + jnp.sum(power.reshape(win // WEIGHT_ROWS, WEIGHT_ROWS, win), axis=0)
        rows = []
        for k in range(modes):
            p_re, p_im = probe_ref[0, k], probe_ref[1, k]
            rows.append(
                jnp.concatenate([p_re * o_re - p_im * o_im, p_re * o_im + p_im * o_re], axis=1)
            )
        y = product(split(jnp.concatenate(rows, axis=0)), w_fwd)
        y = jnp.concatenate(
            [
                jnp.concatenate([y[k * win : (k + 1) * win, :win] for k in range(modes)], axis=1),
                jnp.concatenate([y[k * win : (k + 1) * win, win:] for k in range(modes)], axis=1),
            ],
            axis=0,
        )
        far = product(l_fwd, split(y))
        square = far * far
        square = square[:win] + square[win:]
        total = square[:, :win]
        for k in range(1, modes):
            total = total + square[:, k * win : (k + 1) * win]
        ratio = jnp.sqrt(meas_ref[s]) * lax.rsqrt(jnp.maximum(total, 1.0)) - 1.0
        ratio = jnp.concatenate([ratio] * modes, axis=1)
        far = far * jnp.concatenate([ratio, ratio], axis=0)
        u = product(w_fwd, split(far))
        u = jnp.concatenate(
            [
                jnp.concatenate(
                    [u[:win, k * win : (k + 1) * win], u[win:, k * win : (k + 1) * win]], axis=1
                )
                for k in range(modes)
            ],
            axis=0,
        )
        chi = product(split(u), l_fwd)
        g_re = g_im = None
        for k in range(modes):
            p_re, p_im = probe_ref[0, k], probe_ref[1, k]
            c_re, c_im = chi[k * win : (k + 1) * win, :win], chi[k * win : (k + 1) * win, win:]
            a, b = p_re * c_re + p_im * c_im, p_re * c_im - p_im * c_re
            g_re, g_im = (a, b) if k == 0 else (g_re + a, g_im + b)
            a, b = o_re * c_re + o_im * c_im, o_re * c_im - o_im * c_re
            if s == 0:
                grad_ref[k], grad_ref[modes + k] = a, b
            else:
                grad_ref[k] += a
                grad_ref[modes + k] += b
        for part, g in ((0, g_re), (1, g_im)):
            g = pltpu.roll(jnp.concatenate([g, jnp.zeros((SUBLANES, win), F32)], axis=0), q, 0)
            g = jnp.concatenate([g, jnp.zeros_like(g)], axis=1)
            grid_ref[part, pl.ds(base, tall), :] += pltpu.roll(g, back, 1)
    return weight


def emit_halves(grad_ref, weight, keep_ref, send_ref, half):
    count, win = keep_ref.shape[0], grad_ref.shape[1]
    for j in range(count):
        keep_ref[j, :win, :] = grad_ref[half * count + j]
        send_ref[j, :win, :] = grad_ref[(1 - half) * count + j]
        keep_ref[j, win:, :] = weight
        send_ref[j, win:, :] = weight


def first_kernel(
    n_y, n_x, margin, pos_ref, obj_ref, probe_ref, meas_ref, right_ref, left_ref, *rest
):
    take = iter(rest)
    ty_refs = [next(take) for _ in range(n_y)]
    tx_refs = [next(take) for _ in range(n_x)]
    corner_refs = [[next(take) for _ in range(n_x)] for _ in range(n_y)]
    ext_ref, keep_ref, send_ref, grid_ref, *msg_refs, grad_ref = take
    tile = obj_ref.shape[-1]
    odd_y, odd_x = lax.axis_index("ty") % 2, lax.axis_index("tx") % 2
    pick = lane_pick(tile, margin, odd_x)

    def side(refs, part, rows):
        if not refs:
            return jnp.zeros((rows, tile), F32)
        other = refs[1][part] if len(refs) > 1 else jnp.zeros((rows, tile), F32)
        return jnp.where(rowwise(pick, rows), refs[0][part], other)

    for part in (0, 1):
        ext_ref[part, margin : margin + tile, :tile] = obj_ref[part]
        ext_ref[part, margin : margin + tile, tile:] = side(tx_refs, part, tile)
        bands = [
            jnp.concatenate([ty_refs[i][part], side(corner_refs[i], part, margin)], axis=1)
            for i in range(n_y)
        ]
        while len(bands) < 2:
            bands.append(jnp.zeros((margin, 2 * tile), F32))
        ext_ref[part, :margin, :] = by_parity(odd_y, bands[1], bands[0])
        ext_ref[part, margin + tile : 2 * tile, :] = by_parity(odd_y, bands[0], bands[1])
    weight = compute(
        ext_ref, probe_ref, meas_ref, pos_ref, right_ref, left_ref, grid_ref, grad_ref, margin=margin
    )
    emit_halves(grad_ref, weight, keep_ref, send_ref, odd_x)
    for i, ref in enumerate(msg_refs):
        high = jnp.where(odd_x == i, 1, 0)
        mask = rowwise(lane_pick(tile, margin, high), 2 * tile)
        for part in (0, 1):
            ref[part] = jnp.where(
                mask, grid_ref[part, : 2 * tile, :tile], grid_ref[part, : 2 * tile, tile:]
            )


def combined_probe(probe_ref, own_ref, other_ref, new_ref, half):
    count, win, modes = own_ref.shape[0], probe_ref.shape[-1], probe_ref.shape[1]
    weight = jnp.sum(own_ref[0, win:, :])
    scale = PROBE_RELAX * win * win / jnp.full((8, win), weight, F32)
    scale = jnp.broadcast_to(scale[:1], (win, win))
    for j in range(count):
        for ref, index in ((own_ref, half * count + j), (other_ref, (1 - half) * count + j)):
            part, k = index // modes, index % modes
            new_ref[part, k] = probe_ref[part, k] + scale * ref[j, :win, :]


def second_kernel(
    n_y, n_x, n_ty, n_tx, margin, pos_ref, old_ref, grid_old_ref, probe_ref, meas_ref, right_ref,
    left_ref, own_ref, other_ref, *rest
):
    take = iter(rest)
    tx_refs = [next(take) for _ in range(n_x)]
    ty_refs = [next(take) for _ in range(n_y)]
    tile_ref, new_ref, keep_ref, send_ref, grid_ref, ext_ref, grad_ref = take
    tile = probe_ref.shape[-1]
    at_y, at_x = lax.axis_index("ty"), lax.axis_index("tx")
    odd_y, odd_x = at_y % 2, at_x % 2
    combined_probe(probe_ref, own_ref, other_ref, new_ref, odd_x)
    row = lax.broadcasted_iota(jnp.int32, (2 * tile, 2 * tile), 0)
    lane = lax.broadcasted_iota(jnp.int32, (2 * tile, 2 * tile), 1)
    inside = (row >= jnp.where(at_y == 0, margin, 0)) & (
        row < jnp.where(at_y == n_ty - 1, margin + tile, 2 * tile)
    )
    inside &= (lane < jnp.where(at_x == n_tx - 1, tile, tile + margin)) | (
        lane >= jnp.where(at_x == 0, 2 * tile, tile + margin)
    )
    for part in (0, 1):
        total = grid_old_ref[part, : 2 * tile, :]
        if n_x:
            total = total + spread(tx_refs, part, odd_x, margin, tile)
        ext_ref[part, : 2 * tile, :] = total
        for i, ref in enumerate(ty_refs):
            start = pl.multiple_of(jnp.where(odd_y == i, tile, 0), tile)
            ext_ref[part, pl.ds(start, tile), :] += ref[part]
        step = jnp.where(inside, OBJECT_STEP * ext_ref[part, : 2 * tile, :], 0.0)
        ext_ref[part, : 2 * tile, :] = old_ref[part, : 2 * tile, :] + step
        tile_ref[part] = ext_ref[part, margin : margin + tile, :tile]
    weight = compute(
        ext_ref, new_ref, meas_ref, pos_ref, right_ref, left_ref, grid_ref, grad_ref, margin=margin
    )
    emit_halves(grad_ref, weight, keep_ref, send_ref, odd_x)


def spread(tx_refs, part, odd_x, margin, tile):
    rows = 2 * tile
    first = tx_refs[0][part]
    second = tx_refs[1][part] if len(tx_refs) > 1 else jnp.zeros((rows, tile), F32)
    low = rowwise(lane_pick(tile, margin, odd_x), rows)
    return jnp.concatenate(
        [jnp.where(low, second, first), jnp.where(low, first, second)], axis=1
    )


def last_kernel(n_y, n_x, margin, tile_ref, mid_ref, probe_ref, own_ref, other_ref, *rest):
    take = iter(rest)
    ty_refs = [next(take) for _ in range(n_y)]
    obj_ref, new_ref = take
    tile = probe_ref.shape[-1]
    odd_y, odd_x = lax.axis_index("ty") % 2, lax.axis_index("tx") % 2
    combined_probe(probe_ref, own_ref, other_ref, new_ref, odd_x)
    for part in (0, 1):
        obj_ref[part] = mid_ref[part, margin : margin + tile, :]
        for i, ref in enumerate(ty_refs):
            start = pl.multiple_of(jnp.where(odd_y == i, tile - margin, 0), margin)
            obj_ref[part, pl.ds(start, margin), :] += ref[part]
        obj_ref[part] = tile_ref[part] + OBJECT_STEP * obj_ref[part]


def call(kernel, outs, ins, scratch=()):
    smem = pl.BlockSpec(memory_space=pltpu.SMEM)
    vmem = pl.BlockSpec(memory_space=pltpu.VMEM)
    shapes = [jax.ShapeDtypeStruct(s, F32) for s in outs]
    return pl.pallas_call(
        kernel,
        out_shape=shapes,
        in_specs=[smem if x.dtype == jnp.int32 else vmem for x in ins],
        out_specs=[vmem] * len(outs),
        scratch_shapes=[pltpu.VMEM(s, F32) for s in scratch],
        compiler_params=pltpu.CompilerParams(vmem_limit_bytes=32 * 1024 * 1024),
    )(*ins)


def bit_of(me, bit):
    return (me >> bit) & 1


def masks_of(bits):
    return [sum(((m >> i) & 1) << b for i, b in enumerate(bits)) for m in range(1, 1 << len(bits))]


def local_index(me, bits):
    return sum(bit_of(me, b) << i for i, b in enumerate(bits))


def tree(values):
    while len(values) > 1:
        values = [a + b for a, b in zip(values[::2], values[1::2])] + values[len(values) & ~1 :]
    return values[0]


def scatter_sum(x, me, bits, total):
    here = local_index(me, bits)
    n = 1 << len(bits)
    x = x.reshape((n, x.shape[0] // n) + x.shape[1:])
    parts = [lax.dynamic_index_in_dim(x, here, 0, False)]
    for m, mask in enumerate(masks_of(bits), 1):
        parts.append(xor_permute(lax.dynamic_index_in_dim(x, here ^ m, 0, False), mask, total))
    return tree(parts)


def direct_sum(x, bits, total):
    return tree([x] + [xor_permute(x, mask, total) for mask in masks_of(bits)])


def gather(x, me, bits, total):
    here = local_index(me, bits)
    parts = jnp.stack([x] + [xor_permute(x, mask, total) for mask in masks_of(bits)])
    return jnp.concatenate(
        [lax.dynamic_index_in_dim(parts, here ^ j, 0, False) for j in range(1 << len(bits))]
    )


def summed_halves(keep, send, n_ty, n_tx):
    total = n_ty * n_tx
    me = lax.axis_index("ty") * n_tx + lax.axis_index("tx")
    levels = total.bit_length() - 1
    half = keep + xor_permute(send, 1, total)
    tx_bits = n_tx.bit_length() - 1
    bits = [b for b in (tx_bits, 1) if b < levels]
    rest = [b for b in range(1, levels) if b not in bits]
    half = scatter_sum(half, me, bits, total)
    for i in range(0, len(rest), 2):
        half = direct_sum(half, rest[i : i + 2], total)
    half = gather(half, me, bits, total)
    return half, xor_permute(half, 1, total)


def per_device(n_ty, n_tx, tables, object_field, probe, intensities, positions):
    win, modes = probe.shape[-1], probe.shape[1]
    margin, tile, scans = win // 2, object_field.shape[-1], positions.shape[2]
    spots = positions.reshape(scans, 2)
    measured = intensities.reshape(scans, win, win)
    right, left = (jnp.asarray(t) for t in tables)
    match_y, match_x = pairings(n_ty), pairings(n_tx)
    n_y, n_x = len(match_y), len(match_x)
    odd_y = lax.axis_index("ty") % 2

    def swap(x, pairs_y, pairs_x):
        return lax.ppermute(x, AXES, flat_pairs(pairs_y, pairs_x, n_ty, n_tx))

    def rows_for(x, i, count, low, high):
        start = jnp.where(odd_y == i, high, low)
        return lax.dynamic_slice_in_dim(x, start, count, 1)

    tx_in = [swap(object_field, None, px) for px in match_x]
    rims = [rows_for(object_field, i, margin, 0, tile - margin) for i in range(n_y)]
    ty_in = [swap(rims[i], py, None) for i, py in enumerate(match_y)]
    corners = [swap(rims[i], py, px) for i, py in enumerate(match_y) for px in match_x]

    half_shape = (modes, win + WEIGHT_ROWS, win)
    grid_shape = (2, 2 * tile + SUBLANES, 2 * tile)
    msg_shape = (2, 2 * tile, tile)
    ext, keep, send, grid, *msgs = call(
        functools.partial(first_kernel, n_y, n_x, margin),
        [grid_shape, half_shape, half_shape, grid_shape] + [msg_shape] * n_x,
        [spots, object_field, probe, measured, right, left, *ty_in, *tx_in, *corners],
        [(2 * modes, win, win)],
    )
    own, other = summed_halves(keep, send, n_ty, n_tx)
    tx_in = [swap(m, None, px) for m, px in zip(msgs, match_x)]
    odd_x = lax.axis_index("tx") % 2
    lane = lax.broadcasted_iota(jnp.int32, (1, 1, tile), 2)
    low = jnp.where(lane < margin, 0, 1) == odd_x
    second = tx_in[1] if n_x > 1 else jnp.zeros(msg_shape, F32)
    extra = jnp.concatenate(
        [jnp.where(low, second, tx_in[0]), jnp.where(low, tx_in[0], second)], axis=2
    ) if n_x else jnp.zeros((2, 2 * tile, 2 * tile), F32)
    wide = grid[:, : 2 * tile, :] + extra
    bands = [rows_for(wide, i, tile, 0, tile) for i in range(n_y)]
    ty_in = [swap(bands[i], py, None) for i, py in enumerate(match_y)]
    tile_mid, probe_mid, keep, send, grid = call(
        functools.partial(second_kernel, n_y, n_x, n_ty, n_tx, margin),
        [object_field.shape, probe.shape, half_shape, half_shape, grid_shape],
        [spots, ext, grid, probe, measured, right, left, own, other, *tx_in, *ty_in],
        [grid_shape, (2 * modes, win, win)],
    )
    own, other = summed_halves(keep, send, n_ty, n_tx)
    edge = grid[:, : 2 * tile, tile:]
    tx_in = [swap(edge, None, px) for px in match_x]
    mid = grid[:, : 2 * tile, :tile]
    if n_x:
        second = tx_in[1] if n_x > 1 else jnp.zeros(msg_shape, F32)
        mid = mid + jnp.where(low, second, tx_in[0])
    bands = [rows_for(mid, i, margin, 0, 2 * tile - margin) for i in range(n_y)]
    ty_in = [swap(bands[i], py, None) for i, py in enumerate(match_y)]
    return call(
        functools.partial(last_kernel, n_y, n_x, margin),
        [object_field.shape, probe.shape],
        [tile_mid, mid, probe_mid, own, other, *ty_in],
    )


def solution(mesh):
    n_ty, n_tx = mesh.shape["ty"], mesh.shape["tx"]
    placed = (P(None, "ty", "tx"), P(), P("ty", "tx", None, None, None), P("ty", "tx", None, None))

    def run(object_field, probe, intensities, positions):
        tables = dft_blocks(probe.shape[-1])
        return jax.shard_map(
            functools.partial(per_device, n_ty, n_tx, tables),
            mesh=mesh,
            in_specs=placed,
            out_specs=(P(None, "ty", "tx"), P()),
            check_vma=False,
        )(object_field, probe, intensities, positions)

    return run
```

profile of v0, /device:TPU:4, one launch (start us, length us, event | category | flops | bytes accessed | tf_op | source)
XLA Modules:
  0.0 103.8 jit_solution(3812922033263143622)
XLA Ops:
  0.6 0.1 collective-permute-start.1
  0.7 1.9 %collective-permute-start.2 = (f32[2,128,128]{2,1,0:T(8,128)}, f32[2,128,128]{2,1,0:T(8,128)S(1)}, u32[]{:S(2)}, u32[]{:S(2)}) collective-permute-start(f32[2,128,128]{2,1,0:T(8,128)} %obj_ref.1), channel_id=1, source_target_pairs={{1,2},{2,1},{3,4},{4,3},{5,6},{6,5},{7,8},{8,7},{9,10},{10,9},{11,... | collective-permute-start | bytes 393224 | tf_op jit(solution)/shard_map/ppermute | solution.py:365
  2.7 0.9 constant_dynamic-slice_fusion.7
  3.5 4.7 %collective-permute-start.4 = (f32[2,64,128]{2,1,0:T(8,128)S(1)}, f32[2,64,128]{2,1,0:T(8,128)S(1)}, u32[]{:S(2)}, u32[]{:S(2)}) collective-permute-start(f32[2,64,128]{2,1,0:T(8,128)S(1)} %constant_dynamic-slice_fusion.7), channel_id=1, source_target_pairs={{1,18},{2,17},{3,20},{4,19},{5,22},{6,21},{7,24},{8,23},{9,26},{10... | collective-permute-start | bytes 196616 | tf_op jit(solution)/shard_map/ppermute | solution.py:365
  8.2 1.6 %collective-permute-start.3 = (f32[2,64,128]{2,1,0:T(8,128)S(1)}, f32[2,64,128]{2,1,0:T(8,128)S(1)}, u32[]{:S(2)}, u32[]{:S(2)}) collective-permute-start(f32[2,64,128]{2,1,0:T(8,128)S(1)} %constant_dynamic-slice_fusion.7), channel_id=1, source_target_pairs={{0,17},{1,16},{2,19},{3,18},{4,21},{5,20},{6,23},{7,22},{8,25},{9,... | collective-permute-start | bytes 196616 | tf_op jit(solution)/shard_map/ppermute | solution.py:365
  9.8 1.5 %collective-permute-start = (f32[2,64,128]{2,1,0:T(8,128)S(1)}, f32[2,64,128]{2,1,0:T(8,128)S(1)}, u32[]{:S(2)}, u32[]{:S(2)}) collective-permute-start(f32[2,64,128]{2,1,0:T(8,128)S(1)} %constant_dynamic-slice_fusion.7), channel_id=1, source_target_pairs={{0,16},{1,17},{2,18},{3,19},{4,20},{5,21},{6,22},{7,23},{8,24},{9,... | collective-permute-start | bytes 196616 | tf_op jit(solution)/shard_map/ppermute | solution.py:365
  11.3 0.1 copy.9.pos_ref
  11.4 0.8 collective-permute-done.3.rest_3_
  12.2 2.3 %collective-permute-done.rest_0_ = f32[2,64,128]{2,1,0:T(8,128)S(1)} collective-permute-done((f32[2,64,128]{2,1,0:T(8,128)S(1)}, f32[2,64,128]{2,1,0:T(8,128)S(1)}, u32[]{:S(2)}, u32[]{:S(2)}) %collective-permute-start) | collective-permute-done | bytes 65568 | tf_op jit(solution)/shard_map/ppermute | solution.py:365
  14.5 0.0 collective-permute-done.1.rest_1_
  14.5 0.0 collective-permute-done.2.rest_2_
  14.5 0.0 copy-start
  14.5 1.0 copy-done
  15.5 0.9 copy-done.2
  16.5 0.9 copy-done.4
  17.4 0.9 copy-done.6
  18.4 5.5 %shard_map.77 = (f32[2,264,256]{2,1,0:T(8,128)S(1)}, f32[4,136,128]{2,1,0:T(8,128)S(1)}, f32[4,136,128]{2,1,0:T(8,128)S(1)}, f32[2,264,256]{2,1,0:T(8,128)S(1)},...) custom-call(s32[3,2]{1,0:T(4,128)S(1)} %copy.9.pos_ref, f32[2,128,128]{2,1,0:T(8,128)S(1)} %copy-done.8, ...), custom_call_target="tpu_custom_call" | custom-call | tf_op jit(solution)/shard_map/pallas_call | solution.py:289
  23.9 0.1 collective-permute-start.5
  24.0 1.5 %collective-permute-done.5 = f32[4,136,128]{2,1,0:T(8,128)S(1)} collective-permute-done((f32[4,136,128]{2,1,0:T(8,128)S(1)}, f32[4,136,128]{2,1,0:T(8,128)S(1)}, u32[]{:S(2)}, u32[]{:S(2)}) %collective-permute-start.5) | collective-permute-done | bytes 278560 | tf_op jit(solution)/shard_map/ppermute | solution.py:54
  25.6 1.2 %collective-permute-start.6 = (f32[1,136,128]{2,1,0:T(8,128)S(1)}, f32[1,136,128]{2,1,0:T(8,128)S(1)}, u32[]{:S(2)}, u32[]{:S(2)}) collective-permute-start(f32[1,136,128]{2,1,0:T(8,128)S(1)} %get-tuple-element.37), channel_id=1, source_target_pairs={{0,16},{1,17},{2,18},{3,19},{4,20},{5,21},{6,22},{7,23},{8,24},{9,... | collective-permute-start | bytes 208904 | tf_op jit(solution)/shard_map/ppermute | solution.py:54
  26.8 0.7 collective-permute-start.8
  27.4 1.7 %collective-permute-start.7 = (f32[1,136,128]{2,1,0:T(8,128)S(1)}, f32[1,136,128]{2,1,0:T(8,128)S(1)}, u32[]{:S(2)}, u32[]{:S(2)}) collective-permute-start(f32[1,136,128]{2,1,0:T(8,128)S(1)} %get-tuple-element.39), channel_id=1, source_target_pairs={{0,2},{1,3},{2,0},{3,1},{4,6},{5,7},{6,4},{7,5},{8,10},{9,11},{10,... | collective-permute-start | bytes 208904 | tf_op jit(solution)/shard_map/ppermute | solution.py:54
  29.1 2.3 %collective-permute-start.17 = (f32[2,256,128]{2,1,0:T(8,128)S(1)}, f32[2,256,128]{2,1,0:T(8,128)S(1)}, u32[]{:S(2)}, u32[]{:S(2)}) collective-permute-start(f32[2,256,128]{2,1,0:T(8,128)S(1)} %get-tuple-element.18), channel_id=1, source_target_pairs={{1,2},{2,1},{3,4},{4,3},{5,6},{6,5},{7,8},{8,7},{9,10},{10,9},{11,... | collective-permute-start | bytes 786440 | tf_op jit(solution)/shard_map/ppermute | solution.py:365
  31.5 0.5 collective-permute-done.8
  32.0 0.5 collective-permute-done.7
  32.6 3.9 %collective-permute-start.11 = (f32[1,136,128]{2,1,0:T(8,128)S(1)}, f32[1,136,128]{2,1,0:T(8,128)S(1)}, u32[]{:S(2)}, u32[]{:S(2)}) collective-permute-start(f32[1,136,128]{2,1,0:T(8,128)S(1)} %add_add_fusion.3), channel_id=1, source_target_pairs={{0,12},{1,13},{2,14},{3,15},{4,8},{5,9},{6,10},{7,11},{8,4},{9,5},... | collective-permute-start | bytes 208904 | tf_op jit(solution)/shard_map/ppermute | solution.py:54
  36.5 0.1 collective-permute-start.10
  36.6 0.5 collective-permute-start.9
  37.2 2.4 %collective-permute-done.11 = f32[1,136,128]{2,1,0:T(8,128)S(1)} collective-permute-done((f32[1,136,128]{2,1,0:T(8,128)S(1)}, f32[1,136,128]{2,1,0:T(8,128)S(1)}, u32[]{:S(2)}, u32[]{:S(2)}) %collective-permute-start.11) | collective-permute-done | bytes 69664 | tf_op jit(solution)/shard_map/ppermute | solution.py:54
  39.6 3.5 %collective-permute-done.10 = f32[1,136,128]{2,1,0:T(8,128)S(1)} collective-permute-done((f32[1,136,128]{2,1,0:T(8,128)S(1)}, f32[1,136,128]{2,1,0:T(8,128)S(1)}, u32[]{:S(2)}, u32[]{:S(2)}) %collective-permute-start.10) | collective-permute-done | bytes 69664 | tf_op jit(solution)/shard_map/ppermute | solution.py:54
  43.2 3.8 %collective-permute-start.14 = (f32[1,136,128]{2,1,0:T(8,128)S(1)}, f32[1,136,128]{2,1,0:T(8,128)S(1)}, u32[]{:S(2)}, u32[]{:S(2)}) collective-permute-start(f32[1,136,128]{2,1,0:T(8,128)S(1)} %add_add_fusion.2), channel_id=1, source_target_pairs={{0,18},{1,19},{2,16},{3,17},{4,22},{5,23},{6,20},{7,21},{8,26},{9,... | collective-permute-start | bytes 208904 | tf_op jit(solution)/shard_map/ppermute | solution.py:54
  47.0 0.6 collective-permute-start.12
  47.7 1.6 %collective-permute-done.14 = f32[1,136,128]{2,1,0:T(8,128)S(1)} collective-permute-done((f32[1,136,128]{2,1,0:T(8,128)S(1)}, f32[1,136,128]{2,1,0:T(8,128)S(1)}, u32[]{:S(2)}, u32[]{:S(2)}) %collective-permute-start.14) | collective-permute-done | bytes 69664 | tf_op jit(solution)/shard_map/ppermute | solution.py:54
  49.3 2.0 %collective-permute-done.13 = f32[1,136,128]{2,1,0:T(8,128)S(1)} collective-permute-done((f32[1,136,128]{2,1,0:T(8,128)S(1)}, f32[1,136,128]{2,1,0:T(8,128)S(1)}, u32[]{:S(2)}, u32[]{:S(2)}) %collective-permute-start.13) | collective-permute-done | bytes 69664 | tf_op jit(solution)/shard_map/ppermute | solution.py:54
  51.4 0.0 copy-start.7
  51.4 0.1 collective-permute-start.15
  51.5 0.0 copy-start.1
  51.5 0.0 copy-start.3
  51.5 0.0 copy-start.5
  51.6 0.8 collective-permute-start.18
  52.4 7.9 %collective-permute-done.18.rest_2_ = f32[2,128,256]{2,1,0:T(8,128)S(1)} collective-permute-done((f32[2,128,256]{2,1,0:T(8,128)S(1)}, f32[2,128,256]{2,1,0:T(8,128)S(1)}, u32[]{:S(2)}, u32[]{:S(2)}) %collective-permute-start.18) | collective-permute-done | bytes 262176 | tf_op jit(solution)/shard_map/ppermute | solution.py:365
  60.3 5.6 %shard_map.78 = (f32[2,128,128]{2,1,0:T(8,128)S(1)}, f32[2,4,128,128]{3,2,1,0:T(8,128)S(1)}, f32[4,136,128]{2,1,0:T(8,128)S(1)}, f32[4,136,128]{2,1,0:T(8,128)S(1)}, f32[2,264,256]{2,1,0:T(8,128)S(1)}) custom-call(s32[3,2]{1,0:T(4,128)S(1)} %copy.9.pos_ref, f32[2,264,256]{2,1,0:T(8,128)S(1)} %get-tuple-element.13.old_ref, ...), custom_call_target="tpu_custom_call" | custom-call | tf_op jit(solution)/shard_map/pallas_call | solution.py:289
  65.9 0.1 collective-permute-start.21
  66.0 1.5 %collective-permute-done.21 = f32[4,136,128]{2,1,0:T(8,128)S(1)} collective-permute-done((f32[4,136,128]{2,1,0:T(8,128)S(1)}, f32[4,136,128]{2,1,0:T(8,128)S(1)}, u32[]{:S(2)}, u32[]{:S(2)}) %collective-permute-start.21) | collective-permute-done | bytes 278560 | tf_op jit(solution)/shard_map/ppermute | solution.py:54
  67.6 0.8 collective-permute-start.22
  68.5 2.7 %collective-permute-start.24 = (f32[1,136,128]{2,1,0:T(8,128)S(1)}, f32[1,136,128]{2,1,0:T(8,128)S(1)}, u32[]{:S(2)}, u32[]{:S(2)}) collective-permute-start(f32[1,136,128]{2,1,0:T(8,128)S(1)} %get-tuple-element.31), channel_id=1, source_target_pairs={{0,18},{1,19},{2,16},{3,17},{4,22},{5,23},{6,20},{7,21},{8,26},{9,... | collective-permute-start | bytes 208904 | tf_op jit(solution)/shard_map/ppermute | solution.py:54
  71.2 0.8 collective-permute-done.22
  72.0 3.0 %collective-permute-done.24 = f32[1,136,128]{2,1,0:T(8,128)S(1)} collective-permute-done((f32[1,136,128]{2,1,0:T(8,128)S(1)}, f32[1,136,128]{2,1,0:T(8,128)S(1)}, u32[]{:S(2)}, u32[]{:S(2)}) %collective-permute-start.24) | collective-permute-done | bytes 69664 | tf_op jit(solution)/shard_map/ppermute | solution.py:54
  75.0 1.0 collective-permute-done.23
  76.0 1.1 %collective-permute-start.27 = (f32[1,136,128]{2,1,0:T(8,128)S(1)}, f32[1,136,128]{2,1,0:T(8,128)S(1)}, u32[]{:S(2)}, u32[]{:S(2)}) collective-permute-start(f32[1,136,128]{2,1,0:T(8,128)S(1)} %add_add_fusion.1), channel_id=1, source_target_pairs={{0,12},{1,13},{2,14},{3,15},{4,8},{5,9},{6,10},{7,11},{8,4},{9,5},... | collective-permute-start | bytes 208904 | tf_op jit(solution)/shard_map/ppermute | solution.py:54
  77.1 0.2 collective-permute-start.26
  77.3 3.1 %collective-permute-start.25 = (f32[1,136,128]{2,1,0:T(8,128)S(1)}, f32[1,136,128]{2,1,0:T(8,128)S(1)}, u32[]{:S(2)}, u32[]{:S(2)}) collective-permute-start(f32[1,136,128]{2,1,0:T(8,128)S(1)} %add_add_fusion.1), channel_id=1, source_target_pairs={{0,4},{1,5},{2,6},{3,7},{4,0},{5,1},{6,2},{7,3},{8,12},{9,13},{10,... | collective-permute-start | bytes 208904 | tf_op jit(solution)/shard_map/ppermute | solution.py:54
  80.4 2.6 %collective-permute-done.27 = f32[1,136,128]{2,1,0:T(8,128)S(1)} collective-permute-done((f32[1,136,128]{2,1,0:T(8,128)S(1)}, f32[1,136,128]{2,1,0:T(8,128)S(1)}, u32[]{:S(2)}, u32[]{:S(2)}) %collective-permute-start.27) | collective-permute-done | bytes 69664 | tf_op jit(solution)/shard_map/ppermute | solution.py:54
  83.1 1.1 %collective-permute-done.26 = f32[1,136,128]{2,1,0:T(8,128)S(1)} collective-permute-done((f32[1,136,128]{2,1,0:T(8,128)S(1)}, f32[1,136,128]{2,1,0:T(8,128)S(1)}, u32[]{:S(2)}, u32[]{:S(2)}) %collective-permute-start.26) | collective-permute-done | bytes 69664 | tf_op jit(solution)/shard_map/ppermute | solution.py:54
  84.2 0.7 collective-permute-start.30
  84.9 1.6 %collective-permute-start.29 = (f32[1,136,128]{2,1,0:T(8,128)S(1)}, f32[1,136,128]{2,1,0:T(8,128)S(1)}, u32[]{:S(2)}, u32[]{:S(2)}) collective-permute-start(f32[1,136,128]{2,1,0:T(8,128)S(1)} %add_add_fusion), channel_id=1, source_target_pairs={{0,2},{1,3},{2,0},{3,1},{4,6},{5,7},{6,4},{7,5},{8,10},{9,11},{10,... | collective-permute-start | bytes 208904 | tf_op jit(solution)/shard_map/ppermute | solution.py:54
  86.5 1.2 %collective-permute-start.28 = (f32[1,136,128]{2,1,0:T(8,128)S(1)}, f32[1,136,128]{2,1,0:T(8,128)S(1)}, u32[]{:S(2)}, u32[]{:S(2)}) collective-permute-start(f32[1,136,128]{2,1,0:T(8,128)S(1)} %add_add_fusion), channel_id=1, source_target_pairs={{0,16},{1,17},{2,18},{3,19},{4,20},{5,21},{6,22},{7,23},{8,24},{9,... | collective-permute-start | bytes 208904 | tf_op jit(solution)/shard_map/ppermute | solution.py:54
  87.8 0.1 collective-permute-start.20
  87.9 3.1 %collective-permute-start.19 = (f32[2,256,128]{2,1,0:T(8,128)S(1)}, f32[2,256,128]{2,1,0:T(8,128)S(1)}, u32[]{:S(2)}, u32[]{:S(2)}) collective-permute-start(f32[2,256,128]{2,1,0:T(8,128)S(1)} %slice.11), channel_id=1, source_target_pairs={{1,2},{2,1},{3,4},{4,3},{5,6},{6,5},{7,8},{8,7},{9,10},{10,9},{11,... | collective-permute-start | bytes 786440 | tf_op jit(solution)/shard_map/ppermute | solution.py:365
  91.1 0.1 collective-permute-start.31
  91.2 7.2 %collective-permute-done.19 = f32[2,256,128]{2,1,0:T(8,128)S(1)} collective-permute-done((f32[2,256,128]{2,1,0:T(8,128)S(1)}, f32[2,256,128]{2,1,0:T(8,128)S(1)}, u32[]{:S(2)}, u32[]{:S(2)}) %collective-permute-start.19) | collective-permute-done | bytes 262176 | tf_op jit(solution)/shard_map/ppermute | solution.py:365
  98.4 0.9 collective-permute-start.32
  99.3 3.5 %collective-permute-done.32.rest_0_ = f32[2,64,128]{2,1,0:T(8,128)S(1)} collective-permute-done((f32[2,64,128]{2,1,0:T(8,128)S(1)}, f32[2,64,128]{2,1,0:T(8,128)S(1)}, u32[]{:S(2)}, u32[]{:S(2)}) %collective-permute-start.32) | collective-permute-done | bytes 65568 | tf_op jit(solution)/shard_map/ppermute | solution.py:365
  102.8 1.0 shard_map.79
  (48 shorter events, 0.6 us)
Async XLA Ops:
  0.6 13.8 %copy-start.8 = (f32[2,128,128]{2,1,0:T(8,128)S(1)}, f32[2,128,128]{2,1,0:T(8,128)}, u32[]{:S(2)}) copy-start(f32[2,128,128]{2,1,0:T(8,128)} %obj_ref.1) | copy-start | bytes 393220
  0.6 13.8 %collective-permute-start.1 = (f32[2,128,128]{2,1,0:T(8,128)}, f32[2,128,128]{2,1,0:T(8,128)S(1)}, u32[]{:S(2)}, u32[]{:S(2)}) collective-permute-start(f32[2,128,128]{2,1,0:T(8,128)} %obj_ref.1), channel_id=1, source_target_pairs={{0,1},{1,0},{2,3},{3,2},{4,5},{5,4},{6,7},{7,6},{8,9},{9,8},{10,11... | collective-permute-start | bytes 393224 | tf_op jit(solution)/shard_map/ppermute | solution.py:365
  0.7 13.8 %collective-permute-start.2 = (f32[2,128,128]{2,1,0:T(8,128)}, f32[2,128,128]{2,1,0:T(8,128)S(1)}, u32[]{:S(2)}, u32[]{:S(2)}) collective-permute-start(f32[2,128,128]{2,1,0:T(8,128)} %obj_ref.1), channel_id=1, source_target_pairs={{1,2},{2,1},{3,4},{4,3},{5,6},{6,5},{7,8},{8,7},{9,10},{10,9},{11,... | collective-permute-start | bytes 393224 | tf_op jit(solution)/shard_map/ppermute | solution.py:365
  3.5 7.8 %copy-start.9 = (s32[1,1,3,2]{2,3,1,0:T(2,128)S(1)}, s32[1,1,3,2]{2,3,1,0:T(2,128)}, u32[]{:S(2)}) copy-start(s32[1,1,3,2]{2,3,1,0:T(2,128)} %param.9) | copy-start | bytes 76
  3.5 7.9 %collective-permute-start.4 = (f32[2,64,128]{2,1,0:T(8,128)S(1)}, f32[2,64,128]{2,1,0:T(8,128)S(1)}, u32[]{:S(2)}, u32[]{:S(2)}) collective-permute-start(f32[2,64,128]{2,1,0:T(8,128)S(1)} %constant_dynamic-slice_fusion.7), channel_id=1, source_target_pairs={{1,18},{2,17},{3,20},{4,19},{5,22},{6,21},{7,24},{8,23},{9,26},{10... | collective-permute-start | bytes 196616 | tf_op jit(solution)/shard_map/ppermute | solution.py:365
  8.2 4.0 %collective-permute-start.3 = (f32[2,64,128]{2,1,0:T(8,128)S(1)}, f32[2,64,128]{2,1,0:T(8,128)S(1)}, u32[]{:S(2)}, u32[]{:S(2)}) collective-permute-start(f32[2,64,128]{2,1,0:T(8,128)S(1)} %constant_dynamic-slice_fusion.7), channel_id=1, source_target_pairs={{0,17},{1,16},{2,19},{3,18},{4,21},{5,20},{6,23},{7,22},{8,25},{9,... | collective-permute-start | bytes 196616 | tf_op jit(solution)/shard_map/ppermute | solution.py:365
  9.8 4.6 %collective-permute-start = (f32[2,64,128]{2,1,0:T(8,128)S(1)}, f32[2,64,128]{2,1,0:T(8,128)S(1)}, u32[]{:S(2)}, u32[]{:S(2)}) collective-permute-start(f32[2,64,128]{2,1,0:T(8,128)S(1)} %constant_dynamic-slice_fusion.7), channel_id=1, source_target_pairs={{0,16},{1,17},{2,18},{3,19},{4,20},{5,21},{6,22},{7,23},{8,24},{9,... | collective-permute-start | bytes 196616 | tf_op jit(solution)/shard_map/ppermute | solution.py:365
  14.5 1.0 %copy-start = (f32[2,4,128,128]{3,2,1,0:T(8,128)S(1)}, f32[2,4,128,128]{3,2,1,0:T(8,128)}, u32[]{:S(2)}) copy-start(f32[2,4,128,128]{3,2,1,0:T(8,128)} %probe_ref.3) | copy-start | bytes 1572868
  15.5 0.9 copy-start.2
  16.5 0.9 copy-start.4
  17.4 0.9 copy-start.6
  23.9 1.6 %collective-permute-start.5 = (f32[4,136,128]{2,1,0:T(8,128)S(1)}, f32[4,136,128]{2,1,0:T(8,128)S(1)}, u32[]{:S(2)}, u32[]{:S(2)}) collective-permute-start(f32[4,136,128]{2,1,0:T(8,128)S(1)} %get-tuple-element.16), channel_id=1, source_target_pairs={{0,1},{1,0},{2,3},{3,2},{4,5},{5,4},{6,7},{7,6},{8,9},{9,8},{10,11... | collective-permute-start | bytes 835592 | tf_op jit(solution)/shard_map/ppermute | solution.py:54
  25.6 5.9 %collective-permute-start.6 = (f32[1,136,128]{2,1,0:T(8,128)S(1)}, f32[1,136,128]{2,1,0:T(8,128)S(1)}, u32[]{:S(2)}, u32[]{:S(2)}) collective-permute-start(f32[1,136,128]{2,1,0:T(8,128)S(1)} %get-tuple-element.37), channel_id=1, source_target_pairs={{0,16},{1,17},{2,18},{3,19},{4,20},{5,21},{6,22},{7,23},{8,24},{9,... | collective-permute-start | bytes 208904 | tf_op jit(solution)/shard_map/ppermute | solution.py:54
  26.8 5.3 %collective-permute-start.8 = (f32[1,136,128]{2,1,0:T(8,128)S(1)}, f32[1,136,128]{2,1,0:T(8,128)S(1)}, u32[]{:S(2)}, u32[]{:S(2)}) collective-permute-start(f32[1,136,128]{2,1,0:T(8,128)S(1)} %get-tuple-element.38), channel_id=1, source_target_pairs={{0,18},{1,19},{2,16},{3,17},{4,22},{5,23},{6,20},{7,21},{8,26},{9,... | collective-permute-start | bytes 208904 | tf_op jit(solution)/shard_map/ppermute | solution.py:54
  27.4 5.2 %collective-permute-start.7 = (f32[1,136,128]{2,1,0:T(8,128)S(1)}, f32[1,136,128]{2,1,0:T(8,128)S(1)}, u32[]{:S(2)}, u32[]{:S(2)}) collective-permute-start(f32[1,136,128]{2,1,0:T(8,128)S(1)} %get-tuple-element.39), channel_id=1, source_target_pairs={{0,2},{1,3},{2,0},{3,1},{4,6},{5,7},{6,4},{7,5},{8,10},{9,11},{10,... | collective-permute-start | bytes 208904 | tf_op jit(solution)/shard_map/ppermute | solution.py:54
  29.1 18.5 %collective-permute-start.16 = (f32[2,256,128]{2,1,0:T(8,128)S(1)}, f32[2,256,128]{2,1,0:T(8,128)S(1)}, u32[]{:S(2)}, u32[]{:S(2)}) collective-permute-start(f32[2,256,128]{2,1,0:T(8,128)S(1)} %get-tuple-element.17), channel_id=1, source_target_pairs={{0,1},{1,0},{2,3},{3,2},{4,5},{5,4},{6,7},{7,6},{8,9},{9,8},{10,11... | collective-permute-start | bytes 786440 | tf_op jit(solution)/shard_map/ppermute | solution.py:365
  29.1 18.5 %collective-permute-start.17 = (f32[2,256,128]{2,1,0:T(8,128)S(1)}, f32[2,256,128]{2,1,0:T(8,128)S(1)}, u32[]{:S(2)}, u32[]{:S(2)}) collective-permute-start(f32[2,256,128]{2,1,0:T(8,128)S(1)} %get-tuple-element.18), channel_id=1, source_target_pairs={{1,2},{2,1},{3,4},{4,3},{5,6},{6,5},{7,8},{8,7},{9,10},{10,9},{11,... | collective-permute-start | bytes 786440 | tf_op jit(solution)/shard_map/ppermute | solution.py:365
  32.6 7.1 %collective-permute-start.11 = (f32[1,136,128]{2,1,0:T(8,128)S(1)}, f32[1,136,128]{2,1,0:T(8,128)S(1)}, u32[]{:S(2)}, u32[]{:S(2)}) collective-permute-start(f32[1,136,128]{2,1,0:T(8,128)S(1)} %add_add_fusion.3), channel_id=1, source_target_pairs={{0,12},{1,13},{2,14},{3,15},{4,8},{5,9},{6,10},{7,11},{8,4},{9,5},... | collective-permute-start | bytes 208904 | tf_op jit(solution)/shard_map/ppermute | solution.py:54
  36.5 6.7 %collective-permute-start.10 = (f32[1,136,128]{2,1,0:T(8,128)S(1)}, f32[1,136,128]{2,1,0:T(8,128)S(1)}, u32[]{:S(2)}, u32[]{:S(2)}) collective-permute-start(f32[1,136,128]{2,1,0:T(8,128)S(1)} %add_add_fusion.3), channel_id=1, source_target_pairs={{0,8},{1,9},{2,10},{3,11},{4,12},{5,13},{6,14},{7,15},{8,0},{9,1},... | collective-permute-start | bytes 208904 | tf_op jit(solution)/shard_map/ppermute | solution.py:54
  36.6 6.6 %collective-permute-start.9 = (f32[1,136,128]{2,1,0:T(8,128)S(1)}, f32[1,136,128]{2,1,0:T(8,128)S(1)}, u32[]{:S(2)}, u32[]{:S(2)}) collective-permute-start(f32[1,136,128]{2,1,0:T(8,128)S(1)} %add_add_fusion.3), channel_id=1, source_target_pairs={{0,4},{1,5},{2,6},{3,7},{4,0},{5,1},{6,2},{7,3},{8,12},{9,13},{10,... | collective-permute-start | bytes 208904 | tf_op jit(solution)/shard_map/ppermute | solution.py:54
  43.2 6.1 %collective-permute-start.14 = (f32[1,136,128]{2,1,0:T(8,128)S(1)}, f32[1,136,128]{2,1,0:T(8,128)S(1)}, u32[]{:S(2)}, u32[]{:S(2)}) collective-permute-start(f32[1,136,128]{2,1,0:T(8,128)S(1)} %add_add_fusion.2), channel_id=1, source_target_pairs={{0,18},{1,19},{2,16},{3,17},{4,22},{5,23},{6,20},{7,21},{8,26},{9,... | collective-permute-start | bytes 208904 | tf_op jit(solution)/shard_map/ppermute | solution.py:54
  47.0 4.3 %collective-permute-start.13 = (f32[1,136,128]{2,1,0:T(8,128)S(1)}, f32[1,136,128]{2,1,0:T(8,128)S(1)}, u32[]{:S(2)}, u32[]{:S(2)}) collective-permute-start(f32[1,136,128]{2,1,0:T(8,128)S(1)} %add_add_fusion.2), channel_id=1, source_target_pairs={{0,2},{1,3},{2,0},{3,1},{4,6},{5,7},{6,4},{7,5},{8,10},{9,11},{10,... | collective-permute-start | bytes 208904 | tf_op jit(solution)/shard_map/ppermute | solution.py:54
  47.0 4.3 %collective-permute-start.12 = (f32[1,136,128]{2,1,0:T(8,128)S(1)}, f32[1,136,128]{2,1,0:T(8,128)S(1)}, u32[]{:S(2)}, u32[]{:S(2)}) collective-permute-start(f32[1,136,128]{2,1,0:T(8,128)S(1)} %add_add_fusion.2), channel_id=1, source_target_pairs={{0,16},{1,17},{2,18},{3,19},{4,20},{5,21},{6,22},{7,23},{8,24},{9,... | collective-permute-start | bytes 208904 | tf_op jit(solution)/shard_map/ppermute | solution.py:54
  51.4 8.9 %copy-start.7 = (f32[1,1,3,128,128]{4,3,2,1,0:T(8,128)S(1)}, f32[1,1,3,128,128]{4,3,2,1,0:T(8,128)}, u32[]{:S(2)}) copy-start(f32[1,1,3,128,128]{4,3,2,1,0:T(8,128)} %param.8) | copy-start | bytes 589828
  51.4 8.9 %collective-permute-start.15 = (f32[4,136,128]{2,1,0:T(8,128)S(1)}, f32[4,136,128]{2,1,0:T(8,128)S(1)}, u32[]{:S(2)}, u32[]{:S(2)}) collective-permute-start(f32[4,136,128]{2,1,0:T(8,128)S(1)} %pad_maximum_fusion.1.own_ref), channel_id=1, source_target_pairs={{0,1},{1,0},{2,3},{3,2},{4,5},{5,4},{6,7},{7,6},{8,9},{9,8},{10,11... | collective-permute-start | bytes 835592 | tf_op jit(solution)/shard_map/ppermute | solution.py:54
  51.5 8.8 %copy-start.1 = (f32[2,4,128,128]{3,2,1,0:T(8,128)S(1)}, f32[2,4,128,128]{3,2,1,0:T(8,128)}, u32[]{:S(2)}) copy-start(f32[2,4,128,128]{3,2,1,0:T(8,128)} %probe_ref.3) | copy-start | bytes 1572868
  51.5 8.8 %copy-start.3 = (bf16[2,256,256]{2,1,0:T(8,128)(2,1)S(1)}, bf16[2,256,256]{2,1,0:T(8,128)(2,1)}, u32[]{:S(2)}) copy-start(bf16[2,256,256]{2,1,0:T(8,128)(2,1)} %constant.84.clone.left_ref) | copy-start | bytes 786436
  51.5 8.8 %copy-start.5 = (bf16[2,256,256]{2,1,0:T(8,128)(2,1)S(1)}, bf16[2,256,256]{2,1,0:T(8,128)(2,1)}, u32[]{:S(2)}) copy-start(bf16[2,256,256]{2,1,0:T(8,128)(2,1)} %constant.83.clone.right_ref) | copy-start | bytes 786436
  51.6 8.7 %collective-permute-start.18 = (f32[2,128,256]{2,1,0:T(8,128)S(1)}, f32[2,128,256]{2,1,0:T(8,128)S(1)}, u32[]{:S(2)}, u32[]{:S(2)}) collective-permute-start(f32[2,128,256]{2,1,0:T(8,128)S(1)} %fusion.1), channel_id=1, source_target_pairs={{0,16},{1,17},{2,18},{3,19},{4,20},{5,21},{6,22},{7,23},{8,24},{9,... | collective-permute-start | bytes 786440 | tf_op jit(solution)/shard_map/ppermute | solution.py:365
  65.9 1.6 %collective-permute-start.21 = (f32[4,136,128]{2,1,0:T(8,128)S(1)}, f32[4,136,128]{2,1,0:T(8,128)S(1)}, u32[]{:S(2)}, u32[]{:S(2)}) collective-permute-start(f32[4,136,128]{2,1,0:T(8,128)S(1)} %get-tuple-element.23), channel_id=1, source_target_pairs={{0,1},{1,0},{2,3},{3,2},{4,5},{5,4},{6,7},{7,6},{8,9},{9,8},{10,11... | collective-permute-start | bytes 835592 | tf_op jit(solution)/shard_map/ppermute | solution.py:54
  67.6 4.4 %collective-permute-start.22 = (f32[1,136,128]{2,1,0:T(8,128)S(1)}, f32[1,136,128]{2,1,0:T(8,128)S(1)}, u32[]{:S(2)}, u32[]{:S(2)}) collective-permute-start(f32[1,136,128]{2,1,0:T(8,128)S(1)} %get-tuple-element.30), channel_id=1, source_target_pairs={{0,16},{1,17},{2,18},{3,19},{4,20},{5,21},{6,22},{7,23},{8,24},{9,... | collective-permute-start | bytes 208904 | tf_op jit(solution)/shard_map/ppermute | solution.py:54
  68.5 6.5 %collective-permute-start.24 = (f32[1,136,128]{2,1,0:T(8,128)S(1)}, f32[1,136,128]{2,1,0:T(8,128)S(1)}, u32[]{:S(2)}, u32[]{:S(2)}) collective-permute-start(f32[1,136,128]{2,1,0:T(8,128)S(1)} %get-tuple-element.31), channel_id=1, source_target_pairs={{0,18},{1,19},{2,16},{3,17},{4,22},{5,23},{6,20},{7,21},{8,26},{9,... | collective-permute-start | bytes 208904 | tf_op jit(solution)/shard_map/ppermute | solution.py:54
  71.2 4.8 %collective-permute-start.23 = (f32[1,136,128]{2,1,0:T(8,128)S(1)}, f32[1,136,128]{2,1,0:T(8,128)S(1)}, u32[]{:S(2)}, u32[]{:S(2)}) collective-permute-start(f32[1,136,128]{2,1,0:T(8,128)S(1)} %get-tuple-element.32), channel_id=1, source_target_pairs={{0,2},{1,3},{2,0},{3,1},{4,6},{5,7},{6,4},{7,5},{8,10},{9,11},{10,... | collective-permute-start | bytes 208904 | tf_op jit(solution)/shard_map/ppermute | solution.py:54
  76.0 7.1 %collective-permute-start.27 = (f32[1,136,128]{2,1,0:T(8,128)S(1)}, f32[1,136,128]{2,1,0:T(8,128)S(1)}, u32[]{:S(2)}, u32[]{:S(2)}) collective-permute-start(f32[1,136,128]{2,1,0:T(8,128)S(1)} %add_add_fusion.1), channel_id=1, source_target_pairs={{0,12},{1,13},{2,14},{3,15},{4,8},{5,9},{6,10},{7,11},{8,4},{9,5},... | collective-permute-start | bytes 208904 | tf_op jit(solution)/shard_map/ppermute | solution.py:54
  77.1 7.1 %collective-permute-start.26 = (f32[1,136,128]{2,1,0:T(8,128)S(1)}, f32[1,136,128]{2,1,0:T(8,128)S(1)}, u32[]{:S(2)}, u32[]{:S(2)}) collective-permute-start(f32[1,136,128]{2,1,0:T(8,128)S(1)} %add_add_fusion.1), channel_id=1, source_target_pairs={{0,8},{1,9},{2,10},{3,11},{4,12},{5,13},{6,14},{7,15},{8,0},{9,1},... | collective-permute-start | bytes 208904 | tf_op jit(solution)/shard_map/ppermute | solution.py:54
  77.3 6.9 %collective-permute-start.25 = (f32[1,136,128]{2,1,0:T(8,128)S(1)}, f32[1,136,128]{2,1,0:T(8,128)S(1)}, u32[]{:S(2)}, u32[]{:S(2)}) collective-permute-start(f32[1,136,128]{2,1,0:T(8,128)S(1)} %add_add_fusion.1), channel_id=1, source_target_pairs={{0,4},{1,5},{2,6},{3,7},{4,0},{5,1},{6,2},{7,3},{8,12},{9,13},{10,... | collective-permute-start | bytes 208904 | tf_op jit(solution)/shard_map/ppermute | solution.py:54
  84.2 6.8 %collective-permute-start.30 = (f32[1,136,128]{2,1,0:T(8,128)S(1)}, f32[1,136,128]{2,1,0:T(8,128)S(1)}, u32[]{:S(2)}, u32[]{:S(2)}) collective-permute-start(f32[1,136,128]{2,1,0:T(8,128)S(1)} %add_add_fusion), channel_id=1, source_target_pairs={{0,18},{1,19},{2,16},{3,17},{4,22},{5,23},{6,20},{7,21},{8,26},{9,... | collective-permute-start | bytes 208904 | tf_op jit(solution)/shard_map/ppermute | solution.py:54
  84.9 6.0 %collective-permute-start.29 = (f32[1,136,128]{2,1,0:T(8,128)S(1)}, f32[1,136,128]{2,1,0:T(8,128)S(1)}, u32[]{:S(2)}, u32[]{:S(2)}) collective-permute-start(f32[1,136,128]{2,1,0:T(8,128)S(1)} %add_add_fusion), channel_id=1, source_target_pairs={{0,2},{1,3},{2,0},{3,1},{4,6},{5,7},{6,4},{7,5},{8,10},{9,11},{10,... | collective-permute-start | bytes 208904 | tf_op jit(solution)/shard_map/ppermute | solution.py:54
  86.5 4.4 %collective-permute-start.28 = (f32[1,136,128]{2,1,0:T(8,128)S(1)}, f32[1,136,128]{2,1,0:T(8,128)S(1)}, u32[]{:S(2)}, u32[]{:S(2)}) collective-permute-start(f32[1,136,128]{2,1,0:T(8,128)S(1)} %add_add_fusion), channel_id=1, source_target_pairs={{0,16},{1,17},{2,18},{3,19},{4,20},{5,21},{6,22},{7,23},{8,24},{9,... | collective-permute-start | bytes 208904 | tf_op jit(solution)/shard_map/ppermute | solution.py:54
  87.8 3.4 %collective-permute-start.20 = (f32[2,256,128]{2,1,0:T(8,128)S(1)}, f32[2,256,128]{2,1,0:T(8,128)S(1)}, u32[]{:S(2)}, u32[]{:S(2)}) collective-permute-start(f32[2,256,128]{2,1,0:T(8,128)S(1)} %slice.11), channel_id=1, source_target_pairs={{0,1},{1,0},{2,3},{3,2},{4,5},{5,4},{6,7},{7,6},{8,9},{9,8},{10,11... | collective-permute-start | bytes 786440 | tf_op jit(solution)/shard_map/ppermute | solution.py:365
  87.9 10.5 %collective-permute-start.19 = (f32[2,256,128]{2,1,0:T(8,128)S(1)}, f32[2,256,128]{2,1,0:T(8,128)S(1)}, u32[]{:S(2)}, u32[]{:S(2)}) collective-permute-start(f32[2,256,128]{2,1,0:T(8,128)S(1)} %slice.11), channel_id=1, source_target_pairs={{1,2},{2,1},{3,4},{4,3},{5,6},{6,5},{7,8},{8,7},{9,10},{10,9},{11,... | collective-permute-start | bytes 786440 | tf_op jit(solution)/shard_map/ppermute | solution.py:365
  91.1 11.7 %collective-permute-start.31 = (f32[4,136,128]{2,1,0:T(8,128)S(1)}, f32[4,136,128]{2,1,0:T(8,128)S(1)}, u32[]{:S(2)}, u32[]{:S(2)}) collective-permute-start(f32[4,136,128]{2,1,0:T(8,128)S(1)} %pad_maximum_fusion.3.own_ref), channel_id=1, source_target_pairs={{0,1},{1,0},{2,3},{3,2},{4,5},{5,4},{6,7},{7,6},{8,9},{9,8},{10,11... | collective-permute-start | bytes 835592 | tf_op jit(solution)/shard_map/ppermute | solution.py:54
  98.4 4.3 %collective-permute-start.32 = (f32[2,64,128]{2,1,0:T(8,128)S(1)}, f32[2,64,128]{2,1,0:T(8,128)S(1)}, u32[]{:S(2)}, u32[]{:S(2)}) collective-permute-start(f32[2,64,128]{2,1,0:T(8,128)S(1)} %constant_dynamic-slice_fusion), channel_id=1, source_target_pairs={{0,16},{1,17},{2,18},{3,19},{4,20},{5,21},{6,22},{7,23},{8,24},{9,... | collective-permute-start | bytes 196616 | tf_op jit(solution)/shard_map/ppermute | solution.py:365
where the time goes:
time: 104 us
  waiting for transfers between devices  43.9 us (42%)
  starting transfers between devices  41.3 us (40%)
  Pallas kernels  12.1 us (12%)
  local copies, waits for them, and re-layouts  5.06 us (5%)
    ppermute x22, starting transfers between devices, xor_permute(): return lax.ppermute(x, AXES, [(i, i ^ mask) for i in range(total)])  24.4 us
    ppermute x22, waiting for transfers between devices, xor_permute(): return lax.ppermute(x, AXES, [(i, i ^ mask) for i in range(total)])  22.3 us
    ppermute x11, waiting for transfers between devices, swap(): return lax.ppermute(x, AXES, flat_pairs(pairs_y, pairs_x, n_ty, n_tx))  21.6 us
    ppermute x11, starting transfers between devices, swap(): return lax.ppermute(x, AXES, flat_pairs(pairs_y, pairs_x, n_ty, n_tx))  16.9 us
    pallas_call x3, Pallas kernels, call(): pl.pallas_call(kernel, out_shape=shapes, in_specs=[smem if x.dtype == jnp...  12.1 us
    unnamed x20, local copies, waits for them, and re-layouts  3.9 us
  transfers between devices with their start and end apart: 33, of which 18 were waited for; matrix products, arithmetic and copies ran while one was open for 1% of the time, Pallas kernels for 0%

commit v1 on v0

--- a/solution.py
+++ b/solution.py
@@ -18,14 +18,13 @@
 BF16 = jnp.bfloat16
 
 
-def dft_blocks(win):
+def dft_table(win):
     line = np.arange(win, dtype=np.int64)
     angle = (line[:, None] * line[None, :] % win) * (2.0 * np.pi / win)
-    c, s = np.cos(angle) / np.sqrt(win), np.sin(angle) / np.sqrt(win)
-    full = np.block([[c, -s], [s, c]]).astype(np.float32)
+    full = (np.stack([np.cos(angle), np.sin(angle)]) / np.sqrt(win)).astype(np.float32)
     high = full.astype(jnp.bfloat16)
     low = (full - high.astype(np.float32)).astype(jnp.bfloat16)
-    return np.stack([high, low]), np.stack([high.T, low.T])
+    return np.concatenate([high, low])
 
 
 def pairings(size):
@@ -40,14 +39,27 @@
 
 
 def flat_pairs(pairs_y, pairs_x, n_ty, n_tx):
-    out = []
-    for y in range(n_ty):
-        for x in range(n_tx):
+    out, alone = [], []
+    for x in range(n_tx):
+        for y in range(n_ty):
             to_y = y if pairs_y is None else pairs_y.get(y)
             to_x = x if pairs_x is None else pairs_x.get(x)
-            if to_y is not None and to_x is not None:
+            if to_y is None or to_x is None:
+                alone.append(y * n_tx + x)
+            else:
                 out.append((y * n_tx + x, to_y * n_tx + to_x))
+    for a, b in zip(alone[::2], alone[1::2]):
+        out += [(a, b), (b, a)]
+    if len(alone) % 2:
+        out.append((alone[-1], alone[-1]))
     return out
+
+
+def if_paired(x, at, size, i):
+    last = i + 2 * ((size - i) // 2)
+    if i > 0:
+        x = jnp.where(at >= i, x, 0.0)
+    return jnp.where(at < last, x, 0.0) if last < size else x
 
 
 def xor_permute(x, mask, total):
@@ -65,6 +77,12 @@
     return dot(a_high, b_high) + (dot(a_low, b_high) + dot(a_high, b_low))
 
 
+def block(c, upper, lower):
+    return jnp.concatenate(
+        [jnp.concatenate([c, upper], axis=1), jnp.concatenate([lower, c], axis=1)], axis=0
+    )
+
+
 def lane_pick(width, margin, flag):
     lane = lax.broadcasted_iota(jnp.int32, (8, width), 1)
     below = jnp.where(lane < margin, 0, 1)
@@ -80,13 +98,13 @@
 
 
 def compute(
-    ext_ref, probe_ref, meas_ref, pos_ref, right_ref, left_ref, grid_ref, grad_ref, *, margin
+    ext_ref, probe_ref, root_ref, pos_ref, table_ref, grid_ref, grad_ref, *, margin
 ):
-    scans, win = meas_ref.shape[0], meas_ref.shape[1]
+    scans, win = root_ref.shape[0], root_ref.shape[1]
     modes = probe_ref.shape[1]
     width = 2 * win
-    w_fwd = (right_ref[0], right_ref[1])
-    l_fwd = (left_ref[0], left_ref[1])
+    w_fwd = [block(table_ref[i], -table_ref[i + 1], table_ref[i + 1]) for i in (0, 2)]
+    l_fwd = [block(table_ref[i], table_ref[i + 1], -table_ref[i + 1]) for i in (0, 2)]
     grid_ref[...] = jnp.zeros_like(grid_ref)
     weight = jnp.zeros((WEIGHT_ROWS, win), F32)
     for s in range(scans):
@@ -125,7 +143,7 @@
         total = square[:, :win]
         for k in range(1, modes):
             total = total + square[:, k * win : (k + 1) * win]
-        ratio = jnp.sqrt(meas_ref[s]) * lax.rsqrt(jnp.maximum(total, 1.0)) - 1.0
+        ratio = root_ref[s] * lax.rsqrt(jnp.maximum(total, 1.0)) - 1.0
         ratio = jnp.concatenate([ratio] * modes, axis=1)
         far = far * jnp.concatenate([ratio, ratio], axis=0)
         u = product(w_fwd, split(far))
@@ -167,37 +185,43 @@
         send_ref[j, win:, :] = weight
 
 
-def first_kernel(
-    n_y, n_x, margin, pos_ref, obj_ref, probe_ref, meas_ref, right_ref, left_ref, *rest
-):
+def prepare_kernel(probe_ref, meas_ref, table_ref, probe_out, root_ref, table_out):
+    probe_out[...] = probe_ref[...]
+    root_ref[...] = jnp.sqrt(meas_ref[...])
+    table_out[...] = table_ref[...]
+
+
+def first_kernel(n_ty, n_tx, n_y, n_x, margin, pos_ref, obj_ref, probe_ref, root_ref, table_ref, *rest):
     take = iter(rest)
     ty_refs = [next(take) for _ in range(n_y)]
     tx_refs = [next(take) for _ in range(n_x)]
     corner_refs = [[next(take) for _ in range(n_x)] for _ in range(n_y)]
     ext_ref, keep_ref, send_ref, grid_ref, *msg_refs, grad_ref = take
     tile = obj_ref.shape[-1]
-    odd_y, odd_x = lax.axis_index("ty") % 2, lax.axis_index("tx") % 2
+    at_y, at_x = lax.axis_index("ty"), lax.axis_index("tx")
+    odd_y, odd_x = at_y % 2, at_x % 2
     pick = lane_pick(tile, margin, odd_x)
 
     def side(refs, part, rows):
-        if not refs:
-            return jnp.zeros((rows, tile), F32)
-        other = refs[1][part] if len(refs) > 1 else jnp.zeros((rows, tile), F32)
-        return jnp.where(rowwise(pick, rows), refs[0][part], other)
+        both = [if_paired(ref[part], at_x, n_tx, i) for i, ref in enumerate(refs)]
+        both += [jnp.zeros((rows, tile), F32)] * (2 - n_x)
+        return jnp.where(rowwise(pick, rows), both[0], both[1])
 
     for part in (0, 1):
         ext_ref[part, margin : margin + tile, :tile] = obj_ref[part]
         ext_ref[part, margin : margin + tile, tile:] = side(tx_refs, part, tile)
         bands = [
-            jnp.concatenate([ty_refs[i][part], side(corner_refs[i], part, margin)], axis=1)
+            if_paired(
+                jnp.concatenate([ty_refs[i][part], side(corner_refs[i], part, margin)], axis=1),
+                at_y, n_ty, i,
+            )
             for i in range(n_y)
         ]
-        while len(bands) < 2:
-            bands.append(jnp.zeros((margin, 2 * tile), F32))
+        bands += [jnp.zeros((margin, 2 * tile), F32)] * (2 - n_y)
         ext_ref[part, :margin, :] = by_parity(odd_y, bands[1], bands[0])
         ext_ref[part, margin + tile : 2 * tile, :] = by_parity(odd_y, bands[0], bands[1])
     weight = compute(
-        ext_ref, probe_ref, meas_ref, pos_ref, right_ref, left_ref, grid_ref, grad_ref, margin=margin
+        ext_ref, probe_ref, root_ref, pos_ref, table_ref, grid_ref, grad_ref, margin=margin
     )
     emit_halves(grad_ref, weight, keep_ref, send_ref, odd_x)
     for i, ref in enumerate(msg_refs):
@@ -221,13 +245,13 @@
 
 
 def second_kernel(
-    n_y, n_x, n_ty, n_tx, margin, pos_ref, old_ref, grid_old_ref, probe_ref, meas_ref, right_ref,
-    left_ref, own_ref, other_ref, *rest
+    n_ty, n_tx, n_y, n_x, margin, pos_ref, old_ref, grid_old_ref, probe_ref, root_ref, table_ref,
+    own_ref, other_ref, *rest
 ):
     take = iter(rest)
     tx_refs = [next(take) for _ in range(n_x)]
     ty_refs = [next(take) for _ in range(n_y)]
-    tile_ref, new_ref, keep_ref, send_ref, grid_ref, ext_ref, grad_ref = take
+    tile_ref, new_ref, keep_ref, send_ref, grid_ref, edge_ref, ext_ref, grad_ref = take
     tile = probe_ref.shape[-1]
     at_y, at_x = lax.axis_index("ty"), lax.axis_index("tx")
     odd_y, odd_x = at_y % 2, at_x % 2
@@ -243,56 +267,57 @@
     for part in (0, 1):
         total = grid_old_ref[part, : 2 * tile, :]
         if n_x:
-            total = total + spread(tx_refs, part, odd_x, margin, tile)
+            total = total + spread(tx_refs, part, at_x, n_tx, margin, tile)
         ext_ref[part, : 2 * tile, :] = total
         for i, ref in enumerate(ty_refs):
             start = pl.multiple_of(jnp.where(odd_y == i, tile, 0), tile)
-            ext_ref[part, pl.ds(start, tile), :] += ref[part]
+            ext_ref[part, pl.ds(start, tile), :] += if_paired(ref[part], at_y, n_ty, i)
         step = jnp.where(inside, OBJECT_STEP * ext_ref[part, : 2 * tile, :], 0.0)
         ext_ref[part, : 2 * tile, :] = old_ref[part, : 2 * tile, :] + step
         tile_ref[part] = ext_ref[part, margin : margin + tile, :tile]
     weight = compute(
-        ext_ref, new_ref, meas_ref, pos_ref, right_ref, left_ref, grid_ref, grad_ref, margin=margin
+        ext_ref, new_ref, root_ref, pos_ref, table_ref, grid_ref, grad_ref, margin=margin
     )
     emit_halves(grad_ref, weight, keep_ref, send_ref, odd_x)
-
-
-def spread(tx_refs, part, odd_x, margin, tile):
+    edge_ref[...] = grid_ref[:, : 2 * tile, tile:]
+
+
+def spread(tx_refs, part, at_x, n_tx, margin, tile):
     rows = 2 * tile
-    first = tx_refs[0][part]
-    second = tx_refs[1][part] if len(tx_refs) > 1 else jnp.zeros((rows, tile), F32)
-    low = rowwise(lane_pick(tile, margin, odd_x), rows)
+    both = [if_paired(ref[part], at_x, n_tx, i) for i, ref in enumerate(tx_refs)]
+    both += [jnp.zeros((rows, tile), F32)] * (2 - len(both))
+    low = rowwise(lane_pick(tile, margin, at_x % 2), rows)
     return jnp.concatenate(
-        [jnp.where(low, second, first), jnp.where(low, first, second)], axis=1
-    )
-
-
-def last_kernel(n_y, n_x, margin, tile_ref, mid_ref, probe_ref, own_ref, other_ref, *rest):
+        [jnp.where(low, both[1], both[0]), jnp.where(low, both[0], both[1])], axis=1
+    )
+
+
+def last_kernel(n_ty, n_y, margin, tile_ref, mid_ref, probe_ref, own_ref, other_ref, *rest):
     take = iter(rest)
     ty_refs = [next(take) for _ in range(n_y)]
     obj_ref, new_ref = take
     tile = probe_ref.shape[-1]
-    odd_y, odd_x = lax.axis_index("ty") % 2, lax.axis_index("tx") % 2
-    combined_probe(probe_ref, own_ref, other_ref, new_ref, odd_x)
+    at_y = lax.axis_index("ty")
+    combined_probe(probe_ref, own_ref, other_ref, new_ref, lax.axis_index("tx") % 2)
     for part in (0, 1):
         obj_ref[part] = mid_ref[part, margin : margin + tile, :]
         for i, ref in enumerate(ty_refs):
-            start = pl.multiple_of(jnp.where(odd_y == i, tile - margin, 0), margin)
-            obj_ref[part, pl.ds(start, margin), :] += ref[part]
+            start = pl.multiple_of(jnp.where(at_y % 2 == i, tile - margin, 0), margin)
+            obj_ref[part, pl.ds(start, margin), :] += if_paired(ref[part], at_y, n_ty, i)
         obj_ref[part] = tile_ref[part] + OBJECT_STEP * obj_ref[part]
 
 
 def call(kernel, outs, ins, scratch=()):
     smem = pl.BlockSpec(memory_space=pltpu.SMEM)
     vmem = pl.BlockSpec(memory_space=pltpu.VMEM)
-    shapes = [jax.ShapeDtypeStruct(s, F32) for s in outs]
+    shapes = [s if hasattr(s, "dtype") else jax.ShapeDtypeStruct(s, F32) for s in outs]
     return pl.pallas_call(
         kernel,
         out_shape=shapes,
         in_specs=[smem if x.dtype == jnp.int32 else vmem for x in ins],
         out_specs=[vmem] * len(outs),
         scratch_shapes=[pltpu.VMEM(s, F32) for s in scratch],
-        compiler_params=pltpu.CompilerParams(vmem_limit_bytes=32 * 1024 * 1024),
+        compiler_params=pltpu.CompilerParams(vmem_limit_bytes=16 * 1024 * 1024),
     )(*ins)
 
 
@@ -336,27 +361,37 @@
     )
 
 
-def summed_halves(keep, send, n_ty, n_tx):
+def summed_halves(keep, send, n_ty, n_tx, columns, rows, early):
     total = n_ty * n_tx
     me = lax.axis_index("ty") * n_tx + lax.axis_index("tx")
     levels = total.bit_length() - 1
-    half = keep + xor_permute(send, 1, total)
     tx_bits = n_tx.bit_length() - 1
     bits = [b for b in (tx_bits, 1) if b < levels]
     rest = [b for b in range(1, levels) if b not in bits]
+    half = keep + xor_permute(send, 1, total)
+    across = columns()
     half = scatter_sum(half, me, bits, total)
+    if early:
+        half, across = lax.optimization_barrier((half, across))
+        along = rows(across)
     for i in range(0, len(rest), 2):
         half = direct_sum(half, rest[i : i + 2], total)
+    if early:
+        half, along = lax.optimization_barrier((half, along))
+    else:
+        half, across = lax.optimization_barrier((half, across))
+        along = rows(across)
     half = gather(half, me, bits, total)
-    return half, xor_permute(half, 1, total)
-
-
-def per_device(n_ty, n_tx, tables, object_field, probe, intensities, positions):
+    if not early:
+        half, along = lax.optimization_barrier((half, along))
+    return half, xor_permute(half, 1, total), across, along
+
+
+def per_device(n_ty, n_tx, table, object_field, probe, intensities, positions):
     win, modes = probe.shape[-1], probe.shape[1]
     margin, tile, scans = win // 2, object_field.shape[-1], positions.shape[2]
     spots = positions.reshape(scans, 2)
     measured = intensities.reshape(scans, win, win)
-    right, left = (jnp.asarray(t) for t in tables)
     match_y, match_x = pairings(n_ty), pairings(n_tx)
     n_y, n_x = len(match_y), len(match_x)
     odd_y = lax.axis_index("ty") % 2
@@ -371,48 +406,72 @@
     tx_in = [swap(object_field, None, px) for px in match_x]
     rims = [rows_for(object_field, i, margin, 0, tile - margin) for i in range(n_y)]
     ty_in = [swap(rims[i], py, None) for i, py in enumerate(match_y)]
-    corners = [swap(rims[i], py, px) for i, py in enumerate(match_y) for px in match_x]
+    corners = []
+    for i, py in enumerate(match_y):
+        corners += [swap(ty_in[i], None, px) for px in match_x[:1]]
+        corners += [swap(rims[i], py, px) for px in match_x[1:]]
+
+    shape_of = lambda x: jax.ShapeDtypeStruct(x.shape, x.dtype)
+    ready = (probe, measured, jnp.asarray(table))
+    ready = call(prepare_kernel, [shape_of(x) for x in ready], ready)
+    (tx_in, ty_in, corners), (probe, root, table) = lax.optimization_barrier(
+        ((tx_in, ty_in, corners), tuple(ready))
+    )
+
+    at_x = lax.axis_index("tx")
+    lane = lax.broadcasted_iota(jnp.int32, (1, 1, tile), 2)
+    low = jnp.where(lane < margin, 0, 1) == at_x % 2
+
+    def joined(messages):
+        both = [if_paired(m, at_x, n_tx, i) for i, m in enumerate(messages)]
+        both += [jnp.zeros_like(messages[0])] * (2 - n_x)
+        return jnp.where(low, both[1], both[0]), jnp.where(low, both[0], both[1])
 
     half_shape = (modes, win + WEIGHT_ROWS, win)
     grid_shape = (2, 2 * tile + SUBLANES, 2 * tile)
     msg_shape = (2, 2 * tile, tile)
     ext, keep, send, grid, *msgs = call(
-        functools.partial(first_kernel, n_y, n_x, margin),
+        functools.partial(first_kernel, n_ty, n_tx, n_y, n_x, margin),
         [grid_shape, half_shape, half_shape, grid_shape] + [msg_shape] * n_x,
-        [spots, object_field, probe, measured, right, left, *ty_in, *tx_in, *corners],
+        [spots, object_field, probe, root, table, *ty_in, *tx_in, *corners],
         [(2 * modes, win, win)],
     )
-    own, other = summed_halves(keep, send, n_ty, n_tx)
-    tx_in = [swap(m, None, px) for m, px in zip(msgs, match_x)]
-    odd_x = lax.axis_index("tx") % 2
-    lane = lax.broadcasted_iota(jnp.int32, (1, 1, tile), 2)
-    low = jnp.where(lane < margin, 0, 1) == odd_x
-    second = tx_in[1] if n_x > 1 else jnp.zeros(msg_shape, F32)
-    extra = jnp.concatenate(
-        [jnp.where(low, second, tx_in[0]), jnp.where(low, tx_in[0], second)], axis=2
-    ) if n_x else jnp.zeros((2, 2 * tile, 2 * tile), F32)
-    wide = grid[:, : 2 * tile, :] + extra
-    bands = [rows_for(wide, i, tile, 0, tile) for i in range(n_y)]
-    ty_in = [swap(bands[i], py, None) for i, py in enumerate(match_y)]
-    tile_mid, probe_mid, keep, send, grid = call(
-        functools.partial(second_kernel, n_y, n_x, n_ty, n_tx, margin),
-        [object_field.shape, probe.shape, half_shape, half_shape, grid_shape],
-        [spots, ext, grid, probe, measured, right, left, own, other, *tx_in, *ty_in],
+
+    def columns():
+        return [swap(m, None, px) for m, px in zip(msgs, match_x)]
+
+    def rows(across):
+        wide = grid[:, : 2 * tile, :]
+        if n_x:
+            wide = wide + jnp.concatenate(joined(across), axis=2)
+        bands = [rows_for(wide, i, tile, 0, tile) for i in range(n_y)]
+        return [swap(bands[i], py, None) for i, py in enumerate(match_y)]
+
+    own, other, tx_in, ty_in = summed_halves(keep, send, n_ty, n_tx, columns, rows, True)
+    tile_mid, probe_mid, keep, send, grid_last, edge = call(
+        functools.partial(second_kernel, n_ty, n_tx, n_y, n_x, margin),
+        [object_field.shape, probe.shape, half_shape, half_shape, grid_shape, msg_shape],
+        [spots, ext, grid, probe, root, table, own, other, *tx_in, *ty_in],
         [grid_shape, (2 * modes, win, win)],
     )
-    own, other = summed_halves(keep, send, n_ty, n_tx)
-    edge = grid[:, : 2 * tile, tile:]
-    tx_in = [swap(edge, None, px) for px in match_x]
-    mid = grid[:, : 2 * tile, :tile]
-    if n_x:
-        second = tx_in[1] if n_x > 1 else jnp.zeros(msg_shape, F32)
-        mid = mid + jnp.where(low, second, tx_in[0])
-    bands = [rows_for(mid, i, margin, 0, 2 * tile - margin) for i in range(n_y)]
-    ty_in = [swap(bands[i], py, None) for i, py in enumerate(match_y)]
+
+    def columns():
+        return [swap(edge, None, px) for px in match_x]
+
+    def middle(across):
+        mid = grid_last[:, : 2 * tile, :tile]
+        return mid + joined(across)[0] if n_x else mid
+
+    def rows(across):
+        mid = middle(across)
+        bands = [rows_for(mid, i, margin, 0, 2 * tile - margin) for i in range(n_y)]
+        return [swap(bands[i], py, None) for i, py in enumerate(match_y)]
+
+    own, other, tx_in, ty_in = summed_halves(keep, send, n_ty, n_tx, columns, rows, False)
     return call(
-        functools.partial(last_kernel, n_y, n_x, margin),
+        functools.partial(last_kernel, n_ty, n_y, margin),
         [object_field.shape, probe.shape],
-        [tile_mid, mid, probe_mid, own, other, *ty_in],
+        [tile_mid, middle(tx_in), probe_mid, own, other, *ty_in],
     )
 
 
@@ -421,9 +480,9 @@
     placed = (P(None, "ty", "tx"), P(), P("ty", "tx", None, None, None), P("ty", "tx", None, None))
 
     def run(object_field, probe, intensities, positions):
-        tables = dft_blocks(probe.shape[-1])
+        table = dft_table(probe.shape[-1])
         return jax.shard_map(
-            functools.partial(per_device, n_ty, n_tx, tables),
+            functools.partial(per_device, n_ty, n_tx, table),
             mesh=mesh,
             in_specs=placed,
             out_specs=(P(None, "ty", "tx"), P()),

time: 104 us -> 89.8 us (0.86)
  the two profiles are of different devices: /device:TPU:4 before, /device:TPU:0 now
where the time goes in v1:
time: 89.8 us; the launch traced here: 89.5 us
  starting transfers between devices  36.2 us (40%)
  waiting for transfers between devices  32.1 us (36%)
  Pallas kernels  12.3 us (14%)
  local copies, waits for them, and re-layouts  4.74 us (5%)
  other arithmetic  3.31 us (4%)
    ppermute x22, waiting for transfers between devices, xor_permute(): return lax.ppermute(x, AXES, [(i, i ^ mask) for i in range(total)])  27.2 us
    ppermute x22, starting transfers between devices, xor_permute(): return lax.ppermute(x, AXES, [(i, i ^ mask) for i in range(total)])  25.4 us
    pallas_call x4, Pallas kernels, call(): pl.pallas_call(kernel, out_shape=shapes, in_specs=[smem if x.dtype == jnp...  12.3 us
    ppermute x11, starting transfers between devices, swap(): return lax.ppermute(x, AXES, flat_pairs(pairs_y, pairs_x, n_ty, n_tx))  10.8 us
    ppermute x11, waiting for transfers between devices, swap(): return lax.ppermute(x, AXES, flat_pairs(pairs_y, pairs_x, n_ty, n_tx))  4.95 us
    unnamed x20, local copies, waits for them, and re-layouts  3.59 us
  transfers between devices with their start and end apart: 33, of which 22 were waited for; matrix products, arithmetic and copies ran while one was open for 4% of the time, Pallas kernels for 0%

profile of v1, /device:TPU:0, one launch (start us, length us, event | category | flops | bytes accessed | tf_op | source)
XLA Modules:
  0.0 89.5 jit_solution(15553864904410296710)
XLA Ops:
  0.7 0.9 constant_dynamic-slice_fusion.7
  1.6 2.9 %collective-permute-start.2 = (f32[2,64,128]{2,1,0:T(8,128)S(1)}, f32[2,64,128]{2,1,0:T(8,128)S(1)}, u32[]{:S(2)}, u32[]{:S(2)}) collective-permute-start(f32[2,64,128]{2,1,0:T(8,128)S(1)} %constant_dynamic-slice_fusion.7), channel_id=1, source_target_pairs={{0,16},{16,0},{1,17},{17,1},{2,18},{18,2},{3,19},{19,3},{4,20},{20... | collective-permute-start | bytes 196616 | tf_op jit(solution)/shard_map/ppermute | solution.py:400
  4.5 0.1 collective-permute-start.1
  4.6 1.6 %collective-permute-start = (f32[2,128,128]{2,1,0:T(8,128)S(1)}, f32[2,128,128]{2,1,0:T(8,128)S(1)}, u32[]{:S(2)}, u32[]{:S(2)}) collective-permute-start(f32[2,128,128]{2,1,0:T(8,128)S(1)} %copy-done.1), channel_id=1, source_target_pairs={{0,1},{16,17},{1,0},{17,16},{2,3},{18,19},{3,2},{19,18},{4,5},{20,... | collective-permute-start | bytes 393224 | tf_op jit(solution)/shard_map/ppermute | solution.py:400
  6.1 0.5 collective-permute-start.4
  6.7 0.1 collective-permute-done.2.rest_0_
  6.7 1.0 %collective-permute-start.3 = (f32[2,64,128]{2,1,0:T(8,128)S(1)}, f32[2,64,128]{2,1,0:T(8,128)S(1)}, u32[]{:S(2)}, u32[]{:S(2)}) collective-permute-start(f32[2,64,128]{2,1,0:T(8,128)S(1)} %collective-permute-done.2.rest_0_), channel_id=1, source_target_pairs={{0,1},{16,17},{1,0},{17,16},{2,3},{18,19},{3,2},{19,18},{4,5},{20,... | collective-permute-start | bytes 196616 | tf_op jit(solution)/shard_map/ppermute | solution.py:400
  7.7 0.1 copy.8.pos_ref
  7.8 1.0 %copy-done = f32[2,4,128,128]{3,2,1,0:T(8,128)S(1)} copy-done((f32[2,4,128,128]{3,2,1,0:T(8,128)S(1)}, f32[2,4,128,128]{3,2,1,0:T(8,128)}, u32[]{:S(2)}) %copy-start) | copy-done | bytes 524312
  8.9 0.9 %copy-done.2 = f32[1,1,3,128,128]{4,3,2,1,0:T(8,128)S(1)} copy-done((f32[1,1,3,128,128]{4,3,2,1,0:T(8,128)S(1)}, f32[1,1,3,128,128]{4,3,2,1,0:T(8,128)}, u32[]{:S(2)}) %copy-start.2) | copy-done | bytes 196632
  9.8 0.9 %copy-done.3 = bf16[4,128,128]{2,1,0:T(8,128)(2,1)S(1)} copy-done((bf16[4,128,128]{2,1,0:T(8,128)(2,1)S(1)}, bf16[4,128,128]{2,1,0:T(8,128)(2,1)}, u32[]{:S(2)}) %copy-start.3) | copy-done | bytes 131096
  10.7 0.1 shard_map.68
  10.8 5.5 %shard_map.69 = (f32[2,264,256]{2,1,0:T(8,128)S(1)}, f32[4,136,128]{2,1,0:T(8,128)S(1)}, f32[4,136,128]{2,1,0:T(8,128)S(1)}, f32[2,264,256]{2,1,0:T(8,128)S(1)},...) custom-call(s32[3,2]{1,0:T(4,128)S(1)} %copy.8.pos_ref, f32[2,128,128]{2,1,0:T(8,128)S(1)} %copy-done.1, ...), custom_call_target="tpu_custom_call" | custom-call | tf_op jit(solution)/shard_map/pallas_call | solution.py:314
  16.3 0.7 copy-done.5
  17.0 0.5 collective-permute-start.9
  17.5 1.5 %collective-permute-start.10 = (f32[2,256,128]{2,1,0:T(8,128)S(1)}, f32[2,256,128]{2,1,0:T(8,128)S(1)}, u32[]{:S(2)}, u32[]{:S(2)}) collective-permute-start(f32[2,256,128]{2,1,0:T(8,128)S(1)} %get-tuple-element.51), channel_id=1, source_target_pairs={{1,2},{17,18},{2,1},{18,17},{3,4},{19,20},{4,3},{20,19},{5,6},{21,... | collective-permute-start | bytes 786440 | tf_op jit(solution)/shard_map/ppermute | solution.py:400
  19.0 1.0 %add.95 = f32[4,136,128]{2,1,0:T(8,128)S(1)} add(f32[4,136,128]{2,1,0:T(8,128)S(1)} %get-tuple-element.48, f32[4,136,128]{2,1,0:T(8,128)} %collective-permute-done.5) | non-fusion elementwise | flops 69632 | bytes 835584 | tf_op jit(solution)/shard_map/add | solution.py:371
  20.1 1.2 %collective-permute-start.6 = (f32[1,136,128]{2,1,0:T(8,128)S(1)}, f32[1,136,128]{2,1,0:T(8,128)}, u32[]{:S(2)}, u32[]{:S(2)}) collective-permute-start(f32[1,136,128]{2,1,0:T(8,128)S(1)} %get-tuple-element.81), channel_id=1, source_target_pairs={{0,16},{1,17},{2,18},{3,19},{4,20},{5,21},{6,22},{7,23},{8,24},{9,... | collective-permute-start | bytes 208904 | tf_op jit(solution)/shard_map/ppermute | solution.py:66
  21.3 2.3 %collective-permute-start.8 = (f32[1,136,128]{2,1,0:T(8,128)S(1)}, f32[1,136,128]{2,1,0:T(8,128)}, u32[]{:S(2)}, u32[]{:S(2)}) collective-permute-start(f32[1,136,128]{2,1,0:T(8,128)S(1)} %get-tuple-element.82), channel_id=1, source_target_pairs={{0,18},{1,19},{2,16},{3,17},{4,22},{5,23},{6,20},{7,21},{8,26},{9,... | collective-permute-start | bytes 208904 | tf_op jit(solution)/shard_map/ppermute | solution.py:66
  23.6 0.0 collective-permute-start.7
  23.7 2.1 %collective-permute-done.6 = f32[1,136,128]{2,1,0:T(8,128)} collective-permute-done((f32[1,136,128]{2,1,0:T(8,128)S(1)}, f32[1,136,128]{2,1,0:T(8,128)}, u32[]{:S(2)}, u32[]{:S(2)}) %collective-permute-start.6) | collective-permute-done | bytes 69664 | tf_op jit(solution)/shard_map/ppermute | solution.py:66
  25.8 2.1 %collective-permute-done.8 = f32[1,136,128]{2,1,0:T(8,128)} collective-permute-done((f32[1,136,128]{2,1,0:T(8,128)S(1)}, f32[1,136,128]{2,1,0:T(8,128)}, u32[]{:S(2)}, u32[]{:S(2)}) %collective-permute-start.8) | collective-permute-done | bytes 69664 | tf_op jit(solution)/shard_map/ppermute | solution.py:66
  27.9 1.2 %collective-permute-done.7 = f32[1,136,128]{2,1,0:T(8,128)} collective-permute-done((f32[1,136,128]{2,1,0:T(8,128)S(1)}, f32[1,136,128]{2,1,0:T(8,128)}, u32[]{:S(2)}, u32[]{:S(2)}) %collective-permute-start.7) | collective-permute-done | bytes 69664 | tf_op jit(solution)/shard_map/ppermute | solution.py:66
  29.0 1.0 %add_add_fusion.3 = f32[1,136,128]{2,1,0:T(8,128)S(1)} fusion(f32[1,136,128]{2,1,0:T(8,128)} %collective-permute-done.7, f32[1,136,128]{2,1,0:T(8,128)} %collective-permute-done.8, f32[1,136,128]{2,1,0:T(8,128)} %collective-permute-done.6, f32[4,136,128]{2,1,0:T(8,128)} %copy-done.6, s32[]{:T(128)S(6)} %select_n.97), kind=kLoop, calls=%fused_computation.23 | loop fusion | flops 52224 | bytes 348164 | tf_op jit(solution)/shard_map/add | solution.py:338
  30.1 5.0 %collective-permute-start.13 = (f32[1,136,128]{2,1,0:T(8,128)S(1)}, f32[1,136,128]{2,1,0:T(8,128)S(1)}, u32[]{:S(2)}, u32[]{:S(2)}) collective-permute-start(f32[1,136,128]{2,1,0:T(8,128)S(1)} %add_add_fusion.3), channel_id=1, source_target_pairs={{0,12},{1,13},{2,14},{3,15},{4,8},{5,9},{6,10},{7,11},{8,4},{9,5},... | collective-permute-start | bytes 208904 | tf_op jit(solution)/shard_map/ppermute | solution.py:66
  35.0 0.6 collective-permute-start.11
  35.7 0.1 fusion.1
  35.8 0.9 %collective-permute-start.14 = (f32[2,128,256]{2,1,0:T(8,128)S(1)}, f32[2,128,256]{2,1,0:T(8,128)S(1)}, u32[]{:S(2)}, u32[]{:S(2)}) collective-permute-start(f32[2,128,256]{2,1,0:T(8,128)S(1)} %fusion.1), channel_id=1, source_target_pairs={{0,16},{16,0},{1,17},{17,1},{2,18},{18,2},{3,19},{19,3},{4,20},{20... | collective-permute-start | bytes 786440 | tf_op jit(solution)/shard_map/ppermute | solution.py:400
  36.7 0.8 collective-permute-done.13
  37.6 2.9 %collective-permute-done.12 = f32[1,136,128]{2,1,0:T(8,128)S(1)} collective-permute-done((f32[1,136,128]{2,1,0:T(8,128)S(1)}, f32[1,136,128]{2,1,0:T(8,128)S(1)}, u32[]{:S(2)}, u32[]{:S(2)}) %collective-permute-start.12) | collective-permute-done | bytes 69664 | tf_op jit(solution)/shard_map/ppermute | solution.py:66
  40.5 1.8 %collective-permute-done.14.rest_2_ = f32[2,128,256]{2,1,0:T(8,128)S(1)} collective-permute-done((f32[2,128,256]{2,1,0:T(8,128)S(1)}, f32[2,128,256]{2,1,0:T(8,128)S(1)}, u32[]{:S(2)}, u32[]{:S(2)}) %collective-permute-start.14) | collective-permute-done | bytes 262176 | tf_op jit(solution)/shard_map/ppermute | solution.py:400
  42.2 2.3 %collective-permute-start.17 = (f32[1,136,128]{2,1,0:T(8,128)S(1)}, f32[1,136,128]{2,1,0:T(8,128)S(1)}, u32[]{:S(2)}, u32[]{:S(2)}) collective-permute-start(f32[1,136,128]{2,1,0:T(8,128)S(1)} %add_add_fusion.2), channel_id=1, source_target_pairs={{0,18},{1,19},{2,16},{3,17},{4,22},{5,23},{6,20},{7,21},{8,26},{9,... | collective-permute-start | bytes 208904 | tf_op jit(solution)/shard_map/ppermute | solution.py:66
  44.5 0.4 collective-permute-start.16
  44.9 0.8 collective-permute-start.15
  45.7 2.2 %collective-permute-done.17 = f32[1,136,128]{2,1,0:T(8,128)S(1)} collective-permute-done((f32[1,136,128]{2,1,0:T(8,128)S(1)}, f32[1,136,128]{2,1,0:T(8,128)S(1)}, u32[]{:S(2)}, u32[]{:S(2)}) %collective-permute-start.17) | collective-permute-done | bytes 69664 | tf_op jit(solution)/shard_map/ppermute | solution.py:66
  47.9 0.9 %collective-permute-done.16 = f32[1,136,128]{2,1,0:T(8,128)S(1)} collective-permute-done((f32[1,136,128]{2,1,0:T(8,128)S(1)}, f32[1,136,128]{2,1,0:T(8,128)S(1)}, u32[]{:S(2)}, u32[]{:S(2)}) %collective-permute-start.16) | collective-permute-done | bytes 69664 | tf_op jit(solution)/shard_map/ppermute | solution.py:66
  48.8 0.4 collective-permute-done.15
  49.3 0.1 collective-permute-start.18
  49.3 1.5 %collective-permute-done.18.other_ref = f32[4,136,128]{2,1,0:T(8,128)S(1)} collective-permute-done((f32[4,136,128]{2,1,0:T(8,128)S(1)}, f32[4,136,128]{2,1,0:T(8,128)S(1)}, u32[]{:S(2)}, u32[]{:S(2)}) %collective-permute-start.18) | collective-permute-done | bytes 278560 | tf_op jit(solution)/shard_map/ppermute | solution.py:66
  50.9 5.7 %shard_map.70 = (f32[2,128,128]{2,1,0:T(8,128)S(1)}, f32[2,4,128,128]{3,2,1,0:T(8,128)S(1)}, f32[4,136,128]{2,1,0:T(8,128)S(1)}, f32[4,136,128]{2,1,0:T(8,128)S(...) custom-call(s32[3,2]{1,0:T(4,128)S(1)} %copy.8.pos_ref, f32[2,264,256]{2,1,0:T(8,128)S(1)} %get-tuple-element.46.old_ref, ...), custom_call_target="tpu_custom_call" | custom-call | tf_op jit(solution)/shard_map/pallas_call | solution.py:314
  56.6 0.2 collective-permute-start.19
  56.8 1.4 %collective-permute-done.19 = f32[4,136,128]{2,1,0:T(8,128)S(1)} collective-permute-done((f32[4,136,128]{2,1,0:T(8,128)S(1)}, f32[4,136,128]{2,1,0:T(8,128)S(1)}, u32[]{:S(2)}, u32[]{:S(2)}) %collective-permute-start.19) | collective-permute-done | bytes 278560 | tf_op jit(solution)/shard_map/ppermute | solution.py:66
  58.3 0.9 %collective-permute-start.20 = (f32[1,136,128]{2,1,0:T(8,128)S(1)}, f32[1,136,128]{2,1,0:T(8,128)S(1)}, u32[]{:S(2)}, u32[]{:S(2)}) collective-permute-start(f32[1,136,128]{2,1,0:T(8,128)S(1)} %get-tuple-element.74), channel_id=1, source_target_pairs={{0,16},{1,17},{2,18},{3,19},{4,20},{5,21},{6,22},{7,23},{8,24},{9,... | collective-permute-start | bytes 208904 | tf_op jit(solution)/shard_map/ppermute | solution.py:66
  59.2 2.3 %collective-permute-start.22 = (f32[1,136,128]{2,1,0:T(8,128)S(1)}, f32[1,136,128]{2,1,0:T(8,128)S(1)}, u32[]{:S(2)}, u32[]{:S(2)}) collective-permute-start(f32[1,136,128]{2,1,0:T(8,128)S(1)} %get-tuple-element.75), channel_id=1, source_target_pairs={{0,18},{1,19},{2,16},{3,17},{4,22},{5,23},{6,20},{7,21},{8,26},{9,... | collective-permute-start | bytes 208904 | tf_op jit(solution)/shard_map/ppermute | solution.py:66
  61.5 0.4 collective-permute-start.21
  61.8 0.8 collective-permute-done.20
  62.7 2.6 %collective-permute-done.22 = f32[1,136,128]{2,1,0:T(8,128)S(1)} collective-permute-done((f32[1,136,128]{2,1,0:T(8,128)S(1)}, f32[1,136,128]{2,1,0:T(8,128)S(1)}, u32[]{:S(2)}, u32[]{:S(2)}) %collective-permute-start.22) | collective-permute-done | bytes 69664 | tf_op jit(solution)/shard_map/ppermute | solution.py:66
  65.3 1.0 %collective-permute-done.21 = f32[1,136,128]{2,1,0:T(8,128)S(1)} collective-permute-done((f32[1,136,128]{2,1,0:T(8,128)S(1)}, f32[1,136,128]{2,1,0:T(8,128)S(1)}, u32[]{:S(2)}, u32[]{:S(2)}) %collective-permute-start.21) | collective-permute-done | bytes 69664 | tf_op jit(solution)/shard_map/ppermute | solution.py:66
  66.3 2.6 %collective-permute-start.25 = (f32[1,136,128]{2,1,0:T(8,128)S(1)}, f32[1,136,128]{2,1,0:T(8,128)S(1)}, u32[]{:S(2)}, u32[]{:S(2)}) collective-permute-start(f32[1,136,128]{2,1,0:T(8,128)S(1)} %add_add_fusion.1), channel_id=1, source_target_pairs={{0,12},{1,13},{2,14},{3,15},{4,8},{5,9},{6,10},{7,11},{8,4},{9,5},... | collective-permute-start | bytes 208904 | tf_op jit(solution)/shard_map/ppermute | solution.py:66
  68.9 1.8 %collective-permute-start.23 = (f32[1,136,128]{2,1,0:T(8,128)S(1)}, f32[1,136,128]{2,1,0:T(8,128)S(1)}, u32[]{:S(2)}, u32[]{:S(2)}) collective-permute-start(f32[1,136,128]{2,1,0:T(8,128)S(1)} %add_add_fusion.1), channel_id=1, source_target_pairs={{0,4},{1,5},{2,6},{3,7},{4,0},{5,1},{6,2},{7,3},{8,12},{9,13},{10,... | collective-permute-start | bytes 208904 | tf_op jit(solution)/shard_map/ppermute | solution.py:66
  70.7 0.8 collective-permute-start.27
  71.6 0.0 collective-permute-start.26
  71.6 1.5 %collective-permute-done.25 = f32[1,136,128]{2,1,0:T(8,128)S(1)} collective-permute-done((f32[1,136,128]{2,1,0:T(8,128)S(1)}, f32[1,136,128]{2,1,0:T(8,128)S(1)}, u32[]{:S(2)}, u32[]{:S(2)}) %collective-permute-start.25) | collective-permute-done | bytes 69664 | tf_op jit(solution)/shard_map/ppermute | solution.py:66
  73.1 2.4 %collective-permute-done.24 = f32[1,136,128]{2,1,0:T(8,128)S(1)} collective-permute-done((f32[1,136,128]{2,1,0:T(8,128)S(1)}, f32[1,136,128]{2,1,0:T(8,128)S(1)}, u32[]{:S(2)}, u32[]{:S(2)}) %collective-permute-start.24) | collective-permute-done | bytes 69664 | tf_op jit(solution)/shard_map/ppermute | solution.py:66
  75.6 1.5 %collective-permute-done.27 = f32[2,256,128]{2,1,0:T(8,128)S(1)} collective-permute-done((f32[2,256,128]{2,1,0:T(8,128)S(1)}, f32[2,256,128]{2,1,0:T(8,128)S(1)}, u32[]{:S(2)}, u32[]{:S(2)}) %collective-permute-start.27) | collective-permute-done | bytes 262176 | tf_op jit(solution)/shard_map/ppermute | solution.py:400
  77.1 3.3 %collective-permute-start.30 = (f32[1,136,128]{2,1,0:T(8,128)S(1)}, f32[1,136,128]{2,1,0:T(8,128)S(1)}, u32[]{:S(2)}, u32[]{:S(2)}) collective-permute-start(f32[1,136,128]{2,1,0:T(8,128)S(1)} %add_add_fusion), channel_id=1, source_target_pairs={{0,18},{1,19},{2,16},{3,17},{4,22},{5,23},{6,20},{7,21},{8,26},{9,... | collective-permute-start | bytes 208904 | tf_op jit(solution)/shard_map/ppermute | solution.py:66
  80.4 1.2 %collective-permute-start.28 = (f32[1,136,128]{2,1,0:T(8,128)S(1)}, f32[1,136,128]{2,1,0:T(8,128)S(1)}, u32[]{:S(2)}, u32[]{:S(2)}) collective-permute-start(f32[1,136,128]{2,1,0:T(8,128)S(1)} %add_add_fusion), channel_id=1, source_target_pairs={{0,16},{1,17},{2,18},{3,19},{4,20},{5,21},{6,22},{7,23},{8,24},{9,... | collective-permute-start | bytes 208904 | tf_op jit(solution)/shard_map/ppermute | solution.py:66
  81.6 1.0 %select_add_fusion.mid_ref = f32[2,256,128]{2,1,0:T(8,128)S(1)} fusion(f32[2,256,128]{2,1,0:T(8,128)S(1)} %collective-permute-done.26, f32[2,256,128]{2,1,0:T(8,128)S(1)} %collective-permute-done.27, f32[2,264,256]{2,1,0:T(8,128)} %copy-done.4, pred[]{:T(512)S(6)} %ge.2, pred[]{:T(512)S(6)} %lt.62, pred[128]{0:T(512)(128)(4,1)S(1)} %copy-done.8), kind=kLoop, calls=%fused_computation.8 | loop fusion | flops 262144 | bytes 1048706 | tf_op jit(solution)/shard_map/add | solution.py:463
  82.6 0.9 %collective-permute-start.31 = (f32[2,64,128]{2,1,0:T(8,128)S(1)}, f32[2,64,128]{2,1,0:T(8,128)S(1)}, u32[]{:S(2)}, u32[]{:S(2)}) collective-permute-start(f32[2,64,128]{2,1,0:T(8,128)S(1)} %constant_dynamic-slice_fusion), channel_id=1, source_target_pairs={{0,16},{16,0},{1,17},{17,1},{2,18},{18,2},{3,19},{19,3},{4,20},{20... | collective-permute-start | bytes 196616 | tf_op jit(solution)/shard_map/ppermute | solution.py:400
  83.5 1.2 %collective-permute-done.29 = f32[1,136,128]{2,1,0:T(8,128)S(1)} collective-permute-done((f32[1,136,128]{2,1,0:T(8,128)S(1)}, f32[1,136,128]{2,1,0:T(8,128)S(1)}, u32[]{:S(2)}, u32[]{:S(2)}) %collective-permute-start.29) | collective-permute-done | bytes 69664 | tf_op jit(solution)/shard_map/ppermute | solution.py:66
  84.7 0.6 collective-permute-done.28
  85.4 1.6 %collective-permute-done.31.rest_0_ = f32[2,64,128]{2,1,0:T(8,128)S(1)} collective-permute-done((f32[2,64,128]{2,1,0:T(8,128)S(1)}, f32[2,64,128]{2,1,0:T(8,128)S(1)}, u32[]{:S(2)}, u32[]{:S(2)}) %collective-permute-start.31) | collective-permute-done | bytes 65568 | tf_op jit(solution)/shard_map/ppermute | solution.py:400
  86.9 1.6 %collective-permute-done.32.other_ref = f32[4,136,128]{2,1,0:T(8,128)S(1)} collective-permute-done((f32[4,136,128]{2,1,0:T(8,128)S(1)}, f32[4,136,128]{2,1,0:T(8,128)S(1)}, u32[]{:S(2)}, u32[]{:S(2)}) %collective-permute-start.32) | collective-permute-done | bytes 278560 | tf_op jit(solution)/shard_map/ppermute | solution.py:66
  88.5 1.0 %shard_map.71 = (f32[2,128,128]{2,1,0:T(8,128)}, f32[2,4,128,128]{3,2,1,0:T(8,128)}) custom-call(f32[2,128,128]{2,1,0:T(8,128)S(1)} %get-tuple-element.57.tile_ref, f32[2,256,128]{2,1,0:T(8,128)S(1)} %select_add_fusion.mid_ref, f32[2,4,128,128]{3,2,1,0:T(8,128)S(1)} %get-tuple-element.64.probe_ref, f32[4,136,128]{2,1,0:T(8,128)S(1)} %pad_maximum_fusion.3.own_ref, ...), custom_call_target="tpu_custom_call" | custom-call | tf_op jit(solution)/shard_map/pallas_call | solution.py:314
  (48 shorter events, 0.5 us)
Async XLA Ops:
  0.6 3.9 %copy-start.1 = (f32[2,128,128]{2,1,0:T(8,128)S(1)}, f32[2,128,128]{2,1,0:T(8,128)}, u32[]{:S(2)}) copy-start(f32[2,128,128]{2,1,0:T(8,128)} %obj_ref.1) | copy-start | bytes 393220
  1.5 6.2 %copy-start.9 = (s32[1,1,3,2]{2,3,1,0:T(2,128)S(1)}, s32[1,1,3,2]{2,3,1,0:T(2,128)}, u32[]{:S(2)}) copy-start(s32[1,1,3,2]{2,3,1,0:T(2,128)} %param.8) | copy-start | bytes 76
  1.6 5.2 %collective-permute-start.2 = (f32[2,64,128]{2,1,0:T(8,128)S(1)}, f32[2,64,128]{2,1,0:T(8,128)S(1)}, u32[]{:S(2)}, u32[]{:S(2)}) collective-permute-start(f32[2,64,128]{2,1,0:T(8,128)S(1)} %constant_dynamic-slice_fusion.7), channel_id=1, source_target_pairs={{0,16},{16,0},{1,17},{17,1},{2,18},{18,2},{3,19},{19,3},{4,20},{20... | collective-permute-start | bytes 196616 | tf_op jit(solution)/shard_map/ppermute | solution.py:400
  4.5 6.3 %collective-permute-start.1 = (f32[2,128,128]{2,1,0:T(8,128)S(1)}, f32[2,128,128]{2,1,0:T(8,128)S(1)}, u32[]{:S(2)}, u32[]{:S(2)}) collective-permute-start(f32[2,128,128]{2,1,0:T(8,128)S(1)} %copy-done.1), channel_id=1, source_target_pairs={{1,2},{17,18},{2,1},{18,17},{3,4},{19,20},{4,3},{20,19},{5,6},{21,... | collective-permute-start | bytes 393224 | tf_op jit(solution)/shard_map/ppermute | solution.py:400
  4.6 6.3 %collective-permute-start = (f32[2,128,128]{2,1,0:T(8,128)S(1)}, f32[2,128,128]{2,1,0:T(8,128)S(1)}, u32[]{:S(2)}, u32[]{:S(2)}) collective-permute-start(f32[2,128,128]{2,1,0:T(8,128)S(1)} %copy-done.1), channel_id=1, source_target_pairs={{0,1},{16,17},{1,0},{17,16},{2,3},{18,19},{3,2},{19,18},{4,5},{20,... | collective-permute-start | bytes 393224 | tf_op jit(solution)/shard_map/ppermute | solution.py:400
  6.1 4.7 %collective-permute-start.4 = (f32[2,64,128]{2,1,0:T(8,128)S(1)}, f32[2,64,128]{2,1,0:T(8,128)S(1)}, u32[]{:S(2)}, u32[]{:S(2)}) collective-permute-start(f32[2,64,128]{2,1,0:T(8,128)S(1)} %constant_dynamic-slice_fusion.7), channel_id=1, source_target_pairs={{1,18},{17,2},{2,17},{18,1},{3,20},{19,4},{4,19},{20,3},{5,22},{21... | collective-permute-start | bytes 196616 | tf_op jit(solution)/shard_map/ppermute | solution.py:400
  6.7 4.1 %collective-permute-start.3 = (f32[2,64,128]{2,1,0:T(8,128)S(1)}, f32[2,64,128]{2,1,0:T(8,128)S(1)}, u32[]{:S(2)}, u32[]{:S(2)}) collective-permute-start(f32[2,64,128]{2,1,0:T(8,128)S(1)} %collective-permute-done.2.rest_0_), channel_id=1, source_target_pairs={{0,1},{16,17},{1,0},{17,16},{2,3},{18,19},{3,2},{19,18},{4,5},{20,... | collective-permute-start | bytes 196616 | tf_op jit(solution)/shard_map/ppermute | solution.py:400
  7.8 1.0 %copy-start = (f32[2,4,128,128]{3,2,1,0:T(8,128)S(1)}, f32[2,4,128,128]{3,2,1,0:T(8,128)}, u32[]{:S(2)}) copy-start(f32[2,4,128,128]{3,2,1,0:T(8,128)} %probe_ref.1) | copy-start | bytes 1572868
  8.9 0.9 %copy-start.2 = (f32[1,1,3,128,128]{4,3,2,1,0:T(8,128)S(1)}, f32[1,1,3,128,128]{4,3,2,1,0:T(8,128)}, u32[]{:S(2)}) copy-start(f32[1,1,3,128,128]{4,3,2,1,0:T(8,128)} %param.7) | copy-start | bytes 589828
  9.8 0.9 %copy-start.3 = (bf16[4,128,128]{2,1,0:T(8,128)(2,1)S(1)}, bf16[4,128,128]{2,1,0:T(8,128)(2,1)}, u32[]{:S(2)}) copy-start(bf16[4,128,128]{2,1,0:T(8,128)(2,1)} %constant.85.clone.table_ref) | copy-start | bytes 393220
  16.3 0.7 copy-start.5
  17.0 2.0 %collective-permute-start.5 = (f32[4,136,128]{2,1,0:T(8,128)S(1)}, f32[4,136,128]{2,1,0:T(8,128)}, u32[]{:S(2)}, u32[]{:S(2)}) collective-permute-start(f32[4,136,128]{2,1,0:T(8,128)S(1)} %get-tuple-element.49), channel_id=1, source_target_pairs={{0,1},{1,0},{2,3},{3,2},{4,5},{5,4},{6,7},{7,6},{8,9},{9,8},{10,11... | collective-permute-start | bytes 835592 | tf_op jit(solution)/shard_map/ppermute | solution.py:66
  17.0 13.0 %collective-permute-start.9 = (f32[2,256,128]{2,1,0:T(8,128)}, f32[2,256,128]{2,1,0:T(8,128)S(1)}, u32[]{:S(2)}, u32[]{:S(2)}) collective-permute-start(f32[2,256,128]{2,1,0:T(8,128)} %copy-done.5), channel_id=1, source_target_pairs={{0,1},{16,17},{1,0},{17,16},{2,3},{18,19},{3,2},{19,18},{4,5},{20,... | collective-permute-start | bytes 786440 | tf_op jit(solution)/shard_map/ppermute | solution.py:400
  17.5 12.5 %collective-permute-start.10 = (f32[2,256,128]{2,1,0:T(8,128)S(1)}, f32[2,256,128]{2,1,0:T(8,128)S(1)}, u32[]{:S(2)}, u32[]{:S(2)}) collective-permute-start(f32[2,256,128]{2,1,0:T(8,128)S(1)} %get-tuple-element.51), channel_id=1, source_target_pairs={{1,2},{17,18},{2,1},{18,17},{3,4},{19,20},{4,3},{20,19},{5,6},{21,... | collective-permute-start | bytes 786440 | tf_op jit(solution)/shard_map/ppermute | solution.py:400
  20.0 3.6 %copy-start.6 = (f32[4,136,128]{2,1,0:T(8,128)}, f32[4,136,128]{2,1,0:T(8,128)S(1)}, u32[]{:S(2)}) copy-start(f32[4,136,128]{2,1,0:T(8,128)S(1)} %add.95) | copy-start | bytes 835588
  20.1 5.7 %collective-permute-start.6 = (f32[1,136,128]{2,1,0:T(8,128)S(1)}, f32[1,136,128]{2,1,0:T(8,128)}, u32[]{:S(2)}, u32[]{:S(2)}) collective-permute-start(f32[1,136,128]{2,1,0:T(8,128)S(1)} %get-tuple-element.81), channel_id=1, source_target_pairs={{0,16},{1,17},{2,18},{3,19},{4,20},{5,21},{6,22},{7,23},{8,24},{9,... | collective-permute-start | bytes 208904 | tf_op jit(solution)/shard_map/ppermute | solution.py:66
  21.3 6.6 %collective-permute-start.8 = (f32[1,136,128]{2,1,0:T(8,128)S(1)}, f32[1,136,128]{2,1,0:T(8,128)}, u32[]{:S(2)}, u32[]{:S(2)}) collective-permute-start(f32[1,136,128]{2,1,0:T(8,128)S(1)} %get-tuple-element.82), channel_id=1, source_target_pairs={{0,18},{1,19},{2,16},{3,17},{4,22},{5,23},{6,20},{7,21},{8,26},{9,... | collective-permute-start | bytes 208904 | tf_op jit(solution)/shard_map/ppermute | solution.py:66
  23.6 5.4 %collective-permute-start.7 = (f32[1,136,128]{2,1,0:T(8,128)S(1)}, f32[1,136,128]{2,1,0:T(8,128)}, u32[]{:S(2)}, u32[]{:S(2)}) collective-permute-start(f32[1,136,128]{2,1,0:T(8,128)S(1)} %get-tuple-element.83), channel_id=1, source_target_pairs={{0,2},{1,3},{2,0},{3,1},{4,6},{5,7},{6,4},{7,5},{8,10},{9,11},{10,... | collective-permute-start | bytes 208904 | tf_op jit(solution)/shard_map/ppermute | solution.py:66
  23.6 12.0 %copy-start.7 = (pred[128]{0:T(512)(128)(4,1)}, pred[128]{0:T(512)(128)(4,1)S(1)}, u32[]{:S(2)}) copy-start(pred[128]{0:T(512)(128)(4,1)S(1)} %fusion.4) | copy-start | bytes 388
  30.1 7.5 %collective-permute-start.13 = (f32[1,136,128]{2,1,0:T(8,128)S(1)}, f32[1,136,128]{2,1,0:T(8,128)S(1)}, u32[]{:S(2)}, u32[]{:S(2)}) collective-permute-start(f32[1,136,128]{2,1,0:T(8,128)S(1)} %add_add_fusion.3), channel_id=1, source_target_pairs={{0,12},{1,13},{2,14},{3,15},{4,8},{5,9},{6,10},{7,11},{8,4},{9,5},... | collective-permute-start | bytes 208904 | tf_op jit(solution)/shard_map/ppermute | solution.py:66
  35.0 5.4 %collective-permute-start.12 = (f32[1,136,128]{2,1,0:T(8,128)S(1)}, f32[1,136,128]{2,1,0:T(8,128)S(1)}, u32[]{:S(2)}, u32[]{:S(2)}) collective-permute-start(f32[1,136,128]{2,1,0:T(8,128)S(1)} %add_add_fusion.3), channel_id=1, source_target_pairs={{0,8},{1,9},{2,10},{3,11},{4,12},{5,13},{6,14},{7,15},{8,0},{9,1},... | collective-permute-start | bytes 208904 | tf_op jit(solution)/shard_map/ppermute | solution.py:66
  35.0 5.4 %collective-permute-start.11 = (f32[1,136,128]{2,1,0:T(8,128)S(1)}, f32[1,136,128]{2,1,0:T(8,128)S(1)}, u32[]{:S(2)}, u32[]{:S(2)}) collective-permute-start(f32[1,136,128]{2,1,0:T(8,128)S(1)} %add_add_fusion.3), channel_id=1, source_target_pairs={{0,4},{1,5},{2,6},{3,7},{4,0},{5,1},{6,2},{7,3},{8,12},{9,13},{10,... | collective-permute-start | bytes 208904 | tf_op jit(solution)/shard_map/ppermute | solution.py:66
  35.8 6.4 %collective-permute-start.14 = (f32[2,128,256]{2,1,0:T(8,128)S(1)}, f32[2,128,256]{2,1,0:T(8,128)S(1)}, u32[]{:S(2)}, u32[]{:S(2)}) collective-permute-start(f32[2,128,256]{2,1,0:T(8,128)S(1)} %fusion.1), channel_id=1, source_target_pairs={{0,16},{16,0},{1,17},{17,1},{2,18},{18,2},{3,19},{19,3},{4,20},{20... | collective-permute-start | bytes 786440 | tf_op jit(solution)/shard_map/ppermute | solution.py:400
  42.2 5.7 %collective-permute-start.17 = (f32[1,136,128]{2,1,0:T(8,128)S(1)}, f32[1,136,128]{2,1,0:T(8,128)S(1)}, u32[]{:S(2)}, u32[]{:S(2)}) collective-permute-start(f32[1,136,128]{2,1,0:T(8,128)S(1)} %add_add_fusion.2), channel_id=1, source_target_pairs={{0,18},{1,19},{2,16},{3,17},{4,22},{5,23},{6,20},{7,21},{8,26},{9,... | collective-permute-start | bytes 208904 | tf_op jit(solution)/shard_map/ppermute | solution.py:66
  44.5 4.3 %collective-permute-start.16 = (f32[1,136,128]{2,1,0:T(8,128)S(1)}, f32[1,136,128]{2,1,0:T(8,128)S(1)}, u32[]{:S(2)}, u32[]{:S(2)}) collective-permute-start(f32[1,136,128]{2,1,0:T(8,128)S(1)} %add_add_fusion.2), channel_id=1, source_target_pairs={{0,2},{1,3},{2,0},{3,1},{4,6},{5,7},{6,4},{7,5},{8,10},{9,11},{10,... | collective-permute-start | bytes 208904 | tf_op jit(solution)/shard_map/ppermute | solution.py:66
  44.9 4.3 %collective-permute-start.15 = (f32[1,136,128]{2,1,0:T(8,128)S(1)}, f32[1,136,128]{2,1,0:T(8,128)S(1)}, u32[]{:S(2)}, u32[]{:S(2)}) collective-permute-start(f32[1,136,128]{2,1,0:T(8,128)S(1)} %add_add_fusion.2), channel_id=1, source_target_pairs={{0,16},{1,17},{2,18},{3,19},{4,20},{5,21},{6,22},{7,23},{8,24},{9,... | collective-permute-start | bytes 208904 | tf_op jit(solution)/shard_map/ppermute | solution.py:66
  49.3 1.6 %collective-permute-start.18 = (f32[4,136,128]{2,1,0:T(8,128)S(1)}, f32[4,136,128]{2,1,0:T(8,128)S(1)}, u32[]{:S(2)}, u32[]{:S(2)}) collective-permute-start(f32[4,136,128]{2,1,0:T(8,128)S(1)} %pad_maximum_fusion.1.own_ref), channel_id=1, source_target_pairs={{0,1},{1,0},{2,3},{3,2},{4,5},{5,4},{6,7},{7,6},{8,9},{9,8},{10,11... | collective-permute-start | bytes 835592 | tf_op jit(solution)/shard_map/ppermute | solution.py:66
  56.6 1.7 %copy-start.4 = (f32[2,264,256]{2,1,0:T(8,128)}, f32[2,264,256]{2,1,0:T(8,128)S(1)}, u32[]{:S(2)}) copy-start(f32[2,264,256]{2,1,0:T(8,128)S(1)} %get-tuple-element.58) | copy-start | bytes 1622020
  56.6 1.6 %collective-permute-start.19 = (f32[4,136,128]{2,1,0:T(8,128)S(1)}, f32[4,136,128]{2,1,0:T(8,128)S(1)}, u32[]{:S(2)}, u32[]{:S(2)}) collective-permute-start(f32[4,136,128]{2,1,0:T(8,128)S(1)} %get-tuple-element.60), channel_id=1, source_target_pairs={{0,1},{1,0},{2,3},{3,2},{4,5},{5,4},{6,7},{7,6},{8,9},{9,8},{10,11... | collective-permute-start | bytes 835592 | tf_op jit(solution)/shard_map/ppermute | solution.py:66
  58.3 4.4 %collective-permute-start.20 = (f32[1,136,128]{2,1,0:T(8,128)S(1)}, f32[1,136,128]{2,1,0:T(8,128)S(1)}, u32[]{:S(2)}, u32[]{:S(2)}) collective-permute-start(f32[1,136,128]{2,1,0:T(8,128)S(1)} %get-tuple-element.74), channel_id=1, source_target_pairs={{0,16},{1,17},{2,18},{3,19},{4,20},{5,21},{6,22},{7,23},{8,24},{9,... | collective-permute-start | bytes 208904 | tf_op jit(solution)/shard_map/ppermute | solution.py:66
  59.2 6.1 %collective-permute-start.22 = (f32[1,136,128]{2,1,0:T(8,128)S(1)}, f32[1,136,128]{2,1,0:T(8,128)S(1)}, u32[]{:S(2)}, u32[]{:S(2)}) collective-permute-start(f32[1,136,128]{2,1,0:T(8,128)S(1)} %get-tuple-element.75), channel_id=1, source_target_pairs={{0,18},{1,19},{2,16},{3,17},{4,22},{5,23},{6,20},{7,21},{8,26},{9,... | collective-permute-start | bytes 208904 | tf_op jit(solution)/shard_map/ppermute | solution.py:66
  61.5 4.8 %collective-permute-start.21 = (f32[1,136,128]{2,1,0:T(8,128)S(1)}, f32[1,136,128]{2,1,0:T(8,128)S(1)}, u32[]{:S(2)}, u32[]{:S(2)}) collective-permute-start(f32[1,136,128]{2,1,0:T(8,128)S(1)} %get-tuple-element.76), channel_id=1, source_target_pairs={{0,2},{1,3},{2,0},{3,1},{4,6},{5,7},{6,4},{7,5},{8,10},{9,11},{10,... | collective-permute-start | bytes 208904 | tf_op jit(solution)/shard_map/ppermute | solution.py:66
  66.3 6.9 %collective-permute-start.25 = (f32[1,136,128]{2,1,0:T(8,128)S(1)}, f32[1,136,128]{2,1,0:T(8,128)S(1)}, u32[]{:S(2)}, u32[]{:S(2)}) collective-permute-start(f32[1,136,128]{2,1,0:T(8,128)S(1)} %add_add_fusion.1), channel_id=1, source_target_pairs={{0,12},{1,13},{2,14},{3,15},{4,8},{5,9},{6,10},{7,11},{8,4},{9,5},... | collective-permute-start | bytes 208904 | tf_op jit(solution)/shard_map/ppermute | solution.py:66
  68.9 6.6 %collective-permute-start.24 = (f32[1,136,128]{2,1,0:T(8,128)S(1)}, f32[1,136,128]{2,1,0:T(8,128)S(1)}, u32[]{:S(2)}, u32[]{:S(2)}) collective-permute-start(f32[1,136,128]{2,1,0:T(8,128)S(1)} %add_add_fusion.1), channel_id=1, source_target_pairs={{0,8},{1,9},{2,10},{3,11},{4,12},{5,13},{6,14},{7,15},{8,0},{9,1},... | collective-permute-start | bytes 208904 | tf_op jit(solution)/shard_map/ppermute | solution.py:66
  68.9 6.6 %collective-permute-start.23 = (f32[1,136,128]{2,1,0:T(8,128)S(1)}, f32[1,136,128]{2,1,0:T(8,128)S(1)}, u32[]{:S(2)}, u32[]{:S(2)}) collective-permute-start(f32[1,136,128]{2,1,0:T(8,128)S(1)} %add_add_fusion.1), channel_id=1, source_target_pairs={{0,4},{1,5},{2,6},{3,7},{4,0},{5,1},{6,2},{7,3},{8,12},{9,13},{10,... | collective-permute-start | bytes 208904 | tf_op jit(solution)/shard_map/ppermute | solution.py:66
  70.7 6.4 %collective-permute-start.27 = (f32[2,256,128]{2,1,0:T(8,128)S(1)}, f32[2,256,128]{2,1,0:T(8,128)S(1)}, u32[]{:S(2)}, u32[]{:S(2)}) collective-permute-start(f32[2,256,128]{2,1,0:T(8,128)S(1)} %get-tuple-element.61), channel_id=1, source_target_pairs={{1,2},{17,18},{2,1},{18,17},{3,4},{19,20},{4,3},{20,19},{5,6},{21,... | collective-permute-start | bytes 786440 | tf_op jit(solution)/shard_map/ppermute | solution.py:400
  71.6 5.5 %collective-permute-start.26 = (f32[2,256,128]{2,1,0:T(8,128)S(1)}, f32[2,256,128]{2,1,0:T(8,128)S(1)}, u32[]{:S(2)}, u32[]{:S(2)}) collective-permute-start(f32[2,256,128]{2,1,0:T(8,128)S(1)} %get-tuple-element.61), channel_id=1, source_target_pairs={{0,1},{16,17},{1,0},{17,16},{2,3},{18,19},{3,2},{19,18},{4,5},{20,... | collective-permute-start | bytes 786440 | tf_op jit(solution)/shard_map/ppermute | solution.py:400
  75.6 6.0 %copy-start.8 = (pred[128]{0:T(512)(128)(4,1)S(1)}, pred[128]{0:T(512)(128)(4,1)}, u32[]{:S(2)}) copy-start(pred[128]{0:T(512)(128)(4,1)} %copy-done.7) | copy-start | bytes 388
  77.1 6.4 %collective-permute-start.30 = (f32[1,136,128]{2,1,0:T(8,128)S(1)}, f32[1,136,128]{2,1,0:T(8,128)S(1)}, u32[]{:S(2)}, u32[]{:S(2)}) collective-permute-start(f32[1,136,128]{2,1,0:T(8,128)S(1)} %add_add_fusion), channel_id=1, source_target_pairs={{0,18},{1,19},{2,16},{3,17},{4,22},{5,23},{6,20},{7,21},{8,26},{9,... | collective-permute-start | bytes 208904 | tf_op jit(solution)/shard_map/ppermute | solution.py:66
  80.4 4.3 %collective-permute-start.29 = (f32[1,136,128]{2,1,0:T(8,128)S(1)}, f32[1,136,128]{2,1,0:T(8,128)S(1)}, u32[]{:S(2)}, u32[]{:S(2)}) collective-permute-start(f32[1,136,128]{2,1,0:T(8,128)S(1)} %add_add_fusion), channel_id=1, source_target_pairs={{0,2},{1,3},{2,0},{3,1},{4,6},{5,7},{6,4},{7,5},{8,10},{9,11},{10,... | collective-permute-start | bytes 208904 | tf_op jit(solution)/shard_map/ppermute | solution.py:66
  80.4 4.9 %collective-permute-start.28 = (f32[1,136,128]{2,1,0:T(8,128)S(1)}, f32[1,136,128]{2,1,0:T(8,128)S(1)}, u32[]{:S(2)}, u32[]{:S(2)}) collective-permute-start(f32[1,136,128]{2,1,0:T(8,128)S(1)} %add_add_fusion), channel_id=1, source_target_pairs={{0,16},{1,17},{2,18},{3,19},{4,20},{5,21},{6,22},{7,23},{8,24},{9,... | collective-permute-start | bytes 208904 | tf_op jit(solution)/shard_map/ppermute | solution.py:66
  82.6 4.3 %collective-permute-start.31 = (f32[2,64,128]{2,1,0:T(8,128)S(1)}, f32[2,64,128]{2,1,0:T(8,128)S(1)}, u32[]{:S(2)}, u32[]{:S(2)}) collective-permute-start(f32[2,64,128]{2,1,0:T(8,128)S(1)} %constant_dynamic-slice_fusion), channel_id=1, source_target_pairs={{0,16},{16,0},{1,17},{17,1},{2,18},{18,2},{3,19},{19,3},{4,20},{20... | collective-permute-start | bytes 196616 | tf_op jit(solution)/shard_map/ppermute | solution.py:400
  86.9 1.6 %collective-permute-start.32 = (f32[4,136,128]{2,1,0:T(8,128)S(1)}, f32[4,136,128]{2,1,0:T(8,128)S(1)}, u32[]{:S(2)}, u32[]{:S(2)}) collective-permute-start(f32[4,136,128]{2,1,0:T(8,128)S(1)} %pad_maximum_fusion.3.own_ref), channel_id=1, source_target_pairs={{0,1},{1,0},{2,3},{3,2},{4,5},{5,4},{6,7},{7,6},{8,9},{9,8},{10,11... | collective-permute-start | bytes 835592 | tf_op jit(solution)/shard_map/ppermute | solution.py:66

commit v2 on v1

--- a/solution.py
+++ b/solution.py
@@ -73,8 +73,11 @@
 
 def product(a, b):
     (a_high, a_low), (b_high, b_low) = a, b
-    dot = functools.partial(jnp.dot, preferred_element_type=F32)
-    return dot(a_high, b_high) + (dot(a_low, b_high) + dot(a_high, b_low))
+    return jnp.dot(
+        jnp.concatenate([a_high, a_low, a_high], axis=1),
+        jnp.concatenate([b_high, b_high, b_low], axis=0),
+        preferred_element_type=F32,
+    )
 
 
 def block(c, upper, lower):
@@ -176,13 +179,27 @@
     return weight
 
 
-def emit_halves(grad_ref, weight, keep_ref, send_ref, half):
+def emit(grad_ref, weight, grid_ref, keep_ref, send_ref, first_ref, second_ref, rim_refs, margin):
     count, win = keep_ref.shape[0], grad_ref.shape[1]
+    odd_y, odd_x = lax.axis_index("ty") % 2, lax.axis_index("tx") % 2
     for j in range(count):
-        keep_ref[j, :win, :] = grad_ref[half * count + j]
-        send_ref[j, :win, :] = grad_ref[(1 - half) * count + j]
+        keep_ref[j, :win, :] = grad_ref[odd_x * count + j]
+        send_ref[j, :win, :] = grad_ref[(1 - odd_x) * count + j]
         keep_ref[j, win:, :] = weight
         send_ref[j, win:, :] = weight
+    tile = first_ref.shape[-1]
+    mask = rowwise(lane_pick(tile, margin, odd_x), tile)
+    for part in (0, 1):
+        rows = grid_ref[part, margin : margin + tile, :]
+        first_ref[part], second_ref[part] = chosen(mask, rows[:, tile:], rows[:, :tile])
+        for i, ref in enumerate(rim_refs):
+            start = pl.multiple_of(jnp.where(odd_y == i, 2 * tile - margin, 0), margin)
+            rows = grid_ref[part, pl.ds(start, margin), :]
+            ref[0, part], ref[1, part] = chosen(mask[:margin], rows[:, tile:], rows[:, :tile])
+
+
+def chosen(mask, a, b):
+    return jnp.where(mask, a, b), jnp.where(mask, b, a)
 
 
 def prepare_kernel(probe_ref, meas_ref, table_ref, probe_out, root_ref, table_out):
@@ -196,7 +213,8 @@
     ty_refs = [next(take) for _ in range(n_y)]
     tx_refs = [next(take) for _ in range(n_x)]
     corner_refs = [[next(take) for _ in range(n_x)] for _ in range(n_y)]
-    ext_ref, keep_ref, send_ref, grid_ref, *msg_refs, grad_ref = take
+    ext_ref, keep_ref, send_ref, first_ref, second_ref, *rim_refs = take
+    *rim_refs, grid_ref, grad_ref = rim_refs
     tile = obj_ref.shape[-1]
     at_y, at_x = lax.axis_index("ty"), lax.axis_index("tx")
     odd_y, odd_x = at_y % 2, at_x % 2
@@ -223,14 +241,9 @@
     weight = compute(
         ext_ref, probe_ref, root_ref, pos_ref, table_ref, grid_ref, grad_ref, margin=margin
     )
-    emit_halves(grad_ref, weight, keep_ref, send_ref, odd_x)
-    for i, ref in enumerate(msg_refs):
-        high = jnp.where(odd_x == i, 1, 0)
-        mask = rowwise(lane_pick(tile, margin, high), 2 * tile)
-        for part in (0, 1):
-            ref[part] = jnp.where(
-                mask, grid_ref[part, : 2 * tile, :tile], grid_ref[part, : 2 * tile, tile:]
-            )
+    emit(
+        grad_ref, weight, grid_ref, keep_ref, send_ref, first_ref, second_ref, rim_refs, margin
+    )
 
 
 def combined_probe(probe_ref, own_ref, other_ref, new_ref, half):
@@ -245,13 +258,14 @@
 
 
 def second_kernel(
-    n_ty, n_tx, n_y, n_x, margin, pos_ref, old_ref, grid_old_ref, probe_ref, root_ref, table_ref,
-    own_ref, other_ref, *rest
+    n_ty, n_tx, n_y, n_x, margin, pos_ref, old_ref, first_ref, second_ref, probe_ref, root_ref,
+    table_ref, own_ref, other_ref, *rest
 ):
     take = iter(rest)
     tx_refs = [next(take) for _ in range(n_x)]
-    ty_refs = [next(take) for _ in range(n_y)]
-    tile_ref, new_ref, keep_ref, send_ref, grid_ref, edge_ref, ext_ref, grad_ref = take
+    halo_refs = [next(take) for _ in range(n_y)]
+    tile_ref, new_ref, keep_ref, send_ref, next_first_ref, next_second_ref, *rim_refs = take
+    *rim_refs, ext_ref, grid_ref, grad_ref = rim_refs
     tile = probe_ref.shape[-1]
     at_y, at_x = lax.axis_index("ty"), lax.axis_index("tx")
     odd_y, odd_x = at_y % 2, at_x % 2
@@ -264,47 +278,48 @@
     inside &= (lane < jnp.where(at_x == n_tx - 1, tile, tile + margin)) | (
         lane >= jnp.where(at_x == 0, 2 * tile, tile + margin)
     )
+    mask = rowwise(lane_pick(tile, margin, odd_x), tile)
+    for i in range(2):
+        start = pl.multiple_of(jnp.where(odd_y == i, margin + tile, 0), margin)
+        for part in (0, 1):
+            if i < n_y:
+                ref = halo_refs[i]
+                own, margins = chosen(mask[:margin], ref[1, part], ref[0, part])
+                rows = jnp.concatenate([own, margins], axis=1)
+            else:
+                rows = jnp.zeros((margin, 2 * tile), F32)
+            ext_ref[part, pl.ds(start, margin), :] = rows
     for part in (0, 1):
-        total = grid_old_ref[part, : 2 * tile, :]
-        if n_x:
-            total = total + spread(tx_refs, part, at_x, n_tx, margin, tile)
-        ext_ref[part, : 2 * tile, :] = total
-        for i, ref in enumerate(ty_refs):
-            start = pl.multiple_of(jnp.where(odd_y == i, tile, 0), tile)
-            ext_ref[part, pl.ds(start, tile), :] += if_paired(ref[part], at_y, n_ty, i)
+        both = [first_ref[part], second_ref[part]]
+        for i, ref in enumerate(tx_refs):
+            both[i] = both[i] + if_paired(ref[part], at_x, n_tx, i)
+        own, margins = chosen(mask, both[1], both[0])
+        ext_ref[part, margin : margin + tile, :] = jnp.concatenate([own, margins], axis=1)
         step = jnp.where(inside, OBJECT_STEP * ext_ref[part, : 2 * tile, :], 0.0)
         ext_ref[part, : 2 * tile, :] = old_ref[part, : 2 * tile, :] + step
         tile_ref[part] = ext_ref[part, margin : margin + tile, :tile]
     weight = compute(
         ext_ref, new_ref, root_ref, pos_ref, table_ref, grid_ref, grad_ref, margin=margin
     )
-    emit_halves(grad_ref, weight, keep_ref, send_ref, odd_x)
-    edge_ref[...] = grid_ref[:, : 2 * tile, tile:]
-
-
-def spread(tx_refs, part, at_x, n_tx, margin, tile):
-    rows = 2 * tile
-    both = [if_paired(ref[part], at_x, n_tx, i) for i, ref in enumerate(tx_refs)]
-    both += [jnp.zeros((rows, tile), F32)] * (2 - len(both))
-    low = rowwise(lane_pick(tile, margin, at_x % 2), rows)
-    return jnp.concatenate(
-        [jnp.where(low, both[1], both[0]), jnp.where(low, both[0], both[1])], axis=1
-    )
-
-
-def last_kernel(n_ty, n_y, margin, tile_ref, mid_ref, probe_ref, own_ref, other_ref, *rest):
-    take = iter(rest)
-    ty_refs = [next(take) for _ in range(n_y)]
-    obj_ref, new_ref = take
-    tile = probe_ref.shape[-1]
-    at_y = lax.axis_index("ty")
-    combined_probe(probe_ref, own_ref, other_ref, new_ref, lax.axis_index("tx") % 2)
+    emit(
+        grad_ref, weight, grid_ref, keep_ref, send_ref, next_first_ref, next_second_ref, rim_refs,
+        margin,
+    )
+
+
+def last_kernel(
+    n_tx, n_x, margin, tile_ref, first_ref, second_ref, probe_ref, own_ref, other_ref, *rest
+):
+    *tx_refs, obj_ref, new_ref = rest
+    tile = tile_ref.shape[-1]
+    at_x = lax.axis_index("tx")
+    combined_probe(probe_ref, own_ref, other_ref, new_ref, at_x % 2)
+    mask = rowwise(lane_pick(tile, margin, at_x % 2), tile)
     for part in (0, 1):
-        obj_ref[part] = mid_ref[part, margin : margin + tile, :]
-        for i, ref in enumerate(ty_refs):
-            start = pl.multiple_of(jnp.where(at_y % 2 == i, tile - margin, 0), margin)
-            obj_ref[part, pl.ds(start, margin), :] += if_paired(ref[part], at_y, n_ty, i)
-        obj_ref[part] = tile_ref[part] + OBJECT_STEP * obj_ref[part]
+        both = [first_ref[part], second_ref[part]]
+        for i, ref in enumerate(tx_refs):
+            both[i] = both[i] + if_paired(ref[part], at_x, n_tx, i)
+        obj_ref[part] = tile_ref[part] + OBJECT_STEP * chosen(mask, both[1], both[0])[0]
 
 
 def call(kernel, outs, ins, scratch=()):
@@ -361,7 +376,7 @@
     )
 
 
-def summed_halves(keep, send, n_ty, n_tx, columns, rows, early):
+def summed_halves(keep, send, n_ty, n_tx, steps):
     total = n_ty * n_tx
     me = lax.axis_index("ty") * n_tx + lax.axis_index("tx")
     levels = total.bit_length() - 1
@@ -369,22 +384,18 @@
     bits = [b for b in (tx_bits, 1) if b < levels]
     rest = [b for b in range(1, levels) if b not in bits]
     half = keep + xor_permute(send, 1, total)
-    across = columns()
+    done = [steps[0]()]
     half = scatter_sum(half, me, bits, total)
-    if early:
-        half, across = lax.optimization_barrier((half, across))
-        along = rows(across)
+    half, done[0] = lax.optimization_barrier((half, done[0]))
+    done.append(steps[1](*done))
     for i in range(0, len(rest), 2):
         half = direct_sum(half, rest[i : i + 2], total)
-    if early:
-        half, along = lax.optimization_barrier((half, along))
-    else:
-        half, across = lax.optimization_barrier((half, across))
-        along = rows(across)
+    half, done[1] = lax.optimization_barrier((half, done[1]))
+    done += [step(*done) for step in steps[2:]]
     half = gather(half, me, bits, total)
-    if not early:
-        half, along = lax.optimization_barrier((half, along))
-    return half, xor_permute(half, 1, total), across, along
+    if steps[2:]:
+        half, done[2] = lax.optimization_barrier((half, done[2]))
+    return half, xor_permute(half, 1, total), done
 
 
 def per_device(n_ty, n_tx, table, object_field, probe, intensities, positions):
@@ -418,60 +429,63 @@
         ((tx_in, ty_in, corners), tuple(ready))
     )
 
-    at_x = lax.axis_index("tx")
-    lane = lax.broadcasted_iota(jnp.int32, (1, 1, tile), 2)
-    low = jnp.where(lane < margin, 0, 1) == at_x % 2
-
-    def joined(messages):
-        both = [if_paired(m, at_x, n_tx, i) for i, m in enumerate(messages)]
-        both += [jnp.zeros_like(messages[0])] * (2 - n_x)
-        return jnp.where(low, both[1], both[0]), jnp.where(low, both[0], both[1])
-
+    at_y, at_x = lax.axis_index("ty"), lax.axis_index("tx")
     half_shape = (modes, win + WEIGHT_ROWS, win)
     grid_shape = (2, 2 * tile + SUBLANES, 2 * tile)
-    msg_shape = (2, 2 * tile, tile)
-    ext, keep, send, grid, *msgs = call(
+    sent = [half_shape] * 2 + [object_field.shape] * 2 + [(2, 2, margin, tile)] * n_y
+    scratch = [grid_shape, (2 * modes, win, win)]
+
+    def exchanges(overlaps, rims):
+        def folded(received):
+            halves = [x.reshape(2, 2, margin, tile) for x in overlaps]
+            place = lax.broadcasted_iota(jnp.int32, (1, 2, 1, 1), 1)
+            for i, y in enumerate(received):
+                here = place == jnp.where(odd_y == i, 1, 0)
+                for k in (0, 1):
+                    extra = if_paired(y[k][:, None], at_y, n_ty, i)
+                    halves[k] = halves[k] + jnp.where(here, extra, 0.0)
+            return [x.reshape(object_field.shape) for x in halves]
+
+        def fold():
+            return [swap(rim, py, None) for rim, py in zip(rims, match_y)]
+
+        def across(received):
+            mine = folded(received)
+            return mine, [swap(x, None, px) for x, px in zip(mine, match_x)]
+
+        def halo(received, columns):
+            mine, theirs = columns
+            total = list(mine)
+            for i, x in enumerate(theirs):
+                total[i] = total[i] + if_paired(x, at_x, n_tx, i)
+            bands = [
+                jnp.stack([rows_for(x, i, margin, 0, tile - margin) for x in total])
+                for i in range(n_y)
+            ]
+            return [swap(band, py, None) for band, py in zip(bands, match_y)]
+
+        return fold, across, halo
+
+    ext, keep, send, first, second, *rims = call(
         functools.partial(first_kernel, n_ty, n_tx, n_y, n_x, margin),
-        [grid_shape, half_shape, half_shape, grid_shape] + [msg_shape] * n_x,
+        [grid_shape] + sent,
         [spots, object_field, probe, root, table, *ty_in, *tx_in, *corners],
-        [(2 * modes, win, win)],
-    )
-
-    def columns():
-        return [swap(m, None, px) for m, px in zip(msgs, match_x)]
-
-    def rows(across):
-        wide = grid[:, : 2 * tile, :]
-        if n_x:
-            wide = wide + jnp.concatenate(joined(across), axis=2)
-        bands = [rows_for(wide, i, tile, 0, tile) for i in range(n_y)]
-        return [swap(bands[i], py, None) for i, py in enumerate(match_y)]
-
-    own, other, tx_in, ty_in = summed_halves(keep, send, n_ty, n_tx, columns, rows, True)
-    tile_mid, probe_mid, keep, send, grid_last, edge = call(
+        scratch,
+    )
+    steps = exchanges([first, second], rims)
+    own, other, (_, (overlaps, tx_in), halo) = summed_halves(keep, send, n_ty, n_tx, steps)
+    tile_mid, probe_mid, keep, send, first, second, *rims = call(
         functools.partial(second_kernel, n_ty, n_tx, n_y, n_x, margin),
-        [object_field.shape, probe.shape, half_shape, half_shape, grid_shape, msg_shape],
-        [spots, ext, grid, probe, root, table, own, other, *tx_in, *ty_in],
-        [grid_shape, (2 * modes, win, win)],
-    )
-
-    def columns():
-        return [swap(edge, None, px) for px in match_x]
-
-    def middle(across):
-        mid = grid_last[:, : 2 * tile, :tile]
-        return mid + joined(across)[0] if n_x else mid
-
-    def rows(across):
-        mid = middle(across)
-        bands = [rows_for(mid, i, margin, 0, 2 * tile - margin) for i in range(n_y)]
-        return [swap(bands[i], py, None) for i, py in enumerate(match_y)]
-
-    own, other, tx_in, ty_in = summed_halves(keep, send, n_ty, n_tx, columns, rows, False)
+        [object_field.shape, probe.shape] + sent,
+        [spots, ext, *overlaps, probe, root, table, own, other, *tx_in, *halo],
+        [grid_shape] + scratch,
+    )
+    steps = exchanges([first, second], rims)
+    own, other, (_, (overlaps, tx_in)) = summed_halves(keep, send, n_ty, n_tx, steps[:2])
     return call(
-        functools.partial(last_kernel, n_ty, n_y, margin),
+        functools.partial(last_kernel, n_tx, n_x, margin),
         [object_field.shape, probe.shape],
-        [tile_mid, middle(tx_in), probe_mid, own, other, *ty_in],
+        [tile_mid, *overlaps, probe_mid, own, other, *tx_in],
     )
 
 

time: 89.8 us -> 83.6 us (0.931)
  other arithmetic: 3.31 us -> 0.47 us
  waiting for transfers between devices: 32.1 us -> 30.5 us
    ppermute x22, waiting for transfers between devices: 27.2 us -> 25.2 us  [xor_permute(): return lax.ppermute(x, AXES, [(i, i ^ mask) for i in range(total)])]
    ppermute x22, starting transfers between devices: 25.4 us -> 23.5 us  [xor_permute(): return lax.ppermute(x, AXES, [(i, i ^ mask) for i in range(total)])]
    ppermute x11 -> x12, starting transfers between devices: 10.8 us -> 12 us  [swap(): return lax.ppermute(x, AXES, flat_pairs(pairs_y, pairs_x, n_ty, n_tx))]
    add x4, other arithmetic: 1.05 us -> 0.08 us  [tree(): a + b]
    add x2, other arithmetic: 1.03 us -> 0.06 us  [summed_halves(): half = keep + xor_permute(send, 1, total)]
    unnamed x20 -> x10, local copies, waits for them, and re-layouts: 3.59 us -> 2.88 us
    ppermute x11 -> x12, waiting for transfers between devices: 4.95 us -> 5.29 us  [swap(): return lax.ppermute(x, AXES, flat_pairs(pairs_y, pairs_x, n_ty, n_tx))]
  transfers between devices with their start and end apart: 33 -> 34, of which waited for: 22 -> 24; matrix products, arithmetic and copies ran while one was open for 4% -> 1% of each run, Pallas kernels for 0% -> 0%
where the time goes in v2:
time: 83.6 us; the launch traced here: 83.3 us
  starting transfers between devices  35.5 us (42%)
  waiting for transfers between devices  30.5 us (36%)
  Pallas kernels  11.8 us (14%)
  local copies, waits for them, and re-layouts  4.16 us (5%)
  between operations  0.84 us (1%)
    ppermute x22, waiting for transfers between devices, xor_permute(): return lax.ppermute(x, AXES, [(i, i ^ mask) for i in range(total)])  25.2 us
    ppermute x22, starting transfers between devices, xor_permute(): return lax.ppermute(x, AXES, [(i, i ^ mask) for i in range(total)])  23.5 us
    ppermute x12, starting transfers between devices, swap(): return lax.ppermute(x, AXES, flat_pairs(pairs_y, pairs_x, n_ty, n_tx))  12 us
    pallas_call x4, Pallas kernels, call(): pl.pallas_call(kernel, out_shape=shapes, in_specs=[smem if x.dtype == jnp...  11.8 us
    ppermute x12, waiting for transfers between devices, swap(): return lax.ppermute(x, AXES, flat_pairs(pairs_y, pairs_x, n_ty, n_tx))  5.29 us
    unnamed x10, local copies, waits for them, and re-layouts  2.88 us
  transfers between devices with their start and end apart: 34, of which 24 were waited for; matrix products, arithmetic and copies ran while one was open for 1% of the time, Pallas kernels for 0%

profile of v2, /device:TPU:0, one launch (start us, length us, event | category | flops | bytes accessed | tf_op | source)
XLA Modules:
  0.0 83.3 jit_solution(10048314359412583519)
XLA Ops:
  0.7 0.9 %constant_dynamic-slice_fusion.6 = f32[2,64,128]{2,1,0:T(8,128)S(1)} fusion(f32[2,128,128]{2,1,0:T(8,128)} %obj_ref.1, s32[]{:T(128)S(6)} %select_n.77), kind=kLoop, calls=%fused_computation.41 | loop fusion | bytes 131076 | tf_op jit(solution)/shard_map/dynamic_slice | solution.py:415
  1.6 2.9 %collective-permute-start.2 = (f32[2,64,128]{2,1,0:T(8,128)S(1)}, f32[2,64,128]{2,1,0:T(8,128)S(1)}, u32[]{:S(2)}, u32[]{:S(2)}) collective-permute-start(f32[2,64,128]{2,1,0:T(8,128)S(1)} %constant_dynamic-slice_fusion.6), channel_id=1, source_target_pairs={{0,16},{16,0},{1,17},{17,1},{2,18},{18,2},{3,19},{19,3},{4,20},{20... | collective-permute-start | bytes 196616 | tf_op jit(solution)/shard_map/ppermute | solution.py:411
  4.6 1.6 %collective-permute-start = (f32[2,128,128]{2,1,0:T(8,128)S(1)}, f32[2,128,128]{2,1,0:T(8,128)S(1)}, u32[]{:S(2)}, u32[]{:S(2)}) collective-permute-start(f32[2,128,128]{2,1,0:T(8,128)S(1)} %copy-done.1), channel_id=1, source_target_pairs={{0,1},{16,17},{1,0},{17,16},{2,3},{18,19},{3,2},{19,18},{4,5},{20,... | collective-permute-start | bytes 393224 | tf_op jit(solution)/shard_map/ppermute | solution.py:411
  6.1 0.5 collective-permute-start.4
  6.7 1.0 %collective-permute-start.3 = (f32[2,64,128]{2,1,0:T(8,128)S(1)}, f32[2,64,128]{2,1,0:T(8,128)S(1)}, u32[]{:S(2)}, u32[]{:S(2)}) collective-permute-start(f32[2,64,128]{2,1,0:T(8,128)S(1)} %collective-permute-done.2.rest_0_), channel_id=1, source_target_pairs={{0,1},{16,17},{1,0},{17,16},{2,3},{18,19},{3,2},{19,18},{4,5},{20,... | collective-permute-start | bytes 196616 | tf_op jit(solution)/shard_map/ppermute | solution.py:411
  7.7 0.1 copy.8.pos_ref
  7.8 1.0 %copy-done = f32[2,4,128,128]{3,2,1,0:T(8,128)S(1)} copy-done((f32[2,4,128,128]{3,2,1,0:T(8,128)S(1)}, f32[2,4,128,128]{3,2,1,0:T(8,128)}, u32[]{:S(2)}) %copy-start) | copy-done | bytes 524312
  8.9 0.9 %copy-done.2 = f32[1,1,3,128,128]{4,3,2,1,0:T(8,128)S(1)} copy-done((f32[1,1,3,128,128]{4,3,2,1,0:T(8,128)S(1)}, f32[1,1,3,128,128]{4,3,2,1,0:T(8,128)}, u32[]{:S(2)}) %copy-start.2) | copy-done | bytes 196632
  9.8 0.9 %copy-done.3 = bf16[4,128,128]{2,1,0:T(8,128)(2,1)S(1)} copy-done((bf16[4,128,128]{2,1,0:T(8,128)(2,1)S(1)}, bf16[4,128,128]{2,1,0:T(8,128)(2,1)}, u32[]{:S(2)}) %copy-start.3) | copy-done | bytes 131096
  10.7 0.1 shard_map.68
  10.8 5.3 %shard_map.69 = (f32[2,264,256]{2,1,0:T(8,128)S(1)}, f32[4,136,128]{2,1,0:T(8,128)S(1)}, f32[4,136,128]{2,1,0:T(8,128)S(1)}, f32[2,128,128]{2,1,0:T(8,128)S(1)},...) custom-call(s32[3,2]{1,0:T(4,128)S(1)} %copy.8.pos_ref, f32[2,128,128]{2,1,0:T(8,128)S(1)} %copy-done.1, ...), custom_call_target="tpu_custom_call" | custom-call | tf_op jit(solution)/shard_map/pallas_call | solution.py:329
  16.2 0.1 collective-permute-start.5
  16.3 1.5 %collective-permute-done.5 = f32[4,136,128]{2,1,0:T(8,128)S(1)} collective-permute-done((f32[4,136,128]{2,1,0:T(8,128)S(1)}, f32[4,136,128]{2,1,0:T(8,128)S(1)}, u32[]{:S(2)}, u32[]{:S(2)}) %collective-permute-start.5) | collective-permute-done | bytes 278560 | tf_op jit(solution)/shard_map/ppermute | solution.py:66
  17.8 1.6 %collective-permute-start.6 = (f32[1,136,128]{2,1,0:T(8,128)S(1)}, f32[1,136,128]{2,1,0:T(8,128)S(1)}, u32[]{:S(2)}, u32[]{:S(2)}) collective-permute-start(f32[1,136,128]{2,1,0:T(8,128)S(1)} %get-tuple-element.93), channel_id=1, source_target_pairs={{0,16},{1,17},{2,18},{3,19},{4,20},{5,21},{6,22},{7,23},{8,24},{9,... | collective-permute-start | bytes 208904 | tf_op jit(solution)/shard_map/ppermute | solution.py:66
  19.4 1.9 %collective-permute-start.8 = (f32[1,136,128]{2,1,0:T(8,128)S(1)}, f32[1,136,128]{2,1,0:T(8,128)S(1)}, u32[]{:S(2)}, u32[]{:S(2)}) collective-permute-start(f32[1,136,128]{2,1,0:T(8,128)S(1)} %get-tuple-element.94), channel_id=1, source_target_pairs={{0,18},{1,19},{2,16},{3,17},{4,22},{5,23},{6,20},{7,21},{8,26},{9,... | collective-permute-start | bytes 208904 | tf_op jit(solution)/shard_map/ppermute | solution.py:66
  21.5 0.1 broadcast_in_dim.71
  21.6 1.5 %collective-permute-start.9 = (f32[2,2,64,128]{3,2,1,0:T(8,128)S(1)}, f32[2,2,64,128]{3,2,1,0:T(8,128)S(1)}, u32[]{:S(2)}, u32[]{:S(2)}) collective-permute-start(f32[2,2,64,128]{3,2,1,0:T(8,128)S(1)} %get-tuple-element.56), channel_id=1, source_target_pairs={{0,16},{16,0},{1,17},{17,1},{2,18},{18,2},{3,19},{19,3},{4,20},{20... | collective-permute-start | bytes 393224 | tf_op jit(solution)/shard_map/ppermute | solution.py:411
  23.1 2.3 %collective-permute-done.8 = f32[1,136,128]{2,1,0:T(8,128)S(1)} collective-permute-done((f32[1,136,128]{2,1,0:T(8,128)S(1)}, f32[1,136,128]{2,1,0:T(8,128)S(1)}, u32[]{:S(2)}, u32[]{:S(2)}) %collective-permute-start.8) | collective-permute-done | bytes 69664 | tf_op jit(solution)/shard_map/ppermute | solution.py:66
  25.4 1.1 %collective-permute-done.7 = f32[1,136,128]{2,1,0:T(8,128)S(1)} collective-permute-done((f32[1,136,128]{2,1,0:T(8,128)S(1)}, f32[1,136,128]{2,1,0:T(8,128)S(1)}, u32[]{:S(2)}, u32[]{:S(2)}) %collective-permute-start.7) | collective-permute-done | bytes 69664 | tf_op jit(solution)/shard_map/ppermute | solution.py:66
  26.5 1.0 %collective-permute-done.9 = f32[2,2,64,128]{3,2,1,0:T(8,128)S(1)} collective-permute-done((f32[2,2,64,128]{3,2,1,0:T(8,128)S(1)}, f32[2,2,64,128]{3,2,1,0:T(8,128)S(1)}, u32[]{:S(2)}, u32[]{:S(2)}) %collective-permute-start.9) | collective-permute-done | bytes 131104 | tf_op jit(solution)/shard_map/ppermute | solution.py:411
  27.5 4.0 %collective-permute-start.12 = (f32[1,136,128]{2,1,0:T(8,128)S(1)}, f32[1,136,128]{2,1,0:T(8,128)S(1)}, u32[]{:S(2)}, u32[]{:S(2)}) collective-permute-start(f32[1,136,128]{2,1,0:T(8,128)S(1)} %add_add_fusion.3), channel_id=1, source_target_pairs={{0,12},{1,13},{2,14},{3,15},{4,8},{5,9},{6,10},{7,11},{8,4},{9,5},... | collective-permute-start | bytes 208904 | tf_op jit(solution)/shard_map/ppermute | solution.py:66
  31.5 0.6 collective-permute-start.10
  32.1 0.1 fusion.2
  32.2 0.9 %collective-permute-start.14 = (f32[2,128,128]{2,1,0:T(8,128)S(1)}, f32[2,128,128]{2,1,0:T(8,128)S(1)}, u32[]{:S(2)}, u32[]{:S(2)}) collective-permute-start(f32[2,128,128]{2,1,0:T(8,128)S(1)} %get-tuple-element.62.second_ref), channel_id=1, source_target_pairs={{1,2},{17,18},{2,1},{18,17},{3,4},{19,20},{4,3},{20,19},{5,6},{21,... | collective-permute-start | bytes 393224 | tf_op jit(solution)/shard_map/ppermute | solution.py:411
  33.0 0.3 collective-permute-start.13
  33.3 0.6 collective-permute-done.12
  33.9 2.9 %collective-permute-done.11 = f32[1,136,128]{2,1,0:T(8,128)S(1)} collective-permute-done((f32[1,136,128]{2,1,0:T(8,128)S(1)}, f32[1,136,128]{2,1,0:T(8,128)S(1)}, u32[]{:S(2)}, u32[]{:S(2)}) %collective-permute-start.11) | collective-permute-done | bytes 69664 | tf_op jit(solution)/shard_map/ppermute | solution.py:66
  36.8 0.1 collective-permute-done.10
  36.9 0.3 collective-permute-done.14.rest_1_
  37.2 1.3 %collective-permute-start.17 = (f32[1,136,128]{2,1,0:T(8,128)S(1)}, f32[1,136,128]{2,1,0:T(8,128)S(1)}, u32[]{:S(2)}, u32[]{:S(2)}) collective-permute-start(f32[1,136,128]{2,1,0:T(8,128)S(1)} %add_add_fusion.2), channel_id=1, source_target_pairs={{0,18},{1,19},{2,16},{3,17},{4,22},{5,23},{6,20},{7,21},{8,26},{9,... | collective-permute-start | bytes 208904 | tf_op jit(solution)/shard_map/ppermute | solution.py:66
  38.5 1.0 %collective-permute-start.16 = (f32[1,136,128]{2,1,0:T(8,128)S(1)}, f32[1,136,128]{2,1,0:T(8,128)S(1)}, u32[]{:S(2)}, u32[]{:S(2)}) collective-permute-start(f32[1,136,128]{2,1,0:T(8,128)S(1)} %add_add_fusion.2), channel_id=1, source_target_pairs={{0,2},{1,3},{2,0},{3,1},{4,6},{5,7},{6,4},{7,5},{8,10},{9,11},{10,... | collective-permute-start | bytes 208904 | tf_op jit(solution)/shard_map/ppermute | solution.py:66
  39.5 1.2 %collective-permute-start.15 = (f32[1,136,128]{2,1,0:T(8,128)S(1)}, f32[1,136,128]{2,1,0:T(8,128)S(1)}, u32[]{:S(2)}, u32[]{:S(2)}) collective-permute-start(f32[1,136,128]{2,1,0:T(8,128)S(1)} %add_add_fusion.2), channel_id=1, source_target_pairs={{0,16},{1,17},{2,18},{3,19},{4,20},{5,21},{6,22},{7,23},{8,24},{9,... | collective-permute-start | bytes 208904 | tf_op jit(solution)/shard_map/ppermute | solution.py:66
  40.7 0.9 %collective-permute-start.18 = (f32[2,2,64,128]{3,2,1,0:T(8,128)S(1)}, f32[2,2,64,128]{3,2,1,0:T(8,128)S(1)}, u32[]{:S(2)}, u32[]{:S(2)}) collective-permute-start(f32[2,2,64,128]{3,2,1,0:T(8,128)S(1)} %pad_maximum_fusion.4), channel_id=1, source_target_pairs={{0,16},{16,0},{1,17},{17,1},{2,18},{18,2},{3,19},{19,3},{4,20},{20... | collective-permute-start | bytes 393224 | tf_op jit(solution)/shard_map/ppermute | solution.py:411
  41.6 0.9 %collective-permute-done.17 = f32[1,136,128]{2,1,0:T(8,128)S(1)} collective-permute-done((f32[1,136,128]{2,1,0:T(8,128)S(1)}, f32[1,136,128]{2,1,0:T(8,128)S(1)}, u32[]{:S(2)}, u32[]{:S(2)}) %collective-permute-start.17) | collective-permute-done | bytes 69664 | tf_op jit(solution)/shard_map/ppermute | solution.py:66
  42.5 1.4 %collective-permute-done.16 = f32[1,136,128]{2,1,0:T(8,128)S(1)} collective-permute-done((f32[1,136,128]{2,1,0:T(8,128)S(1)}, f32[1,136,128]{2,1,0:T(8,128)S(1)}, u32[]{:S(2)}, u32[]{:S(2)}) %collective-permute-start.16) | collective-permute-done | bytes 69664 | tf_op jit(solution)/shard_map/ppermute | solution.py:66
  43.9 0.6 collective-permute-done.15
  44.6 2.1 %collective-permute-done.18.rest_2_ = f32[2,2,64,128]{3,2,1,0:T(8,128)S(1)} collective-permute-done((f32[2,2,64,128]{3,2,1,0:T(8,128)S(1)}, f32[2,2,64,128]{3,2,1,0:T(8,128)S(1)}, u32[]{:S(2)}, u32[]{:S(2)}) %collective-permute-start.18) | collective-permute-done | bytes 131104 | tf_op jit(solution)/shard_map/ppermute | solution.py:411
  46.7 1.6 %collective-permute-done.19.other_ref = f32[4,136,128]{2,1,0:T(8,128)S(1)} collective-permute-done((f32[4,136,128]{2,1,0:T(8,128)S(1)}, f32[4,136,128]{2,1,0:T(8,128)S(1)}, u32[]{:S(2)}, u32[]{:S(2)}) %collective-permute-start.19) | collective-permute-done | bytes 278560 | tf_op jit(solution)/shard_map/ppermute | solution.py:66
  48.2 5.4 %shard_map.70 = (f32[2,128,128]{2,1,0:T(8,128)S(1)}, f32[2,4,128,128]{3,2,1,0:T(8,128)S(1)}, f32[4,136,128]{2,1,0:T(8,128)S(1)}, f32[4,136,128]{2,1,0:T(8,128)S(...) custom-call(s32[3,2]{1,0:T(4,128)S(1)} %copy.8.pos_ref, ...), custom_call_target="tpu_custom_call" | custom-call | tf_op jit(solution)/shard_map/pallas_call | solution.py:329
  53.7 0.2 collective-permute-start.20
  53.9 1.4 %collective-permute-done.20 = f32[4,136,128]{2,1,0:T(8,128)S(1)} collective-permute-done((f32[4,136,128]{2,1,0:T(8,128)S(1)}, f32[4,136,128]{2,1,0:T(8,128)S(1)}, u32[]{:S(2)}, u32[]{:S(2)}) %collective-permute-start.20) | collective-permute-done | bytes 278560 | tf_op jit(solution)/shard_map/ppermute | solution.py:66
  55.4 1.3 %collective-permute-start.21 = (f32[1,136,128]{2,1,0:T(8,128)S(1)}, f32[1,136,128]{2,1,0:T(8,128)S(1)}, u32[]{:S(2)}, u32[]{:S(2)}) collective-permute-start(f32[1,136,128]{2,1,0:T(8,128)S(1)} %get-tuple-element.86), channel_id=1, source_target_pairs={{0,16},{1,17},{2,18},{3,19},{4,20},{5,21},{6,22},{7,23},{8,24},{9,... | collective-permute-start | bytes 208904 | tf_op jit(solution)/shard_map/ppermute | solution.py:66
  56.6 1.5 %collective-permute-start.23 = (f32[1,136,128]{2,1,0:T(8,128)S(1)}, f32[1,136,128]{2,1,0:T(8,128)S(1)}, u32[]{:S(2)}, u32[]{:S(2)}) collective-permute-start(f32[1,136,128]{2,1,0:T(8,128)S(1)} %get-tuple-element.87), channel_id=1, source_target_pairs={{0,18},{1,19},{2,16},{3,17},{4,22},{5,23},{6,20},{7,21},{8,26},{9,... | collective-permute-start | bytes 208904 | tf_op jit(solution)/shard_map/ppermute | solution.py:66
  58.2 0.7 collective-permute-start.22
  58.9 1.2 %collective-permute-start.24 = (f32[2,2,64,128]{3,2,1,0:T(8,128)S(1)}, f32[2,2,64,128]{3,2,1,0:T(8,128)S(1)}, u32[]{:S(2)}, u32[]{:S(2)}) collective-permute-start(f32[2,2,64,128]{3,2,1,0:T(8,128)S(1)} %get-tuple-element.71), channel_id=1, source_target_pairs={{0,16},{16,0},{1,17},{17,1},{2,18},{18,2},{3,19},{19,3},{4,20},{20... | collective-permute-start | bytes 393224 | tf_op jit(solution)/shard_map/ppermute | solution.py:411
  60.1 2.2 %collective-permute-done.23 = f32[1,136,128]{2,1,0:T(8,128)S(1)} collective-permute-done((f32[1,136,128]{2,1,0:T(8,128)S(1)}, f32[1,136,128]{2,1,0:T(8,128)S(1)}, u32[]{:S(2)}, u32[]{:S(2)}) %collective-permute-start.23) | collective-permute-done | bytes 69664 | tf_op jit(solution)/shard_map/ppermute | solution.py:66
  62.4 0.8 collective-permute-done.22
  63.2 1.2 %collective-permute-done.24 = f32[2,2,64,128]{3,2,1,0:T(8,128)S(1)} collective-permute-done((f32[2,2,64,128]{3,2,1,0:T(8,128)S(1)}, f32[2,2,64,128]{3,2,1,0:T(8,128)S(1)}, u32[]{:S(2)}, u32[]{:S(2)}) %collective-permute-start.24) | collective-permute-done | bytes 131104 | tf_op jit(solution)/shard_map/ppermute | solution.py:411
  64.4 3.2 %collective-permute-start.27 = (f32[1,136,128]{2,1,0:T(8,128)S(1)}, f32[1,136,128]{2,1,0:T(8,128)S(1)}, u32[]{:S(2)}, u32[]{:S(2)}) collective-permute-start(f32[1,136,128]{2,1,0:T(8,128)S(1)} %add_add_fusion.1), channel_id=1, source_target_pairs={{0,12},{1,13},{2,14},{3,15},{4,8},{5,9},{6,10},{7,11},{8,4},{9,5},... | collective-permute-start | bytes 208904 | tf_op jit(solution)/shard_map/ppermute | solution.py:66
  67.6 1.2 %collective-permute-start.25 = (f32[1,136,128]{2,1,0:T(8,128)S(1)}, f32[1,136,128]{2,1,0:T(8,128)S(1)}, u32[]{:S(2)}, u32[]{:S(2)}) collective-permute-start(f32[1,136,128]{2,1,0:T(8,128)S(1)} %add_add_fusion.1), channel_id=1, source_target_pairs={{0,4},{1,5},{2,6},{3,7},{4,0},{5,1},{6,2},{7,3},{8,12},{9,13},{10,... | collective-permute-start | bytes 208904 | tf_op jit(solution)/shard_map/ppermute | solution.py:66
  68.8 0.1 fusion
  68.9 1.0 %collective-permute-start.29 = (f32[2,128,128]{2,1,0:T(8,128)S(1)}, f32[2,128,128]{2,1,0:T(8,128)S(1)}, u32[]{:S(2)}, u32[]{:S(2)}) collective-permute-start(f32[2,128,128]{2,1,0:T(8,128)S(1)} %get-tuple-element.77.second_ref), channel_id=1, source_target_pairs={{1,2},{17,18},{2,1},{18,17},{3,4},{19,20},{4,3},{20,19},{5,6},{21,... | collective-permute-start | bytes 393224 | tf_op jit(solution)/shard_map/ppermute | solution.py:411
  69.9 0.1 collective-permute-start.28
  70.0 0.5 collective-permute-done.27
  70.5 2.7 %collective-permute-done.26 = f32[1,136,128]{2,1,0:T(8,128)S(1)} collective-permute-done((f32[1,136,128]{2,1,0:T(8,128)S(1)}, f32[1,136,128]{2,1,0:T(8,128)S(1)}, u32[]{:S(2)}, u32[]{:S(2)}) %collective-permute-start.26) | collective-permute-done | bytes 69664 | tf_op jit(solution)/shard_map/ppermute | solution.py:66
  73.2 0.7 collective-permute-done.29.rest_1_
  73.9 1.2 %collective-permute-start.32 = (f32[1,136,128]{2,1,0:T(8,128)S(1)}, f32[1,136,128]{2,1,0:T(8,128)S(1)}, u32[]{:S(2)}, u32[]{:S(2)}) collective-permute-start(f32[1,136,128]{2,1,0:T(8,128)S(1)} %add_add_fusion), channel_id=1, source_target_pairs={{0,18},{1,19},{2,16},{3,17},{4,22},{5,23},{6,20},{7,21},{8,26},{9,... | collective-permute-start | bytes 208904 | tf_op jit(solution)/shard_map/ppermute | solution.py:66
  75.1 1.2 %collective-permute-start.31 = (f32[1,136,128]{2,1,0:T(8,128)S(1)}, f32[1,136,128]{2,1,0:T(8,128)S(1)}, u32[]{:S(2)}, u32[]{:S(2)}) collective-permute-start(f32[1,136,128]{2,1,0:T(8,128)S(1)} %add_add_fusion), channel_id=1, source_target_pairs={{0,2},{1,3},{2,0},{3,1},{4,6},{5,7},{6,4},{7,5},{8,10},{9,11},{10,... | collective-permute-start | bytes 208904 | tf_op jit(solution)/shard_map/ppermute | solution.py:66
  76.3 1.1 %collective-permute-start.30 = (f32[1,136,128]{2,1,0:T(8,128)S(1)}, f32[1,136,128]{2,1,0:T(8,128)S(1)}, u32[]{:S(2)}, u32[]{:S(2)}) collective-permute-start(f32[1,136,128]{2,1,0:T(8,128)S(1)} %add_add_fusion), channel_id=1, source_target_pairs={{0,16},{1,17},{2,18},{3,19},{4,20},{5,21},{6,22},{7,23},{8,24},{9,... | collective-permute-start | bytes 208904 | tf_op jit(solution)/shard_map/ppermute | solution.py:66
  77.4 1.8 %collective-permute-done.32 = f32[1,136,128]{2,1,0:T(8,128)S(1)} collective-permute-done((f32[1,136,128]{2,1,0:T(8,128)S(1)}, f32[1,136,128]{2,1,0:T(8,128)S(1)}, u32[]{:S(2)}, u32[]{:S(2)}) %collective-permute-start.32) | collective-permute-done | bytes 69664 | tf_op jit(solution)/shard_map/ppermute | solution.py:66
  79.2 1.4 %collective-permute-done.31 = f32[1,136,128]{2,1,0:T(8,128)S(1)} collective-permute-done((f32[1,136,128]{2,1,0:T(8,128)S(1)}, f32[1,136,128]{2,1,0:T(8,128)S(1)}, u32[]{:S(2)}, u32[]{:S(2)}) %collective-permute-start.31) | collective-permute-done | bytes 69664 | tf_op jit(solution)/shard_map/ppermute | solution.py:66
  80.7 0.2 collective-permute-start.33
  80.9 1.5 %collective-permute-done.33.other_ref = f32[4,136,128]{2,1,0:T(8,128)S(1)} collective-permute-done((f32[4,136,128]{2,1,0:T(8,128)S(1)}, f32[4,136,128]{2,1,0:T(8,128)S(1)}, u32[]{:S(2)}, u32[]{:S(2)}) %collective-permute-start.33) | collective-permute-done | bytes 278560 | tf_op jit(solution)/shard_map/ppermute | solution.py:66
  82.3 1.0 %shard_map.71 = (f32[2,128,128]{2,1,0:T(8,128)}, f32[2,4,128,128]{3,2,1,0:T(8,128)}) custom-call(f32[2,128,128]{2,1,0:T(8,128)S(1)} %get-tuple-element.68.tile_ref, f32[2,128,128]{2,1,0:T(8,128)S(1)} %get-tuple-element.76.first_ref, f32[2,128,128]{2,1,0:T(8,128)S(1)} %get-tuple-element.77.second_ref, f32[2,4,128,128]{3,2,1,0:T(8,128)S(1)} %get-tuple-element.78.probe_ref, ...), custom_call_target="tpu_custom_call" | custom-call | tf_op jit(solution)/shard_map/pallas_call | solution.py:329
  (43 shorter events, 0.8 us)
Async XLA Ops:
  0.6 3.9 %copy-start.1 = (f32[2,128,128]{2,1,0:T(8,128)S(1)}, f32[2,128,128]{2,1,0:T(8,128)}, u32[]{:S(2)}) copy-start(f32[2,128,128]{2,1,0:T(8,128)} %obj_ref.1) | copy-start | bytes 393220
  1.5 6.2 %copy-start.4 = (s32[1,1,3,2]{2,3,1,0:T(2,128)S(1)}, s32[1,1,3,2]{2,3,1,0:T(2,128)}, u32[]{:S(2)}) copy-start(s32[1,1,3,2]{2,3,1,0:T(2,128)} %param.8) | copy-start | bytes 76
  1.6 5.2 %collective-permute-start.2 = (f32[2,64,128]{2,1,0:T(8,128)S(1)}, f32[2,64,128]{2,1,0:T(8,128)S(1)}, u32[]{:S(2)}, u32[]{:S(2)}) collective-permute-start(f32[2,64,128]{2,1,0:T(8,128)S(1)} %constant_dynamic-slice_fusion.6), channel_id=1, source_target_pairs={{0,16},{16,0},{1,17},{17,1},{2,18},{18,2},{3,19},{19,3},{4,20},{20... | collective-permute-start | bytes 196616 | tf_op jit(solution)/shard_map/ppermute | solution.py:411
  4.5 6.3 %collective-permute-start.1 = (f32[2,128,128]{2,1,0:T(8,128)S(1)}, f32[2,128,128]{2,1,0:T(8,128)S(1)}, u32[]{:S(2)}, u32[]{:S(2)}) collective-permute-start(f32[2,128,128]{2,1,0:T(8,128)S(1)} %copy-done.1), channel_id=1, source_target_pairs={{1,2},{17,18},{2,1},{18,17},{3,4},{19,20},{4,3},{20,19},{5,6},{21,... | collective-permute-start | bytes 393224 | tf_op jit(solution)/shard_map/ppermute | solution.py:411
  4.6 6.3 %collective-permute-start = (f32[2,128,128]{2,1,0:T(8,128)S(1)}, f32[2,128,128]{2,1,0:T(8,128)S(1)}, u32[]{:S(2)}, u32[]{:S(2)}) collective-permute-start(f32[2,128,128]{2,1,0:T(8,128)S(1)} %copy-done.1), channel_id=1, source_target_pairs={{0,1},{16,17},{1,0},{17,16},{2,3},{18,19},{3,2},{19,18},{4,5},{20,... | collective-permute-start | bytes 393224 | tf_op jit(solution)/shard_map/ppermute | solution.py:411
  6.1 4.7 %collective-permute-start.4 = (f32[2,64,128]{2,1,0:T(8,128)S(1)}, f32[2,64,128]{2,1,0:T(8,128)S(1)}, u32[]{:S(2)}, u32[]{:S(2)}) collective-permute-start(f32[2,64,128]{2,1,0:T(8,128)S(1)} %constant_dynamic-slice_fusion.6), channel_id=1, source_target_pairs={{1,18},{17,2},{2,17},{18,1},{3,20},{19,4},{4,19},{20,3},{5,22},{21... | collective-permute-start | bytes 196616 | tf_op jit(solution)/shard_map/ppermute | solution.py:411
  6.7 4.1 %collective-permute-start.3 = (f32[2,64,128]{2,1,0:T(8,128)S(1)}, f32[2,64,128]{2,1,0:T(8,128)S(1)}, u32[]{:S(2)}, u32[]{:S(2)}) collective-permute-start(f32[2,64,128]{2,1,0:T(8,128)S(1)} %collective-permute-done.2.rest_0_), channel_id=1, source_target_pairs={{0,1},{16,17},{1,0},{17,16},{2,3},{18,19},{3,2},{19,18},{4,5},{20,... | collective-permute-start | bytes 196616 | tf_op jit(solution)/shard_map/ppermute | solution.py:411
  7.8 1.0 %copy-start = (f32[2,4,128,128]{3,2,1,0:T(8,128)S(1)}, f32[2,4,128,128]{3,2,1,0:T(8,128)}, u32[]{:S(2)}) copy-start(f32[2,4,128,128]{3,2,1,0:T(8,128)} %probe_ref.1) | copy-start | bytes 1572868
  8.9 0.9 %copy-start.2 = (f32[1,1,3,128,128]{4,3,2,1,0:T(8,128)S(1)}, f32[1,1,3,128,128]{4,3,2,1,0:T(8,128)}, u32[]{:S(2)}) copy-start(f32[1,1,3,128,128]{4,3,2,1,0:T(8,128)} %param.7) | copy-start | bytes 589828
  9.8 0.9 %copy-start.3 = (bf16[4,128,128]{2,1,0:T(8,128)(2,1)S(1)}, bf16[4,128,128]{2,1,0:T(8,128)(2,1)}, u32[]{:S(2)}) copy-start(bf16[4,128,128]{2,1,0:T(8,128)(2,1)} %constant.74.clone.table_ref) | copy-start | bytes 393220
  16.2 1.6 %collective-permute-start.5 = (f32[4,136,128]{2,1,0:T(8,128)S(1)}, f32[4,136,128]{2,1,0:T(8,128)S(1)}, u32[]{:S(2)}, u32[]{:S(2)}) collective-permute-start(f32[4,136,128]{2,1,0:T(8,128)S(1)} %get-tuple-element.55), channel_id=1, source_target_pairs={{0,1},{1,0},{2,3},{3,2},{4,5},{5,4},{6,7},{7,6},{8,9},{9,8},{10,11... | collective-permute-start | bytes 835592 | tf_op jit(solution)/shard_map/ppermute | solution.py:66
  17.8 5.2 %collective-permute-start.6 = (f32[1,136,128]{2,1,0:T(8,128)S(1)}, f32[1,136,128]{2,1,0:T(8,128)S(1)}, u32[]{:S(2)}, u32[]{:S(2)}) collective-permute-start(f32[1,136,128]{2,1,0:T(8,128)S(1)} %get-tuple-element.93), channel_id=1, source_target_pairs={{0,16},{1,17},{2,18},{3,19},{4,20},{5,21},{6,22},{7,23},{8,24},{9,... | collective-permute-start | bytes 208904 | tf_op jit(solution)/shard_map/ppermute | solution.py:66
  19.4 5.9 %collective-permute-start.8 = (f32[1,136,128]{2,1,0:T(8,128)S(1)}, f32[1,136,128]{2,1,0:T(8,128)S(1)}, u32[]{:S(2)}, u32[]{:S(2)}) collective-permute-start(f32[1,136,128]{2,1,0:T(8,128)S(1)} %get-tuple-element.94), channel_id=1, source_target_pairs={{0,18},{1,19},{2,16},{3,17},{4,22},{5,23},{6,20},{7,21},{8,26},{9,... | collective-permute-start | bytes 208904 | tf_op jit(solution)/shard_map/ppermute | solution.py:66
  21.3 5.1 %collective-permute-start.7 = (f32[1,136,128]{2,1,0:T(8,128)S(1)}, f32[1,136,128]{2,1,0:T(8,128)S(1)}, u32[]{:S(2)}, u32[]{:S(2)}) collective-permute-start(f32[1,136,128]{2,1,0:T(8,128)S(1)} %get-tuple-element.95), channel_id=1, source_target_pairs={{0,2},{1,3},{2,0},{3,1},{4,6},{5,7},{6,4},{7,5},{8,10},{9,11},{10,... | collective-permute-start | bytes 208904 | tf_op jit(solution)/shard_map/ppermute | solution.py:66
  21.6 5.9 %collective-permute-start.9 = (f32[2,2,64,128]{3,2,1,0:T(8,128)S(1)}, f32[2,2,64,128]{3,2,1,0:T(8,128)S(1)}, u32[]{:S(2)}, u32[]{:S(2)}) collective-permute-start(f32[2,2,64,128]{3,2,1,0:T(8,128)S(1)} %get-tuple-element.56), channel_id=1, source_target_pairs={{0,16},{16,0},{1,17},{17,1},{2,18},{18,2},{3,19},{19,3},{4,20},{20... | collective-permute-start | bytes 393224 | tf_op jit(solution)/shard_map/ppermute | solution.py:411
  27.5 6.4 %collective-permute-start.12 = (f32[1,136,128]{2,1,0:T(8,128)S(1)}, f32[1,136,128]{2,1,0:T(8,128)S(1)}, u32[]{:S(2)}, u32[]{:S(2)}) collective-permute-start(f32[1,136,128]{2,1,0:T(8,128)S(1)} %add_add_fusion.3), channel_id=1, source_target_pairs={{0,12},{1,13},{2,14},{3,15},{4,8},{5,9},{6,10},{7,11},{8,4},{9,5},... | collective-permute-start | bytes 208904 | tf_op jit(solution)/shard_map/ppermute | solution.py:66
  31.5 5.3 %collective-permute-start.11 = (f32[1,136,128]{2,1,0:T(8,128)S(1)}, f32[1,136,128]{2,1,0:T(8,128)S(1)}, u32[]{:S(2)}, u32[]{:S(2)}) collective-permute-start(f32[1,136,128]{2,1,0:T(8,128)S(1)} %add_add_fusion.3), channel_id=1, source_target_pairs={{0,8},{1,9},{2,10},{3,11},{4,12},{5,13},{6,14},{7,15},{8,0},{9,1},... | collective-permute-start | bytes 208904 | tf_op jit(solution)/shard_map/ppermute | solution.py:66
  31.5 5.4 %collective-permute-start.10 = (f32[1,136,128]{2,1,0:T(8,128)S(1)}, f32[1,136,128]{2,1,0:T(8,128)S(1)}, u32[]{:S(2)}, u32[]{:S(2)}) collective-permute-start(f32[1,136,128]{2,1,0:T(8,128)S(1)} %add_add_fusion.3), channel_id=1, source_target_pairs={{0,4},{1,5},{2,6},{3,7},{4,0},{5,1},{6,2},{7,3},{8,12},{9,13},{10,... | collective-permute-start | bytes 208904 | tf_op jit(solution)/shard_map/ppermute | solution.py:66
  32.2 5.0 %collective-permute-start.14 = (f32[2,128,128]{2,1,0:T(8,128)S(1)}, f32[2,128,128]{2,1,0:T(8,128)S(1)}, u32[]{:S(2)}, u32[]{:S(2)}) collective-permute-start(f32[2,128,128]{2,1,0:T(8,128)S(1)} %get-tuple-element.62.second_ref), channel_id=1, source_target_pairs={{1,2},{17,18},{2,1},{18,17},{3,4},{19,20},{4,3},{20,19},{5,6},{21,... | collective-permute-start | bytes 393224 | tf_op jit(solution)/shard_map/ppermute | solution.py:411
  33.0 4.2 %collective-permute-start.13 = (f32[2,128,128]{2,1,0:T(8,128)S(1)}, f32[2,128,128]{2,1,0:T(8,128)S(1)}, u32[]{:S(2)}, u32[]{:S(2)}) collective-permute-start(f32[2,128,128]{2,1,0:T(8,128)S(1)} %get-tuple-element.61.first_ref), channel_id=1, source_target_pairs={{0,1},{16,17},{1,0},{17,16},{2,3},{18,19},{3,2},{19,18},{4,5},{20,... | collective-permute-start | bytes 393224 | tf_op jit(solution)/shard_map/ppermute | solution.py:411
  37.2 5.3 %collective-permute-start.17 = (f32[1,136,128]{2,1,0:T(8,128)S(1)}, f32[1,136,128]{2,1,0:T(8,128)S(1)}, u32[]{:S(2)}, u32[]{:S(2)}) collective-permute-start(f32[1,136,128]{2,1,0:T(8,128)S(1)} %add_add_fusion.2), channel_id=1, source_target_pairs={{0,18},{1,19},{2,16},{3,17},{4,22},{5,23},{6,20},{7,21},{8,26},{9,... | collective-permute-start | bytes 208904 | tf_op jit(solution)/shard_map/ppermute | solution.py:66
  38.5 5.4 %collective-permute-start.16 = (f32[1,136,128]{2,1,0:T(8,128)S(1)}, f32[1,136,128]{2,1,0:T(8,128)S(1)}, u32[]{:S(2)}, u32[]{:S(2)}) collective-permute-start(f32[1,136,128]{2,1,0:T(8,128)S(1)} %add_add_fusion.2), channel_id=1, source_target_pairs={{0,2},{1,3},{2,0},{3,1},{4,6},{5,7},{6,4},{7,5},{8,10},{9,11},{10,... | collective-permute-start | bytes 208904 | tf_op jit(solution)/shard_map/ppermute | solution.py:66
  39.5 5.0 %collective-permute-start.15 = (f32[1,136,128]{2,1,0:T(8,128)S(1)}, f32[1,136,128]{2,1,0:T(8,128)S(1)}, u32[]{:S(2)}, u32[]{:S(2)}) collective-permute-start(f32[1,136,128]{2,1,0:T(8,128)S(1)} %add_add_fusion.2), channel_id=1, source_target_pairs={{0,16},{1,17},{2,18},{3,19},{4,20},{5,21},{6,22},{7,23},{8,24},{9,... | collective-permute-start | bytes 208904 | tf_op jit(solution)/shard_map/ppermute | solution.py:66
  40.7 5.9 %collective-permute-start.18 = (f32[2,2,64,128]{3,2,1,0:T(8,128)S(1)}, f32[2,2,64,128]{3,2,1,0:T(8,128)S(1)}, u32[]{:S(2)}, u32[]{:S(2)}) collective-permute-start(f32[2,2,64,128]{3,2,1,0:T(8,128)S(1)} %pad_maximum_fusion.4), channel_id=1, source_target_pairs={{0,16},{16,0},{1,17},{17,1},{2,18},{18,2},{3,19},{19,3},{4,20},{20... | collective-permute-start | bytes 393224 | tf_op jit(solution)/shard_map/ppermute | solution.py:411
  46.7 1.6 %collective-permute-start.19 = (f32[4,136,128]{2,1,0:T(8,128)S(1)}, f32[4,136,128]{2,1,0:T(8,128)S(1)}, u32[]{:S(2)}, u32[]{:S(2)}) collective-permute-start(f32[4,136,128]{2,1,0:T(8,128)S(1)} %pad_maximum_fusion.1.own_ref), channel_id=1, source_target_pairs={{0,1},{1,0},{2,3},{3,2},{4,5},{5,4},{6,7},{7,6},{8,9},{9,8},{10,11... | collective-permute-start | bytes 835592 | tf_op jit(solution)/shard_map/ppermute | solution.py:66
  53.7 1.6 %collective-permute-start.20 = (f32[4,136,128]{2,1,0:T(8,128)S(1)}, f32[4,136,128]{2,1,0:T(8,128)S(1)}, u32[]{:S(2)}, u32[]{:S(2)}) collective-permute-start(f32[4,136,128]{2,1,0:T(8,128)S(1)} %get-tuple-element.70), channel_id=1, source_target_pairs={{0,1},{1,0},{2,3},{3,2},{4,5},{5,4},{6,7},{7,6},{8,9},{9,8},{10,11... | collective-permute-start | bytes 835592 | tf_op jit(solution)/shard_map/ppermute | solution.py:66
  55.4 4.8 %collective-permute-start.21 = (f32[1,136,128]{2,1,0:T(8,128)S(1)}, f32[1,136,128]{2,1,0:T(8,128)S(1)}, u32[]{:S(2)}, u32[]{:S(2)}) collective-permute-start(f32[1,136,128]{2,1,0:T(8,128)S(1)} %get-tuple-element.86), channel_id=1, source_target_pairs={{0,16},{1,17},{2,18},{3,19},{4,20},{5,21},{6,22},{7,23},{8,24},{9,... | collective-permute-start | bytes 208904 | tf_op jit(solution)/shard_map/ppermute | solution.py:66
  56.6 5.7 %collective-permute-start.23 = (f32[1,136,128]{2,1,0:T(8,128)S(1)}, f32[1,136,128]{2,1,0:T(8,128)S(1)}, u32[]{:S(2)}, u32[]{:S(2)}) collective-permute-start(f32[1,136,128]{2,1,0:T(8,128)S(1)} %get-tuple-element.87), channel_id=1, source_target_pairs={{0,18},{1,19},{2,16},{3,17},{4,22},{5,23},{6,20},{7,21},{8,26},{9,... | collective-permute-start | bytes 208904 | tf_op jit(solution)/shard_map/ppermute | solution.py:66
  58.2 5.0 %collective-permute-start.22 = (f32[1,136,128]{2,1,0:T(8,128)S(1)}, f32[1,136,128]{2,1,0:T(8,128)S(1)}, u32[]{:S(2)}, u32[]{:S(2)}) collective-permute-start(f32[1,136,128]{2,1,0:T(8,128)S(1)} %get-tuple-element.88), channel_id=1, source_target_pairs={{0,2},{1,3},{2,0},{3,1},{4,6},{5,7},{6,4},{7,5},{8,10},{9,11},{10,... | collective-permute-start | bytes 208904 | tf_op jit(solution)/shard_map/ppermute | solution.py:66
  58.9 5.5 %collective-permute-start.24 = (f32[2,2,64,128]{3,2,1,0:T(8,128)S(1)}, f32[2,2,64,128]{3,2,1,0:T(8,128)S(1)}, u32[]{:S(2)}, u32[]{:S(2)}) collective-permute-start(f32[2,2,64,128]{3,2,1,0:T(8,128)S(1)} %get-tuple-element.71), channel_id=1, source_target_pairs={{0,16},{16,0},{1,17},{17,1},{2,18},{18,2},{3,19},{19,3},{4,20},{20... | collective-permute-start | bytes 393224 | tf_op jit(solution)/shard_map/ppermute | solution.py:411
  64.4 6.1 %collective-permute-start.27 = (f32[1,136,128]{2,1,0:T(8,128)S(1)}, f32[1,136,128]{2,1,0:T(8,128)S(1)}, u32[]{:S(2)}, u32[]{:S(2)}) collective-permute-start(f32[1,136,128]{2,1,0:T(8,128)S(1)} %add_add_fusion.1), channel_id=1, source_target_pairs={{0,12},{1,13},{2,14},{3,15},{4,8},{5,9},{6,10},{7,11},{8,4},{9,5},... | collective-permute-start | bytes 208904 | tf_op jit(solution)/shard_map/ppermute | solution.py:66
  67.6 5.6 %collective-permute-start.26 = (f32[1,136,128]{2,1,0:T(8,128)S(1)}, f32[1,136,128]{2,1,0:T(8,128)S(1)}, u32[]{:S(2)}, u32[]{:S(2)}) collective-permute-start(f32[1,136,128]{2,1,0:T(8,128)S(1)} %add_add_fusion.1), channel_id=1, source_target_pairs={{0,8},{1,9},{2,10},{3,11},{4,12},{5,13},{6,14},{7,15},{8,0},{9,1},... | collective-permute-start | bytes 208904 | tf_op jit(solution)/shard_map/ppermute | solution.py:66
  67.6 5.6 %collective-permute-start.25 = (f32[1,136,128]{2,1,0:T(8,128)S(1)}, f32[1,136,128]{2,1,0:T(8,128)S(1)}, u32[]{:S(2)}, u32[]{:S(2)}) collective-permute-start(f32[1,136,128]{2,1,0:T(8,128)S(1)} %add_add_fusion.1), channel_id=1, source_target_pairs={{0,4},{1,5},{2,6},{3,7},{4,0},{5,1},{6,2},{7,3},{8,12},{9,13},{10,... | collective-permute-start | bytes 208904 | tf_op jit(solution)/shard_map/ppermute | solution.py:66
  68.9 5.0 %collective-permute-start.29 = (f32[2,128,128]{2,1,0:T(8,128)S(1)}, f32[2,128,128]{2,1,0:T(8,128)S(1)}, u32[]{:S(2)}, u32[]{:S(2)}) collective-permute-start(f32[2,128,128]{2,1,0:T(8,128)S(1)} %get-tuple-element.77.second_ref), channel_id=1, source_target_pairs={{1,2},{17,18},{2,1},{18,17},{3,4},{19,20},{4,3},{20,19},{5,6},{21,... | collective-permute-start | bytes 393224 | tf_op jit(solution)/shard_map/ppermute | solution.py:411
  69.9 4.0 %collective-permute-start.28 = (f32[2,128,128]{2,1,0:T(8,128)S(1)}, f32[2,128,128]{2,1,0:T(8,128)S(1)}, u32[]{:S(2)}, u32[]{:S(2)}) collective-permute-start(f32[2,128,128]{2,1,0:T(8,128)S(1)} %get-tuple-element.76.first_ref), channel_id=1, source_target_pairs={{0,1},{16,17},{1,0},{17,16},{2,3},{18,19},{3,2},{19,18},{4,5},{20,... | collective-permute-start | bytes 393224 | tf_op jit(solution)/shard_map/ppermute | solution.py:411
  73.9 5.3 %collective-permute-start.32 = (f32[1,136,128]{2,1,0:T(8,128)S(1)}, f32[1,136,128]{2,1,0:T(8,128)S(1)}, u32[]{:S(2)}, u32[]{:S(2)}) collective-permute-start(f32[1,136,128]{2,1,0:T(8,128)S(1)} %add_add_fusion), channel_id=1, source_target_pairs={{0,18},{1,19},{2,16},{3,17},{4,22},{5,23},{6,20},{7,21},{8,26},{9,... | collective-permute-start | bytes 208904 | tf_op jit(solution)/shard_map/ppermute | solution.py:66
  75.1 5.5 %collective-permute-start.31 = (f32[1,136,128]{2,1,0:T(8,128)S(1)}, f32[1,136,128]{2,1,0:T(8,128)S(1)}, u32[]{:S(2)}, u32[]{:S(2)}) collective-permute-start(f32[1,136,128]{2,1,0:T(8,128)S(1)} %add_add_fusion), channel_id=1, source_target_pairs={{0,2},{1,3},{2,0},{3,1},{4,6},{5,7},{6,4},{7,5},{8,10},{9,11},{10,... | collective-permute-start | bytes 208904 | tf_op jit(solution)/shard_map/ppermute | solution.py:66
  76.3 4.3 %collective-permute-start.30 = (f32[1,136,128]{2,1,0:T(8,128)S(1)}, f32[1,136,128]{2,1,0:T(8,128)S(1)}, u32[]{:S(2)}, u32[]{:S(2)}) collective-permute-start(f32[1,136,128]{2,1,0:T(8,128)S(1)} %add_add_fusion), channel_id=1, source_target_pairs={{0,16},{1,17},{2,18},{3,19},{4,20},{5,21},{6,22},{7,23},{8,24},{9,... | collective-permute-start | bytes 208904 | tf_op jit(solution)/shard_map/ppermute | solution.py:66
  80.7 1.6 %collective-permute-start.33 = (f32[4,136,128]{2,1,0:T(8,128)S(1)}, f32[4,136,128]{2,1,0:T(8,128)S(1)}, u32[]{:S(2)}, u32[]{:S(2)}) collective-permute-start(f32[4,136,128]{2,1,0:T(8,128)S(1)} %pad_maximum_fusion.3.own_ref), channel_id=1, source_target_pairs={{0,1},{1,0},{2,3},{3,2},{4,5},{5,4},{6,7},{7,6},{8,9},{9,8},{10,11... | collective-permute-start | bytes 835592 | tf_op jit(solution)/shard_map/ppermute | solution.py:66

commit v3 on v2

--- a/solution.py
+++ b/solution.py
@@ -105,34 +105,39 @@
 ):
     scans, win = root_ref.shape[0], root_ref.shape[1]
     modes = probe_ref.shape[1]
-    width = 2 * win
+    width, tall = 2 * win, win + SUBLANES
     w_fwd = [block(table_ref[i], -table_ref[i + 1], table_ref[i + 1]) for i in (0, 2)]
     l_fwd = [block(table_ref[i], table_ref[i + 1], -table_ref[i + 1]) for i in (0, 2)]
     grid_ref[...] = jnp.zeros_like(grid_ref)
-    weight = jnp.zeros((WEIGHT_ROWS, win), F32)
-    for s in range(scans):
+    windows, state, weights = {}, {}, []
+
+    def corner(s):
         r, c = pos_ref[s, 0], pos_ref[s, 1]
+        q = r % SUBLANES
+        return pl.multiple_of(r - q, SUBLANES), q, c
+
+    def enter(s):
+        base, q, c = corner(s)
         turn = jnp.where(c <= margin, margin - c, margin + width - c)
-        back = jnp.where(c >= margin, c - margin, c + width - margin)
-        q = r % SUBLANES
-        base = pl.multiple_of(r - q, SUBLANES)
-        tall = win + SUBLANES
         lift = jnp.where(q == 0, 0, tall - q)
 
         def window(part):
             band = pltpu.roll(ext_ref[part, pl.ds(base, tall), :], turn, 1)[:, :win]
             return pltpu.roll(band, lift, 0)[:win]
 
-        o_re, o_im = window(0), window(1)
+        o_re, o_im = windows[s] = window(0), window(1)
         power = o_re * o_re + o_im * o_im
-        weight = weight + jnp.sum(power.reshape(win // WEIGHT_ROWS, WEIGHT_ROWS, win), axis=0)
+        weights.append(jnp.sum(power.reshape(win // WEIGHT_ROWS, WEIGHT_ROWS, win), axis=0))
         rows = []
         for k in range(modes):
             p_re, p_im = probe_ref[0, k], probe_ref[1, k]
             rows.append(
                 jnp.concatenate([p_re * o_re - p_im * o_im, p_re * o_im + p_im * o_re], axis=1)
             )
-        y = product(split(jnp.concatenate(rows, axis=0)), w_fwd)
+        state[s] = product(split(jnp.concatenate(rows, axis=0)), w_fwd)
+
+    def forward(s):
+        y = state[s]
         y = jnp.concatenate(
             [
                 jnp.concatenate([y[k * win : (k + 1) * win, :win] for k in range(modes)], axis=1),
@@ -140,7 +145,10 @@
             ],
             axis=0,
         )
-        far = product(l_fwd, split(y))
+        state[s] = product(l_fwd, split(y))
+
+    def scale(s):
+        far = state[s]
         square = far * far
         square = square[:win] + square[win:]
         total = square[:, :win]
@@ -149,7 +157,10 @@
         ratio = root_ref[s] * lax.rsqrt(jnp.maximum(total, 1.0)) - 1.0
         ratio = jnp.concatenate([ratio] * modes, axis=1)
         far = far * jnp.concatenate([ratio, ratio], axis=0)
-        u = product(w_fwd, split(far))
+        state[s] = product(w_fwd, split(far))
+
+    def backward(s):
+        u = state[s]
         u = jnp.concatenate(
             [
                 jnp.concatenate(
@@ -159,7 +170,11 @@
             ],
             axis=0,
         )
-        chi = product(split(u), l_fwd)
+        state[s] = product(split(u), l_fwd)
+
+    def leave(s):
+        chi = state[s]
+        o_re, o_im = windows[s]
         g_re = g_im = None
         for k in range(modes):
             p_re, p_im = probe_ref[0, k], probe_ref[1, k]
@@ -172,11 +187,18 @@
             else:
                 grad_ref[k] += a
                 grad_ref[modes + k] += b
+        base, q, c = corner(s)
+        back = jnp.where(c >= margin, c - margin, c + width - margin)
         for part, g in ((0, g_re), (1, g_im)):
             g = pltpu.roll(jnp.concatenate([g, jnp.zeros((SUBLANES, win), F32)], axis=0), q, 0)
             g = jnp.concatenate([g, jnp.zeros_like(g)], axis=1)
             grid_ref[part, pl.ds(base, tall), :] += pltpu.roll(g, back, 1)
-    return weight
+
+    stages = (enter, forward, scale, backward, leave)
+    for stage in stages:
+        for s in range(scans):
+            stage(s)
+    return functools.reduce(jnp.add, weights)
 
 
 def emit(grad_ref, weight, grid_ref, keep_ref, send_ref, first_ref, second_ref, rim_refs, margin):

time: 83.6 us -> 81.2 us (0.971)
  Pallas kernels: 11.8 us -> 9.44 us
    pallas_call x4, Pallas kernels: 11.8 us -> 9.44 us  [call(): pl.pallas_call(kernel, out_shape=shapes, in_specs=[smem if x.dtype == jnp...]
where the time goes in v3:
time: 81.2 us; the launch traced here: 80.9 us
  starting transfers between devices  35.4 us (44%)
  waiting for transfers between devices  30.6 us (38%)
  Pallas kernels  9.44 us (12%)
  local copies, waits for them, and re-layouts  4.16 us (5%)
  between operations  0.87 us (1%)
    ppermute x22, waiting for transfers between devices, xor_permute(): return lax.ppermute(x, AXES, [(i, i ^ mask) for i in range(total)])  25.3 us
    ppermute x22, starting transfers between devices, xor_permute(): return lax.ppermute(x, AXES, [(i, i ^ mask) for i in range(total)])  23.5 us
    ppermute x12, starting transfers between devices, swap(): return lax.ppermute(x, AXES, flat_pairs(pairs_y, pairs_x, n_ty, n_tx))  12 us
    pallas_call x4, Pallas kernels, call(): pl.pallas_call(kernel, out_shape=shapes, in_specs=[smem if x.dtype == jnp...  9.44 us
    ppermute x12, waiting for transfers between devices, swap(): return lax.ppermute(x, AXES, flat_pairs(pairs_y, pairs_x, n_ty, n_tx))  5.3 us
    unnamed x10, local copies, waits for them, and re-layouts  2.88 us
  transfers between devices with their start and end apart: 34, of which 24 were waited for; matrix products, arithmetic and copies ran while one was open for 1% of the time, Pallas kernels for 0%

profile of v3, /device:TPU:0, one launch (start us, length us, event | category | flops | bytes accessed | tf_op | source)
XLA Modules:
  0.0 80.9 jit_solution(6072544122819105598)
XLA Ops:
  0.7 0.9 %constant_dynamic-slice_fusion.6 = f32[2,64,128]{2,1,0:T(8,128)S(1)} fusion(f32[2,128,128]{2,1,0:T(8,128)} %obj_ref.1, s32[]{:T(128)S(6)} %select_n.77), kind=kLoop, calls=%fused_computation.41 | loop fusion | bytes 131076 | tf_op jit(solution)/shard_map/dynamic_slice | solution.py:437
  1.6 2.9 %collective-permute-start.2 = (f32[2,64,128]{2,1,0:T(8,128)S(1)}, f32[2,64,128]{2,1,0:T(8,128)S(1)}, u32[]{:S(2)}, u32[]{:S(2)}) collective-permute-start(f32[2,64,128]{2,1,0:T(8,128)S(1)} %constant_dynamic-slice_fusion.6), channel_id=1, source_target_pairs={{0,16},{16,0},{1,17},{17,1},{2,18},{18,2},{3,19},{19,3},{4,20},{20... | collective-permute-start | bytes 196616 | tf_op jit(solution)/shard_map/ppermute | solution.py:433
  4.5 0.1 collective-permute-start.1
  4.6 1.6 %collective-permute-start = (f32[2,128,128]{2,1,0:T(8,128)S(1)}, f32[2,128,128]{2,1,0:T(8,128)S(1)}, u32[]{:S(2)}, u32[]{:S(2)}) collective-permute-start(f32[2,128,128]{2,1,0:T(8,128)S(1)} %copy-done.1), channel_id=1, source_target_pairs={{0,1},{16,17},{1,0},{17,16},{2,3},{18,19},{3,2},{19,18},{4,5},{20,... | collective-permute-start | bytes 393224 | tf_op jit(solution)/shard_map/ppermute | solution.py:433
  6.1 0.5 collective-permute-start.4
  6.7 1.0 %collective-permute-start.3 = (f32[2,64,128]{2,1,0:T(8,128)S(1)}, f32[2,64,128]{2,1,0:T(8,128)S(1)}, u32[]{:S(2)}, u32[]{:S(2)}) collective-permute-start(f32[2,64,128]{2,1,0:T(8,128)S(1)} %collective-permute-done.2.rest_0_), channel_id=1, source_target_pairs={{0,1},{16,17},{1,0},{17,16},{2,3},{18,19},{3,2},{19,18},{4,5},{20,... | collective-permute-start | bytes 196616 | tf_op jit(solution)/shard_map/ppermute | solution.py:433
  7.7 0.1 copy.8.pos_ref
  7.8 1.0 %copy-done = f32[2,4,128,128]{3,2,1,0:T(8,128)S(1)} copy-done((f32[2,4,128,128]{3,2,1,0:T(8,128)S(1)}, f32[2,4,128,128]{3,2,1,0:T(8,128)}, u32[]{:S(2)}) %copy-start) | copy-done | bytes 524312
  8.9 0.9 %copy-done.2 = f32[1,1,3,128,128]{4,3,2,1,0:T(8,128)S(1)} copy-done((f32[1,1,3,128,128]{4,3,2,1,0:T(8,128)S(1)}, f32[1,1,3,128,128]{4,3,2,1,0:T(8,128)}, u32[]{:S(2)}) %copy-start.2) | copy-done | bytes 196632
  9.8 0.9 %copy-done.3 = bf16[4,128,128]{2,1,0:T(8,128)(2,1)S(1)} copy-done((bf16[4,128,128]{2,1,0:T(8,128)(2,1)S(1)}, bf16[4,128,128]{2,1,0:T(8,128)(2,1)}, u32[]{:S(2)}) %copy-start.3) | copy-done | bytes 131096
  10.7 0.1 shard_map.68
  10.8 4.1 %shard_map.69 = (f32[2,264,256]{2,1,0:T(8,128)S(1)}, f32[4,136,128]{2,1,0:T(8,128)S(1)}, f32[4,136,128]{2,1,0:T(8,128)S(1)}, f32[2,128,128]{2,1,0:T(8,128)S(1)},...) custom-call(s32[3,2]{1,0:T(4,128)S(1)} %copy.8.pos_ref, f32[2,128,128]{2,1,0:T(8,128)S(1)} %copy-done.1, ...), custom_call_target="tpu_custom_call" | custom-call | tf_op jit(solution)/shard_map/pallas_call | solution.py:351
  15.0 1.5 %collective-permute-done.5 = f32[4,136,128]{2,1,0:T(8,128)S(1)} collective-permute-done((f32[4,136,128]{2,1,0:T(8,128)S(1)}, f32[4,136,128]{2,1,0:T(8,128)S(1)}, u32[]{:S(2)}, u32[]{:S(2)}) %collective-permute-start.5) | collective-permute-done | bytes 278560 | tf_op jit(solution)/shard_map/ppermute | solution.py:66
  16.6 1.6 %collective-permute-start.6 = (f32[1,136,128]{2,1,0:T(8,128)S(1)}, f32[1,136,128]{2,1,0:T(8,128)S(1)}, u32[]{:S(2)}, u32[]{:S(2)}) collective-permute-start(f32[1,136,128]{2,1,0:T(8,128)S(1)} %get-tuple-element.93), channel_id=1, source_target_pairs={{0,16},{1,17},{2,18},{3,19},{4,20},{5,21},{6,22},{7,23},{8,24},{9,... | collective-permute-start | bytes 208904 | tf_op jit(solution)/shard_map/ppermute | solution.py:66
  18.2 1.9 %collective-permute-start.8 = (f32[1,136,128]{2,1,0:T(8,128)S(1)}, f32[1,136,128]{2,1,0:T(8,128)S(1)}, u32[]{:S(2)}, u32[]{:S(2)}) collective-permute-start(f32[1,136,128]{2,1,0:T(8,128)S(1)} %get-tuple-element.94), channel_id=1, source_target_pairs={{0,18},{1,19},{2,16},{3,17},{4,22},{5,23},{6,20},{7,21},{8,26},{9,... | collective-permute-start | bytes 208904 | tf_op jit(solution)/shard_map/ppermute | solution.py:66
  20.2 0.1 broadcast_in_dim.71
  20.3 1.5 %collective-permute-start.9 = (f32[2,2,64,128]{3,2,1,0:T(8,128)S(1)}, f32[2,2,64,128]{3,2,1,0:T(8,128)S(1)}, u32[]{:S(2)}, u32[]{:S(2)}) collective-permute-start(f32[2,2,64,128]{3,2,1,0:T(8,128)S(1)} %get-tuple-element.56), channel_id=1, source_target_pairs={{0,16},{16,0},{1,17},{17,1},{2,18},{18,2},{3,19},{19,3},{4,20},{20... | collective-permute-start | bytes 393224 | tf_op jit(solution)/shard_map/ppermute | solution.py:433
  21.8 2.3 %collective-permute-done.8 = f32[1,136,128]{2,1,0:T(8,128)S(1)} collective-permute-done((f32[1,136,128]{2,1,0:T(8,128)S(1)}, f32[1,136,128]{2,1,0:T(8,128)S(1)}, u32[]{:S(2)}, u32[]{:S(2)}) %collective-permute-start.8) | collective-permute-done | bytes 69664 | tf_op jit(solution)/shard_map/ppermute | solution.py:66
  24.1 1.1 %collective-permute-done.7 = f32[1,136,128]{2,1,0:T(8,128)S(1)} collective-permute-done((f32[1,136,128]{2,1,0:T(8,128)S(1)}, f32[1,136,128]{2,1,0:T(8,128)S(1)}, u32[]{:S(2)}, u32[]{:S(2)}) %collective-permute-start.7) | collective-permute-done | bytes 69664 | tf_op jit(solution)/shard_map/ppermute | solution.py:66
  25.2 1.0 %collective-permute-done.9 = f32[2,2,64,128]{3,2,1,0:T(8,128)S(1)} collective-permute-done((f32[2,2,64,128]{3,2,1,0:T(8,128)S(1)}, f32[2,2,64,128]{3,2,1,0:T(8,128)S(1)}, u32[]{:S(2)}, u32[]{:S(2)}) %collective-permute-start.9) | collective-permute-done | bytes 131104 | tf_op jit(solution)/shard_map/ppermute | solution.py:433
  26.2 4.0 %collective-permute-start.12 = (f32[1,136,128]{2,1,0:T(8,128)S(1)}, f32[1,136,128]{2,1,0:T(8,128)S(1)}, u32[]{:S(2)}, u32[]{:S(2)}) collective-permute-start(f32[1,136,128]{2,1,0:T(8,128)S(1)} %add_add_fusion.3), channel_id=1, source_target_pairs={{0,12},{1,13},{2,14},{3,15},{4,8},{5,9},{6,10},{7,11},{8,4},{9,5},... | collective-permute-start | bytes 208904 | tf_op jit(solution)/shard_map/ppermute | solution.py:66
  30.2 0.6 collective-permute-start.10
  30.8 0.1 fusion.2
  30.9 0.9 %collective-permute-start.14 = (f32[2,128,128]{2,1,0:T(8,128)S(1)}, f32[2,128,128]{2,1,0:T(8,128)S(1)}, u32[]{:S(2)}, u32[]{:S(2)}) collective-permute-start(f32[2,128,128]{2,1,0:T(8,128)S(1)} %get-tuple-element.62.second_ref), channel_id=1, source_target_pairs={{1,2},{17,18},{2,1},{18,17},{3,4},{19,20},{4,3},{20,19},{5,6},{21,... | collective-permute-start | bytes 393224 | tf_op jit(solution)/shard_map/ppermute | solution.py:433
  31.8 0.3 collective-permute-start.13
  32.0 0.6 collective-permute-done.12
  32.6 2.9 %collective-permute-done.11 = f32[1,136,128]{2,1,0:T(8,128)S(1)} collective-permute-done((f32[1,136,128]{2,1,0:T(8,128)S(1)}, f32[1,136,128]{2,1,0:T(8,128)S(1)}, u32[]{:S(2)}, u32[]{:S(2)}) %collective-permute-start.11) | collective-permute-done | bytes 69664 | tf_op jit(solution)/shard_map/ppermute | solution.py:66
  35.5 0.1 collective-permute-done.10
  35.6 0.3 collective-permute-done.14.rest_1_
  35.9 1.3 %collective-permute-start.17 = (f32[1,136,128]{2,1,0:T(8,128)S(1)}, f32[1,136,128]{2,1,0:T(8,128)S(1)}, u32[]{:S(2)}, u32[]{:S(2)}) collective-permute-start(f32[1,136,128]{2,1,0:T(8,128)S(1)} %add_add_fusion.2), channel_id=1, source_target_pairs={{0,18},{1,19},{2,16},{3,17},{4,22},{5,23},{6,20},{7,21},{8,26},{9,... | collective-permute-start | bytes 208904 | tf_op jit(solution)/shard_map/ppermute | solution.py:66
  37.2 1.0 %collective-permute-start.16 = (f32[1,136,128]{2,1,0:T(8,128)S(1)}, f32[1,136,128]{2,1,0:T(8,128)S(1)}, u32[]{:S(2)}, u32[]{:S(2)}) collective-permute-start(f32[1,136,128]{2,1,0:T(8,128)S(1)} %add_add_fusion.2), channel_id=1, source_target_pairs={{0,2},{1,3},{2,0},{3,1},{4,6},{5,7},{6,4},{7,5},{8,10},{9,11},{10,... | collective-permute-start | bytes 208904 | tf_op jit(solution)/shard_map/ppermute | solution.py:66
  38.2 1.2 %collective-permute-start.15 = (f32[1,136,128]{2,1,0:T(8,128)S(1)}, f32[1,136,128]{2,1,0:T(8,128)S(1)}, u32[]{:S(2)}, u32[]{:S(2)}) collective-permute-start(f32[1,136,128]{2,1,0:T(8,128)S(1)} %add_add_fusion.2), channel_id=1, source_target_pairs={{0,16},{1,17},{2,18},{3,19},{4,20},{5,21},{6,22},{7,23},{8,24},{9,... | collective-permute-start | bytes 208904 | tf_op jit(solution)/shard_map/ppermute | solution.py:66
  39.5 0.9 %collective-permute-start.18 = (f32[2,2,64,128]{3,2,1,0:T(8,128)S(1)}, f32[2,2,64,128]{3,2,1,0:T(8,128)S(1)}, u32[]{:S(2)}, u32[]{:S(2)}) collective-permute-start(f32[2,2,64,128]{3,2,1,0:T(8,128)S(1)} %pad_maximum_fusion.4), channel_id=1, source_target_pairs={{0,16},{16,0},{1,17},{17,1},{2,18},{18,2},{3,19},{19,3},{4,20},{20... | collective-permute-start | bytes 393224 | tf_op jit(solution)/shard_map/ppermute | solution.py:433
  40.3 0.9 %collective-permute-done.17 = f32[1,136,128]{2,1,0:T(8,128)S(1)} collective-permute-done((f32[1,136,128]{2,1,0:T(8,128)S(1)}, f32[1,136,128]{2,1,0:T(8,128)S(1)}, u32[]{:S(2)}, u32[]{:S(2)}) %collective-permute-start.17) | collective-permute-done | bytes 69664 | tf_op jit(solution)/shard_map/ppermute | solution.py:66
  41.2 1.4 %collective-permute-done.16 = f32[1,136,128]{2,1,0:T(8,128)S(1)} collective-permute-done((f32[1,136,128]{2,1,0:T(8,128)S(1)}, f32[1,136,128]{2,1,0:T(8,128)S(1)}, u32[]{:S(2)}, u32[]{:S(2)}) %collective-permute-start.16) | collective-permute-done | bytes 69664 | tf_op jit(solution)/shard_map/ppermute | solution.py:66
  42.6 0.6 collective-permute-done.15
  43.3 2.1 %collective-permute-done.18.rest_2_ = f32[2,2,64,128]{3,2,1,0:T(8,128)S(1)} collective-permute-done((f32[2,2,64,128]{3,2,1,0:T(8,128)S(1)}, f32[2,2,64,128]{3,2,1,0:T(8,128)S(1)}, u32[]{:S(2)}, u32[]{:S(2)}) %collective-permute-start.18) | collective-permute-done | bytes 131104 | tf_op jit(solution)/shard_map/ppermute | solution.py:433
  45.4 1.6 %collective-permute-done.19.other_ref = f32[4,136,128]{2,1,0:T(8,128)S(1)} collective-permute-done((f32[4,136,128]{2,1,0:T(8,128)S(1)}, f32[4,136,128]{2,1,0:T(8,128)S(1)}, u32[]{:S(2)}, u32[]{:S(2)}) %collective-permute-start.19) | collective-permute-done | bytes 278560 | tf_op jit(solution)/shard_map/ppermute | solution.py:66
  46.9 4.3 %shard_map.70 = (f32[2,128,128]{2,1,0:T(8,128)S(1)}, f32[2,4,128,128]{3,2,1,0:T(8,128)S(1)}, f32[4,136,128]{2,1,0:T(8,128)S(1)}, f32[4,136,128]{2,1,0:T(8,128)S(...) custom-call(s32[3,2]{1,0:T(4,128)S(1)} %copy.8.pos_ref, ...), custom_call_target="tpu_custom_call" | custom-call | tf_op jit(solution)/shard_map/pallas_call | solution.py:351
  51.2 0.2 collective-permute-start.20
  51.4 1.4 %collective-permute-done.20 = f32[4,136,128]{2,1,0:T(8,128)S(1)} collective-permute-done((f32[4,136,128]{2,1,0:T(8,128)S(1)}, f32[4,136,128]{2,1,0:T(8,128)S(1)}, u32[]{:S(2)}, u32[]{:S(2)}) %collective-permute-start.20) | collective-permute-done | bytes 278560 | tf_op jit(solution)/shard_map/ppermute | solution.py:66
  52.9 1.2 %collective-permute-start.21 = (f32[1,136,128]{2,1,0:T(8,128)S(1)}, f32[1,136,128]{2,1,0:T(8,128)S(1)}, u32[]{:S(2)}, u32[]{:S(2)}) collective-permute-start(f32[1,136,128]{2,1,0:T(8,128)S(1)} %get-tuple-element.86), channel_id=1, source_target_pairs={{0,16},{1,17},{2,18},{3,19},{4,20},{5,21},{6,22},{7,23},{8,24},{9,... | collective-permute-start | bytes 208904 | tf_op jit(solution)/shard_map/ppermute | solution.py:66
  54.2 1.6 %collective-permute-start.23 = (f32[1,136,128]{2,1,0:T(8,128)S(1)}, f32[1,136,128]{2,1,0:T(8,128)S(1)}, u32[]{:S(2)}, u32[]{:S(2)}) collective-permute-start(f32[1,136,128]{2,1,0:T(8,128)S(1)} %get-tuple-element.87), channel_id=1, source_target_pairs={{0,18},{1,19},{2,16},{3,17},{4,22},{5,23},{6,20},{7,21},{8,26},{9,... | collective-permute-start | bytes 208904 | tf_op jit(solution)/shard_map/ppermute | solution.py:66
  55.8 0.7 collective-permute-start.22
  56.5 1.2 %collective-permute-start.24 = (f32[2,2,64,128]{3,2,1,0:T(8,128)S(1)}, f32[2,2,64,128]{3,2,1,0:T(8,128)S(1)}, u32[]{:S(2)}, u32[]{:S(2)}) collective-permute-start(f32[2,2,64,128]{3,2,1,0:T(8,128)S(1)} %get-tuple-element.71), channel_id=1, source_target_pairs={{0,16},{16,0},{1,17},{17,1},{2,18},{18,2},{3,19},{19,3},{4,20},{20... | collective-permute-start | bytes 393224 | tf_op jit(solution)/shard_map/ppermute | solution.py:433
  57.7 2.3 %collective-permute-done.23 = f32[1,136,128]{2,1,0:T(8,128)S(1)} collective-permute-done((f32[1,136,128]{2,1,0:T(8,128)S(1)}, f32[1,136,128]{2,1,0:T(8,128)S(1)}, u32[]{:S(2)}, u32[]{:S(2)}) %collective-permute-start.23) | collective-permute-done | bytes 69664 | tf_op jit(solution)/shard_map/ppermute | solution.py:66
  60.0 0.7 collective-permute-done.22
  60.7 1.2 %collective-permute-done.24 = f32[2,2,64,128]{3,2,1,0:T(8,128)S(1)} collective-permute-done((f32[2,2,64,128]{3,2,1,0:T(8,128)S(1)}, f32[2,2,64,128]{3,2,1,0:T(8,128)S(1)}, u32[]{:S(2)}, u32[]{:S(2)}) %collective-permute-start.24) | collective-permute-done | bytes 131104 | tf_op jit(solution)/shard_map/ppermute | solution.py:433
  61.9 3.2 %collective-permute-start.27 = (f32[1,136,128]{2,1,0:T(8,128)S(1)}, f32[1,136,128]{2,1,0:T(8,128)S(1)}, u32[]{:S(2)}, u32[]{:S(2)}) collective-permute-start(f32[1,136,128]{2,1,0:T(8,128)S(1)} %add_add_fusion.1), channel_id=1, source_target_pairs={{0,12},{1,13},{2,14},{3,15},{4,8},{5,9},{6,10},{7,11},{8,4},{9,5},... | collective-permute-start | bytes 208904 | tf_op jit(solution)/shard_map/ppermute | solution.py:66
  65.2 1.1 %collective-permute-start.25 = (f32[1,136,128]{2,1,0:T(8,128)S(1)}, f32[1,136,128]{2,1,0:T(8,128)S(1)}, u32[]{:S(2)}, u32[]{:S(2)}) collective-permute-start(f32[1,136,128]{2,1,0:T(8,128)S(1)} %add_add_fusion.1), channel_id=1, source_target_pairs={{0,4},{1,5},{2,6},{3,7},{4,0},{5,1},{6,2},{7,3},{8,12},{9,13},{10,... | collective-permute-start | bytes 208904 | tf_op jit(solution)/shard_map/ppermute | solution.py:66
  66.3 0.1 fusion
  66.4 1.0 %collective-permute-start.29 = (f32[2,128,128]{2,1,0:T(8,128)S(1)}, f32[2,128,128]{2,1,0:T(8,128)S(1)}, u32[]{:S(2)}, u32[]{:S(2)}) collective-permute-start(f32[2,128,128]{2,1,0:T(8,128)S(1)} %get-tuple-element.77.second_ref), channel_id=1, source_target_pairs={{1,2},{17,18},{2,1},{18,17},{3,4},{19,20},{4,3},{20,19},{5,6},{21,... | collective-permute-start | bytes 393224 | tf_op jit(solution)/shard_map/ppermute | solution.py:433
  67.5 0.1 collective-permute-start.28
  67.6 0.4 collective-permute-done.27
  68.0 2.7 %collective-permute-done.26 = f32[1,136,128]{2,1,0:T(8,128)S(1)} collective-permute-done((f32[1,136,128]{2,1,0:T(8,128)S(1)}, f32[1,136,128]{2,1,0:T(8,128)S(1)}, u32[]{:S(2)}, u32[]{:S(2)}) %collective-permute-start.26) | collective-permute-done | bytes 69664 | tf_op jit(solution)/shard_map/ppermute | solution.py:66
  70.8 0.7 collective-permute-done.29.rest_1_
  71.5 1.2 %collective-permute-start.32 = (f32[1,136,128]{2,1,0:T(8,128)S(1)}, f32[1,136,128]{2,1,0:T(8,128)S(1)}, u32[]{:S(2)}, u32[]{:S(2)}) collective-permute-start(f32[1,136,128]{2,1,0:T(8,128)S(1)} %add_add_fusion), channel_id=1, source_target_pairs={{0,18},{1,19},{2,16},{3,17},{4,22},{5,23},{6,20},{7,21},{8,26},{9,... | collective-permute-start | bytes 208904 | tf_op jit(solution)/shard_map/ppermute | solution.py:66
  72.6 1.3 %collective-permute-start.31 = (f32[1,136,128]{2,1,0:T(8,128)S(1)}, f32[1,136,128]{2,1,0:T(8,128)S(1)}, u32[]{:S(2)}, u32[]{:S(2)}) collective-permute-start(f32[1,136,128]{2,1,0:T(8,128)S(1)} %add_add_fusion), channel_id=1, source_target_pairs={{0,2},{1,3},{2,0},{3,1},{4,6},{5,7},{6,4},{7,5},{8,10},{9,11},{10,... | collective-permute-start | bytes 208904 | tf_op jit(solution)/shard_map/ppermute | solution.py:66
  73.9 1.1 %collective-permute-start.30 = (f32[1,136,128]{2,1,0:T(8,128)S(1)}, f32[1,136,128]{2,1,0:T(8,128)S(1)}, u32[]{:S(2)}, u32[]{:S(2)}) collective-permute-start(f32[1,136,128]{2,1,0:T(8,128)S(1)} %add_add_fusion), channel_id=1, source_target_pairs={{0,16},{1,17},{2,18},{3,19},{4,20},{5,21},{6,22},{7,23},{8,24},{9,... | collective-permute-start | bytes 208904 | tf_op jit(solution)/shard_map/ppermute | solution.py:66
  75.0 1.8 %collective-permute-done.32 = f32[1,136,128]{2,1,0:T(8,128)S(1)} collective-permute-done((f32[1,136,128]{2,1,0:T(8,128)S(1)}, f32[1,136,128]{2,1,0:T(8,128)S(1)}, u32[]{:S(2)}, u32[]{:S(2)}) %collective-permute-start.32) | collective-permute-done | bytes 69664 | tf_op jit(solution)/shard_map/ppermute | solution.py:66
  76.7 1.4 %collective-permute-done.31 = f32[1,136,128]{2,1,0:T(8,128)S(1)} collective-permute-done((f32[1,136,128]{2,1,0:T(8,128)S(1)}, f32[1,136,128]{2,1,0:T(8,128)S(1)}, u32[]{:S(2)}, u32[]{:S(2)}) %collective-permute-start.31) | collective-permute-done | bytes 69664 | tf_op jit(solution)/shard_map/ppermute | solution.py:66
  78.3 0.1 collective-permute-start.33
  78.4 1.5 %collective-permute-done.33.other_ref = f32[4,136,128]{2,1,0:T(8,128)S(1)} collective-permute-done((f32[4,136,128]{2,1,0:T(8,128)S(1)}, f32[4,136,128]{2,1,0:T(8,128)S(1)}, u32[]{:S(2)}, u32[]{:S(2)}) %collective-permute-start.33) | collective-permute-done | bytes 278560 | tf_op jit(solution)/shard_map/ppermute | solution.py:66
  79.9 1.0 %shard_map.71 = (f32[2,128,128]{2,1,0:T(8,128)}, f32[2,4,128,128]{3,2,1,0:T(8,128)}) custom-call(f32[2,128,128]{2,1,0:T(8,128)S(1)} %get-tuple-element.68.tile_ref, f32[2,128,128]{2,1,0:T(8,128)S(1)} %get-tuple-element.76.first_ref, f32[2,128,128]{2,1,0:T(8,128)S(1)} %get-tuple-element.77.second_ref, f32[2,4,128,128]{3,2,1,0:T(8,128)S(1)} %get-tuple-element.78.probe_ref, ...), custom_call_target="tpu_custom_call" | custom-call | tf_op jit(solution)/shard_map/pallas_call | solution.py:351
  (43 shorter events, 0.8 us)
Async XLA Ops:
  0.6 3.9 %copy-start.1 = (f32[2,128,128]{2,1,0:T(8,128)S(1)}, f32[2,128,128]{2,1,0:T(8,128)}, u32[]{:S(2)}) copy-start(f32[2,128,128]{2,1,0:T(8,128)} %obj_ref.1) | copy-start | bytes 393220
  1.5 6.2 %copy-start.4 = (s32[1,1,3,2]{2,3,1,0:T(2,128)S(1)}, s32[1,1,3,2]{2,3,1,0:T(2,128)}, u32[]{:S(2)}) copy-start(s32[1,1,3,2]{2,3,1,0:T(2,128)} %param.8) | copy-start | bytes 76
  1.6 5.2 %collective-permute-start.2 = (f32[2,64,128]{2,1,0:T(8,128)S(1)}, f32[2,64,128]{2,1,0:T(8,128)S(1)}, u32[]{:S(2)}, u32[]{:S(2)}) collective-permute-start(f32[2,64,128]{2,1,0:T(8,128)S(1)} %constant_dynamic-slice_fusion.6), channel_id=1, source_target_pairs={{0,16},{16,0},{1,17},{17,1},{2,18},{18,2},{3,19},{19,3},{4,20},{20... | collective-permute-start | bytes 196616 | tf_op jit(solution)/shard_map/ppermute | solution.py:433
  4.5 6.3 %collective-permute-start.1 = (f32[2,128,128]{2,1,0:T(8,128)S(1)}, f32[2,128,128]{2,1,0:T(8,128)S(1)}, u32[]{:S(2)}, u32[]{:S(2)}) collective-permute-start(f32[2,128,128]{2,1,0:T(8,128)S(1)} %copy-done.1), channel_id=1, source_target_pairs={{1,2},{17,18},{2,1},{18,17},{3,4},{19,20},{4,3},{20,19},{5,6},{21,... | collective-permute-start | bytes 393224 | tf_op jit(solution)/shard_map/ppermute | solution.py:433
  4.6 6.3 %collective-permute-start = (f32[2,128,128]{2,1,0:T(8,128)S(1)}, f32[2,128,128]{2,1,0:T(8,128)S(1)}, u32[]{:S(2)}, u32[]{:S(2)}) collective-permute-start(f32[2,128,128]{2,1,0:T(8,128)S(1)} %copy-done.1), channel_id=1, source_target_pairs={{0,1},{16,17},{1,0},{17,16},{2,3},{18,19},{3,2},{19,18},{4,5},{20,... | collective-permute-start | bytes 393224 | tf_op jit(solution)/shard_map/ppermute | solution.py:433
  6.1 4.7 %collective-permute-start.4 = (f32[2,64,128]{2,1,0:T(8,128)S(1)}, f32[2,64,128]{2,1,0:T(8,128)S(1)}, u32[]{:S(2)}, u32[]{:S(2)}) collective-permute-start(f32[2,64,128]{2,1,0:T(8,128)S(1)} %constant_dynamic-slice_fusion.6), channel_id=1, source_target_pairs={{1,18},{17,2},{2,17},{18,1},{3,20},{19,4},{4,19},{20,3},{5,22},{21... | collective-permute-start | bytes 196616 | tf_op jit(solution)/shard_map/ppermute | solution.py:433
  6.7 4.1 %collective-permute-start.3 = (f32[2,64,128]{2,1,0:T(8,128)S(1)}, f32[2,64,128]{2,1,0:T(8,128)S(1)}, u32[]{:S(2)}, u32[]{:S(2)}) collective-permute-start(f32[2,64,128]{2,1,0:T(8,128)S(1)} %collective-permute-done.2.rest_0_), channel_id=1, source_target_pairs={{0,1},{16,17},{1,0},{17,16},{2,3},{18,19},{3,2},{19,18},{4,5},{20,... | collective-permute-start | bytes 196616 | tf_op jit(solution)/shard_map/ppermute | solution.py:433
  7.8 1.0 %copy-start = (f32[2,4,128,128]{3,2,1,0:T(8,128)S(1)}, f32[2,4,128,128]{3,2,1,0:T(8,128)}, u32[]{:S(2)}) copy-start(f32[2,4,128,128]{3,2,1,0:T(8,128)} %probe_ref.1) | copy-start | bytes 1572868
  8.9 0.9 %copy-start.2 = (f32[1,1,3,128,128]{4,3,2,1,0:T(8,128)S(1)}, f32[1,1,3,128,128]{4,3,2,1,0:T(8,128)}, u32[]{:S(2)}) copy-start(f32[1,1,3,128,128]{4,3,2,1,0:T(8,128)} %param.7) | copy-start | bytes 589828
  9.8 0.9 %copy-start.3 = (bf16[4,128,128]{2,1,0:T(8,128)(2,1)S(1)}, bf16[4,128,128]{2,1,0:T(8,128)(2,1)}, u32[]{:S(2)}) copy-start(bf16[4,128,128]{2,1,0:T(8,128)(2,1)} %constant.74.clone.table_ref) | copy-start | bytes 393220
  14.9 1.6 %collective-permute-start.5 = (f32[4,136,128]{2,1,0:T(8,128)S(1)}, f32[4,136,128]{2,1,0:T(8,128)S(1)}, u32[]{:S(2)}, u32[]{:S(2)}) collective-permute-start(f32[4,136,128]{2,1,0:T(8,128)S(1)} %get-tuple-element.55), channel_id=1, source_target_pairs={{0,1},{1,0},{2,3},{3,2},{4,5},{5,4},{6,7},{7,6},{8,9},{9,8},{10,11... | collective-permute-start | bytes 835592 | tf_op jit(solution)/shard_map/ppermute | solution.py:66
  16.6 5.2 %collective-permute-start.6 = (f32[1,136,128]{2,1,0:T(8,128)S(1)}, f32[1,136,128]{2,1,0:T(8,128)S(1)}, u32[]{:S(2)}, u32[]{:S(2)}) collective-permute-start(f32[1,136,128]{2,1,0:T(8,128)S(1)} %get-tuple-element.93), channel_id=1, source_target_pairs={{0,16},{1,17},{2,18},{3,19},{4,20},{5,21},{6,22},{7,23},{8,24},{9,... | collective-permute-start | bytes 208904 | tf_op jit(solution)/shard_map/ppermute | solution.py:66
  18.2 5.9 %collective-permute-start.8 = (f32[1,136,128]{2,1,0:T(8,128)S(1)}, f32[1,136,128]{2,1,0:T(8,128)S(1)}, u32[]{:S(2)}, u32[]{:S(2)}) collective-permute-start(f32[1,136,128]{2,1,0:T(8,128)S(1)} %get-tuple-element.94), channel_id=1, source_target_pairs={{0,18},{1,19},{2,16},{3,17},{4,22},{5,23},{6,20},{7,21},{8,26},{9,... | collective-permute-start | bytes 208904 | tf_op jit(solution)/shard_map/ppermute | solution.py:66
  20.1 5.1 %collective-permute-start.7 = (f32[1,136,128]{2,1,0:T(8,128)S(1)}, f32[1,136,128]{2,1,0:T(8,128)S(1)}, u32[]{:S(2)}, u32[]{:S(2)}) collective-permute-start(f32[1,136,128]{2,1,0:T(8,128)S(1)} %get-tuple-element.95), channel_id=1, source_target_pairs={{0,2},{1,3},{2,0},{3,1},{4,6},{5,7},{6,4},{7,5},{8,10},{9,11},{10,... | collective-permute-start | bytes 208904 | tf_op jit(solution)/shard_map/ppermute | solution.py:66
  20.3 5.9 %collective-permute-start.9 = (f32[2,2,64,128]{3,2,1,0:T(8,128)S(1)}, f32[2,2,64,128]{3,2,1,0:T(8,128)S(1)}, u32[]{:S(2)}, u32[]{:S(2)}) collective-permute-start(f32[2,2,64,128]{3,2,1,0:T(8,128)S(1)} %get-tuple-element.56), channel_id=1, source_target_pairs={{0,16},{16,0},{1,17},{17,1},{2,18},{18,2},{3,19},{19,3},{4,20},{20... | collective-permute-start | bytes 393224 | tf_op jit(solution)/shard_map/ppermute | solution.py:433
  26.2 6.4 %collective-permute-start.12 = (f32[1,136,128]{2,1,0:T(8,128)S(1)}, f32[1,136,128]{2,1,0:T(8,128)S(1)}, u32[]{:S(2)}, u32[]{:S(2)}) collective-permute-start(f32[1,136,128]{2,1,0:T(8,128)S(1)} %add_add_fusion.3), channel_id=1, source_target_pairs={{0,12},{1,13},{2,14},{3,15},{4,8},{5,9},{6,10},{7,11},{8,4},{9,5},... | collective-permute-start | bytes 208904 | tf_op jit(solution)/shard_map/ppermute | solution.py:66
  30.2 5.3 %collective-permute-start.11 = (f32[1,136,128]{2,1,0:T(8,128)S(1)}, f32[1,136,128]{2,1,0:T(8,128)S(1)}, u32[]{:S(2)}, u32[]{:S(2)}) collective-permute-start(f32[1,136,128]{2,1,0:T(8,128)S(1)} %add_add_fusion.3), channel_id=1, source_target_pairs={{0,8},{1,9},{2,10},{3,11},{4,12},{5,13},{6,14},{7,15},{8,0},{9,1},... | collective-permute-start | bytes 208904 | tf_op jit(solution)/shard_map/ppermute | solution.py:66
  30.2 5.4 %collective-permute-start.10 = (f32[1,136,128]{2,1,0:T(8,128)S(1)}, f32[1,136,128]{2,1,0:T(8,128)S(1)}, u32[]{:S(2)}, u32[]{:S(2)}) collective-permute-start(f32[1,136,128]{2,1,0:T(8,128)S(1)} %add_add_fusion.3), channel_id=1, source_target_pairs={{0,4},{1,5},{2,6},{3,7},{4,0},{5,1},{6,2},{7,3},{8,12},{9,13},{10,... | collective-permute-start | bytes 208904 | tf_op jit(solution)/shard_map/ppermute | solution.py:66
  30.9 5.0 %collective-permute-start.14 = (f32[2,128,128]{2,1,0:T(8,128)S(1)}, f32[2,128,128]{2,1,0:T(8,128)S(1)}, u32[]{:S(2)}, u32[]{:S(2)}) collective-permute-start(f32[2,128,128]{2,1,0:T(8,128)S(1)} %get-tuple-element.62.second_ref), channel_id=1, source_target_pairs={{1,2},{17,18},{2,1},{18,17},{3,4},{19,20},{4,3},{20,19},{5,6},{21,... | collective-permute-start | bytes 393224 | tf_op jit(solution)/shard_map/ppermute | solution.py:433
  31.8 4.2 %collective-permute-start.13 = (f32[2,128,128]{2,1,0:T(8,128)S(1)}, f32[2,128,128]{2,1,0:T(8,128)S(1)}, u32[]{:S(2)}, u32[]{:S(2)}) collective-permute-start(f32[2,128,128]{2,1,0:T(8,128)S(1)} %get-tuple-element.61.first_ref), channel_id=1, source_target_pairs={{0,1},{16,17},{1,0},{17,16},{2,3},{18,19},{3,2},{19,18},{4,5},{20,... | collective-permute-start | bytes 393224 | tf_op jit(solution)/shard_map/ppermute | solution.py:433
  35.9 5.3 %collective-permute-start.17 = (f32[1,136,128]{2,1,0:T(8,128)S(1)}, f32[1,136,128]{2,1,0:T(8,128)S(1)}, u32[]{:S(2)}, u32[]{:S(2)}) collective-permute-start(f32[1,136,128]{2,1,0:T(8,128)S(1)} %add_add_fusion.2), channel_id=1, source_target_pairs={{0,18},{1,19},{2,16},{3,17},{4,22},{5,23},{6,20},{7,21},{8,26},{9,... | collective-permute-start | bytes 208904 | tf_op jit(solution)/shard_map/ppermute | solution.py:66
  37.2 5.4 %collective-permute-start.16 = (f32[1,136,128]{2,1,0:T(8,128)S(1)}, f32[1,136,128]{2,1,0:T(8,128)S(1)}, u32[]{:S(2)}, u32[]{:S(2)}) collective-permute-start(f32[1,136,128]{2,1,0:T(8,128)S(1)} %add_add_fusion.2), channel_id=1, source_target_pairs={{0,2},{1,3},{2,0},{3,1},{4,6},{5,7},{6,4},{7,5},{8,10},{9,11},{10,... | collective-permute-start | bytes 208904 | tf_op jit(solution)/shard_map/ppermute | solution.py:66
  38.2 5.0 %collective-permute-start.15 = (f32[1,136,128]{2,1,0:T(8,128)S(1)}, f32[1,136,128]{2,1,0:T(8,128)S(1)}, u32[]{:S(2)}, u32[]{:S(2)}) collective-permute-start(f32[1,136,128]{2,1,0:T(8,128)S(1)} %add_add_fusion.2), channel_id=1, source_target_pairs={{0,16},{1,17},{2,18},{3,19},{4,20},{5,21},{6,22},{7,23},{8,24},{9,... | collective-permute-start | bytes 208904 | tf_op jit(solution)/shard_map/ppermute | solution.py:66
  39.5 5.9 %collective-permute-start.18 = (f32[2,2,64,128]{3,2,1,0:T(8,128)S(1)}, f32[2,2,64,128]{3,2,1,0:T(8,128)S(1)}, u32[]{:S(2)}, u32[]{:S(2)}) collective-permute-start(f32[2,2,64,128]{3,2,1,0:T(8,128)S(1)} %pad_maximum_fusion.4), channel_id=1, source_target_pairs={{0,16},{16,0},{1,17},{17,1},{2,18},{18,2},{3,19},{19,3},{4,20},{20... | collective-permute-start | bytes 393224 | tf_op jit(solution)/shard_map/ppermute | solution.py:433
  45.4 1.6 %collective-permute-start.19 = (f32[4,136,128]{2,1,0:T(8,128)S(1)}, f32[4,136,128]{2,1,0:T(8,128)S(1)}, u32[]{:S(2)}, u32[]{:S(2)}) collective-permute-start(f32[4,136,128]{2,1,0:T(8,128)S(1)} %pad_maximum_fusion.1.own_ref), channel_id=1, source_target_pairs={{0,1},{1,0},{2,3},{3,2},{4,5},{5,4},{6,7},{7,6},{8,9},{9,8},{10,11... | collective-permute-start | bytes 835592 | tf_op jit(solution)/shard_map/ppermute | solution.py:66
  51.2 1.6 %collective-permute-start.20 = (f32[4,136,128]{2,1,0:T(8,128)S(1)}, f32[4,136,128]{2,1,0:T(8,128)S(1)}, u32[]{:S(2)}, u32[]{:S(2)}) collective-permute-start(f32[4,136,128]{2,1,0:T(8,128)S(1)} %get-tuple-element.70), channel_id=1, source_target_pairs={{0,1},{1,0},{2,3},{3,2},{4,5},{5,4},{6,7},{7,6},{8,9},{9,8},{10,11... | collective-permute-start | bytes 835592 | tf_op jit(solution)/shard_map/ppermute | solution.py:66
  52.9 4.7 %collective-permute-start.21 = (f32[1,136,128]{2,1,0:T(8,128)S(1)}, f32[1,136,128]{2,1,0:T(8,128)S(1)}, u32[]{:S(2)}, u32[]{:S(2)}) collective-permute-start(f32[1,136,128]{2,1,0:T(8,128)S(1)} %get-tuple-element.86), channel_id=1, source_target_pairs={{0,16},{1,17},{2,18},{3,19},{4,20},{5,21},{6,22},{7,23},{8,24},{9,... | collective-permute-start | bytes 208904 | tf_op jit(solution)/shard_map/ppermute | solution.py:66
  54.2 5.8 %collective-permute-start.23 = (f32[1,136,128]{2,1,0:T(8,128)S(1)}, f32[1,136,128]{2,1,0:T(8,128)S(1)}, u32[]{:S(2)}, u32[]{:S(2)}) collective-permute-start(f32[1,136,128]{2,1,0:T(8,128)S(1)} %get-tuple-element.87), channel_id=1, source_target_pairs={{0,18},{1,19},{2,16},{3,17},{4,22},{5,23},{6,20},{7,21},{8,26},{9,... | collective-permute-start | bytes 208904 | tf_op jit(solution)/shard_map/ppermute | solution.py:66
  55.8 4.9 %collective-permute-start.22 = (f32[1,136,128]{2,1,0:T(8,128)S(1)}, f32[1,136,128]{2,1,0:T(8,128)S(1)}, u32[]{:S(2)}, u32[]{:S(2)}) collective-permute-start(f32[1,136,128]{2,1,0:T(8,128)S(1)} %get-tuple-element.88), channel_id=1, source_target_pairs={{0,2},{1,3},{2,0},{3,1},{4,6},{5,7},{6,4},{7,5},{8,10},{9,11},{10,... | collective-permute-start | bytes 208904 | tf_op jit(solution)/shard_map/ppermute | solution.py:66
  56.5 5.4 %collective-permute-start.24 = (f32[2,2,64,128]{3,2,1,0:T(8,128)S(1)}, f32[2,2,64,128]{3,2,1,0:T(8,128)S(1)}, u32[]{:S(2)}, u32[]{:S(2)}) collective-permute-start(f32[2,2,64,128]{3,2,1,0:T(8,128)S(1)} %get-tuple-element.71), channel_id=1, source_target_pairs={{0,16},{16,0},{1,17},{17,1},{2,18},{18,2},{3,19},{19,3},{4,20},{20... | collective-permute-start | bytes 393224 | tf_op jit(solution)/shard_map/ppermute | solution.py:433
  61.9 6.1 %collective-permute-start.27 = (f32[1,136,128]{2,1,0:T(8,128)S(1)}, f32[1,136,128]{2,1,0:T(8,128)S(1)}, u32[]{:S(2)}, u32[]{:S(2)}) collective-permute-start(f32[1,136,128]{2,1,0:T(8,128)S(1)} %add_add_fusion.1), channel_id=1, source_target_pairs={{0,12},{1,13},{2,14},{3,15},{4,8},{5,9},{6,10},{7,11},{8,4},{9,5},... | collective-permute-start | bytes 208904 | tf_op jit(solution)/shard_map/ppermute | solution.py:66
  65.2 5.6 %collective-permute-start.26 = (f32[1,136,128]{2,1,0:T(8,128)S(1)}, f32[1,136,128]{2,1,0:T(8,128)S(1)}, u32[]{:S(2)}, u32[]{:S(2)}) collective-permute-start(f32[1,136,128]{2,1,0:T(8,128)S(1)} %add_add_fusion.1), channel_id=1, source_target_pairs={{0,8},{1,9},{2,10},{3,11},{4,12},{5,13},{6,14},{7,15},{8,0},{9,1},... | collective-permute-start | bytes 208904 | tf_op jit(solution)/shard_map/ppermute | solution.py:66
  65.2 5.6 %collective-permute-start.25 = (f32[1,136,128]{2,1,0:T(8,128)S(1)}, f32[1,136,128]{2,1,0:T(8,128)S(1)}, u32[]{:S(2)}, u32[]{:S(2)}) collective-permute-start(f32[1,136,128]{2,1,0:T(8,128)S(1)} %add_add_fusion.1), channel_id=1, source_target_pairs={{0,4},{1,5},{2,6},{3,7},{4,0},{5,1},{6,2},{7,3},{8,12},{9,13},{10,... | collective-permute-start | bytes 208904 | tf_op jit(solution)/shard_map/ppermute | solution.py:66
  66.4 5.0 %collective-permute-start.29 = (f32[2,128,128]{2,1,0:T(8,128)S(1)}, f32[2,128,128]{2,1,0:T(8,128)S(1)}, u32[]{:S(2)}, u32[]{:S(2)}) collective-permute-start(f32[2,128,128]{2,1,0:T(8,128)S(1)} %get-tuple-element.77.second_ref), channel_id=1, source_target_pairs={{1,2},{17,18},{2,1},{18,17},{3,4},{19,20},{4,3},{20,19},{5,6},{21,... | collective-permute-start | bytes 393224 | tf_op jit(solution)/shard_map/ppermute | solution.py:433
  67.5 4.0 %collective-permute-start.28 = (f32[2,128,128]{2,1,0:T(8,128)S(1)}, f32[2,128,128]{2,1,0:T(8,128)S(1)}, u32[]{:S(2)}, u32[]{:S(2)}) collective-permute-start(f32[2,128,128]{2,1,0:T(8,128)S(1)} %get-tuple-element.76.first_ref), channel_id=1, source_target_pairs={{0,1},{16,17},{1,0},{17,16},{2,3},{18,19},{3,2},{19,18},{4,5},{20,... | collective-permute-start | bytes 393224 | tf_op jit(solution)/shard_map/ppermute | solution.py:433
  71.5 5.3 %collective-permute-start.32 = (f32[1,136,128]{2,1,0:T(8,128)S(1)}, f32[1,136,128]{2,1,0:T(8,128)S(1)}, u32[]{:S(2)}, u32[]{:S(2)}) collective-permute-start(f32[1,136,128]{2,1,0:T(8,128)S(1)} %add_add_fusion), channel_id=1, source_target_pairs={{0,18},{1,19},{2,16},{3,17},{4,22},{5,23},{6,20},{7,21},{8,26},{9,... | collective-permute-start | bytes 208904 | tf_op jit(solution)/shard_map/ppermute | solution.py:66
  72.6 5.5 %collective-permute-start.31 = (f32[1,136,128]{2,1,0:T(8,128)S(1)}, f32[1,136,128]{2,1,0:T(8,128)S(1)}, u32[]{:S(2)}, u32[]{:S(2)}) collective-permute-start(f32[1,136,128]{2,1,0:T(8,128)S(1)} %add_add_fusion), channel_id=1, source_target_pairs={{0,2},{1,3},{2,0},{3,1},{4,6},{5,7},{6,4},{7,5},{8,10},{9,11},{10,... | collective-permute-start | bytes 208904 | tf_op jit(solution)/shard_map/ppermute | solution.py:66
  73.9 4.3 %collective-permute-start.30 = (f32[1,136,128]{2,1,0:T(8,128)S(1)}, f32[1,136,128]{2,1,0:T(8,128)S(1)}, u32[]{:S(2)}, u32[]{:S(2)}) collective-permute-start(f32[1,136,128]{2,1,0:T(8,128)S(1)} %add_add_fusion), channel_id=1, source_target_pairs={{0,16},{1,17},{2,18},{3,19},{4,20},{5,21},{6,22},{7,23},{8,24},{9,... | collective-permute-start | bytes 208904 | tf_op jit(solution)/shard_map/ppermute | solution.py:66
  78.3 1.6 %collective-permute-start.33 = (f32[4,136,128]{2,1,0:T(8,128)S(1)}, f32[4,136,128]{2,1,0:T(8,128)S(1)}, u32[]{:S(2)}, u32[]{:S(2)}) collective-permute-start(f32[4,136,128]{2,1,0:T(8,128)S(1)} %pad_maximum_fusion.3.own_ref), channel_id=1, source_target_pairs={{0,1},{1,0},{2,3},{3,2},{4,5},{5,4},{6,7},{7,6},{8,9},{9,8},{10,11... | collective-permute-start | bytes 835592 | tf_op jit(solution)/shard_map/ppermute | solution.py:66

commit v4 on v3

--- a/solution.py
+++ b/solution.py
@@ -376,18 +376,21 @@
     return values[0]
 
 
-def scatter_sum(x, me, bits, total):
+def scatter_sum(x, me, bits, total, beside):
     here = local_index(me, bits)
     n = 1 << len(bits)
     x = x.reshape((n, x.shape[0] // n) + x.shape[1:])
     parts = [lax.dynamic_index_in_dim(x, here, 0, False)]
     for m, mask in enumerate(masks_of(bits), 1):
         parts.append(xor_permute(lax.dynamic_index_in_dim(x, here ^ m, 0, False), mask, total))
-    return tree(parts)
-
-
-def direct_sum(x, bits, total):
-    return tree([x] + [xor_permute(x, mask, total) for mask in masks_of(bits)])
+    parts[0], beside = lax.optimization_barrier((parts[0], beside))
+    return tree(parts), beside
+
+
+def direct_sum(x, bits, total, beside):
+    parts = [xor_permute(x, mask, total) for mask in masks_of(bits)]
+    x, beside = lax.optimization_barrier((x, beside))
+    return tree([x] + parts), beside
 
 
 def gather(x, me, bits, total):
@@ -407,11 +410,10 @@
     rest = [b for b in range(1, levels) if b not in bits]
     half = keep + xor_permute(send, 1, total)
     done = [steps[0]()]
-    half = scatter_sum(half, me, bits, total)
-    half, done[0] = lax.optimization_barrier((half, done[0]))
+    half, done[0] = scatter_sum(half, me, bits, total, done[0])
     done.append(steps[1](*done))
     for i in range(0, len(rest), 2):
-        half = direct_sum(half, rest[i : i + 2], total)
+        half, _ = direct_sum(half, rest[i : i + 2], total, ())
     half, done[1] = lax.optimization_barrier((half, done[1]))
     done += [step(*done) for step in steps[2:]]
     half = gather(half, me, bits, total)

time: 81.2 us -> 80.1 us (0.986)
  waiting for transfers between devices: 30.6 us -> 28.8 us
    ppermute x22, waiting for transfers between devices: 25.3 us -> 23.9 us  [xor_permute(): return lax.ppermute(x, AXES, [(i, i ^ mask) for i in range(total)])]
    ppermute x12, starting transfers between devices: 12 us -> 12.8 us  [swap(): return lax.ppermute(x, AXES, flat_pairs(pairs_y, pairs_x, n_ty, n_tx))]
  transfers between devices with their start and end apart: 34 -> 34, of which waited for: 24 -> 25; matrix products, arithmetic and copies ran while one was open for 1% -> 1% of each run, Pallas kernels for 0% -> 0%
where the time goes in v4:
time: 80.1 us; the launch traced here: 79.8 us
  starting transfers between devices  36.1 us (45%)
  waiting for transfers between devices  28.8 us (36%)
  Pallas kernels  9.43 us (12%)
  local copies, waits for them, and re-layouts  4.17 us (5%)
  between operations  0.88 us (1%)
    ppermute x22, waiting for transfers between devices, xor_permute(): return lax.ppermute(x, AXES, [(i, i ^ mask) for i in range(total)])  23.9 us
    ppermute x22, starting transfers between devices, xor_permute(): return lax.ppermute(x, AXES, [(i, i ^ mask) for i in range(total)])  23.3 us
    ppermute x12, starting transfers between devices, swap(): return lax.ppermute(x, AXES, flat_pairs(pairs_y, pairs_x, n_ty, n_tx))  12.8 us
    pallas_call x4, Pallas kernels, call(): pl.pallas_call(kernel, out_shape=shapes, in_specs=[smem if x.dtype == jnp...  9.43 us
    ppermute x12, waiting for transfers between devices, swap(): return lax.ppermute(x, AXES, flat_pairs(pairs_y, pairs_x, n_ty, n_tx))  4.84 us
    unnamed x10, local copies, waits for them, and re-layouts  2.88 us
  transfers between devices with their start and end apart: 34, of which 25 were waited for; matrix products, arithmetic and copies ran while one was open for 1% of the time, Pallas kernels for 0%

profile of v4, /device:TPU:0, one launch (start us, length us, event | category | flops | bytes accessed | tf_op | source)
XLA Modules:
  0.0 79.8 jit_solution(9371927490807771576)
XLA Ops:
  0.7 0.9 %constant_dynamic-slice_fusion.8 = f32[2,64,128]{2,1,0:T(8,128)S(1)} fusion(f32[2,128,128]{2,1,0:T(8,128)} %obj_ref.1, s32[]{:T(128)S(6)} %select_n.77), kind=kLoop, calls=%fused_computation.43 | loop fusion | bytes 131076 | tf_op jit(solution)/shard_map/dynamic_slice | solution.py:439
  1.6 2.9 %collective-permute-start.2 = (f32[2,64,128]{2,1,0:T(8,128)S(1)}, f32[2,64,128]{2,1,0:T(8,128)S(1)}, u32[]{:S(2)}, u32[]{:S(2)}) collective-permute-start(f32[2,64,128]{2,1,0:T(8,128)S(1)} %constant_dynamic-slice_fusion.8), channel_id=1, source_target_pairs={{0,16},{16,0},{1,17},{17,1},{2,18},{18,2},{3,19},{19,3},{4,20},{20... | collective-permute-start | bytes 196616 | tf_op jit(solution)/shard_map/ppermute | solution.py:435
  4.5 0.1 collective-permute-start.1
  4.6 1.6 %collective-permute-start = (f32[2,128,128]{2,1,0:T(8,128)S(1)}, f32[2,128,128]{2,1,0:T(8,128)S(1)}, u32[]{:S(2)}, u32[]{:S(2)}) collective-permute-start(f32[2,128,128]{2,1,0:T(8,128)S(1)} %copy-done.1), channel_id=1, source_target_pairs={{0,1},{16,17},{1,0},{17,16},{2,3},{18,19},{3,2},{19,18},{4,5},{20,... | collective-permute-start | bytes 393224 | tf_op jit(solution)/shard_map/ppermute | solution.py:435
  6.1 0.5 collective-permute-start.4
  6.7 1.0 %collective-permute-start.3 = (f32[2,64,128]{2,1,0:T(8,128)S(1)}, f32[2,64,128]{2,1,0:T(8,128)S(1)}, u32[]{:S(2)}, u32[]{:S(2)}) collective-permute-start(f32[2,64,128]{2,1,0:T(8,128)S(1)} %collective-permute-done.2.rest_0_), channel_id=1, source_target_pairs={{0,1},{16,17},{1,0},{17,16},{2,3},{18,19},{3,2},{19,18},{4,5},{20,... | collective-permute-start | bytes 196616 | tf_op jit(solution)/shard_map/ppermute | solution.py:435
  7.7 0.1 copy.8.pos_ref
  7.8 1.0 %copy-done = f32[2,4,128,128]{3,2,1,0:T(8,128)S(1)} copy-done((f32[2,4,128,128]{3,2,1,0:T(8,128)S(1)}, f32[2,4,128,128]{3,2,1,0:T(8,128)}, u32[]{:S(2)}) %copy-start) | copy-done | bytes 524312
  8.9 0.9 %copy-done.2 = f32[1,1,3,128,128]{4,3,2,1,0:T(8,128)S(1)} copy-done((f32[1,1,3,128,128]{4,3,2,1,0:T(8,128)S(1)}, f32[1,1,3,128,128]{4,3,2,1,0:T(8,128)}, u32[]{:S(2)}) %copy-start.2) | copy-done | bytes 196632
  9.8 0.9 %copy-done.3 = bf16[4,128,128]{2,1,0:T(8,128)(2,1)S(1)} copy-done((bf16[4,128,128]{2,1,0:T(8,128)(2,1)S(1)}, bf16[4,128,128]{2,1,0:T(8,128)(2,1)}, u32[]{:S(2)}) %copy-start.3) | copy-done | bytes 131096
  10.7 0.1 shard_map.68
  10.8 4.1 %shard_map.69 = (f32[2,264,256]{2,1,0:T(8,128)S(1)}, f32[4,136,128]{2,1,0:T(8,128)S(1)}, f32[4,136,128]{2,1,0:T(8,128)S(1)}, f32[2,128,128]{2,1,0:T(8,128)S(1)},...) custom-call(s32[3,2]{1,0:T(4,128)S(1)} %copy.8.pos_ref, f32[2,128,128]{2,1,0:T(8,128)S(1)} %copy-done.1, ...), custom_call_target="tpu_custom_call" | custom-call | tf_op jit(solution)/shard_map/pallas_call | solution.py:351
  15.0 1.6 %collective-permute-start.6 = (f32[2,2,64,128]{3,2,1,0:T(8,128)S(1)}, f32[2,2,64,128]{3,2,1,0:T(8,128)S(1)}, u32[]{:S(2)}, u32[]{:S(2)}) collective-permute-start(f32[2,2,64,128]{3,2,1,0:T(8,128)S(1)} %get-tuple-element.56), channel_id=1, source_target_pairs={{0,16},{16,0},{1,17},{17,1},{2,18},{18,2},{3,19},{19,3},{4,20},{20... | collective-permute-start | bytes 393224 | tf_op jit(solution)/shard_map/ppermute | solution.py:435
  16.7 1.5 %collective-permute-start.7 = (f32[1,136,128]{2,1,0:T(8,128)S(1)}, f32[1,136,128]{2,1,0:T(8,128)S(1)}, u32[]{:S(2)}, u32[]{:S(2)}) collective-permute-start(f32[1,136,128]{2,1,0:T(8,128)S(1)} %get-tuple-element.94), channel_id=1, source_target_pairs={{0,16},{1,17},{2,18},{3,19},{4,20},{5,21},{6,22},{7,23},{8,24},{9,... | collective-permute-start | bytes 208904 | tf_op jit(solution)/shard_map/ppermute | solution.py:66
  18.2 1.9 %collective-permute-start.9 = (f32[1,136,128]{2,1,0:T(8,128)S(1)}, f32[1,136,128]{2,1,0:T(8,128)S(1)}, u32[]{:S(2)}, u32[]{:S(2)}) collective-permute-start(f32[1,136,128]{2,1,0:T(8,128)S(1)} %get-tuple-element.95), channel_id=1, source_target_pairs={{0,18},{1,19},{2,16},{3,17},{4,22},{5,23},{6,20},{7,21},{8,26},{9,... | collective-permute-start | bytes 208904 | tf_op jit(solution)/shard_map/ppermute | solution.py:66
  20.1 0.1 collective-permute-start.8
  20.3 0.1 broadcast_in_dim.71
  20.4 1.0 %collective-permute-done.6 = f32[2,2,64,128]{3,2,1,0:T(8,128)S(1)} collective-permute-done((f32[2,2,64,128]{3,2,1,0:T(8,128)S(1)}, f32[2,2,64,128]{3,2,1,0:T(8,128)S(1)}, u32[]{:S(2)}, u32[]{:S(2)}) %collective-permute-start.6) | collective-permute-done | bytes 131104 | tf_op jit(solution)/shard_map/ppermute | solution.py:435
  21.4 1.5 %collective-permute-done.7 = f32[1,136,128]{2,1,0:T(8,128)S(1)} collective-permute-done((f32[1,136,128]{2,1,0:T(8,128)S(1)}, f32[1,136,128]{2,1,0:T(8,128)S(1)}, u32[]{:S(2)}, u32[]{:S(2)}) %collective-permute-start.7) | collective-permute-done | bytes 69664 | tf_op jit(solution)/shard_map/ppermute | solution.py:66
  22.9 2.4 %collective-permute-done.9 = f32[1,136,128]{2,1,0:T(8,128)S(1)} collective-permute-done((f32[1,136,128]{2,1,0:T(8,128)S(1)}, f32[1,136,128]{2,1,0:T(8,128)S(1)}, u32[]{:S(2)}, u32[]{:S(2)}) %collective-permute-start.9) | collective-permute-done | bytes 69664 | tf_op jit(solution)/shard_map/ppermute | solution.py:66
  25.3 0.2 collective-permute-done.8
  25.5 3.7 %collective-permute-start.12 = (f32[1,136,128]{2,1,0:T(8,128)S(1)}, f32[1,136,128]{2,1,0:T(8,128)S(1)}, u32[]{:S(2)}, u32[]{:S(2)}) collective-permute-start(f32[1,136,128]{2,1,0:T(8,128)S(1)} %add_add_fusion.3), channel_id=1, source_target_pairs={{0,12},{1,13},{2,14},{3,15},{4,8},{5,9},{6,10},{7,11},{8,4},{9,5},... | collective-permute-start | bytes 208904 | tf_op jit(solution)/shard_map/ppermute | solution.py:66
  29.3 0.7 collective-permute-start.10
  30.0 0.1 fusion.2
  30.1 1.4 %collective-permute-start.14 = (f32[2,128,128]{2,1,0:T(8,128)S(1)}, f32[2,128,128]{2,1,0:T(8,128)S(1)}, u32[]{:S(2)}, u32[]{:S(2)}) collective-permute-start(f32[2,128,128]{2,1,0:T(8,128)S(1)} %get-tuple-element.62.second_ref), channel_id=1, source_target_pairs={{1,2},{17,18},{2,1},{18,17},{3,4},{19,20},{4,3},{20,19},{5,6},{21,... | collective-permute-start | bytes 393224 | tf_op jit(solution)/shard_map/ppermute | solution.py:435
  31.5 0.2 collective-permute-done.12
  31.7 3.0 %collective-permute-done.11 = f32[1,136,128]{2,1,0:T(8,128)S(1)} collective-permute-done((f32[1,136,128]{2,1,0:T(8,128)S(1)}, f32[1,136,128]{2,1,0:T(8,128)S(1)}, u32[]{:S(2)}, u32[]{:S(2)}) %collective-permute-start.11) | collective-permute-done | bytes 69664 | tf_op jit(solution)/shard_map/ppermute | solution.py:66
  34.7 0.4 collective-permute-done.14.rest_1_
  35.1 0.8 collective-permute-start.17
  35.9 2.0 %collective-permute-start.16 = (f32[1,136,128]{2,1,0:T(8,128)S(1)}, f32[1,136,128]{2,1,0:T(8,128)S(1)}, u32[]{:S(2)}, u32[]{:S(2)}) collective-permute-start(f32[1,136,128]{2,1,0:T(8,128)S(1)} %add_add_fusion.2), channel_id=1, source_target_pairs={{0,2},{1,3},{2,0},{3,1},{4,6},{5,7},{6,4},{7,5},{8,10},{9,11},{10,... | collective-permute-start | bytes 208904 | tf_op jit(solution)/shard_map/ppermute | solution.py:66
  37.9 0.7 collective-permute-start.15
  38.7 1.4 %collective-permute-start.18 = (f32[2,2,64,128]{3,2,1,0:T(8,128)S(1)}, f32[2,2,64,128]{3,2,1,0:T(8,128)S(1)}, u32[]{:S(2)}, u32[]{:S(2)}) collective-permute-start(f32[2,2,64,128]{3,2,1,0:T(8,128)S(1)} %pad_maximum_fusion.4), channel_id=1, source_target_pairs={{0,16},{16,0},{1,17},{17,1},{2,18},{18,2},{3,19},{19,3},{4,20},{20... | collective-permute-start | bytes 393224 | tf_op jit(solution)/shard_map/ppermute | solution.py:435
  40.1 0.6 collective-permute-done.17
  40.6 1.3 %collective-permute-done.16 = f32[1,136,128]{2,1,0:T(8,128)S(1)} collective-permute-done((f32[1,136,128]{2,1,0:T(8,128)S(1)}, f32[1,136,128]{2,1,0:T(8,128)S(1)}, u32[]{:S(2)}, u32[]{:S(2)}) %collective-permute-start.16) | collective-permute-done | bytes 69664 | tf_op jit(solution)/shard_map/ppermute | solution.py:66
  41.9 1.1 %collective-permute-done.15 = f32[1,136,128]{2,1,0:T(8,128)S(1)} collective-permute-done((f32[1,136,128]{2,1,0:T(8,128)S(1)}, f32[1,136,128]{2,1,0:T(8,128)S(1)}, u32[]{:S(2)}, u32[]{:S(2)}) %collective-permute-start.15) | collective-permute-done | bytes 69664 | tf_op jit(solution)/shard_map/ppermute | solution.py:66
  43.1 1.7 %collective-permute-done.18.rest_2_ = f32[2,2,64,128]{3,2,1,0:T(8,128)S(1)} collective-permute-done((f32[2,2,64,128]{3,2,1,0:T(8,128)S(1)}, f32[2,2,64,128]{3,2,1,0:T(8,128)S(1)}, u32[]{:S(2)}, u32[]{:S(2)}) %collective-permute-start.18) | collective-permute-done | bytes 131104 | tf_op jit(solution)/shard_map/ppermute | solution.py:435
  44.8 1.6 %collective-permute-done.19.other_ref = f32[4,136,128]{2,1,0:T(8,128)S(1)} collective-permute-done((f32[4,136,128]{2,1,0:T(8,128)S(1)}, f32[4,136,128]{2,1,0:T(8,128)S(1)}, u32[]{:S(2)}, u32[]{:S(2)}) %collective-permute-start.19) | collective-permute-done | bytes 278560 | tf_op jit(solution)/shard_map/ppermute | solution.py:66
  46.3 4.3 %shard_map.70 = (f32[2,128,128]{2,1,0:T(8,128)S(1)}, f32[2,4,128,128]{3,2,1,0:T(8,128)S(1)}, f32[4,136,128]{2,1,0:T(8,128)S(1)}, f32[4,136,128]{2,1,0:T(8,128)S(...) custom-call(s32[3,2]{1,0:T(4,128)S(1)} %copy.8.pos_ref, ...), custom_call_target="tpu_custom_call" | custom-call | tf_op jit(solution)/shard_map/pallas_call | solution.py:351
  50.6 0.2 collective-permute-start.20
  50.8 1.0 %collective-permute-start.21 = (f32[2,2,64,128]{3,2,1,0:T(8,128)S(1)}, f32[2,2,64,128]{3,2,1,0:T(8,128)S(1)}, u32[]{:S(2)}, u32[]{:S(2)}) collective-permute-start(f32[2,2,64,128]{3,2,1,0:T(8,128)S(1)} %get-tuple-element.71), channel_id=1, source_target_pairs={{0,16},{16,0},{1,17},{17,1},{2,18},{18,2},{3,19},{19,3},{4,20},{20... | collective-permute-start | bytes 393224 | tf_op jit(solution)/shard_map/ppermute | solution.py:435
  51.9 0.4 collective-permute-done.20
  52.3 1.1 %collective-permute-start.22 = (f32[1,136,128]{2,1,0:T(8,128)S(1)}, f32[1,136,128]{2,1,0:T(8,128)S(1)}, u32[]{:S(2)}, u32[]{:S(2)}) collective-permute-start(f32[1,136,128]{2,1,0:T(8,128)S(1)} %get-tuple-element.86), channel_id=1, source_target_pairs={{0,16},{1,17},{2,18},{3,19},{4,20},{5,21},{6,22},{7,23},{8,24},{9,... | collective-permute-start | bytes 208904 | tf_op jit(solution)/shard_map/ppermute | solution.py:66
  53.4 1.5 %collective-permute-start.24 = (f32[1,136,128]{2,1,0:T(8,128)S(1)}, f32[1,136,128]{2,1,0:T(8,128)S(1)}, u32[]{:S(2)}, u32[]{:S(2)}) collective-permute-start(f32[1,136,128]{2,1,0:T(8,128)S(1)} %get-tuple-element.87), channel_id=1, source_target_pairs={{0,18},{1,19},{2,16},{3,17},{4,22},{5,23},{6,20},{7,21},{8,26},{9,... | collective-permute-start | bytes 208904 | tf_op jit(solution)/shard_map/ppermute | solution.py:66
  54.9 1.0 %collective-permute-start.23 = (f32[1,136,128]{2,1,0:T(8,128)S(1)}, f32[1,136,128]{2,1,0:T(8,128)S(1)}, u32[]{:S(2)}, u32[]{:S(2)}) collective-permute-start(f32[1,136,128]{2,1,0:T(8,128)S(1)} %get-tuple-element.88), channel_id=1, source_target_pairs={{0,2},{1,3},{2,0},{3,1},{4,6},{5,7},{6,4},{7,5},{8,10},{9,11},{10,... | collective-permute-start | bytes 208904 | tf_op jit(solution)/shard_map/ppermute | solution.py:66
  55.9 1.3 %collective-permute-done.21 = f32[2,2,64,128]{3,2,1,0:T(8,128)S(1)} collective-permute-done((f32[2,2,64,128]{3,2,1,0:T(8,128)S(1)}, f32[2,2,64,128]{3,2,1,0:T(8,128)S(1)}, u32[]{:S(2)}, u32[]{:S(2)}) %collective-permute-start.21) | collective-permute-done | bytes 131104 | tf_op jit(solution)/shard_map/ppermute | solution.py:435
  57.2 1.5 %collective-permute-done.22 = f32[1,136,128]{2,1,0:T(8,128)S(1)} collective-permute-done((f32[1,136,128]{2,1,0:T(8,128)S(1)}, f32[1,136,128]{2,1,0:T(8,128)S(1)}, u32[]{:S(2)}, u32[]{:S(2)}) %collective-permute-start.22) | collective-permute-done | bytes 69664 | tf_op jit(solution)/shard_map/ppermute | solution.py:66
  58.7 1.5 %collective-permute-done.24 = f32[1,136,128]{2,1,0:T(8,128)S(1)} collective-permute-done((f32[1,136,128]{2,1,0:T(8,128)S(1)}, f32[1,136,128]{2,1,0:T(8,128)S(1)}, u32[]{:S(2)}, u32[]{:S(2)}) %collective-permute-start.24) | collective-permute-done | bytes 69664 | tf_op jit(solution)/shard_map/ppermute | solution.py:66
  60.2 0.3 collective-permute-done.23
  60.5 2.3 %collective-permute-start.27 = (f32[1,136,128]{2,1,0:T(8,128)S(1)}, f32[1,136,128]{2,1,0:T(8,128)S(1)}, u32[]{:S(2)}, u32[]{:S(2)}) collective-permute-start(f32[1,136,128]{2,1,0:T(8,128)S(1)} %add_add_fusion.1), channel_id=1, source_target_pairs={{0,12},{1,13},{2,14},{3,15},{4,8},{5,9},{6,10},{7,11},{8,4},{9,5},... | collective-permute-start | bytes 208904 | tf_op jit(solution)/shard_map/ppermute | solution.py:66
  62.8 1.0 %collective-permute-start.26 = (f32[1,136,128]{2,1,0:T(8,128)S(1)}, f32[1,136,128]{2,1,0:T(8,128)S(1)}, u32[]{:S(2)}, u32[]{:S(2)}) collective-permute-start(f32[1,136,128]{2,1,0:T(8,128)S(1)} %add_add_fusion.1), channel_id=1, source_target_pairs={{0,8},{1,9},{2,10},{3,11},{4,12},{5,13},{6,14},{7,15},{8,0},{9,1},... | collective-permute-start | bytes 208904 | tf_op jit(solution)/shard_map/ppermute | solution.py:66
  63.8 1.2 %collective-permute-start.25 = (f32[1,136,128]{2,1,0:T(8,128)S(1)}, f32[1,136,128]{2,1,0:T(8,128)S(1)}, u32[]{:S(2)}, u32[]{:S(2)}) collective-permute-start(f32[1,136,128]{2,1,0:T(8,128)S(1)} %add_add_fusion.1), channel_id=1, source_target_pairs={{0,4},{1,5},{2,6},{3,7},{4,0},{5,1},{6,2},{7,3},{8,12},{9,13},{10,... | collective-permute-start | bytes 208904 | tf_op jit(solution)/shard_map/ppermute | solution.py:66
  65.0 0.1 fusion
  65.1 1.3 %collective-permute-start.29 = (f32[2,128,128]{2,1,0:T(8,128)S(1)}, f32[2,128,128]{2,1,0:T(8,128)S(1)}, u32[]{:S(2)}, u32[]{:S(2)}) collective-permute-start(f32[2,128,128]{2,1,0:T(8,128)S(1)} %get-tuple-element.77.second_ref), channel_id=1, source_target_pairs={{1,2},{17,18},{2,1},{18,17},{3,4},{19,20},{4,3},{20,19},{5,6},{21,... | collective-permute-start | bytes 393224 | tf_op jit(solution)/shard_map/ppermute | solution.py:435
  66.4 1.1 %collective-permute-done.27 = f32[1,136,128]{2,1,0:T(8,128)S(1)} collective-permute-done((f32[1,136,128]{2,1,0:T(8,128)S(1)}, f32[1,136,128]{2,1,0:T(8,128)S(1)}, u32[]{:S(2)}, u32[]{:S(2)}) %collective-permute-start.27) | collective-permute-done | bytes 69664 | tf_op jit(solution)/shard_map/ppermute | solution.py:66
  67.5 2.3 %collective-permute-done.26 = f32[1,136,128]{2,1,0:T(8,128)S(1)} collective-permute-done((f32[1,136,128]{2,1,0:T(8,128)S(1)}, f32[1,136,128]{2,1,0:T(8,128)S(1)}, u32[]{:S(2)}, u32[]{:S(2)}) %collective-permute-start.26) | collective-permute-done | bytes 69664 | tf_op jit(solution)/shard_map/ppermute | solution.py:66
  69.8 0.3 collective-permute-done.29.rest_1_
  70.1 1.3 %collective-permute-start.32 = (f32[1,136,128]{2,1,0:T(8,128)S(1)}, f32[1,136,128]{2,1,0:T(8,128)S(1)}, u32[]{:S(2)}, u32[]{:S(2)}) collective-permute-start(f32[1,136,128]{2,1,0:T(8,128)S(1)} %add_add_fusion), channel_id=1, source_target_pairs={{0,18},{1,19},{2,16},{3,17},{4,22},{5,23},{6,20},{7,21},{8,26},{9,... | collective-permute-start | bytes 208904 | tf_op jit(solution)/shard_map/ppermute | solution.py:66
  71.4 1.4 %collective-permute-start.31 = (f32[1,136,128]{2,1,0:T(8,128)S(1)}, f32[1,136,128]{2,1,0:T(8,128)S(1)}, u32[]{:S(2)}, u32[]{:S(2)}) collective-permute-start(f32[1,136,128]{2,1,0:T(8,128)S(1)} %add_add_fusion), channel_id=1, source_target_pairs={{0,2},{1,3},{2,0},{3,1},{4,6},{5,7},{6,4},{7,5},{8,10},{9,11},{10,... | collective-permute-start | bytes 208904 | tf_op jit(solution)/shard_map/ppermute | solution.py:66
  72.8 0.8 collective-permute-start.30
  73.6 1.8 %collective-permute-done.32 = f32[1,136,128]{2,1,0:T(8,128)S(1)} collective-permute-done((f32[1,136,128]{2,1,0:T(8,128)S(1)}, f32[1,136,128]{2,1,0:T(8,128)S(1)}, u32[]{:S(2)}, u32[]{:S(2)}) %collective-permute-start.32) | collective-permute-done | bytes 69664 | tf_op jit(solution)/shard_map/ppermute | solution.py:66
  75.4 1.4 %collective-permute-done.31 = f32[1,136,128]{2,1,0:T(8,128)S(1)} collective-permute-done((f32[1,136,128]{2,1,0:T(8,128)S(1)}, f32[1,136,128]{2,1,0:T(8,128)S(1)}, u32[]{:S(2)}, u32[]{:S(2)}) %collective-permute-start.31) | collective-permute-done | bytes 69664 | tf_op jit(solution)/shard_map/ppermute | solution.py:66
  76.8 0.3 collective-permute-done.30
  77.3 1.5 %collective-permute-done.33.other_ref = f32[4,136,128]{2,1,0:T(8,128)S(1)} collective-permute-done((f32[4,136,128]{2,1,0:T(8,128)S(1)}, f32[4,136,128]{2,1,0:T(8,128)S(1)}, u32[]{:S(2)}, u32[]{:S(2)}) %collective-permute-start.33) | collective-permute-done | bytes 278560 | tf_op jit(solution)/shard_map/ppermute | solution.py:66
  78.8 1.0 %shard_map.71 = (f32[2,128,128]{2,1,0:T(8,128)}, f32[2,4,128,128]{3,2,1,0:T(8,128)}) custom-call(f32[2,128,128]{2,1,0:T(8,128)S(1)} %get-tuple-element.68.tile_ref, f32[2,128,128]{2,1,0:T(8,128)S(1)} %get-tuple-element.76.first_ref, f32[2,128,128]{2,1,0:T(8,128)S(1)} %get-tuple-element.77.second_ref, f32[2,4,128,128]{3,2,1,0:T(8,128)S(1)} %get-tuple-element.78.probe_ref, ...), custom_call_target="tpu_custom_call" | custom-call | tf_op jit(solution)/shard_map/pallas_call | solution.py:351
  (43 shorter events, 0.8 us)
Async XLA Ops:
  0.6 3.9 %copy-start.1 = (f32[2,128,128]{2,1,0:T(8,128)S(1)}, f32[2,128,128]{2,1,0:T(8,128)}, u32[]{:S(2)}) copy-start(f32[2,128,128]{2,1,0:T(8,128)} %obj_ref.1) | copy-start | bytes 393220
  1.5 6.2 %copy-start.4 = (s32[1,1,3,2]{2,3,1,0:T(2,128)S(1)}, s32[1,1,3,2]{2,3,1,0:T(2,128)}, u32[]{:S(2)}) copy-start(s32[1,1,3,2]{2,3,1,0:T(2,128)} %param.8) | copy-start | bytes 76
  1.6 5.2 %collective-permute-start.2 = (f32[2,64,128]{2,1,0:T(8,128)S(1)}, f32[2,64,128]{2,1,0:T(8,128)S(1)}, u32[]{:S(2)}, u32[]{:S(2)}) collective-permute-start(f32[2,64,128]{2,1,0:T(8,128)S(1)} %constant_dynamic-slice_fusion.8), channel_id=1, source_target_pairs={{0,16},{16,0},{1,17},{17,1},{2,18},{18,2},{3,19},{19,3},{4,20},{20... | collective-permute-start | bytes 196616 | tf_op jit(solution)/shard_map/ppermute | solution.py:435
  4.5 6.3 %collective-permute-start.1 = (f32[2,128,128]{2,1,0:T(8,128)S(1)}, f32[2,128,128]{2,1,0:T(8,128)S(1)}, u32[]{:S(2)}, u32[]{:S(2)}) collective-permute-start(f32[2,128,128]{2,1,0:T(8,128)S(1)} %copy-done.1), channel_id=1, source_target_pairs={{1,2},{17,18},{2,1},{18,17},{3,4},{19,20},{4,3},{20,19},{5,6},{21,... | collective-permute-start | bytes 393224 | tf_op jit(solution)/shard_map/ppermute | solution.py:435
  4.6 6.3 %collective-permute-start = (f32[2,128,128]{2,1,0:T(8,128)S(1)}, f32[2,128,128]{2,1,0:T(8,128)S(1)}, u32[]{:S(2)}, u32[]{:S(2)}) collective-permute-start(f32[2,128,128]{2,1,0:T(8,128)S(1)} %copy-done.1), channel_id=1, source_target_pairs={{0,1},{16,17},{1,0},{17,16},{2,3},{18,19},{3,2},{19,18},{4,5},{20,... | collective-permute-start | bytes 393224 | tf_op jit(solution)/shard_map/ppermute | solution.py:435
  6.1 4.7 %collective-permute-start.4 = (f32[2,64,128]{2,1,0:T(8,128)S(1)}, f32[2,64,128]{2,1,0:T(8,128)S(1)}, u32[]{:S(2)}, u32[]{:S(2)}) collective-permute-start(f32[2,64,128]{2,1,0:T(8,128)S(1)} %constant_dynamic-slice_fusion.8), channel_id=1, source_target_pairs={{1,18},{17,2},{2,17},{18,1},{3,20},{19,4},{4,19},{20,3},{5,22},{21... | collective-permute-start | bytes 196616 | tf_op jit(solution)/shard_map/ppermute | solution.py:435
  6.7 4.1 %collective-permute-start.3 = (f32[2,64,128]{2,1,0:T(8,128)S(1)}, f32[2,64,128]{2,1,0:T(8,128)S(1)}, u32[]{:S(2)}, u32[]{:S(2)}) collective-permute-start(f32[2,64,128]{2,1,0:T(8,128)S(1)} %collective-permute-done.2.rest_0_), channel_id=1, source_target_pairs={{0,1},{16,17},{1,0},{17,16},{2,3},{18,19},{3,2},{19,18},{4,5},{20,... | collective-permute-start | bytes 196616 | tf_op jit(solution)/shard_map/ppermute | solution.py:435
  7.8 1.0 %copy-start = (f32[2,4,128,128]{3,2,1,0:T(8,128)S(1)}, f32[2,4,128,128]{3,2,1,0:T(8,128)}, u32[]{:S(2)}) copy-start(f32[2,4,128,128]{3,2,1,0:T(8,128)} %probe_ref.1) | copy-start | bytes 1572868
  8.9 0.9 %copy-start.2 = (f32[1,1,3,128,128]{4,3,2,1,0:T(8,128)S(1)}, f32[1,1,3,128,128]{4,3,2,1,0:T(8,128)}, u32[]{:S(2)}) copy-start(f32[1,1,3,128,128]{4,3,2,1,0:T(8,128)} %param.7) | copy-start | bytes 589828
  9.8 0.9 %copy-start.3 = (bf16[4,128,128]{2,1,0:T(8,128)(2,1)S(1)}, bf16[4,128,128]{2,1,0:T(8,128)(2,1)}, u32[]{:S(2)}) copy-start(bf16[4,128,128]{2,1,0:T(8,128)(2,1)} %constant.74.clone.table_ref) | copy-start | bytes 393220
  14.9 1.7 %collective-permute-start.5 = (f32[4,136,128]{2,1,0:T(8,128)S(1)}, f32[4,136,128]{2,1,0:T(8,128)S(1)}, u32[]{:S(2)}, u32[]{:S(2)}) collective-permute-start(f32[4,136,128]{2,1,0:T(8,128)S(1)} %get-tuple-element.55), channel_id=1, source_target_pairs={{0,1},{1,0},{2,3},{3,2},{4,5},{5,4},{6,7},{7,6},{8,9},{9,8},{10,11... | collective-permute-start | bytes 835592 | tf_op jit(solution)/shard_map/ppermute | solution.py:66
  15.0 6.4 %collective-permute-start.6 = (f32[2,2,64,128]{3,2,1,0:T(8,128)S(1)}, f32[2,2,64,128]{3,2,1,0:T(8,128)S(1)}, u32[]{:S(2)}, u32[]{:S(2)}) collective-permute-start(f32[2,2,64,128]{3,2,1,0:T(8,128)S(1)} %get-tuple-element.56), channel_id=1, source_target_pairs={{0,16},{16,0},{1,17},{17,1},{2,18},{18,2},{3,19},{19,3},{4,20},{20... | collective-permute-start | bytes 393224 | tf_op jit(solution)/shard_map/ppermute | solution.py:435
  16.7 6.2 %collective-permute-start.7 = (f32[1,136,128]{2,1,0:T(8,128)S(1)}, f32[1,136,128]{2,1,0:T(8,128)S(1)}, u32[]{:S(2)}, u32[]{:S(2)}) collective-permute-start(f32[1,136,128]{2,1,0:T(8,128)S(1)} %get-tuple-element.94), channel_id=1, source_target_pairs={{0,16},{1,17},{2,18},{3,19},{4,20},{5,21},{6,22},{7,23},{8,24},{9,... | collective-permute-start | bytes 208904 | tf_op jit(solution)/shard_map/ppermute | solution.py:66
  18.2 7.2 %collective-permute-start.9 = (f32[1,136,128]{2,1,0:T(8,128)S(1)}, f32[1,136,128]{2,1,0:T(8,128)S(1)}, u32[]{:S(2)}, u32[]{:S(2)}) collective-permute-start(f32[1,136,128]{2,1,0:T(8,128)S(1)} %get-tuple-element.95), channel_id=1, source_target_pairs={{0,18},{1,19},{2,16},{3,17},{4,22},{5,23},{6,20},{7,21},{8,26},{9,... | collective-permute-start | bytes 208904 | tf_op jit(solution)/shard_map/ppermute | solution.py:66
  20.1 5.4 %collective-permute-start.8 = (f32[1,136,128]{2,1,0:T(8,128)S(1)}, f32[1,136,128]{2,1,0:T(8,128)S(1)}, u32[]{:S(2)}, u32[]{:S(2)}) collective-permute-start(f32[1,136,128]{2,1,0:T(8,128)S(1)} %get-tuple-element.96), channel_id=1, source_target_pairs={{0,2},{1,3},{2,0},{3,1},{4,6},{5,7},{6,4},{7,5},{8,10},{9,11},{10,... | collective-permute-start | bytes 208904 | tf_op jit(solution)/shard_map/ppermute | solution.py:66
  25.5 6.2 %collective-permute-start.12 = (f32[1,136,128]{2,1,0:T(8,128)S(1)}, f32[1,136,128]{2,1,0:T(8,128)S(1)}, u32[]{:S(2)}, u32[]{:S(2)}) collective-permute-start(f32[1,136,128]{2,1,0:T(8,128)S(1)} %add_add_fusion.3), channel_id=1, source_target_pairs={{0,12},{1,13},{2,14},{3,15},{4,8},{5,9},{6,10},{7,11},{8,4},{9,5},... | collective-permute-start | bytes 208904 | tf_op jit(solution)/shard_map/ppermute | solution.py:66
  29.3 5.4 %collective-permute-start.11 = (f32[1,136,128]{2,1,0:T(8,128)S(1)}, f32[1,136,128]{2,1,0:T(8,128)S(1)}, u32[]{:S(2)}, u32[]{:S(2)}) collective-permute-start(f32[1,136,128]{2,1,0:T(8,128)S(1)} %add_add_fusion.3), channel_id=1, source_target_pairs={{0,8},{1,9},{2,10},{3,11},{4,12},{5,13},{6,14},{7,15},{8,0},{9,1},... | collective-permute-start | bytes 208904 | tf_op jit(solution)/shard_map/ppermute | solution.py:66
  29.3 5.4 %collective-permute-start.10 = (f32[1,136,128]{2,1,0:T(8,128)S(1)}, f32[1,136,128]{2,1,0:T(8,128)S(1)}, u32[]{:S(2)}, u32[]{:S(2)}) collective-permute-start(f32[1,136,128]{2,1,0:T(8,128)S(1)} %add_add_fusion.3), channel_id=1, source_target_pairs={{0,4},{1,5},{2,6},{3,7},{4,0},{5,1},{6,2},{7,3},{8,12},{9,13},{10,... | collective-permute-start | bytes 208904 | tf_op jit(solution)/shard_map/ppermute | solution.py:66
  30.1 5.0 %collective-permute-start.14 = (f32[2,128,128]{2,1,0:T(8,128)S(1)}, f32[2,128,128]{2,1,0:T(8,128)S(1)}, u32[]{:S(2)}, u32[]{:S(2)}) collective-permute-start(f32[2,128,128]{2,1,0:T(8,128)S(1)} %get-tuple-element.62.second_ref), channel_id=1, source_target_pairs={{1,2},{17,18},{2,1},{18,17},{3,4},{19,20},{4,3},{20,19},{5,6},{21,... | collective-permute-start | bytes 393224 | tf_op jit(solution)/shard_map/ppermute | solution.py:435
  31.5 3.7 %collective-permute-start.13 = (f32[2,128,128]{2,1,0:T(8,128)S(1)}, f32[2,128,128]{2,1,0:T(8,128)S(1)}, u32[]{:S(2)}, u32[]{:S(2)}) collective-permute-start(f32[2,128,128]{2,1,0:T(8,128)S(1)} %get-tuple-element.61.first_ref), channel_id=1, source_target_pairs={{0,1},{16,17},{1,0},{17,16},{2,3},{18,19},{3,2},{19,18},{4,5},{20,... | collective-permute-start | bytes 393224 | tf_op jit(solution)/shard_map/ppermute | solution.py:435
  35.1 5.5 %collective-permute-start.17 = (f32[1,136,128]{2,1,0:T(8,128)S(1)}, f32[1,136,128]{2,1,0:T(8,128)S(1)}, u32[]{:S(2)}, u32[]{:S(2)}) collective-permute-start(f32[1,136,128]{2,1,0:T(8,128)S(1)} %add_add_fusion.2), channel_id=1, source_target_pairs={{0,18},{1,19},{2,16},{3,17},{4,22},{5,23},{6,20},{7,21},{8,26},{9,... | collective-permute-start | bytes 208904 | tf_op jit(solution)/shard_map/ppermute | solution.py:66
  35.9 6.0 %collective-permute-start.16 = (f32[1,136,128]{2,1,0:T(8,128)S(1)}, f32[1,136,128]{2,1,0:T(8,128)S(1)}, u32[]{:S(2)}, u32[]{:S(2)}) collective-permute-start(f32[1,136,128]{2,1,0:T(8,128)S(1)} %add_add_fusion.2), channel_id=1, source_target_pairs={{0,2},{1,3},{2,0},{3,1},{4,6},{5,7},{6,4},{7,5},{8,10},{9,11},{10,... | collective-permute-start | bytes 208904 | tf_op jit(solution)/shard_map/ppermute | solution.py:66
  37.9 5.1 %collective-permute-start.15 = (f32[1,136,128]{2,1,0:T(8,128)S(1)}, f32[1,136,128]{2,1,0:T(8,128)S(1)}, u32[]{:S(2)}, u32[]{:S(2)}) collective-permute-start(f32[1,136,128]{2,1,0:T(8,128)S(1)} %add_add_fusion.2), channel_id=1, source_target_pairs={{0,16},{1,17},{2,18},{3,19},{4,20},{5,21},{6,22},{7,23},{8,24},{9,... | collective-permute-start | bytes 208904 | tf_op jit(solution)/shard_map/ppermute | solution.py:66
  38.7 6.1 %collective-permute-start.18 = (f32[2,2,64,128]{3,2,1,0:T(8,128)S(1)}, f32[2,2,64,128]{3,2,1,0:T(8,128)S(1)}, u32[]{:S(2)}, u32[]{:S(2)}) collective-permute-start(f32[2,2,64,128]{3,2,1,0:T(8,128)S(1)} %pad_maximum_fusion.4), channel_id=1, source_target_pairs={{0,16},{16,0},{1,17},{17,1},{2,18},{18,2},{3,19},{19,3},{4,20},{20... | collective-permute-start | bytes 393224 | tf_op jit(solution)/shard_map/ppermute | solution.py:435
  44.8 1.6 %collective-permute-start.19 = (f32[4,136,128]{2,1,0:T(8,128)S(1)}, f32[4,136,128]{2,1,0:T(8,128)S(1)}, u32[]{:S(2)}, u32[]{:S(2)}) collective-permute-start(f32[4,136,128]{2,1,0:T(8,128)S(1)} %pad_maximum_fusion.1.own_ref), channel_id=1, source_target_pairs={{0,1},{1,0},{2,3},{3,2},{4,5},{5,4},{6,7},{7,6},{8,9},{9,8},{10,11... | collective-permute-start | bytes 835592 | tf_op jit(solution)/shard_map/ppermute | solution.py:66
  50.6 1.6 %collective-permute-start.20 = (f32[4,136,128]{2,1,0:T(8,128)S(1)}, f32[4,136,128]{2,1,0:T(8,128)S(1)}, u32[]{:S(2)}, u32[]{:S(2)}) collective-permute-start(f32[4,136,128]{2,1,0:T(8,128)S(1)} %get-tuple-element.70), channel_id=1, source_target_pairs={{0,1},{1,0},{2,3},{3,2},{4,5},{5,4},{6,7},{7,6},{8,9},{9,8},{10,11... | collective-permute-start | bytes 835592 | tf_op jit(solution)/shard_map/ppermute | solution.py:66
  50.8 6.3 %collective-permute-start.21 = (f32[2,2,64,128]{3,2,1,0:T(8,128)S(1)}, f32[2,2,64,128]{3,2,1,0:T(8,128)S(1)}, u32[]{:S(2)}, u32[]{:S(2)}) collective-permute-start(f32[2,2,64,128]{3,2,1,0:T(8,128)S(1)} %get-tuple-element.71), channel_id=1, source_target_pairs={{0,16},{16,0},{1,17},{17,1},{2,18},{18,2},{3,19},{19,3},{4,20},{20... | collective-permute-start | bytes 393224 | tf_op jit(solution)/shard_map/ppermute | solution.py:435
  52.3 6.3 %collective-permute-start.22 = (f32[1,136,128]{2,1,0:T(8,128)S(1)}, f32[1,136,128]{2,1,0:T(8,128)S(1)}, u32[]{:S(2)}, u32[]{:S(2)}) collective-permute-start(f32[1,136,128]{2,1,0:T(8,128)S(1)} %get-tuple-element.86), channel_id=1, source_target_pairs={{0,16},{1,17},{2,18},{3,19},{4,20},{5,21},{6,22},{7,23},{8,24},{9,... | collective-permute-start | bytes 208904 | tf_op jit(solution)/shard_map/ppermute | solution.py:66
  53.4 6.8 %collective-permute-start.24 = (f32[1,136,128]{2,1,0:T(8,128)S(1)}, f32[1,136,128]{2,1,0:T(8,128)S(1)}, u32[]{:S(2)}, u32[]{:S(2)}) collective-permute-start(f32[1,136,128]{2,1,0:T(8,128)S(1)} %get-tuple-element.87), channel_id=1, source_target_pairs={{0,18},{1,19},{2,16},{3,17},{4,22},{5,23},{6,20},{7,21},{8,26},{9,... | collective-permute-start | bytes 208904 | tf_op jit(solution)/shard_map/ppermute | solution.py:66
  54.9 5.6 %collective-permute-start.23 = (f32[1,136,128]{2,1,0:T(8,128)S(1)}, f32[1,136,128]{2,1,0:T(8,128)S(1)}, u32[]{:S(2)}, u32[]{:S(2)}) collective-permute-start(f32[1,136,128]{2,1,0:T(8,128)S(1)} %get-tuple-element.88), channel_id=1, source_target_pairs={{0,2},{1,3},{2,0},{3,1},{4,6},{5,7},{6,4},{7,5},{8,10},{9,11},{10,... | collective-permute-start | bytes 208904 | tf_op jit(solution)/shard_map/ppermute | solution.py:66
  60.5 7.0 %collective-permute-start.27 = (f32[1,136,128]{2,1,0:T(8,128)S(1)}, f32[1,136,128]{2,1,0:T(8,128)S(1)}, u32[]{:S(2)}, u32[]{:S(2)}) collective-permute-start(f32[1,136,128]{2,1,0:T(8,128)S(1)} %add_add_fusion.1), channel_id=1, source_target_pairs={{0,12},{1,13},{2,14},{3,15},{4,8},{5,9},{6,10},{7,11},{8,4},{9,5},... | collective-permute-start | bytes 208904 | tf_op jit(solution)/shard_map/ppermute | solution.py:66
  62.8 6.9 %collective-permute-start.26 = (f32[1,136,128]{2,1,0:T(8,128)S(1)}, f32[1,136,128]{2,1,0:T(8,128)S(1)}, u32[]{:S(2)}, u32[]{:S(2)}) collective-permute-start(f32[1,136,128]{2,1,0:T(8,128)S(1)} %add_add_fusion.1), channel_id=1, source_target_pairs={{0,8},{1,9},{2,10},{3,11},{4,12},{5,13},{6,14},{7,15},{8,0},{9,1},... | collective-permute-start | bytes 208904 | tf_op jit(solution)/shard_map/ppermute | solution.py:66
  63.8 6.0 %collective-permute-start.25 = (f32[1,136,128]{2,1,0:T(8,128)S(1)}, f32[1,136,128]{2,1,0:T(8,128)S(1)}, u32[]{:S(2)}, u32[]{:S(2)}) collective-permute-start(f32[1,136,128]{2,1,0:T(8,128)S(1)} %add_add_fusion.1), channel_id=1, source_target_pairs={{0,4},{1,5},{2,6},{3,7},{4,0},{5,1},{6,2},{7,3},{8,12},{9,13},{10,... | collective-permute-start | bytes 208904 | tf_op jit(solution)/shard_map/ppermute | solution.py:66
  65.1 5.0 %collective-permute-start.29 = (f32[2,128,128]{2,1,0:T(8,128)S(1)}, f32[2,128,128]{2,1,0:T(8,128)S(1)}, u32[]{:S(2)}, u32[]{:S(2)}) collective-permute-start(f32[2,128,128]{2,1,0:T(8,128)S(1)} %get-tuple-element.77.second_ref), channel_id=1, source_target_pairs={{1,2},{17,18},{2,1},{18,17},{3,4},{19,20},{4,3},{20,19},{5,6},{21,... | collective-permute-start | bytes 393224 | tf_op jit(solution)/shard_map/ppermute | solution.py:435
  66.4 3.7 %collective-permute-start.28 = (f32[2,128,128]{2,1,0:T(8,128)S(1)}, f32[2,128,128]{2,1,0:T(8,128)S(1)}, u32[]{:S(2)}, u32[]{:S(2)}) collective-permute-start(f32[2,128,128]{2,1,0:T(8,128)S(1)} %get-tuple-element.76.first_ref), channel_id=1, source_target_pairs={{0,1},{16,17},{1,0},{17,16},{2,3},{18,19},{3,2},{19,18},{4,5},{20,... | collective-permute-start | bytes 393224 | tf_op jit(solution)/shard_map/ppermute | solution.py:435
  70.1 5.3 %collective-permute-start.32 = (f32[1,136,128]{2,1,0:T(8,128)S(1)}, f32[1,136,128]{2,1,0:T(8,128)S(1)}, u32[]{:S(2)}, u32[]{:S(2)}) collective-permute-start(f32[1,136,128]{2,1,0:T(8,128)S(1)} %add_add_fusion), channel_id=1, source_target_pairs={{0,18},{1,19},{2,16},{3,17},{4,22},{5,23},{6,20},{7,21},{8,26},{9,... | collective-permute-start | bytes 208904 | tf_op jit(solution)/shard_map/ppermute | solution.py:66
  71.4 5.4 %collective-permute-start.31 = (f32[1,136,128]{2,1,0:T(8,128)S(1)}, f32[1,136,128]{2,1,0:T(8,128)S(1)}, u32[]{:S(2)}, u32[]{:S(2)}) collective-permute-start(f32[1,136,128]{2,1,0:T(8,128)S(1)} %add_add_fusion), channel_id=1, source_target_pairs={{0,2},{1,3},{2,0},{3,1},{4,6},{5,7},{6,4},{7,5},{8,10},{9,11},{10,... | collective-permute-start | bytes 208904 | tf_op jit(solution)/shard_map/ppermute | solution.py:66
  72.8 4.3 %collective-permute-start.30 = (f32[1,136,128]{2,1,0:T(8,128)S(1)}, f32[1,136,128]{2,1,0:T(8,128)S(1)}, u32[]{:S(2)}, u32[]{:S(2)}) collective-permute-start(f32[1,136,128]{2,1,0:T(8,128)S(1)} %add_add_fusion), channel_id=1, source_target_pairs={{0,16},{1,17},{2,18},{3,19},{4,20},{5,21},{6,22},{7,23},{8,24},{9,... | collective-permute-start | bytes 208904 | tf_op jit(solution)/shard_map/ppermute | solution.py:66
  77.2 1.6 %collective-permute-start.33 = (f32[4,136,128]{2,1,0:T(8,128)S(1)}, f32[4,136,128]{2,1,0:T(8,128)S(1)}, u32[]{:S(2)}, u32[]{:S(2)}) collective-permute-start(f32[4,136,128]{2,1,0:T(8,128)S(1)} %pad_maximum_fusion.3.own_ref), channel_id=1, source_target_pairs={{0,1},{1,0},{2,3},{3,2},{4,5},{5,4},{6,7},{7,6},{8,9},{9,8},{10,11... | collective-permute-start | bytes 835592 | tf_op jit(solution)/shard_map/ppermute | solution.py:66

commit v5 on v4

--- a/solution.py
+++ b/solution.py
@@ -362,12 +362,18 @@
     return (me >> bit) & 1
 
 
-def masks_of(bits):
-    return [sum(((m >> i) & 1) << b for i, b in enumerate(bits)) for m in range(1, 1 << len(bits))]
+def mask_of(bits, m):
+    return sum(((m >> i) & 1) << b for i, b in enumerate(bits))
+
+
+def swap_over(x, bits, m, total):
+    masks = [mask_of(b, m) for b in bits]
+    return lax.ppermute(x, AXES, [(i, i ^ masks[i & 1]) for i in range(total)])
 
 
 def local_index(me, bits):
-    return sum(bit_of(me, b) << i for i, b in enumerate(bits))
+    even, odd = (sum(bit_of(me, b) << i for i, b in enumerate(side)) for side in bits)
+    return even if bits[0] == bits[1] else jnp.where(me & 1 == 0, even, odd)
 
 
 def tree(values):
@@ -378,47 +384,54 @@
 
 def scatter_sum(x, me, bits, total, beside):
     here = local_index(me, bits)
-    n = 1 << len(bits)
+    n = 1 << len(bits[0])
     x = x.reshape((n, x.shape[0] // n) + x.shape[1:])
     parts = [lax.dynamic_index_in_dim(x, here, 0, False)]
-    for m, mask in enumerate(masks_of(bits), 1):
-        parts.append(xor_permute(lax.dynamic_index_in_dim(x, here ^ m, 0, False), mask, total))
+    for m in range(1, n):
+        part = lax.dynamic_index_in_dim(x, here ^ m, 0, False)
+        parts.append(swap_over(part, bits, m, total))
     parts[0], beside = lax.optimization_barrier((parts[0], beside))
     return tree(parts), beside
 
 
-def direct_sum(x, bits, total, beside):
-    parts = [xor_permute(x, mask, total) for mask in masks_of(bits)]
+def direct_sum(x, bits, total):
+    return tree([x] + [swap_over(x, bits, m, total) for m in range(1, 1 << len(bits[0]))])
+
+
+def gather(x, me, bits, total, beside):
+    here = local_index(me, bits)
+    n = 1 << len(bits[0])
+    parts = [swap_over(x, bits, m, total) for m in range(1, n)]
     x, beside = lax.optimization_barrier((x, beside))
-    return tree([x] + parts), beside
-
-
-def gather(x, me, bits, total):
-    here = local_index(me, bits)
-    parts = jnp.stack([x] + [xor_permute(x, mask, total) for mask in masks_of(bits)])
-    return jnp.concatenate(
-        [lax.dynamic_index_in_dim(parts, here ^ j, 0, False) for j in range(1 << len(bits))]
-    )
+    parts = jnp.stack([x] + parts)
+    whole = [lax.dynamic_index_in_dim(parts, here ^ j, 0, False) for j in range(n)]
+    return jnp.concatenate(whole), beside
+
+
+def stages_of(n_ty, n_tx):
+    levels, tx_bits = (n_ty * n_tx).bit_length() - 1, n_tx.bit_length() - 1
+    near = tuple(b for b in dict.fromkeys((tx_bits, 1)) if b < levels)
+    rest = [b for b in range(1, levels) if b not in near]
+    far = tuple(rest[:2])
+    if len(near) == len(far):
+        return (near, far), [(far, near)] + [((b,), (b,)) for b in rest[2:]]
+    return (near, near), [((b,), (b,)) for b in rest]
 
 
 def summed_halves(keep, send, n_ty, n_tx, steps):
     total = n_ty * n_tx
     me = lax.axis_index("ty") * n_tx + lax.axis_index("tx")
-    levels = total.bit_length() - 1
-    tx_bits = n_tx.bit_length() - 1
-    bits = [b for b in (tx_bits, 1) if b < levels]
-    rest = [b for b in range(1, levels) if b not in bits]
+    bits, summed = stages_of(n_ty, n_tx)
     half = keep + xor_permute(send, 1, total)
     done = [steps[0]()]
     half, done[0] = scatter_sum(half, me, bits, total, done[0])
     done.append(steps[1](*done))
-    for i in range(0, len(rest), 2):
-        half, _ = direct_sum(half, rest[i : i + 2], total, ())
-    half, done[1] = lax.optimization_barrier((half, done[1]))
-    done += [step(*done) for step in steps[2:]]
-    half = gather(half, me, bits, total)
+    for pair in summed:
+        half = direct_sum(half, pair, total)
     if steps[2:]:
-        half, done[2] = lax.optimization_barrier((half, done[2]))
+        half, done[1] = lax.optimization_barrier((half, done[1]))
+        done += [step(*done) for step in steps[2:]]
+    half, done[-1] = gather(half, me, bits, total, done[-1])
     return half, xor_permute(half, 1, total), done
 
 

time: 80.1 us -> 76 us (0.949)
  waiting for transfers between devices: 28.8 us -> 23.5 us
  starting transfers between devices: 36.1 us -> 37.4 us
    ppermute x0 -> x18, starting transfers between devices: none -> 23.1 us  [swap_over(): return lax.ppermute(x, AXES, [(i, i ^ masks[i & 1]) for i in range(total)])]
    ppermute x22 -> x4, starting transfers between devices: 23.3 us -> 1.06 us  [xor_permute(): return lax.ppermute(x, AXES, [(i, i ^ mask) for i in range(total)])]
    ppermute x22 -> x4, waiting for transfers between devices: 23.9 us -> 2.74 us  [xor_permute(): return lax.ppermute(x, AXES, [(i, i ^ mask) for i in range(total)])]
    ppermute x0 -> x18, waiting for transfers between devices: none -> 19.3 us  [swap_over(): return lax.ppermute(x, AXES, [(i, i ^ masks[i & 1]) for i in range(total)])]
    ppermute x12, waiting for transfers between devices: 4.84 us -> 1.43 us  [swap(): return lax.ppermute(x, AXES, flat_pairs(pairs_y, pairs_x, n_ty, n_tx))]
  transfers between devices with their start and end apart: 34 -> 34, of which waited for: 25 -> 21; matrix products, arithmetic and copies ran while one was open for 1% -> 1% of each run, Pallas kernels for 0% -> 0%
where the time goes in v5:
time: 76 us; the launch traced here: 75.8 us
  starting transfers between devices  37.4 us (49%)
  waiting for transfers between devices  23.5 us (31%)
  Pallas kernels  9.42 us (12%)
  local copies, waits for them, and re-layouts  4.17 us (5%)
  between operations  0.89 us (1%)
    ppermute x18, starting transfers between devices, swap_over(): return lax.ppermute(x, AXES, [(i, i ^ masks[i & 1]) for i in range(total)])  23.1 us
    ppermute x18, waiting for transfers between devices, swap_over(): return lax.ppermute(x, AXES, [(i, i ^ masks[i & 1]) for i in range(total)])  19.3 us
    ppermute x12, starting transfers between devices, swap(): return lax.ppermute(x, AXES, flat_pairs(pairs_y, pairs_x, n_ty, n_tx))  13.2 us
    pallas_call x4, Pallas kernels, call(): pl.pallas_call(kernel, out_shape=shapes, in_specs=[smem if x.dtype == jnp...  9.42 us
    unnamed x10, local copies, waits for them, and re-layouts  2.88 us
    ppermute x4, waiting for transfers between devices, xor_permute(): return lax.ppermute(x, AXES, [(i, i ^ mask) for i in range(total)])  2.74 us
  transfers between devices with their start and end apart: 34, of which 21 were waited for; matrix products, arithmetic and copies ran while one was open for 1% of the time, Pallas kernels for 0%

profile of v5, /device:TPU:0, one launch (start us, length us, event | category | flops | bytes accessed | tf_op | source)
XLA Modules:
  0.0 75.8 jit_solution(5484508930283776210)
XLA Ops:
  0.7 0.9 %constant_dynamic-slice_fusion.8 = f32[2,64,128]{2,1,0:T(8,128)S(1)} fusion(f32[2,128,128]{2,1,0:T(8,128)} %obj_ref.1, s32[]{:T(128)S(6)} %select_n.83), kind=kLoop, calls=%fused_computation.43 | loop fusion | bytes 131076 | tf_op jit(solution)/shard_map/dynamic_slice | solution.py:452
  1.6 2.9 %collective-permute-start.2 = (f32[2,64,128]{2,1,0:T(8,128)S(1)}, f32[2,64,128]{2,1,0:T(8,128)S(1)}, u32[]{:S(2)}, u32[]{:S(2)}) collective-permute-start(f32[2,64,128]{2,1,0:T(8,128)S(1)} %constant_dynamic-slice_fusion.8), channel_id=1, source_target_pairs={{0,16},{16,0},{1,17},{17,1},{2,18},{18,2},{3,19},{19,3},{4,20},{20... | collective-permute-start | bytes 196616 | tf_op jit(solution)/shard_map/ppermute | solution.py:448
  4.5 0.1 collective-permute-start.1
  4.6 1.6 %collective-permute-start = (f32[2,128,128]{2,1,0:T(8,128)S(1)}, f32[2,128,128]{2,1,0:T(8,128)S(1)}, u32[]{:S(2)}, u32[]{:S(2)}) collective-permute-start(f32[2,128,128]{2,1,0:T(8,128)S(1)} %copy-done.1), channel_id=1, source_target_pairs={{0,1},{16,17},{1,0},{17,16},{2,3},{18,19},{3,2},{19,18},{4,5},{20,... | collective-permute-start | bytes 393224 | tf_op jit(solution)/shard_map/ppermute | solution.py:448
  6.1 0.5 collective-permute-start.4
  6.7 1.0 %collective-permute-start.3 = (f32[2,64,128]{2,1,0:T(8,128)S(1)}, f32[2,64,128]{2,1,0:T(8,128)S(1)}, u32[]{:S(2)}, u32[]{:S(2)}) collective-permute-start(f32[2,64,128]{2,1,0:T(8,128)S(1)} %collective-permute-done.2.rest_0_), channel_id=1, source_target_pairs={{0,1},{16,17},{1,0},{17,16},{2,3},{18,19},{3,2},{19,18},{4,5},{20,... | collective-permute-start | bytes 196616 | tf_op jit(solution)/shard_map/ppermute | solution.py:448
  7.7 0.1 copy.8.pos_ref
  7.8 1.0 %copy-done = f32[2,4,128,128]{3,2,1,0:T(8,128)S(1)} copy-done((f32[2,4,128,128]{3,2,1,0:T(8,128)S(1)}, f32[2,4,128,128]{3,2,1,0:T(8,128)}, u32[]{:S(2)}) %copy-start) | copy-done | bytes 524312
  8.9 0.9 %copy-done.2 = f32[1,1,3,128,128]{4,3,2,1,0:T(8,128)S(1)} copy-done((f32[1,1,3,128,128]{4,3,2,1,0:T(8,128)S(1)}, f32[1,1,3,128,128]{4,3,2,1,0:T(8,128)}, u32[]{:S(2)}) %copy-start.2) | copy-done | bytes 196632
  9.8 0.9 %copy-done.3 = bf16[4,128,128]{2,1,0:T(8,128)(2,1)S(1)} copy-done((bf16[4,128,128]{2,1,0:T(8,128)(2,1)S(1)}, bf16[4,128,128]{2,1,0:T(8,128)(2,1)}, u32[]{:S(2)}) %copy-start.3) | copy-done | bytes 131096
  10.7 0.1 shard_map.68
  10.8 4.1 %shard_map.69 = (f32[2,264,256]{2,1,0:T(8,128)S(1)}, f32[4,136,128]{2,1,0:T(8,128)S(1)}, f32[4,136,128]{2,1,0:T(8,128)S(1)}, f32[2,128,128]{2,1,0:T(8,128)S(1)},...) custom-call(s32[3,2]{1,0:T(4,128)S(1)} %copy.8.pos_ref, f32[2,128,128]{2,1,0:T(8,128)S(1)} %copy-done.1, ...), custom_call_target="tpu_custom_call" | custom-call | tf_op jit(solution)/shard_map/pallas_call | solution.py:351
  14.9 0.1 collective-permute-start.5
  15.0 1.6 %collective-permute-start.6 = (f32[2,2,64,128]{3,2,1,0:T(8,128)S(1)}, f32[2,2,64,128]{3,2,1,0:T(8,128)S(1)}, u32[]{:S(2)}, u32[]{:S(2)}) collective-permute-start(f32[2,2,64,128]{3,2,1,0:T(8,128)S(1)} %get-tuple-element.56), channel_id=1, source_target_pairs={{0,16},{16,0},{1,17},{17,1},{2,18},{18,2},{3,19},{19,3},{4,20},{20... | collective-permute-start | bytes 393224 | tf_op jit(solution)/shard_map/ppermute | solution.py:448
  16.7 1.5 %collective-permute-start.7 = (f32[1,136,128]{2,1,0:T(8,128)S(1)}, f32[1,136,128]{2,1,0:T(8,128)S(1)}, u32[]{:S(2)}, u32[]{:S(2)}) collective-permute-start(f32[1,136,128]{2,1,0:T(8,128)S(1)} %get-tuple-element.94), channel_id=1, source_target_pairs={{0,16},{1,5},{2,18},{3,7},{4,20},{5,1},{6,22},{7,3},{8,24},{9,13},... | collective-permute-start | bytes 208904 | tf_op jit(solution)/shard_map/ppermute | solution.py:371
  18.2 1.9 %collective-permute-start.9 = (f32[1,136,128]{2,1,0:T(8,128)S(1)}, f32[1,136,128]{2,1,0:T(8,128)S(1)}, u32[]{:S(2)}, u32[]{:S(2)}) collective-permute-start(f32[1,136,128]{2,1,0:T(8,128)S(1)} %get-tuple-element.95), channel_id=1, source_target_pairs={{0,18},{1,13},{2,16},{3,15},{4,22},{5,9},{6,20},{7,11},{8,26},{9,5... | collective-permute-start | bytes 208904 | tf_op jit(solution)/shard_map/ppermute | solution.py:371
  20.1 0.2 collective-permute-start.8
  20.3 0.1 broadcast_in_dim.70
  20.3 0.1 broadcast_in_dim.71
  20.4 0.5 collective-permute-done.6
  20.9 0.7 collective-permute-done.7
  21.6 2.1 %collective-permute-done.9 = f32[1,136,128]{2,1,0:T(8,128)S(1)} collective-permute-done((f32[1,136,128]{2,1,0:T(8,128)S(1)}, f32[1,136,128]{2,1,0:T(8,128)S(1)}, u32[]{:S(2)}, u32[]{:S(2)}) %collective-permute-start.9) | collective-permute-done | bytes 69664 | tf_op jit(solution)/shard_map/ppermute | solution.py:371
  23.8 0.7 collective-permute-done.8
  24.5 3.8 %collective-permute-start.12 = (f32[1,136,128]{2,1,0:T(8,128)S(1)}, f32[1,136,128]{2,1,0:T(8,128)S(1)}, u32[]{:S(2)}, u32[]{:S(2)}) collective-permute-start(f32[1,136,128]{2,1,0:T(8,128)S(1)} %add_add_fusion.3), channel_id=1, source_target_pairs={{0,12},{1,19},{2,14},{3,17},{4,8},{5,23},{6,10},{7,21},{8,4},{9,27... | collective-permute-start | bytes 208904 | tf_op jit(solution)/shard_map/ppermute | solution.py:371
  28.3 0.6 collective-permute-start.10
  29.0 0.1 fusion.2
  29.1 1.4 %collective-permute-start.14 = (f32[2,128,128]{2,1,0:T(8,128)S(1)}, f32[2,128,128]{2,1,0:T(8,128)S(1)}, u32[]{:S(2)}, u32[]{:S(2)}) collective-permute-start(f32[2,128,128]{2,1,0:T(8,128)S(1)} %get-tuple-element.62.second_ref), channel_id=1, source_target_pairs={{1,2},{17,18},{2,1},{18,17},{3,4},{19,20},{4,3},{20,19},{5,6},{21,... | collective-permute-start | bytes 393224 | tf_op jit(solution)/shard_map/ppermute | solution.py:448
  30.4 0.2 collective-permute-start.13
  30.7 3.0 %collective-permute-done.11 = f32[1,136,128]{2,1,0:T(8,128)S(1)} collective-permute-done((f32[1,136,128]{2,1,0:T(8,128)S(1)}, f32[1,136,128]{2,1,0:T(8,128)S(1)}, u32[]{:S(2)}, u32[]{:S(2)}) %collective-permute-start.11) | collective-permute-done | bytes 69664 | tf_op jit(solution)/shard_map/ppermute | solution.py:371
  33.7 0.5 collective-permute-done.14.rest_1_
  34.2 1.4 %collective-permute-start.15 = (f32[2,2,64,128]{3,2,1,0:T(8,128)S(1)}, f32[2,2,64,128]{3,2,1,0:T(8,128)S(1)}, u32[]{:S(2)}, u32[]{:S(2)}) collective-permute-start(f32[2,2,64,128]{3,2,1,0:T(8,128)S(1)} %pad_maximum_fusion.4), channel_id=1, source_target_pairs={{0,16},{16,0},{1,17},{17,1},{2,18},{18,2},{3,19},{19,3},{4,20},{20... | collective-permute-start | bytes 393224 | tf_op jit(solution)/shard_map/ppermute | solution.py:448
  35.5 1.1 %collective-permute-start.18 = (f32[1,136,128]{2,1,0:T(8,128)S(1)}, f32[1,136,128]{2,1,0:T(8,128)S(1)}, u32[]{:S(2)}, u32[]{:S(2)}) collective-permute-start(f32[1,136,128]{2,1,0:T(8,128)S(1)} %add_add_fusion.2), channel_id=1, source_target_pairs={{0,18},{1,13},{2,16},{3,15},{4,22},{5,9},{6,20},{7,11},{8,26},{9,5... | collective-permute-start | bytes 208904 | tf_op jit(solution)/shard_map/ppermute | solution.py:371
  36.6 1.1 %collective-permute-start.17 = (f32[1,136,128]{2,1,0:T(8,128)S(1)}, f32[1,136,128]{2,1,0:T(8,128)S(1)}, u32[]{:S(2)}, u32[]{:S(2)}) collective-permute-start(f32[1,136,128]{2,1,0:T(8,128)S(1)} %add_add_fusion.2), channel_id=1, source_target_pairs={{0,2},{1,9},{2,0},{3,11},{4,6},{5,13},{6,4},{7,15},{8,10},{9,1},{1... | collective-permute-start | bytes 208904 | tf_op jit(solution)/shard_map/ppermute | solution.py:371
  37.7 1.3 %collective-permute-start.16 = (f32[1,136,128]{2,1,0:T(8,128)S(1)}, f32[1,136,128]{2,1,0:T(8,128)S(1)}, u32[]{:S(2)}, u32[]{:S(2)}) collective-permute-start(f32[1,136,128]{2,1,0:T(8,128)S(1)} %add_add_fusion.2), channel_id=1, source_target_pairs={{0,16},{1,5},{2,18},{3,7},{4,20},{5,1},{6,22},{7,3},{8,24},{9,13},... | collective-permute-start | bytes 208904 | tf_op jit(solution)/shard_map/ppermute | solution.py:371
  39.0 0.2 collective-permute-done.15.rest_2_
  39.2 2.5 %collective-permute-done.18 = f32[1,136,128]{2,1,0:T(8,128)S(1)} collective-permute-done((f32[1,136,128]{2,1,0:T(8,128)S(1)}, f32[1,136,128]{2,1,0:T(8,128)S(1)}, u32[]{:S(2)}, u32[]{:S(2)}) %collective-permute-start.18) | collective-permute-done | bytes 69664 | tf_op jit(solution)/shard_map/ppermute | solution.py:371
  41.7 0.3 collective-permute-done.16
  42.1 0.4 collective-permute-start.19
  42.6 1.2 %collective-permute-done.19.other_ref = f32[4,136,128]{2,1,0:T(8,128)S(1)} collective-permute-done((f32[4,136,128]{2,1,0:T(8,128)S(1)}, f32[4,136,128]{2,1,0:T(8,128)S(1)}, u32[]{:S(2)}, u32[]{:S(2)}) %collective-permute-start.19) | collective-permute-done | bytes 278560 | tf_op jit(solution)/shard_map/ppermute | solution.py:66
  43.8 4.3 %shard_map.70 = (f32[2,128,128]{2,1,0:T(8,128)S(1)}, f32[2,4,128,128]{3,2,1,0:T(8,128)S(1)}, f32[4,136,128]{2,1,0:T(8,128)S(1)}, f32[4,136,128]{2,1,0:T(8,128)S(...) custom-call(s32[3,2]{1,0:T(4,128)S(1)} %copy.8.pos_ref, ...), custom_call_target="tpu_custom_call" | custom-call | tf_op jit(solution)/shard_map/pallas_call | solution.py:351
  48.0 0.5 collective-permute-start.20
  48.5 1.7 %collective-permute-start.21 = (f32[2,2,64,128]{3,2,1,0:T(8,128)S(1)}, f32[2,2,64,128]{3,2,1,0:T(8,128)S(1)}, u32[]{:S(2)}, u32[]{:S(2)}) collective-permute-start(f32[2,2,64,128]{3,2,1,0:T(8,128)S(1)} %get-tuple-element.71), channel_id=1, source_target_pairs={{0,16},{16,0},{1,17},{17,1},{2,18},{18,2},{3,19},{19,3},{4,20},{20... | collective-permute-start | bytes 393224 | tf_op jit(solution)/shard_map/ppermute | solution.py:448
  50.2 1.3 %collective-permute-start.22 = (f32[1,136,128]{2,1,0:T(8,128)S(1)}, f32[1,136,128]{2,1,0:T(8,128)S(1)}, u32[]{:S(2)}, u32[]{:S(2)}) collective-permute-start(f32[1,136,128]{2,1,0:T(8,128)S(1)} %get-tuple-element.86), channel_id=1, source_target_pairs={{0,16},{1,5},{2,18},{3,7},{4,20},{5,1},{6,22},{7,3},{8,24},{9,13},... | collective-permute-start | bytes 208904 | tf_op jit(solution)/shard_map/ppermute | solution.py:371
  51.5 0.8 %collective-permute-start.24 = (f32[1,136,128]{2,1,0:T(8,128)S(1)}, f32[1,136,128]{2,1,0:T(8,128)S(1)}, u32[]{:S(2)}, u32[]{:S(2)}) collective-permute-start(f32[1,136,128]{2,1,0:T(8,128)S(1)} %get-tuple-element.87), channel_id=1, source_target_pairs={{0,18},{1,13},{2,16},{3,15},{4,22},{5,9},{6,20},{7,11},{8,26},{9,5... | collective-permute-start | bytes 208904 | tf_op jit(solution)/shard_map/ppermute | solution.py:371
  52.2 1.5 %collective-permute-start.23 = (f32[1,136,128]{2,1,0:T(8,128)S(1)}, f32[1,136,128]{2,1,0:T(8,128)S(1)}, u32[]{:S(2)}, u32[]{:S(2)}) collective-permute-start(f32[1,136,128]{2,1,0:T(8,128)S(1)} %get-tuple-element.88), channel_id=1, source_target_pairs={{0,2},{1,9},{2,0},{3,11},{4,6},{5,13},{6,4},{7,15},{8,10},{9,1},{1... | collective-permute-start | bytes 208904 | tf_op jit(solution)/shard_map/ppermute | solution.py:371
  53.8 0.2 collective-permute-done.21
  54.0 0.7 collective-permute-done.22
  54.8 2.0 %collective-permute-done.24 = f32[1,136,128]{2,1,0:T(8,128)S(1)} collective-permute-done((f32[1,136,128]{2,1,0:T(8,128)S(1)}, f32[1,136,128]{2,1,0:T(8,128)S(1)}, u32[]{:S(2)}, u32[]{:S(2)}) %collective-permute-start.24) | collective-permute-done | bytes 69664 | tf_op jit(solution)/shard_map/ppermute | solution.py:371
  56.8 0.5 collective-permute-done.23
  57.3 3.9 %collective-permute-start.27 = (f32[1,136,128]{2,1,0:T(8,128)S(1)}, f32[1,136,128]{2,1,0:T(8,128)S(1)}, u32[]{:S(2)}, u32[]{:S(2)}) collective-permute-start(f32[1,136,128]{2,1,0:T(8,128)S(1)} %add_add_fusion.1), channel_id=1, source_target_pairs={{0,12},{1,19},{2,14},{3,17},{4,8},{5,23},{6,10},{7,21},{8,4},{9,27... | collective-permute-start | bytes 208904 | tf_op jit(solution)/shard_map/ppermute | solution.py:371
  61.2 0.6 collective-permute-start.25
  61.9 0.1 fusion
  62.0 0.8 %collective-permute-start.29 = (f32[2,128,128]{2,1,0:T(8,128)S(1)}, f32[2,128,128]{2,1,0:T(8,128)S(1)}, u32[]{:S(2)}, u32[]{:S(2)}) collective-permute-start(f32[2,128,128]{2,1,0:T(8,128)S(1)} %get-tuple-element.77.second_ref), channel_id=1, source_target_pairs={{1,2},{17,18},{2,1},{18,17},{3,4},{19,20},{4,3},{20,19},{5,6},{21,... | collective-permute-start | bytes 393224 | tf_op jit(solution)/shard_map/ppermute | solution.py:448
  62.7 0.2 collective-permute-start.28
  62.9 0.7 collective-permute-done.27
  63.6 2.9 %collective-permute-done.26 = f32[1,136,128]{2,1,0:T(8,128)S(1)} collective-permute-done((f32[1,136,128]{2,1,0:T(8,128)S(1)}, f32[1,136,128]{2,1,0:T(8,128)S(1)}, u32[]{:S(2)}, u32[]{:S(2)}) %collective-permute-start.26) | collective-permute-done | bytes 69664 | tf_op jit(solution)/shard_map/ppermute | solution.py:371
  66.5 1.4 %collective-permute-start.32 = (f32[1,136,128]{2,1,0:T(8,128)S(1)}, f32[1,136,128]{2,1,0:T(8,128)S(1)}, u32[]{:S(2)}, u32[]{:S(2)}) collective-permute-start(f32[1,136,128]{2,1,0:T(8,128)S(1)} %add_add_fusion), channel_id=1, source_target_pairs={{0,18},{1,13},{2,16},{3,15},{4,22},{5,9},{6,20},{7,11},{8,26},{9,5... | collective-permute-start | bytes 208904 | tf_op jit(solution)/shard_map/ppermute | solution.py:371
  67.9 0.9 %collective-permute-start.31 = (f32[1,136,128]{2,1,0:T(8,128)S(1)}, f32[1,136,128]{2,1,0:T(8,128)S(1)}, u32[]{:S(2)}, u32[]{:S(2)}) collective-permute-start(f32[1,136,128]{2,1,0:T(8,128)S(1)} %add_add_fusion), channel_id=1, source_target_pairs={{0,2},{1,9},{2,0},{3,11},{4,6},{5,13},{6,4},{7,15},{8,10},{9,1},{1... | collective-permute-start | bytes 208904 | tf_op jit(solution)/shard_map/ppermute | solution.py:371
  68.8 1.3 %collective-permute-start.30 = (f32[1,136,128]{2,1,0:T(8,128)S(1)}, f32[1,136,128]{2,1,0:T(8,128)S(1)}, u32[]{:S(2)}, u32[]{:S(2)}) collective-permute-start(f32[1,136,128]{2,1,0:T(8,128)S(1)} %add_add_fusion), channel_id=1, source_target_pairs={{0,16},{1,5},{2,18},{3,7},{4,20},{5,1},{6,22},{7,3},{8,24},{9,13},... | collective-permute-start | bytes 208904 | tf_op jit(solution)/shard_map/ppermute | solution.py:371
  70.1 1.7 %collective-permute-done.32 = f32[1,136,128]{2,1,0:T(8,128)S(1)} collective-permute-done((f32[1,136,128]{2,1,0:T(8,128)S(1)}, f32[1,136,128]{2,1,0:T(8,128)S(1)}, u32[]{:S(2)}, u32[]{:S(2)}) %collective-permute-start.32) | collective-permute-done | bytes 69664 | tf_op jit(solution)/shard_map/ppermute | solution.py:371
  71.8 0.7 collective-permute-done.31
  72.6 0.5 collective-permute-done.30
  73.2 1.5 %collective-permute-done.33.other_ref = f32[4,136,128]{2,1,0:T(8,128)S(1)} collective-permute-done((f32[4,136,128]{2,1,0:T(8,128)S(1)}, f32[4,136,128]{2,1,0:T(8,128)S(1)}, u32[]{:S(2)}, u32[]{:S(2)}) %collective-permute-start.33) | collective-permute-done | bytes 278560 | tf_op jit(solution)/shard_map/ppermute | solution.py:66
  74.8 1.0 %shard_map.71 = (f32[2,128,128]{2,1,0:T(8,128)}, f32[2,4,128,128]{3,2,1,0:T(8,128)}) custom-call(f32[2,128,128]{2,1,0:T(8,128)S(1)} %get-tuple-element.68.tile_ref, f32[2,128,128]{2,1,0:T(8,128)S(1)} %get-tuple-element.76.first_ref, f32[2,128,128]{2,1,0:T(8,128)S(1)} %get-tuple-element.77.second_ref, f32[2,4,128,128]{3,2,1,0:T(8,128)S(1)} %get-tuple-element.78.probe_ref, ...), custom_call_target="tpu_custom_call" | custom-call | tf_op jit(solution)/shard_map/pallas_call | solution.py:351
  (43 shorter events, 0.7 us)
Async XLA Ops:
  0.6 3.9 %copy-start.1 = (f32[2,128,128]{2,1,0:T(8,128)S(1)}, f32[2,128,128]{2,1,0:T(8,128)}, u32[]{:S(2)}) copy-start(f32[2,128,128]{2,1,0:T(8,128)} %obj_ref.1) | copy-start | bytes 393220
  1.5 6.2 %copy-start.4 = (s32[1,1,3,2]{2,3,1,0:T(2,128)S(1)}, s32[1,1,3,2]{2,3,1,0:T(2,128)}, u32[]{:S(2)}) copy-start(s32[1,1,3,2]{2,3,1,0:T(2,128)} %param.8) | copy-start | bytes 76
  1.6 5.2 %collective-permute-start.2 = (f32[2,64,128]{2,1,0:T(8,128)S(1)}, f32[2,64,128]{2,1,0:T(8,128)S(1)}, u32[]{:S(2)}, u32[]{:S(2)}) collective-permute-start(f32[2,64,128]{2,1,0:T(8,128)S(1)} %constant_dynamic-slice_fusion.8), channel_id=1, source_target_pairs={{0,16},{16,0},{1,17},{17,1},{2,18},{18,2},{3,19},{19,3},{4,20},{20... | collective-permute-start | bytes 196616 | tf_op jit(solution)/shard_map/ppermute | solution.py:448
  4.5 6.3 %collective-permute-start.1 = (f32[2,128,128]{2,1,0:T(8,128)S(1)}, f32[2,128,128]{2,1,0:T(8,128)S(1)}, u32[]{:S(2)}, u32[]{:S(2)}) collective-permute-start(f32[2,128,128]{2,1,0:T(8,128)S(1)} %copy-done.1), channel_id=1, source_target_pairs={{1,2},{17,18},{2,1},{18,17},{3,4},{19,20},{4,3},{20,19},{5,6},{21,... | collective-permute-start | bytes 393224 | tf_op jit(solution)/shard_map/ppermute | solution.py:448
  4.6 6.3 %collective-permute-start = (f32[2,128,128]{2,1,0:T(8,128)S(1)}, f32[2,128,128]{2,1,0:T(8,128)S(1)}, u32[]{:S(2)}, u32[]{:S(2)}) collective-permute-start(f32[2,128,128]{2,1,0:T(8,128)S(1)} %copy-done.1), channel_id=1, source_target_pairs={{0,1},{16,17},{1,0},{17,16},{2,3},{18,19},{3,2},{19,18},{4,5},{20,... | collective-permute-start | bytes 393224 | tf_op jit(solution)/shard_map/ppermute | solution.py:448
  6.1 4.7 %collective-permute-start.4 = (f32[2,64,128]{2,1,0:T(8,128)S(1)}, f32[2,64,128]{2,1,0:T(8,128)S(1)}, u32[]{:S(2)}, u32[]{:S(2)}) collective-permute-start(f32[2,64,128]{2,1,0:T(8,128)S(1)} %constant_dynamic-slice_fusion.8), channel_id=1, source_target_pairs={{1,18},{17,2},{2,17},{18,1},{3,20},{19,4},{4,19},{20,3},{5,22},{21... | collective-permute-start | bytes 196616 | tf_op jit(solution)/shard_map/ppermute | solution.py:448
  6.7 4.1 %collective-permute-start.3 = (f32[2,64,128]{2,1,0:T(8,128)S(1)}, f32[2,64,128]{2,1,0:T(8,128)S(1)}, u32[]{:S(2)}, u32[]{:S(2)}) collective-permute-start(f32[2,64,128]{2,1,0:T(8,128)S(1)} %collective-permute-done.2.rest_0_), channel_id=1, source_target_pairs={{0,1},{16,17},{1,0},{17,16},{2,3},{18,19},{3,2},{19,18},{4,5},{20,... | collective-permute-start | bytes 196616 | tf_op jit(solution)/shard_map/ppermute | solution.py:448
  7.8 1.0 %copy-start = (f32[2,4,128,128]{3,2,1,0:T(8,128)S(1)}, f32[2,4,128,128]{3,2,1,0:T(8,128)}, u32[]{:S(2)}) copy-start(f32[2,4,128,128]{3,2,1,0:T(8,128)} %probe_ref.1) | copy-start | bytes 1572868
  8.9 0.9 %copy-start.2 = (f32[1,1,3,128,128]{4,3,2,1,0:T(8,128)S(1)}, f32[1,1,3,128,128]{4,3,2,1,0:T(8,128)}, u32[]{:S(2)}) copy-start(f32[1,1,3,128,128]{4,3,2,1,0:T(8,128)} %param.7) | copy-start | bytes 589828
  9.8 0.9 %copy-start.3 = (bf16[4,128,128]{2,1,0:T(8,128)(2,1)S(1)}, bf16[4,128,128]{2,1,0:T(8,128)(2,1)}, u32[]{:S(2)}) copy-start(bf16[4,128,128]{2,1,0:T(8,128)(2,1)} %constant.74.clone.table_ref) | copy-start | bytes 393220
  14.9 1.7 %collective-permute-start.5 = (f32[4,136,128]{2,1,0:T(8,128)S(1)}, f32[4,136,128]{2,1,0:T(8,128)S(1)}, u32[]{:S(2)}, u32[]{:S(2)}) collective-permute-start(f32[4,136,128]{2,1,0:T(8,128)S(1)} %get-tuple-element.55), channel_id=1, source_target_pairs={{0,1},{1,0},{2,3},{3,2},{4,5},{5,4},{6,7},{7,6},{8,9},{9,8},{10,11... | collective-permute-start | bytes 835592 | tf_op jit(solution)/shard_map/ppermute | solution.py:66
  15.0 5.9 %collective-permute-start.6 = (f32[2,2,64,128]{3,2,1,0:T(8,128)S(1)}, f32[2,2,64,128]{3,2,1,0:T(8,128)S(1)}, u32[]{:S(2)}, u32[]{:S(2)}) collective-permute-start(f32[2,2,64,128]{3,2,1,0:T(8,128)S(1)} %get-tuple-element.56), channel_id=1, source_target_pairs={{0,16},{16,0},{1,17},{17,1},{2,18},{18,2},{3,19},{19,3},{4,20},{20... | collective-permute-start | bytes 393224 | tf_op jit(solution)/shard_map/ppermute | solution.py:448
  16.7 4.9 %collective-permute-start.7 = (f32[1,136,128]{2,1,0:T(8,128)S(1)}, f32[1,136,128]{2,1,0:T(8,128)S(1)}, u32[]{:S(2)}, u32[]{:S(2)}) collective-permute-start(f32[1,136,128]{2,1,0:T(8,128)S(1)} %get-tuple-element.94), channel_id=1, source_target_pairs={{0,16},{1,5},{2,18},{3,7},{4,20},{5,1},{6,22},{7,3},{8,24},{9,13},... | collective-permute-start | bytes 208904 | tf_op jit(solution)/shard_map/ppermute | solution.py:371
  18.2 5.6 %collective-permute-start.9 = (f32[1,136,128]{2,1,0:T(8,128)S(1)}, f32[1,136,128]{2,1,0:T(8,128)S(1)}, u32[]{:S(2)}, u32[]{:S(2)}) collective-permute-start(f32[1,136,128]{2,1,0:T(8,128)S(1)} %get-tuple-element.95), channel_id=1, source_target_pairs={{0,18},{1,13},{2,16},{3,15},{4,22},{5,9},{6,20},{7,11},{8,26},{9,5... | collective-permute-start | bytes 208904 | tf_op jit(solution)/shard_map/ppermute | solution.py:371
  20.1 4.4 %collective-permute-start.8 = (f32[1,136,128]{2,1,0:T(8,128)S(1)}, f32[1,136,128]{2,1,0:T(8,128)S(1)}, u32[]{:S(2)}, u32[]{:S(2)}) collective-permute-start(f32[1,136,128]{2,1,0:T(8,128)S(1)} %get-tuple-element.96), channel_id=1, source_target_pairs={{0,2},{1,9},{2,0},{3,11},{4,6},{5,13},{6,4},{7,15},{8,10},{9,1},{1... | collective-permute-start | bytes 208904 | tf_op jit(solution)/shard_map/ppermute | solution.py:371
  24.5 6.2 %collective-permute-start.12 = (f32[1,136,128]{2,1,0:T(8,128)S(1)}, f32[1,136,128]{2,1,0:T(8,128)S(1)}, u32[]{:S(2)}, u32[]{:S(2)}) collective-permute-start(f32[1,136,128]{2,1,0:T(8,128)S(1)} %add_add_fusion.3), channel_id=1, source_target_pairs={{0,12},{1,19},{2,14},{3,17},{4,8},{5,23},{6,10},{7,21},{8,4},{9,27... | collective-permute-start | bytes 208904 | tf_op jit(solution)/shard_map/ppermute | solution.py:371
  28.3 5.3 %collective-permute-start.11 = (f32[1,136,128]{2,1,0:T(8,128)S(1)}, f32[1,136,128]{2,1,0:T(8,128)S(1)}, u32[]{:S(2)}, u32[]{:S(2)}) collective-permute-start(f32[1,136,128]{2,1,0:T(8,128)S(1)} %add_add_fusion.3), channel_id=1, source_target_pairs={{0,8},{1,3},{2,10},{3,1},{4,12},{5,7},{6,14},{7,5},{8,0},{9,11},{1... | collective-permute-start | bytes 208904 | tf_op jit(solution)/shard_map/ppermute | solution.py:371
  28.3 5.3 %collective-permute-start.10 = (f32[1,136,128]{2,1,0:T(8,128)S(1)}, f32[1,136,128]{2,1,0:T(8,128)S(1)}, u32[]{:S(2)}, u32[]{:S(2)}) collective-permute-start(f32[1,136,128]{2,1,0:T(8,128)S(1)} %add_add_fusion.3), channel_id=1, source_target_pairs={{0,4},{1,17},{2,6},{3,19},{4,0},{5,21},{6,2},{7,23},{8,12},{9,25},... | collective-permute-start | bytes 208904 | tf_op jit(solution)/shard_map/ppermute | solution.py:371
  29.1 5.0 %collective-permute-start.14 = (f32[2,128,128]{2,1,0:T(8,128)S(1)}, f32[2,128,128]{2,1,0:T(8,128)S(1)}, u32[]{:S(2)}, u32[]{:S(2)}) collective-permute-start(f32[2,128,128]{2,1,0:T(8,128)S(1)} %get-tuple-element.62.second_ref), channel_id=1, source_target_pairs={{1,2},{17,18},{2,1},{18,17},{3,4},{19,20},{4,3},{20,19},{5,6},{21,... | collective-permute-start | bytes 393224 | tf_op jit(solution)/shard_map/ppermute | solution.py:448
  30.4 3.7 %collective-permute-start.13 = (f32[2,128,128]{2,1,0:T(8,128)S(1)}, f32[2,128,128]{2,1,0:T(8,128)S(1)}, u32[]{:S(2)}, u32[]{:S(2)}) collective-permute-start(f32[2,128,128]{2,1,0:T(8,128)S(1)} %get-tuple-element.61.first_ref), channel_id=1, source_target_pairs={{0,1},{16,17},{1,0},{17,16},{2,3},{18,19},{3,2},{19,18},{4,5},{20,... | collective-permute-start | bytes 393224 | tf_op jit(solution)/shard_map/ppermute | solution.py:448
  34.2 5.0 %collective-permute-start.15 = (f32[2,2,64,128]{3,2,1,0:T(8,128)S(1)}, f32[2,2,64,128]{3,2,1,0:T(8,128)S(1)}, u32[]{:S(2)}, u32[]{:S(2)}) collective-permute-start(f32[2,2,64,128]{3,2,1,0:T(8,128)S(1)} %pad_maximum_fusion.4), channel_id=1, source_target_pairs={{0,16},{16,0},{1,17},{17,1},{2,18},{18,2},{3,19},{19,3},{4,20},{20... | collective-permute-start | bytes 393224 | tf_op jit(solution)/shard_map/ppermute | solution.py:448
  35.5 6.2 %collective-permute-start.18 = (f32[1,136,128]{2,1,0:T(8,128)S(1)}, f32[1,136,128]{2,1,0:T(8,128)S(1)}, u32[]{:S(2)}, u32[]{:S(2)}) collective-permute-start(f32[1,136,128]{2,1,0:T(8,128)S(1)} %add_add_fusion.2), channel_id=1, source_target_pairs={{0,18},{1,13},{2,16},{3,15},{4,22},{5,9},{6,20},{7,11},{8,26},{9,5... | collective-permute-start | bytes 208904 | tf_op jit(solution)/shard_map/ppermute | solution.py:371
  36.6 5.1 %collective-permute-start.17 = (f32[1,136,128]{2,1,0:T(8,128)S(1)}, f32[1,136,128]{2,1,0:T(8,128)S(1)}, u32[]{:S(2)}, u32[]{:S(2)}) collective-permute-start(f32[1,136,128]{2,1,0:T(8,128)S(1)} %add_add_fusion.2), channel_id=1, source_target_pairs={{0,2},{1,9},{2,0},{3,11},{4,6},{5,13},{6,4},{7,15},{8,10},{9,1},{1... | collective-permute-start | bytes 208904 | tf_op jit(solution)/shard_map/ppermute | solution.py:371
  37.7 4.3 %collective-permute-start.16 = (f32[1,136,128]{2,1,0:T(8,128)S(1)}, f32[1,136,128]{2,1,0:T(8,128)S(1)}, u32[]{:S(2)}, u32[]{:S(2)}) collective-permute-start(f32[1,136,128]{2,1,0:T(8,128)S(1)} %add_add_fusion.2), channel_id=1, source_target_pairs={{0,16},{1,5},{2,18},{3,7},{4,20},{5,1},{6,22},{7,3},{8,24},{9,13},... | collective-permute-start | bytes 208904 | tf_op jit(solution)/shard_map/ppermute | solution.py:371
  42.1 1.6 %collective-permute-start.19 = (f32[4,136,128]{2,1,0:T(8,128)S(1)}, f32[4,136,128]{2,1,0:T(8,128)S(1)}, u32[]{:S(2)}, u32[]{:S(2)}) collective-permute-start(f32[4,136,128]{2,1,0:T(8,128)S(1)} %pad_maximum_fusion.1.own_ref), channel_id=1, source_target_pairs={{0,1},{1,0},{2,3},{3,2},{4,5},{5,4},{6,7},{7,6},{8,9},{9,8},{10,11... | collective-permute-start | bytes 835592 | tf_op jit(solution)/shard_map/ppermute | solution.py:66
  48.0 2.1 %collective-permute-start.20 = (f32[4,136,128]{2,1,0:T(8,128)S(1)}, f32[4,136,128]{2,1,0:T(8,128)S(1)}, u32[]{:S(2)}, u32[]{:S(2)}) collective-permute-start(f32[4,136,128]{2,1,0:T(8,128)S(1)} %get-tuple-element.70), channel_id=1, source_target_pairs={{0,1},{1,0},{2,3},{3,2},{4,5},{5,4},{6,7},{7,6},{8,9},{9,8},{10,11... | collective-permute-start | bytes 835592 | tf_op jit(solution)/shard_map/ppermute | solution.py:66
  48.5 5.5 %collective-permute-start.21 = (f32[2,2,64,128]{3,2,1,0:T(8,128)S(1)}, f32[2,2,64,128]{3,2,1,0:T(8,128)S(1)}, u32[]{:S(2)}, u32[]{:S(2)}) collective-permute-start(f32[2,2,64,128]{3,2,1,0:T(8,128)S(1)} %get-tuple-element.71), channel_id=1, source_target_pairs={{0,16},{16,0},{1,17},{17,1},{2,18},{18,2},{3,19},{19,3},{4,20},{20... | collective-permute-start | bytes 393224 | tf_op jit(solution)/shard_map/ppermute | solution.py:448
  50.2 4.5 %collective-permute-start.22 = (f32[1,136,128]{2,1,0:T(8,128)S(1)}, f32[1,136,128]{2,1,0:T(8,128)S(1)}, u32[]{:S(2)}, u32[]{:S(2)}) collective-permute-start(f32[1,136,128]{2,1,0:T(8,128)S(1)} %get-tuple-element.86), channel_id=1, source_target_pairs={{0,16},{1,5},{2,18},{3,7},{4,20},{5,1},{6,22},{7,3},{8,24},{9,13},... | collective-permute-start | bytes 208904 | tf_op jit(solution)/shard_map/ppermute | solution.py:371
  51.5 5.3 %collective-permute-start.24 = (f32[1,136,128]{2,1,0:T(8,128)S(1)}, f32[1,136,128]{2,1,0:T(8,128)S(1)}, u32[]{:S(2)}, u32[]{:S(2)}) collective-permute-start(f32[1,136,128]{2,1,0:T(8,128)S(1)} %get-tuple-element.87), channel_id=1, source_target_pairs={{0,18},{1,13},{2,16},{3,15},{4,22},{5,9},{6,20},{7,11},{8,26},{9,5... | collective-permute-start | bytes 208904 | tf_op jit(solution)/shard_map/ppermute | solution.py:371
  52.2 5.1 %collective-permute-start.23 = (f32[1,136,128]{2,1,0:T(8,128)S(1)}, f32[1,136,128]{2,1,0:T(8,128)S(1)}, u32[]{:S(2)}, u32[]{:S(2)}) collective-permute-start(f32[1,136,128]{2,1,0:T(8,128)S(1)} %get-tuple-element.88), channel_id=1, source_target_pairs={{0,2},{1,9},{2,0},{3,11},{4,6},{5,13},{6,4},{7,15},{8,10},{9,1},{1... | collective-permute-start | bytes 208904 | tf_op jit(solution)/shard_map/ppermute | solution.py:371
  57.3 6.3 %collective-permute-start.27 = (f32[1,136,128]{2,1,0:T(8,128)S(1)}, f32[1,136,128]{2,1,0:T(8,128)S(1)}, u32[]{:S(2)}, u32[]{:S(2)}) collective-permute-start(f32[1,136,128]{2,1,0:T(8,128)S(1)} %add_add_fusion.1), channel_id=1, source_target_pairs={{0,12},{1,19},{2,14},{3,17},{4,8},{5,23},{6,10},{7,21},{8,4},{9,27... | collective-permute-start | bytes 208904 | tf_op jit(solution)/shard_map/ppermute | solution.py:371
  61.2 5.3 %collective-permute-start.26 = (f32[1,136,128]{2,1,0:T(8,128)S(1)}, f32[1,136,128]{2,1,0:T(8,128)S(1)}, u32[]{:S(2)}, u32[]{:S(2)}) collective-permute-start(f32[1,136,128]{2,1,0:T(8,128)S(1)} %add_add_fusion.1), channel_id=1, source_target_pairs={{0,8},{1,3},{2,10},{3,1},{4,12},{5,7},{6,14},{7,5},{8,0},{9,11},{1... | collective-permute-start | bytes 208904 | tf_op jit(solution)/shard_map/ppermute | solution.py:371
  61.2 5.3 %collective-permute-start.25 = (f32[1,136,128]{2,1,0:T(8,128)S(1)}, f32[1,136,128]{2,1,0:T(8,128)S(1)}, u32[]{:S(2)}, u32[]{:S(2)}) collective-permute-start(f32[1,136,128]{2,1,0:T(8,128)S(1)} %add_add_fusion.1), channel_id=1, source_target_pairs={{0,4},{1,17},{2,6},{3,19},{4,0},{5,21},{6,2},{7,23},{8,12},{9,25},... | collective-permute-start | bytes 208904 | tf_op jit(solution)/shard_map/ppermute | solution.py:371
  62.0 8.1 %collective-permute-start.29 = (f32[2,128,128]{2,1,0:T(8,128)S(1)}, f32[2,128,128]{2,1,0:T(8,128)S(1)}, u32[]{:S(2)}, u32[]{:S(2)}) collective-permute-start(f32[2,128,128]{2,1,0:T(8,128)S(1)} %get-tuple-element.77.second_ref), channel_id=1, source_target_pairs={{1,2},{17,18},{2,1},{18,17},{3,4},{19,20},{4,3},{20,19},{5,6},{21,... | collective-permute-start | bytes 393224 | tf_op jit(solution)/shard_map/ppermute | solution.py:448
  62.7 7.4 %collective-permute-start.28 = (f32[2,128,128]{2,1,0:T(8,128)S(1)}, f32[2,128,128]{2,1,0:T(8,128)S(1)}, u32[]{:S(2)}, u32[]{:S(2)}) collective-permute-start(f32[2,128,128]{2,1,0:T(8,128)S(1)} %get-tuple-element.76.first_ref), channel_id=1, source_target_pairs={{0,1},{16,17},{1,0},{17,16},{2,3},{18,19},{3,2},{19,18},{4,5},{20,... | collective-permute-start | bytes 393224 | tf_op jit(solution)/shard_map/ppermute | solution.py:448
  66.5 5.3 %collective-permute-start.32 = (f32[1,136,128]{2,1,0:T(8,128)S(1)}, f32[1,136,128]{2,1,0:T(8,128)S(1)}, u32[]{:S(2)}, u32[]{:S(2)}) collective-permute-start(f32[1,136,128]{2,1,0:T(8,128)S(1)} %add_add_fusion), channel_id=1, source_target_pairs={{0,18},{1,13},{2,16},{3,15},{4,22},{5,9},{6,20},{7,11},{8,26},{9,5... | collective-permute-start | bytes 208904 | tf_op jit(solution)/shard_map/ppermute | solution.py:371
  67.9 4.7 %collective-permute-start.31 = (f32[1,136,128]{2,1,0:T(8,128)S(1)}, f32[1,136,128]{2,1,0:T(8,128)S(1)}, u32[]{:S(2)}, u32[]{:S(2)}) collective-permute-start(f32[1,136,128]{2,1,0:T(8,128)S(1)} %add_add_fusion), channel_id=1, source_target_pairs={{0,2},{1,9},{2,0},{3,11},{4,6},{5,13},{6,4},{7,15},{8,10},{9,1},{1... | collective-permute-start | bytes 208904 | tf_op jit(solution)/shard_map/ppermute | solution.py:371
  68.8 4.3 %collective-permute-start.30 = (f32[1,136,128]{2,1,0:T(8,128)S(1)}, f32[1,136,128]{2,1,0:T(8,128)S(1)}, u32[]{:S(2)}, u32[]{:S(2)}) collective-permute-start(f32[1,136,128]{2,1,0:T(8,128)S(1)} %add_add_fusion), channel_id=1, source_target_pairs={{0,16},{1,5},{2,18},{3,7},{4,20},{5,1},{6,22},{7,3},{8,24},{9,13},... | collective-permute-start | bytes 208904 | tf_op jit(solution)/shard_map/ppermute | solution.py:371
  73.2 1.6 %collective-permute-start.33 = (f32[4,136,128]{2,1,0:T(8,128)S(1)}, f32[4,136,128]{2,1,0:T(8,128)S(1)}, u32[]{:S(2)}, u32[]{:S(2)}) collective-permute-start(f32[4,136,128]{2,1,0:T(8,128)S(1)} %pad_maximum_fusion.3.own_ref), channel_id=1, source_target_pairs={{0,1},{1,0},{2,3},{3,2},{4,5},{5,4},{6,7},{7,6},{8,9},{9,8},{10,11... | collective-permute-start | bytes 835592 | tf_op jit(solution)/shard_map/ppermute | solution.py:66

commit v6 on v5

--- a/solution.py
+++ b/solution.py
@@ -16,15 +16,6 @@
 WEIGHT_ROWS = SUBLANES
 F32 = jnp.float32
 BF16 = jnp.bfloat16
-
-
-def dft_table(win):
-    line = np.arange(win, dtype=np.int64)
-    angle = (line[:, None] * line[None, :] % win) * (2.0 * np.pi / win)
-    full = (np.stack([np.cos(angle), np.sin(angle)]) / np.sqrt(win)).astype(np.float32)
-    high = full.astype(jnp.bfloat16)
-    low = (full - high.astype(np.float32)).astype(jnp.bfloat16)
-    return np.concatenate([high, low])
 
 
 def pairings(size):
@@ -224,10 +215,15 @@
     return jnp.where(mask, a, b), jnp.where(mask, b, a)
 
 
-def prepare_kernel(probe_ref, meas_ref, table_ref, probe_out, root_ref, table_out):
+def prepare_kernel(probe_ref, meas_ref, probe_out, root_ref, table_ref):
     probe_out[...] = probe_ref[...]
     root_ref[...] = jnp.sqrt(meas_ref[...])
-    table_out[...] = table_ref[...]
+    win = probe_ref.shape[-1]
+    line = lax.broadcasted_iota(jnp.int32, (win, win), 0)
+    product_of = line * lax.broadcasted_iota(jnp.int32, (win, win), 1) % win
+    angle = product_of.astype(F32) * (2.0 * np.pi / win)
+    for i, values in enumerate((jnp.cos(angle), jnp.sin(angle))):
+        table_ref[i], table_ref[i + 2] = split(values * win**-0.5)
 
 
 def first_kernel(n_ty, n_tx, n_y, n_x, margin, pos_ref, obj_ref, probe_ref, root_ref, table_ref, *rest):
@@ -435,7 +431,7 @@
     return half, xor_permute(half, 1, total), done
 
 
-def per_device(n_ty, n_tx, table, object_field, probe, intensities, positions):
+def per_device(n_ty, n_tx, object_field, probe, intensities, positions):
     win, modes = probe.shape[-1], probe.shape[1]
     margin, tile, scans = win // 2, object_field.shape[-1], positions.shape[2]
     spots = positions.reshape(scans, 2)
@@ -460,8 +456,11 @@
         corners += [swap(rims[i], py, px) for px in match_x[1:]]
 
     shape_of = lambda x: jax.ShapeDtypeStruct(x.shape, x.dtype)
-    ready = (probe, measured, jnp.asarray(table))
-    ready = call(prepare_kernel, [shape_of(x) for x in ready], ready)
+    outs = [shape_of(probe), shape_of(measured), jax.ShapeDtypeStruct((4, win, win), BF16)]
+    ready = call(prepare_kernel, outs, (probe, measured))
+    ty_in, ready = lax.optimization_barrier((ty_in, ready))
+    for i, rim in enumerate(ty_in[: len(match_y) if match_x else 0]):
+        corners[i * n_x] = swap(rim, None, match_x[0])
     (tx_in, ty_in, corners), (probe, root, table) = lax.optimization_barrier(
         ((tx_in, ty_in, corners), tuple(ready))
     )
@@ -531,9 +530,8 @@
     placed = (P(None, "ty", "tx"), P(), P("ty", "tx", None, None, None), P("ty", "tx", None, None))
 
     def run(object_field, probe, intensities, positions):
-        table = dft_table(probe.shape[-1])
         return jax.shard_map(
-            functools.partial(per_device, n_ty, n_tx, table),
+            functools.partial(per_device, n_ty, n_tx),
             mesh=mesh,
             in_specs=placed,
             out_specs=(P(None, "ty", "tx"), P()),

time: 76 us -> 75.5 us (level)
  waiting for transfers between devices: 23.5 us -> 24.7 us
  starting transfers between devices: 37.4 us -> 36.4 us
  local copies, waits for them, and re-layouts: 4.17 us -> 3.27 us
    ppermute x12, waiting for transfers between devices: 1.43 us -> 2.88 us  [swap(): return lax.ppermute(x, AXES, flat_pairs(pairs_y, pairs_x, n_ty, n_tx))]
    unnamed x10 -> x8, local copies, waits for them, and re-layouts: 2.88 us -> 1.98 us
    ppermute x18, waiting for transfers between devices: 19.3 us -> 18.5 us  [swap_over(): return lax.ppermute(x, AXES, [(i, i ^ masks[i & 1]) for i in range(total)])]
  transfers between devices with their start and end apart: 34 -> 34, of which waited for: 21 -> 24; matrix products, arithmetic and copies ran while one was open for 1% -> 1% of each run, Pallas kernels for 0% -> 0%
where the time goes in v6:
time: 75.5 us; the launch traced here: 75.3 us
  starting transfers between devices  36.4 us (48%)
  waiting for transfers between devices  24.7 us (33%)
  Pallas kernels  9.7 us (13%)
  local copies, waits for them, and re-layouts  3.27 us (4%)
  between operations  0.84 us (1%)
    ppermute x18, starting transfers between devices, swap_over(): return lax.ppermute(x, AXES, [(i, i ^ masks[i & 1]) for i in range(total)])  23.1 us
    ppermute x18, waiting for transfers between devices, swap_over(): return lax.ppermute(x, AXES, [(i, i ^ masks[i & 1]) for i in range(total)])  18.5 us
    ppermute x12, starting transfers between devices, swap(): return lax.ppermute(x, AXES, flat_pairs(pairs_y, pairs_x, n_ty, n_tx))  12.6 us
    pallas_call x4, Pallas kernels, call(): pl.pallas_call(kernel, out_shape=shapes, in_specs=[smem if x.dtype == jnp...  9.7 us
    ppermute x4, waiting for transfers between devices, xor_permute(): return lax.ppermute(x, AXES, [(i, i ^ mask) for i in range(total)])  3.31 us
    ppermute x12, waiting for transfers between devices, swap(): return lax.ppermute(x, AXES, flat_pairs(pairs_y, pairs_x, n_ty, n_tx))  2.88 us
    unnamed x8, local copies, waits for them, and re-layouts  1.98 us
  transfers between devices with their start and end apart: 34, of which 24 were waited for; matrix products, arithmetic and copies ran while one was open for 1% of the time, Pallas kernels for 0%

profile of v6, /device:TPU:0, one launch (start us, length us, event | category | flops | bytes accessed | tf_op | source)
XLA Modules:
  0.0 75.3 jit_solution(3931569244913273749)
XLA Ops:
  0.7 0.9 %constant_dynamic-slice_fusion.8 = f32[2,64,128]{2,1,0:T(8,128)S(1)} fusion(f32[2,128,128]{2,1,0:T(8,128)} %obj_ref.1, s32[]{:T(128)S(6)} %select_n.83), kind=kLoop, calls=%fused_computation.43 | loop fusion | bytes 131076 | tf_op jit(solution)/shard_map/dynamic_slice | solution.py:448
  1.5 2.9 %collective-permute-start.2 = (f32[2,64,128]{2,1,0:T(8,128)S(1)}, f32[2,64,128]{2,1,0:T(8,128)S(1)}, u32[]{:S(2)}, u32[]{:S(2)}) collective-permute-start(f32[2,64,128]{2,1,0:T(8,128)S(1)} %constant_dynamic-slice_fusion.8), channel_id=1, source_target_pairs={{0,16},{16,0},{1,17},{17,1},{2,18},{18,2},{3,19},{19,3},{4,20},{20... | collective-permute-start | bytes 196616 | tf_op jit(solution)/shard_map/ppermute | solution.py:444
  4.6 1.6 %collective-permute-start = (f32[2,128,128]{2,1,0:T(8,128)S(1)}, f32[2,128,128]{2,1,0:T(8,128)S(1)}, u32[]{:S(2)}, u32[]{:S(2)}) collective-permute-start(f32[2,128,128]{2,1,0:T(8,128)S(1)} %copy-done.1), channel_id=1, source_target_pairs={{0,1},{16,17},{1,0},{17,16},{2,3},{18,19},{3,2},{19,18},{4,5},{20,... | collective-permute-start | bytes 393224 | tf_op jit(solution)/shard_map/ppermute | solution.py:444
  6.1 0.5 collective-permute-start.4
  6.7 1.0 %copy-done = f32[2,4,128,128]{3,2,1,0:T(8,128)S(1)} copy-done((f32[2,4,128,128]{3,2,1,0:T(8,128)S(1)}, f32[2,4,128,128]{3,2,1,0:T(8,128)}, u32[]{:S(2)}) %copy-start) | copy-done | bytes 524312
  7.7 0.9 %copy-done.2 = f32[1,1,3,128,128]{4,3,2,1,0:T(8,128)S(1)} copy-done((f32[1,1,3,128,128]{4,3,2,1,0:T(8,128)S(1)}, f32[1,1,3,128,128]{4,3,2,1,0:T(8,128)}, u32[]{:S(2)}) %copy-start.2) | copy-done | bytes 196632
  8.6 0.4 shard_map.59
  9.0 1.1 %collective-permute-start.3 = (f32[2,64,128]{2,1,0:T(8,128)S(1)}, f32[2,64,128]{2,1,0:T(8,128)S(1)}, u32[]{:S(2)}, u32[]{:S(2)}) collective-permute-start(f32[2,64,128]{2,1,0:T(8,128)S(1)} %collective-permute-done.2.rest_0_), channel_id=1, source_target_pairs={{0,1},{16,17},{1,0},{17,16},{2,3},{18,19},{3,2},{19,18},{4,5},{20,... | collective-permute-start | bytes 196616 | tf_op jit(solution)/shard_map/ppermute | solution.py:444
  10.1 0.1 copy.7.pos_ref
  10.2 0.6 collective-permute-done.4.rest_4_
  10.8 0.2 collective-permute-done.3.rest_3_
  11.0 4.1 %shard_map.60 = (f32[2,264,256]{2,1,0:T(8,128)S(1)}, f32[4,136,128]{2,1,0:T(8,128)S(1)}, f32[4,136,128]{2,1,0:T(8,128)S(1)}, f32[2,128,128]{2,1,0:T(8,128)S(1)},...) custom-call(s32[3,2]{1,0:T(4,128)S(1)} %copy.7.pos_ref, f32[2,128,128]{2,1,0:T(8,128)S(1)} %copy-done.1, ...), custom_call_target="tpu_custom_call" | custom-call | tf_op jit(solution)/shard_map/pallas_call | solution.py:347
  15.1 0.4 collective-permute-start.5
  15.5 1.5 %collective-permute-start.6 = (f32[2,2,64,128]{3,2,1,0:T(8,128)S(1)}, f32[2,2,64,128]{3,2,1,0:T(8,128)S(1)}, u32[]{:S(2)}, u32[]{:S(2)}) collective-permute-start(f32[2,2,64,128]{3,2,1,0:T(8,128)S(1)} %get-tuple-element.64), channel_id=1, source_target_pairs={{0,16},{16,0},{1,17},{17,1},{2,18},{18,2},{3,19},{19,3},{4,20},{20... | collective-permute-start | bytes 393224 | tf_op jit(solution)/shard_map/ppermute | solution.py:444
  17.1 1.3 %collective-permute-start.7 = (f32[1,136,128]{2,1,0:T(8,128)S(1)}, f32[1,136,128]{2,1,0:T(8,128)S(1)}, u32[]{:S(2)}, u32[]{:S(2)}) collective-permute-start(f32[1,136,128]{2,1,0:T(8,128)S(1)} %get-tuple-element.102), channel_id=1, source_target_pairs={{0,16},{1,5},{2,18},{3,7},{4,20},{5,1},{6,22},{7,3},{8,24},{9,13},... | collective-permute-start | bytes 208904 | tf_op jit(solution)/shard_map/ppermute | solution.py:367
  18.4 1.8 %collective-permute-start.9 = (f32[1,136,128]{2,1,0:T(8,128)S(1)}, f32[1,136,128]{2,1,0:T(8,128)S(1)}, u32[]{:S(2)}, u32[]{:S(2)}) collective-permute-start(f32[1,136,128]{2,1,0:T(8,128)S(1)} %get-tuple-element.103), channel_id=1, source_target_pairs={{0,18},{1,13},{2,16},{3,15},{4,22},{5,9},{6,20},{7,11},{8,26},{9,5... | collective-permute-start | bytes 208904 | tf_op jit(solution)/shard_map/ppermute | solution.py:367
  20.2 0.5 collective-permute-start.8
  20.7 0.1 broadcast_in_dim.70
  20.7 0.1 broadcast_in_dim.71
  20.8 0.3 collective-permute-done.6
  21.1 0.7 collective-permute-done.7
  21.8 1.9 %collective-permute-done.9 = f32[1,136,128]{2,1,0:T(8,128)S(1)} collective-permute-done((f32[1,136,128]{2,1,0:T(8,128)S(1)}, f32[1,136,128]{2,1,0:T(8,128)S(1)}, u32[]{:S(2)}, u32[]{:S(2)}) %collective-permute-start.9) | collective-permute-done | bytes 69664 | tf_op jit(solution)/shard_map/ppermute | solution.py:367
  23.7 0.7 collective-permute-done.8
  24.5 3.3 %collective-permute-start.12 = (f32[1,136,128]{2,1,0:T(8,128)S(1)}, f32[1,136,128]{2,1,0:T(8,128)S(1)}, u32[]{:S(2)}, u32[]{:S(2)}) collective-permute-start(f32[1,136,128]{2,1,0:T(8,128)S(1)} %add_add_fusion.3), channel_id=1, source_target_pairs={{0,12},{1,19},{2,14},{3,17},{4,8},{5,23},{6,10},{7,21},{8,4},{9,27... | collective-permute-start | bytes 208904 | tf_op jit(solution)/shard_map/ppermute | solution.py:367
  27.8 1.2 %collective-permute-start.10 = (f32[1,136,128]{2,1,0:T(8,128)S(1)}, f32[1,136,128]{2,1,0:T(8,128)S(1)}, u32[]{:S(2)}, u32[]{:S(2)}) collective-permute-start(f32[1,136,128]{2,1,0:T(8,128)S(1)} %add_add_fusion.3), channel_id=1, source_target_pairs={{0,4},{1,17},{2,6},{3,19},{4,0},{5,21},{6,2},{7,23},{8,12},{9,25},... | collective-permute-start | bytes 208904 | tf_op jit(solution)/shard_map/ppermute | solution.py:367
  29.0 0.1 fusion.2
  29.1 1.3 %collective-permute-start.14 = (f32[2,128,128]{2,1,0:T(8,128)S(1)}, f32[2,128,128]{2,1,0:T(8,128)S(1)}, u32[]{:S(2)}, u32[]{:S(2)}) collective-permute-start(f32[2,128,128]{2,1,0:T(8,128)S(1)} %get-tuple-element.70.second_ref), channel_id=1, source_target_pairs={{1,2},{17,18},{2,1},{18,17},{3,4},{19,20},{4,3},{20,19},{5,6},{21,... | collective-permute-start | bytes 393224 | tf_op jit(solution)/shard_map/ppermute | solution.py:444
  30.5 0.2 collective-permute-done.12
  30.7 2.5 %collective-permute-done.11 = f32[1,136,128]{2,1,0:T(8,128)S(1)} collective-permute-done((f32[1,136,128]{2,1,0:T(8,128)S(1)}, f32[1,136,128]{2,1,0:T(8,128)S(1)}, u32[]{:S(2)}, u32[]{:S(2)}) %collective-permute-start.11) | collective-permute-done | bytes 69664 | tf_op jit(solution)/shard_map/ppermute | solution.py:367
  33.2 0.9 %collective-permute-done.14.rest_1_ = f32[2,128,128]{2,1,0:T(8,128)S(1)} collective-permute-done((f32[2,128,128]{2,1,0:T(8,128)S(1)}, f32[2,128,128]{2,1,0:T(8,128)S(1)}, u32[]{:S(2)}, u32[]{:S(2)}) %collective-permute-start.14) | collective-permute-done | bytes 131104 | tf_op jit(solution)/shard_map/ppermute | solution.py:444
  34.2 1.3 %collective-permute-start.15 = (f32[2,2,64,128]{3,2,1,0:T(8,128)S(1)}, f32[2,2,64,128]{3,2,1,0:T(8,128)S(1)}, u32[]{:S(2)}, u32[]{:S(2)}) collective-permute-start(f32[2,2,64,128]{3,2,1,0:T(8,128)S(1)} %pad_maximum_fusion.4), channel_id=1, source_target_pairs={{0,16},{16,0},{1,17},{17,1},{2,18},{18,2},{3,19},{19,3},{4,20},{20... | collective-permute-start | bytes 393224 | tf_op jit(solution)/shard_map/ppermute | solution.py:444
  35.5 2.2 %collective-permute-start.18 = (f32[1,136,128]{2,1,0:T(8,128)S(1)}, f32[1,136,128]{2,1,0:T(8,128)S(1)}, u32[]{:S(2)}, u32[]{:S(2)}) collective-permute-start(f32[1,136,128]{2,1,0:T(8,128)S(1)} %add_add_fusion.2), channel_id=1, source_target_pairs={{0,18},{1,13},{2,16},{3,15},{4,22},{5,9},{6,20},{7,11},{8,26},{9,5... | collective-permute-start | bytes 208904 | tf_op jit(solution)/shard_map/ppermute | solution.py:367
  37.7 1.2 %collective-permute-start.16 = (f32[1,136,128]{2,1,0:T(8,128)S(1)}, f32[1,136,128]{2,1,0:T(8,128)S(1)}, u32[]{:S(2)}, u32[]{:S(2)}) collective-permute-start(f32[1,136,128]{2,1,0:T(8,128)S(1)} %add_add_fusion.2), channel_id=1, source_target_pairs={{0,16},{1,5},{2,18},{3,7},{4,20},{5,1},{6,22},{7,3},{8,24},{9,13},... | collective-permute-start | bytes 208904 | tf_op jit(solution)/shard_map/ppermute | solution.py:367
  39.0 0.2 collective-permute-done.15.rest_2_
  39.2 2.3 %collective-permute-done.18 = f32[1,136,128]{2,1,0:T(8,128)S(1)} collective-permute-done((f32[1,136,128]{2,1,0:T(8,128)S(1)}, f32[1,136,128]{2,1,0:T(8,128)S(1)}, u32[]{:S(2)}, u32[]{:S(2)}) %collective-permute-start.18) | collective-permute-done | bytes 69664 | tf_op jit(solution)/shard_map/ppermute | solution.py:367
  41.5 0.7 collective-permute-done.17
  42.4 1.5 %collective-permute-done.19.other_ref = f32[4,136,128]{2,1,0:T(8,128)S(1)} collective-permute-done((f32[4,136,128]{2,1,0:T(8,128)S(1)}, f32[4,136,128]{2,1,0:T(8,128)S(1)}, u32[]{:S(2)}, u32[]{:S(2)}) %collective-permute-start.19) | collective-permute-done | bytes 278560 | tf_op jit(solution)/shard_map/ppermute | solution.py:57
  44.0 4.3 %shard_map.61 = (f32[2,128,128]{2,1,0:T(8,128)S(1)}, f32[2,4,128,128]{3,2,1,0:T(8,128)S(1)}, f32[4,136,128]{2,1,0:T(8,128)S(1)}, f32[4,136,128]{2,1,0:T(8,128)S(...) custom-call(s32[3,2]{1,0:T(4,128)S(1)} %copy.7.pos_ref, ...), custom_call_target="tpu_custom_call" | custom-call | tf_op jit(solution)/shard_map/pallas_call | solution.py:347
  48.2 0.2 collective-permute-start.20
  48.4 1.2 %collective-permute-start.21 = (f32[2,2,64,128]{3,2,1,0:T(8,128)S(1)}, f32[2,2,64,128]{3,2,1,0:T(8,128)S(1)}, u32[]{:S(2)}, u32[]{:S(2)}) collective-permute-start(f32[2,2,64,128]{3,2,1,0:T(8,128)S(1)} %get-tuple-element.79), channel_id=1, source_target_pairs={{0,16},{16,0},{1,17},{17,1},{2,18},{18,2},{3,19},{19,3},{4,20},{20... | collective-permute-start | bytes 393224 | tf_op jit(solution)/shard_map/ppermute | solution.py:444
  49.7 0.2 collective-permute-done.20
  49.9 1.1 %collective-permute-start.22 = (f32[1,136,128]{2,1,0:T(8,128)S(1)}, f32[1,136,128]{2,1,0:T(8,128)S(1)}, u32[]{:S(2)}, u32[]{:S(2)}) collective-permute-start(f32[1,136,128]{2,1,0:T(8,128)S(1)} %get-tuple-element.94), channel_id=1, source_target_pairs={{0,16},{1,5},{2,18},{3,7},{4,20},{5,1},{6,22},{7,3},{8,24},{9,13},... | collective-permute-start | bytes 208904 | tf_op jit(solution)/shard_map/ppermute | solution.py:367
  51.1 2.2 %collective-permute-start.24 = (f32[1,136,128]{2,1,0:T(8,128)S(1)}, f32[1,136,128]{2,1,0:T(8,128)S(1)}, u32[]{:S(2)}, u32[]{:S(2)}) collective-permute-start(f32[1,136,128]{2,1,0:T(8,128)S(1)} %get-tuple-element.95), channel_id=1, source_target_pairs={{0,18},{1,13},{2,16},{3,15},{4,22},{5,9},{6,20},{7,11},{8,26},{9,5... | collective-permute-start | bytes 208904 | tf_op jit(solution)/shard_map/ppermute | solution.py:367
  53.3 0.2 collective-permute-start.23
  53.5 0.7 collective-permute-done.21
  54.2 0.7 collective-permute-done.22
  55.0 2.0 %collective-permute-done.24 = f32[1,136,128]{2,1,0:T(8,128)S(1)} collective-permute-done((f32[1,136,128]{2,1,0:T(8,128)S(1)}, f32[1,136,128]{2,1,0:T(8,128)S(1)}, u32[]{:S(2)}, u32[]{:S(2)}) %collective-permute-start.24) | collective-permute-done | bytes 69664 | tf_op jit(solution)/shard_map/ppermute | solution.py:367
  57.0 0.7 collective-permute-done.23
  57.7 2.8 %collective-permute-start.27 = (f32[1,136,128]{2,1,0:T(8,128)S(1)}, f32[1,136,128]{2,1,0:T(8,128)S(1)}, u32[]{:S(2)}, u32[]{:S(2)}) collective-permute-start(f32[1,136,128]{2,1,0:T(8,128)S(1)} %add_add_fusion.1), channel_id=1, source_target_pairs={{0,12},{1,19},{2,14},{3,17},{4,8},{5,23},{6,10},{7,21},{8,4},{9,27... | collective-permute-start | bytes 208904 | tf_op jit(solution)/shard_map/ppermute | solution.py:367
  60.5 1.7 %collective-permute-start.25 = (f32[1,136,128]{2,1,0:T(8,128)S(1)}, f32[1,136,128]{2,1,0:T(8,128)S(1)}, u32[]{:S(2)}, u32[]{:S(2)}) collective-permute-start(f32[1,136,128]{2,1,0:T(8,128)S(1)} %add_add_fusion.1), channel_id=1, source_target_pairs={{0,4},{1,17},{2,6},{3,19},{4,0},{5,21},{6,2},{7,23},{8,12},{9,25},... | collective-permute-start | bytes 208904 | tf_op jit(solution)/shard_map/ppermute | solution.py:367
  62.2 0.1 fusion
  62.3 0.6 collective-permute-start.29
  62.9 0.3 collective-permute-start.28
  63.2 0.7 collective-permute-done.27
  63.9 1.9 %collective-permute-done.26 = f32[1,136,128]{2,1,0:T(8,128)S(1)} collective-permute-done((f32[1,136,128]{2,1,0:T(8,128)S(1)}, f32[1,136,128]{2,1,0:T(8,128)S(1)}, u32[]{:S(2)}, u32[]{:S(2)}) %collective-permute-start.26) | collective-permute-done | bytes 69664 | tf_op jit(solution)/shard_map/ppermute | solution.py:367
  65.8 1.4 %collective-permute-start.32 = (f32[1,136,128]{2,1,0:T(8,128)S(1)}, f32[1,136,128]{2,1,0:T(8,128)S(1)}, u32[]{:S(2)}, u32[]{:S(2)}) collective-permute-start(f32[1,136,128]{2,1,0:T(8,128)S(1)} %add_add_fusion), channel_id=1, source_target_pairs={{0,18},{1,13},{2,16},{3,15},{4,22},{5,9},{6,20},{7,11},{8,26},{9,5... | collective-permute-start | bytes 208904 | tf_op jit(solution)/shard_map/ppermute | solution.py:367
  67.2 1.1 %collective-permute-start.31 = (f32[1,136,128]{2,1,0:T(8,128)S(1)}, f32[1,136,128]{2,1,0:T(8,128)S(1)}, u32[]{:S(2)}, u32[]{:S(2)}) collective-permute-start(f32[1,136,128]{2,1,0:T(8,128)S(1)} %add_add_fusion), channel_id=1, source_target_pairs={{0,2},{1,9},{2,0},{3,11},{4,6},{5,13},{6,4},{7,15},{8,10},{9,1},{1... | collective-permute-start | bytes 208904 | tf_op jit(solution)/shard_map/ppermute | solution.py:367
  68.3 1.1 %collective-permute-start.30 = (f32[1,136,128]{2,1,0:T(8,128)S(1)}, f32[1,136,128]{2,1,0:T(8,128)S(1)}, u32[]{:S(2)}, u32[]{:S(2)}) collective-permute-start(f32[1,136,128]{2,1,0:T(8,128)S(1)} %add_add_fusion), channel_id=1, source_target_pairs={{0,16},{1,5},{2,18},{3,7},{4,20},{5,1},{6,22},{7,3},{8,24},{9,13},... | collective-permute-start | bytes 208904 | tf_op jit(solution)/shard_map/ppermute | solution.py:367
  69.4 1.7 %collective-permute-done.32 = f32[1,136,128]{2,1,0:T(8,128)S(1)} collective-permute-done((f32[1,136,128]{2,1,0:T(8,128)S(1)}, f32[1,136,128]{2,1,0:T(8,128)S(1)}, u32[]{:S(2)}, u32[]{:S(2)}) %collective-permute-start.32) | collective-permute-done | bytes 69664 | tf_op jit(solution)/shard_map/ppermute | solution.py:367
  71.2 0.7 collective-permute-done.31
  71.9 0.7 collective-permute-done.30
  72.7 0.1 collective-permute-start.33
  72.8 1.5 %collective-permute-done.33.other_ref = f32[4,136,128]{2,1,0:T(8,128)S(1)} collective-permute-done((f32[4,136,128]{2,1,0:T(8,128)S(1)}, f32[4,136,128]{2,1,0:T(8,128)S(1)}, u32[]{:S(2)}, u32[]{:S(2)}) %collective-permute-start.33) | collective-permute-done | bytes 278560 | tf_op jit(solution)/shard_map/ppermute | solution.py:57
  74.3 1.0 %shard_map.62 = (f32[2,128,128]{2,1,0:T(8,128)}, f32[2,4,128,128]{3,2,1,0:T(8,128)}) custom-call(f32[2,128,128]{2,1,0:T(8,128)S(1)} %get-tuple-element.76.tile_ref, f32[2,128,128]{2,1,0:T(8,128)S(1)} %get-tuple-element.84.first_ref, f32[2,128,128]{2,1,0:T(8,128)S(1)} %get-tuple-element.85.second_ref, f32[2,4,128,128]{3,2,1,0:T(8,128)S(1)} %get-tuple-element.86.probe_ref, ...), custom_call_target="tpu_custom_call" | custom-call | tf_op jit(solution)/shard_map/pallas_call | solution.py:347
  (41 shorter events, 0.7 us)
Async XLA Ops:
  0.6 3.9 %copy-start.1 = (f32[2,128,128]{2,1,0:T(8,128)S(1)}, f32[2,128,128]{2,1,0:T(8,128)}, u32[]{:S(2)}) copy-start(f32[2,128,128]{2,1,0:T(8,128)} %obj_ref.1) | copy-start | bytes 393220
  1.5 7.4 %collective-permute-start.2 = (f32[2,64,128]{2,1,0:T(8,128)S(1)}, f32[2,64,128]{2,1,0:T(8,128)S(1)}, u32[]{:S(2)}, u32[]{:S(2)}) collective-permute-start(f32[2,64,128]{2,1,0:T(8,128)S(1)} %constant_dynamic-slice_fusion.8), channel_id=1, source_target_pairs={{0,16},{16,0},{1,17},{17,1},{2,18},{18,2},{3,19},{19,3},{4,20},{20... | collective-permute-start | bytes 196616 | tf_op jit(solution)/shard_map/ppermute | solution.py:444
  4.5 6.3 %collective-permute-start.1 = (f32[2,128,128]{2,1,0:T(8,128)S(1)}, f32[2,128,128]{2,1,0:T(8,128)S(1)}, u32[]{:S(2)}, u32[]{:S(2)}) collective-permute-start(f32[2,128,128]{2,1,0:T(8,128)S(1)} %copy-done.1), channel_id=1, source_target_pairs={{1,2},{17,18},{2,1},{18,17},{3,4},{19,20},{4,3},{20,19},{5,6},{21,... | collective-permute-start | bytes 393224 | tf_op jit(solution)/shard_map/ppermute | solution.py:444
  4.6 6.2 %collective-permute-start = (f32[2,128,128]{2,1,0:T(8,128)S(1)}, f32[2,128,128]{2,1,0:T(8,128)S(1)}, u32[]{:S(2)}, u32[]{:S(2)}) collective-permute-start(f32[2,128,128]{2,1,0:T(8,128)S(1)} %copy-done.1), channel_id=1, source_target_pairs={{0,1},{16,17},{1,0},{17,16},{2,3},{18,19},{3,2},{19,18},{4,5},{20,... | collective-permute-start | bytes 393224 | tf_op jit(solution)/shard_map/ppermute | solution.py:444
  6.1 4.7 %collective-permute-start.4 = (f32[2,64,128]{2,1,0:T(8,128)S(1)}, f32[2,64,128]{2,1,0:T(8,128)S(1)}, u32[]{:S(2)}, u32[]{:S(2)}) collective-permute-start(f32[2,64,128]{2,1,0:T(8,128)S(1)} %constant_dynamic-slice_fusion.8), channel_id=1, source_target_pairs={{1,18},{17,2},{2,17},{18,1},{3,20},{19,4},{4,19},{20,3},{5,22},{21... | collective-permute-start | bytes 196616 | tf_op jit(solution)/shard_map/ppermute | solution.py:444
  6.7 1.0 %copy-start = (f32[2,4,128,128]{3,2,1,0:T(8,128)S(1)}, f32[2,4,128,128]{3,2,1,0:T(8,128)}, u32[]{:S(2)}) copy-start(f32[2,4,128,128]{3,2,1,0:T(8,128)} %probe_ref.1) | copy-start | bytes 1572868
  7.7 0.9 %copy-start.2 = (f32[1,1,3,128,128]{4,3,2,1,0:T(8,128)S(1)}, f32[1,1,3,128,128]{4,3,2,1,0:T(8,128)}, u32[]{:S(2)}) copy-start(f32[1,1,3,128,128]{4,3,2,1,0:T(8,128)} %param.6) | copy-start | bytes 589828
  9.0 1.2 %copy-start.3 = (s32[1,1,3,2]{2,3,1,0:T(2,128)S(1)}, s32[1,1,3,2]{2,3,1,0:T(2,128)}, u32[]{:S(2)}) copy-start(s32[1,1,3,2]{2,3,1,0:T(2,128)} %param.7) | copy-start | bytes 76
  9.0 2.0 %collective-permute-start.3 = (f32[2,64,128]{2,1,0:T(8,128)S(1)}, f32[2,64,128]{2,1,0:T(8,128)S(1)}, u32[]{:S(2)}, u32[]{:S(2)}) collective-permute-start(f32[2,64,128]{2,1,0:T(8,128)S(1)} %collective-permute-done.2.rest_0_), channel_id=1, source_target_pairs={{0,1},{16,17},{1,0},{17,16},{2,3},{18,19},{3,2},{19,18},{4,5},{20,... | collective-permute-start | bytes 196616 | tf_op jit(solution)/shard_map/ppermute | solution.py:444
  15.1 1.9 %collective-permute-start.5 = (f32[4,136,128]{2,1,0:T(8,128)S(1)}, f32[4,136,128]{2,1,0:T(8,128)S(1)}, u32[]{:S(2)}, u32[]{:S(2)}) collective-permute-start(f32[4,136,128]{2,1,0:T(8,128)S(1)} %get-tuple-element.63), channel_id=1, source_target_pairs={{0,1},{1,0},{2,3},{3,2},{4,5},{5,4},{6,7},{7,6},{8,9},{9,8},{10,11... | collective-permute-start | bytes 835592 | tf_op jit(solution)/shard_map/ppermute | solution.py:57
  15.5 5.6 %collective-permute-start.6 = (f32[2,2,64,128]{3,2,1,0:T(8,128)S(1)}, f32[2,2,64,128]{3,2,1,0:T(8,128)S(1)}, u32[]{:S(2)}, u32[]{:S(2)}) collective-permute-start(f32[2,2,64,128]{3,2,1,0:T(8,128)S(1)} %get-tuple-element.64), channel_id=1, source_target_pairs={{0,16},{16,0},{1,17},{17,1},{2,18},{18,2},{3,19},{19,3},{4,20},{20... | collective-permute-start | bytes 393224 | tf_op jit(solution)/shard_map/ppermute | solution.py:444
  17.1 4.7 %collective-permute-start.7 = (f32[1,136,128]{2,1,0:T(8,128)S(1)}, f32[1,136,128]{2,1,0:T(8,128)S(1)}, u32[]{:S(2)}, u32[]{:S(2)}) collective-permute-start(f32[1,136,128]{2,1,0:T(8,128)S(1)} %get-tuple-element.102), channel_id=1, source_target_pairs={{0,16},{1,5},{2,18},{3,7},{4,20},{5,1},{6,22},{7,3},{8,24},{9,13},... | collective-permute-start | bytes 208904 | tf_op jit(solution)/shard_map/ppermute | solution.py:367
  18.4 5.4 %collective-permute-start.9 = (f32[1,136,128]{2,1,0:T(8,128)S(1)}, f32[1,136,128]{2,1,0:T(8,128)S(1)}, u32[]{:S(2)}, u32[]{:S(2)}) collective-permute-start(f32[1,136,128]{2,1,0:T(8,128)S(1)} %get-tuple-element.103), channel_id=1, source_target_pairs={{0,18},{1,13},{2,16},{3,15},{4,22},{5,9},{6,20},{7,11},{8,26},{9,5... | collective-permute-start | bytes 208904 | tf_op jit(solution)/shard_map/ppermute | solution.py:367
  20.2 4.3 %collective-permute-start.8 = (f32[1,136,128]{2,1,0:T(8,128)S(1)}, f32[1,136,128]{2,1,0:T(8,128)S(1)}, u32[]{:S(2)}, u32[]{:S(2)}) collective-permute-start(f32[1,136,128]{2,1,0:T(8,128)S(1)} %get-tuple-element.104), channel_id=1, source_target_pairs={{0,2},{1,9},{2,0},{3,11},{4,6},{5,13},{6,4},{7,15},{8,10},{9,1},{1... | collective-permute-start | bytes 208904 | tf_op jit(solution)/shard_map/ppermute | solution.py:367
  24.5 6.2 %collective-permute-start.12 = (f32[1,136,128]{2,1,0:T(8,128)S(1)}, f32[1,136,128]{2,1,0:T(8,128)S(1)}, u32[]{:S(2)}, u32[]{:S(2)}) collective-permute-start(f32[1,136,128]{2,1,0:T(8,128)S(1)} %add_add_fusion.3), channel_id=1, source_target_pairs={{0,12},{1,19},{2,14},{3,17},{4,8},{5,23},{6,10},{7,21},{8,4},{9,27... | collective-permute-start | bytes 208904 | tf_op jit(solution)/shard_map/ppermute | solution.py:367
  27.8 5.4 %collective-permute-start.11 = (f32[1,136,128]{2,1,0:T(8,128)S(1)}, f32[1,136,128]{2,1,0:T(8,128)S(1)}, u32[]{:S(2)}, u32[]{:S(2)}) collective-permute-start(f32[1,136,128]{2,1,0:T(8,128)S(1)} %add_add_fusion.3), channel_id=1, source_target_pairs={{0,8},{1,3},{2,10},{3,1},{4,12},{5,7},{6,14},{7,5},{8,0},{9,11},{1... | collective-permute-start | bytes 208904 | tf_op jit(solution)/shard_map/ppermute | solution.py:367
  27.8 5.4 %collective-permute-start.10 = (f32[1,136,128]{2,1,0:T(8,128)S(1)}, f32[1,136,128]{2,1,0:T(8,128)S(1)}, u32[]{:S(2)}, u32[]{:S(2)}) collective-permute-start(f32[1,136,128]{2,1,0:T(8,128)S(1)} %add_add_fusion.3), channel_id=1, source_target_pairs={{0,4},{1,17},{2,6},{3,19},{4,0},{5,21},{6,2},{7,23},{8,12},{9,25},... | collective-permute-start | bytes 208904 | tf_op jit(solution)/shard_map/ppermute | solution.py:367
  29.1 5.0 %collective-permute-start.14 = (f32[2,128,128]{2,1,0:T(8,128)S(1)}, f32[2,128,128]{2,1,0:T(8,128)S(1)}, u32[]{:S(2)}, u32[]{:S(2)}) collective-permute-start(f32[2,128,128]{2,1,0:T(8,128)S(1)} %get-tuple-element.70.second_ref), channel_id=1, source_target_pairs={{1,2},{17,18},{2,1},{18,17},{3,4},{19,20},{4,3},{20,19},{5,6},{21,... | collective-permute-start | bytes 393224 | tf_op jit(solution)/shard_map/ppermute | solution.py:444
  30.4 3.7 %collective-permute-start.13 = (f32[2,128,128]{2,1,0:T(8,128)S(1)}, f32[2,128,128]{2,1,0:T(8,128)S(1)}, u32[]{:S(2)}, u32[]{:S(2)}) collective-permute-start(f32[2,128,128]{2,1,0:T(8,128)S(1)} %get-tuple-element.69.first_ref), channel_id=1, source_target_pairs={{0,1},{16,17},{1,0},{17,16},{2,3},{18,19},{3,2},{19,18},{4,5},{20,... | collective-permute-start | bytes 393224 | tf_op jit(solution)/shard_map/ppermute | solution.py:444
  34.2 5.0 %collective-permute-start.15 = (f32[2,2,64,128]{3,2,1,0:T(8,128)S(1)}, f32[2,2,64,128]{3,2,1,0:T(8,128)S(1)}, u32[]{:S(2)}, u32[]{:S(2)}) collective-permute-start(f32[2,2,64,128]{3,2,1,0:T(8,128)S(1)} %pad_maximum_fusion.4), channel_id=1, source_target_pairs={{0,16},{16,0},{1,17},{17,1},{2,18},{18,2},{3,19},{19,3},{4,20},{20... | collective-permute-start | bytes 393224 | tf_op jit(solution)/shard_map/ppermute | solution.py:444
  35.5 6.0 %collective-permute-start.18 = (f32[1,136,128]{2,1,0:T(8,128)S(1)}, f32[1,136,128]{2,1,0:T(8,128)S(1)}, u32[]{:S(2)}, u32[]{:S(2)}) collective-permute-start(f32[1,136,128]{2,1,0:T(8,128)S(1)} %add_add_fusion.2), channel_id=1, source_target_pairs={{0,18},{1,13},{2,16},{3,15},{4,22},{5,9},{6,20},{7,11},{8,26},{9,5... | collective-permute-start | bytes 208904 | tf_op jit(solution)/shard_map/ppermute | solution.py:367
  37.7 4.5 %collective-permute-start.17 = (f32[1,136,128]{2,1,0:T(8,128)S(1)}, f32[1,136,128]{2,1,0:T(8,128)S(1)}, u32[]{:S(2)}, u32[]{:S(2)}) collective-permute-start(f32[1,136,128]{2,1,0:T(8,128)S(1)} %add_add_fusion.2), channel_id=1, source_target_pairs={{0,2},{1,9},{2,0},{3,11},{4,6},{5,13},{6,4},{7,15},{8,10},{9,1},{1... | collective-permute-start | bytes 208904 | tf_op jit(solution)/shard_map/ppermute | solution.py:367
  37.7 4.5 %collective-permute-start.16 = (f32[1,136,128]{2,1,0:T(8,128)S(1)}, f32[1,136,128]{2,1,0:T(8,128)S(1)}, u32[]{:S(2)}, u32[]{:S(2)}) collective-permute-start(f32[1,136,128]{2,1,0:T(8,128)S(1)} %add_add_fusion.2), channel_id=1, source_target_pairs={{0,16},{1,5},{2,18},{3,7},{4,20},{5,1},{6,22},{7,3},{8,24},{9,13},... | collective-permute-start | bytes 208904 | tf_op jit(solution)/shard_map/ppermute | solution.py:367
  42.3 1.6 %collective-permute-start.19 = (f32[4,136,128]{2,1,0:T(8,128)S(1)}, f32[4,136,128]{2,1,0:T(8,128)S(1)}, u32[]{:S(2)}, u32[]{:S(2)}) collective-permute-start(f32[4,136,128]{2,1,0:T(8,128)S(1)} %pad_maximum_fusion.1.own_ref), channel_id=1, source_target_pairs={{0,1},{1,0},{2,3},{3,2},{4,5},{5,4},{6,7},{7,6},{8,9},{9,8},{10,11... | collective-permute-start | bytes 835592 | tf_op jit(solution)/shard_map/ppermute | solution.py:57
  48.2 1.6 %collective-permute-start.20 = (f32[4,136,128]{2,1,0:T(8,128)S(1)}, f32[4,136,128]{2,1,0:T(8,128)S(1)}, u32[]{:S(2)}, u32[]{:S(2)}) collective-permute-start(f32[4,136,128]{2,1,0:T(8,128)S(1)} %get-tuple-element.78), channel_id=1, source_target_pairs={{0,1},{1,0},{2,3},{3,2},{4,5},{5,4},{6,7},{7,6},{8,9},{9,8},{10,11... | collective-permute-start | bytes 835592 | tf_op jit(solution)/shard_map/ppermute | solution.py:57
  48.4 5.8 %collective-permute-start.21 = (f32[2,2,64,128]{3,2,1,0:T(8,128)S(1)}, f32[2,2,64,128]{3,2,1,0:T(8,128)S(1)}, u32[]{:S(2)}, u32[]{:S(2)}) collective-permute-start(f32[2,2,64,128]{3,2,1,0:T(8,128)S(1)} %get-tuple-element.79), channel_id=1, source_target_pairs={{0,16},{16,0},{1,17},{17,1},{2,18},{18,2},{3,19},{19,3},{4,20},{20... | collective-permute-start | bytes 393224 | tf_op jit(solution)/shard_map/ppermute | solution.py:444
  49.9 5.0 %collective-permute-start.22 = (f32[1,136,128]{2,1,0:T(8,128)S(1)}, f32[1,136,128]{2,1,0:T(8,128)S(1)}, u32[]{:S(2)}, u32[]{:S(2)}) collective-permute-start(f32[1,136,128]{2,1,0:T(8,128)S(1)} %get-tuple-element.94), channel_id=1, source_target_pairs={{0,16},{1,5},{2,18},{3,7},{4,20},{5,1},{6,22},{7,3},{8,24},{9,13},... | collective-permute-start | bytes 208904 | tf_op jit(solution)/shard_map/ppermute | solution.py:367
  51.1 5.9 %collective-permute-start.24 = (f32[1,136,128]{2,1,0:T(8,128)S(1)}, f32[1,136,128]{2,1,0:T(8,128)S(1)}, u32[]{:S(2)}, u32[]{:S(2)}) collective-permute-start(f32[1,136,128]{2,1,0:T(8,128)S(1)} %get-tuple-element.95), channel_id=1, source_target_pairs={{0,18},{1,13},{2,16},{3,15},{4,22},{5,9},{6,20},{7,11},{8,26},{9,5... | collective-permute-start | bytes 208904 | tf_op jit(solution)/shard_map/ppermute | solution.py:367
  53.3 4.4 %collective-permute-start.23 = (f32[1,136,128]{2,1,0:T(8,128)S(1)}, f32[1,136,128]{2,1,0:T(8,128)S(1)}, u32[]{:S(2)}, u32[]{:S(2)}) collective-permute-start(f32[1,136,128]{2,1,0:T(8,128)S(1)} %get-tuple-element.96), channel_id=1, source_target_pairs={{0,2},{1,9},{2,0},{3,11},{4,6},{5,13},{6,4},{7,15},{8,10},{9,1},{1... | collective-permute-start | bytes 208904 | tf_op jit(solution)/shard_map/ppermute | solution.py:367
  57.7 6.2 %collective-permute-start.27 = (f32[1,136,128]{2,1,0:T(8,128)S(1)}, f32[1,136,128]{2,1,0:T(8,128)S(1)}, u32[]{:S(2)}, u32[]{:S(2)}) collective-permute-start(f32[1,136,128]{2,1,0:T(8,128)S(1)} %add_add_fusion.1), channel_id=1, source_target_pairs={{0,12},{1,19},{2,14},{3,17},{4,8},{5,23},{6,10},{7,21},{8,4},{9,27... | collective-permute-start | bytes 208904 | tf_op jit(solution)/shard_map/ppermute | solution.py:367
  60.5 5.3 %collective-permute-start.26 = (f32[1,136,128]{2,1,0:T(8,128)S(1)}, f32[1,136,128]{2,1,0:T(8,128)S(1)}, u32[]{:S(2)}, u32[]{:S(2)}) collective-permute-start(f32[1,136,128]{2,1,0:T(8,128)S(1)} %add_add_fusion.1), channel_id=1, source_target_pairs={{0,8},{1,3},{2,10},{3,1},{4,12},{5,7},{6,14},{7,5},{8,0},{9,11},{1... | collective-permute-start | bytes 208904 | tf_op jit(solution)/shard_map/ppermute | solution.py:367
  60.5 5.3 %collective-permute-start.25 = (f32[1,136,128]{2,1,0:T(8,128)S(1)}, f32[1,136,128]{2,1,0:T(8,128)S(1)}, u32[]{:S(2)}, u32[]{:S(2)}) collective-permute-start(f32[1,136,128]{2,1,0:T(8,128)S(1)} %add_add_fusion.1), channel_id=1, source_target_pairs={{0,4},{1,17},{2,6},{3,19},{4,0},{5,21},{6,2},{7,23},{8,12},{9,25},... | collective-permute-start | bytes 208904 | tf_op jit(solution)/shard_map/ppermute | solution.py:367
  62.3 7.1 %collective-permute-start.29 = (f32[2,128,128]{2,1,0:T(8,128)S(1)}, f32[2,128,128]{2,1,0:T(8,128)S(1)}, u32[]{:S(2)}, u32[]{:S(2)}) collective-permute-start(f32[2,128,128]{2,1,0:T(8,128)S(1)} %get-tuple-element.85.second_ref), channel_id=1, source_target_pairs={{1,2},{17,18},{2,1},{18,17},{3,4},{19,20},{4,3},{20,19},{5,6},{21,... | collective-permute-start | bytes 393224 | tf_op jit(solution)/shard_map/ppermute | solution.py:444
  62.9 6.5 %collective-permute-start.28 = (f32[2,128,128]{2,1,0:T(8,128)S(1)}, f32[2,128,128]{2,1,0:T(8,128)S(1)}, u32[]{:S(2)}, u32[]{:S(2)}) collective-permute-start(f32[2,128,128]{2,1,0:T(8,128)S(1)} %get-tuple-element.84.first_ref), channel_id=1, source_target_pairs={{0,1},{16,17},{1,0},{17,16},{2,3},{18,19},{3,2},{19,18},{4,5},{20,... | collective-permute-start | bytes 393224 | tf_op jit(solution)/shard_map/ppermute | solution.py:444
  65.8 5.3 %collective-permute-start.32 = (f32[1,136,128]{2,1,0:T(8,128)S(1)}, f32[1,136,128]{2,1,0:T(8,128)S(1)}, u32[]{:S(2)}, u32[]{:S(2)}) collective-permute-start(f32[1,136,128]{2,1,0:T(8,128)S(1)} %add_add_fusion), channel_id=1, source_target_pairs={{0,18},{1,13},{2,16},{3,15},{4,22},{5,9},{6,20},{7,11},{8,26},{9,5... | collective-permute-start | bytes 208904 | tf_op jit(solution)/shard_map/ppermute | solution.py:367
  67.2 4.7 %collective-permute-start.31 = (f32[1,136,128]{2,1,0:T(8,128)S(1)}, f32[1,136,128]{2,1,0:T(8,128)S(1)}, u32[]{:S(2)}, u32[]{:S(2)}) collective-permute-start(f32[1,136,128]{2,1,0:T(8,128)S(1)} %add_add_fusion), channel_id=1, source_target_pairs={{0,2},{1,9},{2,0},{3,11},{4,6},{5,13},{6,4},{7,15},{8,10},{9,1},{1... | collective-permute-start | bytes 208904 | tf_op jit(solution)/shard_map/ppermute | solution.py:367
  68.3 4.3 %collective-permute-start.30 = (f32[1,136,128]{2,1,0:T(8,128)S(1)}, f32[1,136,128]{2,1,0:T(8,128)S(1)}, u32[]{:S(2)}, u32[]{:S(2)}) collective-permute-start(f32[1,136,128]{2,1,0:T(8,128)S(1)} %add_add_fusion), channel_id=1, source_target_pairs={{0,16},{1,5},{2,18},{3,7},{4,20},{5,1},{6,22},{7,3},{8,24},{9,13},... | collective-permute-start | bytes 208904 | tf_op jit(solution)/shard_map/ppermute | solution.py:367
  72.7 1.6 %collective-permute-start.33 = (f32[4,136,128]{2,1,0:T(8,128)S(1)}, f32[4,136,128]{2,1,0:T(8,128)S(1)}, u32[]{:S(2)}, u32[]{:S(2)}) collective-permute-start(f32[4,136,128]{2,1,0:T(8,128)S(1)} %pad_maximum_fusion.3.own_ref), channel_id=1, source_target_pairs={{0,1},{1,0},{2,3},{3,2},{4,5},{5,4},{6,7},{7,6},{8,9},{9,8},{10,11... | collective-permute-start | bytes 835592 | tf_op jit(solution)/shard_map/ppermute | solution.py:57

commit v7 on v6

--- a/solution.py
+++ b/solution.py
@@ -410,7 +410,7 @@
     rest = [b for b in range(1, levels) if b not in near]
     far = tuple(rest[:2])
     if len(near) == len(far):
-        return (near, far), [(far, near)] + [((b,), (b,)) for b in rest[2:]]
+        return (near, far[::-1]), [(far[::-1], near)] + [((b,), (b,)) for b in rest[2:]]
     return (near, near), [((b,), (b,)) for b in rest]
 
 

time: 75.5 us -> 75.5 us (level)
  transfers between devices with their start and end apart: 34 -> 34, of which waited for: 24 -> 26; matrix products, arithmetic and copies ran while one was open for 1% -> 1% of each run, Pallas kernels for 0% -> 0%
where the time goes in v7:
time: 75.5 us; the launch traced here: 75.3 us
  starting transfers between devices  36.6 us (48%)
  waiting for transfers between devices  24.4 us (32%)
  Pallas kernels  9.7 us (13%)
  local copies, waits for them, and re-layouts  3.27 us (4%)
  between operations  0.84 us (1%)
    ppermute x18, starting transfers between devices, swap_over(): return lax.ppermute(x, AXES, [(i, i ^ masks[i & 1]) for i in range(total)])  23.1 us
    ppermute x18, waiting for transfers between devices, swap_over(): return lax.ppermute(x, AXES, [(i, i ^ masks[i & 1]) for i in range(total)])  18.1 us
    ppermute x12, starting transfers between devices, swap(): return lax.ppermute(x, AXES, flat_pairs(pairs_y, pairs_x, n_ty, n_tx))  12.8 us
    pallas_call x4, Pallas kernels, call(): pl.pallas_call(kernel, out_shape=shapes, in_specs=[smem if x.dtype == jnp...  9.7 us
    ppermute x4, waiting for transfers between devices, xor_permute(): return lax.ppermute(x, AXES, [(i, i ^ mask) for i in range(total)])  3.25 us
    ppermute x12, waiting for transfers between devices, swap(): return lax.ppermute(x, AXES, flat_pairs(pairs_y, pairs_x, n_ty, n_tx))  3.09 us
    unnamed x8, local copies, waits for them, and re-layouts  1.98 us
  transfers between devices with their start and end apart: 34, of which 26 were waited for; matrix products, arithmetic and copies ran while one was open for 1% of the time, Pallas kernels for 0%

profile of v7, /device:TPU:0, one launch (start us, length us, event | category | flops | bytes accessed | tf_op | source)
XLA Modules:
  0.0 75.3 jit_solution(6670178193548008773)
XLA Ops:
  0.7 0.9 %constant_dynamic-slice_fusion.8 = f32[2,64,128]{2,1,0:T(8,128)S(1)} fusion(f32[2,128,128]{2,1,0:T(8,128)} %obj_ref.1, s32[]{:T(128)S(6)} %select_n.83), kind=kLoop, calls=%fused_computation.43 | loop fusion | bytes 131076 | tf_op jit(solution)/shard_map/dynamic_slice | solution.py:448
  1.5 2.9 %collective-permute-start.2 = (f32[2,64,128]{2,1,0:T(8,128)S(1)}, f32[2,64,128]{2,1,0:T(8,128)S(1)}, u32[]{:S(2)}, u32[]{:S(2)}) collective-permute-start(f32[2,64,128]{2,1,0:T(8,128)S(1)} %constant_dynamic-slice_fusion.8), channel_id=1, source_target_pairs={{0,16},{16,0},{1,17},{17,1},{2,18},{18,2},{3,19},{19,3},{4,20},{20... | collective-permute-start | bytes 196616 | tf_op jit(solution)/shard_map/ppermute | solution.py:444
  4.6 1.6 %collective-permute-start = (f32[2,128,128]{2,1,0:T(8,128)S(1)}, f32[2,128,128]{2,1,0:T(8,128)S(1)}, u32[]{:S(2)}, u32[]{:S(2)}) collective-permute-start(f32[2,128,128]{2,1,0:T(8,128)S(1)} %copy-done.1), channel_id=1, source_target_pairs={{0,1},{16,17},{1,0},{17,16},{2,3},{18,19},{3,2},{19,18},{4,5},{20,... | collective-permute-start | bytes 393224 | tf_op jit(solution)/shard_map/ppermute | solution.py:444
  6.1 0.5 collective-permute-start.4
  6.7 1.0 %copy-done = f32[2,4,128,128]{3,2,1,0:T(8,128)S(1)} copy-done((f32[2,4,128,128]{3,2,1,0:T(8,128)S(1)}, f32[2,4,128,128]{3,2,1,0:T(8,128)}, u32[]{:S(2)}) %copy-start) | copy-done | bytes 524312
  7.7 0.9 %copy-done.2 = f32[1,1,3,128,128]{4,3,2,1,0:T(8,128)S(1)} copy-done((f32[1,1,3,128,128]{4,3,2,1,0:T(8,128)S(1)}, f32[1,1,3,128,128]{4,3,2,1,0:T(8,128)}, u32[]{:S(2)}) %copy-start.2) | copy-done | bytes 196632
  8.6 0.4 shard_map.59
  9.0 1.1 %collective-permute-start.3 = (f32[2,64,128]{2,1,0:T(8,128)S(1)}, f32[2,64,128]{2,1,0:T(8,128)S(1)}, u32[]{:S(2)}, u32[]{:S(2)}) collective-permute-start(f32[2,64,128]{2,1,0:T(8,128)S(1)} %collective-permute-done.2.rest_0_), channel_id=1, source_target_pairs={{0,1},{16,17},{1,0},{17,16},{2,3},{18,19},{3,2},{19,18},{4,5},{20,... | collective-permute-start | bytes 196616 | tf_op jit(solution)/shard_map/ppermute | solution.py:444
  10.1 0.1 copy.7.pos_ref
  10.2 0.6 collective-permute-done.4.rest_4_
  10.8 0.2 collective-permute-done.3.rest_3_
  11.0 4.1 %shard_map.60 = (f32[2,264,256]{2,1,0:T(8,128)S(1)}, f32[4,136,128]{2,1,0:T(8,128)S(1)}, f32[4,136,128]{2,1,0:T(8,128)S(1)}, f32[2,128,128]{2,1,0:T(8,128)S(1)},...) custom-call(s32[3,2]{1,0:T(4,128)S(1)} %copy.7.pos_ref, f32[2,128,128]{2,1,0:T(8,128)S(1)} %copy-done.1, ...), custom_call_target="tpu_custom_call" | custom-call | tf_op jit(solution)/shard_map/pallas_call | solution.py:347
  15.1 0.4 collective-permute-start.5
  15.5 1.5 %collective-permute-start.6 = (f32[2,2,64,128]{3,2,1,0:T(8,128)S(1)}, f32[2,2,64,128]{3,2,1,0:T(8,128)S(1)}, u32[]{:S(2)}, u32[]{:S(2)}) collective-permute-start(f32[2,2,64,128]{3,2,1,0:T(8,128)S(1)} %get-tuple-element.64), channel_id=1, source_target_pairs={{0,16},{16,0},{1,17},{17,1},{2,18},{18,2},{3,19},{19,3},{4,20},{20... | collective-permute-start | bytes 393224 | tf_op jit(solution)/shard_map/ppermute | solution.py:444
  17.1 1.3 %collective-permute-start.7 = (f32[1,136,128]{2,1,0:T(8,128)S(1)}, f32[1,136,128]{2,1,0:T(8,128)S(1)}, u32[]{:S(2)}, u32[]{:S(2)}) collective-permute-start(f32[1,136,128]{2,1,0:T(8,128)S(1)} %get-tuple-element.102), channel_id=1, source_target_pairs={{0,16},{1,9},{2,18},{3,11},{4,20},{5,13},{6,22},{7,15},{8,24},{9,1... | collective-permute-start | bytes 208904 | tf_op jit(solution)/shard_map/ppermute | solution.py:367
  18.4 1.8 %collective-permute-start.9 = (f32[1,136,128]{2,1,0:T(8,128)S(1)}, f32[1,136,128]{2,1,0:T(8,128)S(1)}, u32[]{:S(2)}, u32[]{:S(2)}) collective-permute-start(f32[1,136,128]{2,1,0:T(8,128)S(1)} %get-tuple-element.103), channel_id=1, source_target_pairs={{0,18},{1,13},{2,16},{3,15},{4,22},{5,9},{6,20},{7,11},{8,26},{9,5... | collective-permute-start | bytes 208904 | tf_op jit(solution)/shard_map/ppermute | solution.py:367
  20.2 0.5 collective-permute-start.8
  20.7 0.1 broadcast_in_dim.70
  20.7 0.1 broadcast_in_dim.71
  20.8 0.3 collective-permute-done.6
  21.1 0.7 collective-permute-done.7
  21.8 1.9 %collective-permute-done.9 = f32[1,136,128]{2,1,0:T(8,128)S(1)} collective-permute-done((f32[1,136,128]{2,1,0:T(8,128)S(1)}, f32[1,136,128]{2,1,0:T(8,128)S(1)}, u32[]{:S(2)}, u32[]{:S(2)}) %collective-permute-start.9) | collective-permute-done | bytes 69664 | tf_op jit(solution)/shard_map/ppermute | solution.py:367
  23.7 0.7 collective-permute-done.8
  24.5 3.3 %collective-permute-start.12 = (f32[1,136,128]{2,1,0:T(8,128)S(1)}, f32[1,136,128]{2,1,0:T(8,128)S(1)}, u32[]{:S(2)}, u32[]{:S(2)}) collective-permute-start(f32[1,136,128]{2,1,0:T(8,128)S(1)} %add_add_fusion.3), channel_id=1, source_target_pairs={{0,12},{1,19},{2,14},{3,17},{4,8},{5,23},{6,10},{7,21},{8,4},{9,27... | collective-permute-start | bytes 208904 | tf_op jit(solution)/shard_map/ppermute | solution.py:367
  27.8 1.2 %collective-permute-start.10 = (f32[1,136,128]{2,1,0:T(8,128)S(1)}, f32[1,136,128]{2,1,0:T(8,128)S(1)}, u32[]{:S(2)}, u32[]{:S(2)}) collective-permute-start(f32[1,136,128]{2,1,0:T(8,128)S(1)} %add_add_fusion.3), channel_id=1, source_target_pairs={{0,8},{1,17},{2,10},{3,19},{4,12},{5,21},{6,14},{7,23},{8,0},{9,25... | collective-permute-start | bytes 208904 | tf_op jit(solution)/shard_map/ppermute | solution.py:367
  29.0 0.1 fusion.2
  29.1 1.3 %collective-permute-start.14 = (f32[2,128,128]{2,1,0:T(8,128)S(1)}, f32[2,128,128]{2,1,0:T(8,128)S(1)}, u32[]{:S(2)}, u32[]{:S(2)}) collective-permute-start(f32[2,128,128]{2,1,0:T(8,128)S(1)} %get-tuple-element.70.second_ref), channel_id=1, source_target_pairs={{1,2},{17,18},{2,1},{18,17},{3,4},{19,20},{4,3},{20,19},{5,6},{21,... | collective-permute-start | bytes 393224 | tf_op jit(solution)/shard_map/ppermute | solution.py:444
  30.5 0.2 collective-permute-done.12
  30.7 1.4 %collective-permute-done.11 = f32[1,136,128]{2,1,0:T(8,128)S(1)} collective-permute-done((f32[1,136,128]{2,1,0:T(8,128)S(1)}, f32[1,136,128]{2,1,0:T(8,128)S(1)}, u32[]{:S(2)}, u32[]{:S(2)}) %collective-permute-start.11) | collective-permute-done | bytes 69664 | tf_op jit(solution)/shard_map/ppermute | solution.py:367
  32.1 1.0 %collective-permute-done.10 = f32[1,136,128]{2,1,0:T(8,128)S(1)} collective-permute-done((f32[1,136,128]{2,1,0:T(8,128)S(1)}, f32[1,136,128]{2,1,0:T(8,128)S(1)}, u32[]{:S(2)}, u32[]{:S(2)}) %collective-permute-start.10) | collective-permute-done | bytes 69664 | tf_op jit(solution)/shard_map/ppermute | solution.py:367
  33.1 1.0 %collective-permute-done.14.rest_1_ = f32[2,128,128]{2,1,0:T(8,128)S(1)} collective-permute-done((f32[2,128,128]{2,1,0:T(8,128)S(1)}, f32[2,128,128]{2,1,0:T(8,128)S(1)}, u32[]{:S(2)}, u32[]{:S(2)}) %collective-permute-start.14) | collective-permute-done | bytes 131104 | tf_op jit(solution)/shard_map/ppermute | solution.py:444
  34.2 1.3 %collective-permute-start.15 = (f32[2,2,64,128]{3,2,1,0:T(8,128)S(1)}, f32[2,2,64,128]{3,2,1,0:T(8,128)S(1)}, u32[]{:S(2)}, u32[]{:S(2)}) collective-permute-start(f32[2,2,64,128]{3,2,1,0:T(8,128)S(1)} %pad_maximum_fusion.4), channel_id=1, source_target_pairs={{0,16},{16,0},{1,17},{17,1},{2,18},{18,2},{3,19},{19,3},{4,20},{20... | collective-permute-start | bytes 393224 | tf_op jit(solution)/shard_map/ppermute | solution.py:444
  35.5 2.2 %collective-permute-start.18 = (f32[1,136,128]{2,1,0:T(8,128)S(1)}, f32[1,136,128]{2,1,0:T(8,128)S(1)}, u32[]{:S(2)}, u32[]{:S(2)}) collective-permute-start(f32[1,136,128]{2,1,0:T(8,128)S(1)} %add_add_fusion.2), channel_id=1, source_target_pairs={{0,18},{1,13},{2,16},{3,15},{4,22},{5,9},{6,20},{7,11},{8,26},{9,5... | collective-permute-start | bytes 208904 | tf_op jit(solution)/shard_map/ppermute | solution.py:367
  37.7 1.2 %collective-permute-start.16 = (f32[1,136,128]{2,1,0:T(8,128)S(1)}, f32[1,136,128]{2,1,0:T(8,128)S(1)}, u32[]{:S(2)}, u32[]{:S(2)}) collective-permute-start(f32[1,136,128]{2,1,0:T(8,128)S(1)} %add_add_fusion.2), channel_id=1, source_target_pairs={{0,16},{1,9},{2,18},{3,11},{4,20},{5,13},{6,22},{7,15},{8,24},{9,1... | collective-permute-start | bytes 208904 | tf_op jit(solution)/shard_map/ppermute | solution.py:367
  39.0 0.3 collective-permute-done.15.rest_2_
  39.3 2.1 %collective-permute-done.18 = f32[1,136,128]{2,1,0:T(8,128)S(1)} collective-permute-done((f32[1,136,128]{2,1,0:T(8,128)S(1)}, f32[1,136,128]{2,1,0:T(8,128)S(1)}, u32[]{:S(2)}, u32[]{:S(2)}) %collective-permute-start.18) | collective-permute-done | bytes 69664 | tf_op jit(solution)/shard_map/ppermute | solution.py:367
  41.4 0.7 collective-permute-done.17
  42.4 1.5 %collective-permute-done.19.other_ref = f32[4,136,128]{2,1,0:T(8,128)S(1)} collective-permute-done((f32[4,136,128]{2,1,0:T(8,128)S(1)}, f32[4,136,128]{2,1,0:T(8,128)S(1)}, u32[]{:S(2)}, u32[]{:S(2)}) %collective-permute-start.19) | collective-permute-done | bytes 278560 | tf_op jit(solution)/shard_map/ppermute | solution.py:57
  43.9 4.3 %shard_map.61 = (f32[2,128,128]{2,1,0:T(8,128)S(1)}, f32[2,4,128,128]{3,2,1,0:T(8,128)S(1)}, f32[4,136,128]{2,1,0:T(8,128)S(1)}, f32[4,136,128]{2,1,0:T(8,128)S(...) custom-call(s32[3,2]{1,0:T(4,128)S(1)} %copy.7.pos_ref, ...), custom_call_target="tpu_custom_call" | custom-call | tf_op jit(solution)/shard_map/pallas_call | solution.py:347
  48.2 0.2 collective-permute-start.20
  48.4 1.3 %collective-permute-start.21 = (f32[2,2,64,128]{3,2,1,0:T(8,128)S(1)}, f32[2,2,64,128]{3,2,1,0:T(8,128)S(1)}, u32[]{:S(2)}, u32[]{:S(2)}) collective-permute-start(f32[2,2,64,128]{3,2,1,0:T(8,128)S(1)} %get-tuple-element.79), channel_id=1, source_target_pairs={{0,16},{16,0},{1,17},{17,1},{2,18},{18,2},{3,19},{19,3},{4,20},{20... | collective-permute-start | bytes 393224 | tf_op jit(solution)/shard_map/ppermute | solution.py:444
  49.7 0.2 collective-permute-done.20
  49.9 1.2 %collective-permute-start.22 = (f32[1,136,128]{2,1,0:T(8,128)S(1)}, f32[1,136,128]{2,1,0:T(8,128)S(1)}, u32[]{:S(2)}, u32[]{:S(2)}) collective-permute-start(f32[1,136,128]{2,1,0:T(8,128)S(1)} %get-tuple-element.94), channel_id=1, source_target_pairs={{0,16},{1,9},{2,18},{3,11},{4,20},{5,13},{6,22},{7,15},{8,24},{9,1... | collective-permute-start | bytes 208904 | tf_op jit(solution)/shard_map/ppermute | solution.py:367
  51.1 2.2 %collective-permute-start.24 = (f32[1,136,128]{2,1,0:T(8,128)S(1)}, f32[1,136,128]{2,1,0:T(8,128)S(1)}, u32[]{:S(2)}, u32[]{:S(2)}) collective-permute-start(f32[1,136,128]{2,1,0:T(8,128)S(1)} %get-tuple-element.95), channel_id=1, source_target_pairs={{0,18},{1,13},{2,16},{3,15},{4,22},{5,9},{6,20},{7,11},{8,26},{9,5... | collective-permute-start | bytes 208904 | tf_op jit(solution)/shard_map/ppermute | solution.py:367
  53.3 0.1 collective-permute-start.23
  53.4 0.7 collective-permute-done.21
  54.2 0.7 collective-permute-done.22
  54.9 2.1 %collective-permute-done.24 = f32[1,136,128]{2,1,0:T(8,128)S(1)} collective-permute-done((f32[1,136,128]{2,1,0:T(8,128)S(1)}, f32[1,136,128]{2,1,0:T(8,128)S(1)}, u32[]{:S(2)}, u32[]{:S(2)}) %collective-permute-start.24) | collective-permute-done | bytes 69664 | tf_op jit(solution)/shard_map/ppermute | solution.py:367
  57.0 0.7 collective-permute-done.23
  57.8 2.7 %collective-permute-start.27 = (f32[1,136,128]{2,1,0:T(8,128)S(1)}, f32[1,136,128]{2,1,0:T(8,128)S(1)}, u32[]{:S(2)}, u32[]{:S(2)}) collective-permute-start(f32[1,136,128]{2,1,0:T(8,128)S(1)} %add_add_fusion.1), channel_id=1, source_target_pairs={{0,12},{1,19},{2,14},{3,17},{4,8},{5,23},{6,10},{7,21},{8,4},{9,27... | collective-permute-start | bytes 208904 | tf_op jit(solution)/shard_map/ppermute | solution.py:367
  60.5 1.7 %collective-permute-start.25 = (f32[1,136,128]{2,1,0:T(8,128)S(1)}, f32[1,136,128]{2,1,0:T(8,128)S(1)}, u32[]{:S(2)}, u32[]{:S(2)}) collective-permute-start(f32[1,136,128]{2,1,0:T(8,128)S(1)} %add_add_fusion.1), channel_id=1, source_target_pairs={{0,8},{1,17},{2,10},{3,19},{4,12},{5,21},{6,14},{7,23},{8,0},{9,25... | collective-permute-start | bytes 208904 | tf_op jit(solution)/shard_map/ppermute | solution.py:367
  62.2 0.1 fusion
  62.3 1.0 %collective-permute-start.29 = (f32[2,128,128]{2,1,0:T(8,128)S(1)}, f32[2,128,128]{2,1,0:T(8,128)S(1)}, u32[]{:S(2)}, u32[]{:S(2)}) collective-permute-start(f32[2,128,128]{2,1,0:T(8,128)S(1)} %get-tuple-element.85.second_ref), channel_id=1, source_target_pairs={{1,2},{17,18},{2,1},{18,17},{3,4},{19,20},{4,3},{20,19},{5,6},{21,... | collective-permute-start | bytes 393224 | tf_op jit(solution)/shard_map/ppermute | solution.py:444
  63.3 0.6 collective-permute-done.27
  63.9 0.9 %collective-permute-done.26 = f32[1,136,128]{2,1,0:T(8,128)S(1)} collective-permute-done((f32[1,136,128]{2,1,0:T(8,128)S(1)}, f32[1,136,128]{2,1,0:T(8,128)S(1)}, u32[]{:S(2)}, u32[]{:S(2)}) %collective-permute-start.26) | collective-permute-done | bytes 69664 | tf_op jit(solution)/shard_map/ppermute | solution.py:367
  64.8 1.0 %collective-permute-done.25 = f32[1,136,128]{2,1,0:T(8,128)S(1)} collective-permute-done((f32[1,136,128]{2,1,0:T(8,128)S(1)}, f32[1,136,128]{2,1,0:T(8,128)S(1)}, u32[]{:S(2)}, u32[]{:S(2)}) %collective-permute-start.25) | collective-permute-done | bytes 69664 | tf_op jit(solution)/shard_map/ppermute | solution.py:367
  65.8 1.4 %collective-permute-start.32 = (f32[1,136,128]{2,1,0:T(8,128)S(1)}, f32[1,136,128]{2,1,0:T(8,128)S(1)}, u32[]{:S(2)}, u32[]{:S(2)}) collective-permute-start(f32[1,136,128]{2,1,0:T(8,128)S(1)} %add_add_fusion), channel_id=1, source_target_pairs={{0,18},{1,13},{2,16},{3,15},{4,22},{5,9},{6,20},{7,11},{8,26},{9,5... | collective-permute-start | bytes 208904 | tf_op jit(solution)/shard_map/ppermute | solution.py:367
  67.2 1.1 %collective-permute-start.31 = (f32[1,136,128]{2,1,0:T(8,128)S(1)}, f32[1,136,128]{2,1,0:T(8,128)S(1)}, u32[]{:S(2)}, u32[]{:S(2)}) collective-permute-start(f32[1,136,128]{2,1,0:T(8,128)S(1)} %add_add_fusion), channel_id=1, source_target_pairs={{0,2},{1,5},{2,0},{3,7},{4,6},{5,1},{6,4},{7,3},{8,10},{9,13},{10,... | collective-permute-start | bytes 208904 | tf_op jit(solution)/shard_map/ppermute | solution.py:367
  68.3 1.1 %collective-permute-start.30 = (f32[1,136,128]{2,1,0:T(8,128)S(1)}, f32[1,136,128]{2,1,0:T(8,128)S(1)}, u32[]{:S(2)}, u32[]{:S(2)}) collective-permute-start(f32[1,136,128]{2,1,0:T(8,128)S(1)} %add_add_fusion), channel_id=1, source_target_pairs={{0,16},{1,9},{2,18},{3,11},{4,20},{5,13},{6,22},{7,15},{8,24},{9,1... | collective-permute-start | bytes 208904 | tf_op jit(solution)/shard_map/ppermute | solution.py:367
  69.4 1.7 %collective-permute-done.32 = f32[1,136,128]{2,1,0:T(8,128)S(1)} collective-permute-done((f32[1,136,128]{2,1,0:T(8,128)S(1)}, f32[1,136,128]{2,1,0:T(8,128)S(1)}, u32[]{:S(2)}, u32[]{:S(2)}) %collective-permute-start.32) | collective-permute-done | bytes 69664 | tf_op jit(solution)/shard_map/ppermute | solution.py:367
  71.1 0.7 collective-permute-done.31
  71.9 0.7 collective-permute-done.30
  72.8 1.5 %collective-permute-done.33.other_ref = f32[4,136,128]{2,1,0:T(8,128)S(1)} collective-permute-done((f32[4,136,128]{2,1,0:T(8,128)S(1)}, f32[4,136,128]{2,1,0:T(8,128)S(1)}, u32[]{:S(2)}, u32[]{:S(2)}) %collective-permute-start.33) | collective-permute-done | bytes 278560 | tf_op jit(solution)/shard_map/ppermute | solution.py:57
  74.3 1.0 %shard_map.62 = (f32[2,128,128]{2,1,0:T(8,128)}, f32[2,4,128,128]{3,2,1,0:T(8,128)}) custom-call(f32[2,128,128]{2,1,0:T(8,128)S(1)} %get-tuple-element.76.tile_ref, f32[2,128,128]{2,1,0:T(8,128)S(1)} %get-tuple-element.84.first_ref, f32[2,128,128]{2,1,0:T(8,128)S(1)} %get-tuple-element.85.second_ref, f32[2,4,128,128]{3,2,1,0:T(8,128)S(1)} %get-tuple-element.86.probe_ref, ...), custom_call_target="tpu_custom_call" | custom-call | tf_op jit(solution)/shard_map/pallas_call | solution.py:347
  (41 shorter events, 0.7 us)
Async XLA Ops:
  0.6 3.9 %copy-start.1 = (f32[2,128,128]{2,1,0:T(8,128)S(1)}, f32[2,128,128]{2,1,0:T(8,128)}, u32[]{:S(2)}) copy-start(f32[2,128,128]{2,1,0:T(8,128)} %obj_ref.1) | copy-start | bytes 393220
  1.5 7.4 %collective-permute-start.2 = (f32[2,64,128]{2,1,0:T(8,128)S(1)}, f32[2,64,128]{2,1,0:T(8,128)S(1)}, u32[]{:S(2)}, u32[]{:S(2)}) collective-permute-start(f32[2,64,128]{2,1,0:T(8,128)S(1)} %constant_dynamic-slice_fusion.8), channel_id=1, source_target_pairs={{0,16},{16,0},{1,17},{17,1},{2,18},{18,2},{3,19},{19,3},{4,20},{20... | collective-permute-start | bytes 196616 | tf_op jit(solution)/shard_map/ppermute | solution.py:444
  4.5 6.3 %collective-permute-start.1 = (f32[2,128,128]{2,1,0:T(8,128)S(1)}, f32[2,128,128]{2,1,0:T(8,128)S(1)}, u32[]{:S(2)}, u32[]{:S(2)}) collective-permute-start(f32[2,128,128]{2,1,0:T(8,128)S(1)} %copy-done.1), channel_id=1, source_target_pairs={{1,2},{17,18},{2,1},{18,17},{3,4},{19,20},{4,3},{20,19},{5,6},{21,... | collective-permute-start | bytes 393224 | tf_op jit(solution)/shard_map/ppermute | solution.py:444
  4.6 6.2 %collective-permute-start = (f32[2,128,128]{2,1,0:T(8,128)S(1)}, f32[2,128,128]{2,1,0:T(8,128)S(1)}, u32[]{:S(2)}, u32[]{:S(2)}) collective-permute-start(f32[2,128,128]{2,1,0:T(8,128)S(1)} %copy-done.1), channel_id=1, source_target_pairs={{0,1},{16,17},{1,0},{17,16},{2,3},{18,19},{3,2},{19,18},{4,5},{20,... | collective-permute-start | bytes 393224 | tf_op jit(solution)/shard_map/ppermute | solution.py:444
  6.1 4.7 %collective-permute-start.4 = (f32[2,64,128]{2,1,0:T(8,128)S(1)}, f32[2,64,128]{2,1,0:T(8,128)S(1)}, u32[]{:S(2)}, u32[]{:S(2)}) collective-permute-start(f32[2,64,128]{2,1,0:T(8,128)S(1)} %constant_dynamic-slice_fusion.8), channel_id=1, source_target_pairs={{1,18},{17,2},{2,17},{18,1},{3,20},{19,4},{4,19},{20,3},{5,22},{21... | collective-permute-start | bytes 196616 | tf_op jit(solution)/shard_map/ppermute | solution.py:444
  6.7 1.0 %copy-start = (f32[2,4,128,128]{3,2,1,0:T(8,128)S(1)}, f32[2,4,128,128]{3,2,1,0:T(8,128)}, u32[]{:S(2)}) copy-start(f32[2,4,128,128]{3,2,1,0:T(8,128)} %probe_ref.1) | copy-start | bytes 1572868
  7.7 0.9 %copy-start.2 = (f32[1,1,3,128,128]{4,3,2,1,0:T(8,128)S(1)}, f32[1,1,3,128,128]{4,3,2,1,0:T(8,128)}, u32[]{:S(2)}) copy-start(f32[1,1,3,128,128]{4,3,2,1,0:T(8,128)} %param.6) | copy-start | bytes 589828
  9.0 1.2 %copy-start.3 = (s32[1,1,3,2]{2,3,1,0:T(2,128)S(1)}, s32[1,1,3,2]{2,3,1,0:T(2,128)}, u32[]{:S(2)}) copy-start(s32[1,1,3,2]{2,3,1,0:T(2,128)} %param.7) | copy-start | bytes 76
  9.0 2.0 %collective-permute-start.3 = (f32[2,64,128]{2,1,0:T(8,128)S(1)}, f32[2,64,128]{2,1,0:T(8,128)S(1)}, u32[]{:S(2)}, u32[]{:S(2)}) collective-permute-start(f32[2,64,128]{2,1,0:T(8,128)S(1)} %collective-permute-done.2.rest_0_), channel_id=1, source_target_pairs={{0,1},{16,17},{1,0},{17,16},{2,3},{18,19},{3,2},{19,18},{4,5},{20,... | collective-permute-start | bytes 196616 | tf_op jit(solution)/shard_map/ppermute | solution.py:444
  15.1 1.9 %collective-permute-start.5 = (f32[4,136,128]{2,1,0:T(8,128)S(1)}, f32[4,136,128]{2,1,0:T(8,128)S(1)}, u32[]{:S(2)}, u32[]{:S(2)}) collective-permute-start(f32[4,136,128]{2,1,0:T(8,128)S(1)} %get-tuple-element.63), channel_id=1, source_target_pairs={{0,1},{1,0},{2,3},{3,2},{4,5},{5,4},{6,7},{7,6},{8,9},{9,8},{10,11... | collective-permute-start | bytes 835592 | tf_op jit(solution)/shard_map/ppermute | solution.py:57
  15.5 5.6 %collective-permute-start.6 = (f32[2,2,64,128]{3,2,1,0:T(8,128)S(1)}, f32[2,2,64,128]{3,2,1,0:T(8,128)S(1)}, u32[]{:S(2)}, u32[]{:S(2)}) collective-permute-start(f32[2,2,64,128]{3,2,1,0:T(8,128)S(1)} %get-tuple-element.64), channel_id=1, source_target_pairs={{0,16},{16,0},{1,17},{17,1},{2,18},{18,2},{3,19},{19,3},{4,20},{20... | collective-permute-start | bytes 393224 | tf_op jit(solution)/shard_map/ppermute | solution.py:444
  17.1 4.7 %collective-permute-start.7 = (f32[1,136,128]{2,1,0:T(8,128)S(1)}, f32[1,136,128]{2,1,0:T(8,128)S(1)}, u32[]{:S(2)}, u32[]{:S(2)}) collective-permute-start(f32[1,136,128]{2,1,0:T(8,128)S(1)} %get-tuple-element.102), channel_id=1, source_target_pairs={{0,16},{1,9},{2,18},{3,11},{4,20},{5,13},{6,22},{7,15},{8,24},{9,1... | collective-permute-start | bytes 208904 | tf_op jit(solution)/shard_map/ppermute | solution.py:367
  18.4 5.4 %collective-permute-start.9 = (f32[1,136,128]{2,1,0:T(8,128)S(1)}, f32[1,136,128]{2,1,0:T(8,128)S(1)}, u32[]{:S(2)}, u32[]{:S(2)}) collective-permute-start(f32[1,136,128]{2,1,0:T(8,128)S(1)} %get-tuple-element.103), channel_id=1, source_target_pairs={{0,18},{1,13},{2,16},{3,15},{4,22},{5,9},{6,20},{7,11},{8,26},{9,5... | collective-permute-start | bytes 208904 | tf_op jit(solution)/shard_map/ppermute | solution.py:367
  20.2 4.3 %collective-permute-start.8 = (f32[1,136,128]{2,1,0:T(8,128)S(1)}, f32[1,136,128]{2,1,0:T(8,128)S(1)}, u32[]{:S(2)}, u32[]{:S(2)}) collective-permute-start(f32[1,136,128]{2,1,0:T(8,128)S(1)} %get-tuple-element.104), channel_id=1, source_target_pairs={{0,2},{1,5},{2,0},{3,7},{4,6},{5,1},{6,4},{7,3},{8,10},{9,13},{10,... | collective-permute-start | bytes 208904 | tf_op jit(solution)/shard_map/ppermute | solution.py:367
  24.5 6.2 %collective-permute-start.12 = (f32[1,136,128]{2,1,0:T(8,128)S(1)}, f32[1,136,128]{2,1,0:T(8,128)S(1)}, u32[]{:S(2)}, u32[]{:S(2)}) collective-permute-start(f32[1,136,128]{2,1,0:T(8,128)S(1)} %add_add_fusion.3), channel_id=1, source_target_pairs={{0,12},{1,19},{2,14},{3,17},{4,8},{5,23},{6,10},{7,21},{8,4},{9,27... | collective-permute-start | bytes 208904 | tf_op jit(solution)/shard_map/ppermute | solution.py:367
  27.8 4.3 %collective-permute-start.11 = (f32[1,136,128]{2,1,0:T(8,128)S(1)}, f32[1,136,128]{2,1,0:T(8,128)S(1)}, u32[]{:S(2)}, u32[]{:S(2)}) collective-permute-start(f32[1,136,128]{2,1,0:T(8,128)S(1)} %add_add_fusion.3), channel_id=1, source_target_pairs={{0,4},{1,3},{2,6},{3,1},{4,0},{5,7},{6,2},{7,5},{8,12},{9,11},{10,... | collective-permute-start | bytes 208904 | tf_op jit(solution)/shard_map/ppermute | solution.py:367
  27.8 5.3 %collective-permute-start.10 = (f32[1,136,128]{2,1,0:T(8,128)S(1)}, f32[1,136,128]{2,1,0:T(8,128)S(1)}, u32[]{:S(2)}, u32[]{:S(2)}) collective-permute-start(f32[1,136,128]{2,1,0:T(8,128)S(1)} %add_add_fusion.3), channel_id=1, source_target_pairs={{0,8},{1,17},{2,10},{3,19},{4,12},{5,21},{6,14},{7,23},{8,0},{9,25... | collective-permute-start | bytes 208904 | tf_op jit(solution)/shard_map/ppermute | solution.py:367
  29.1 5.0 %collective-permute-start.14 = (f32[2,128,128]{2,1,0:T(8,128)S(1)}, f32[2,128,128]{2,1,0:T(8,128)S(1)}, u32[]{:S(2)}, u32[]{:S(2)}) collective-permute-start(f32[2,128,128]{2,1,0:T(8,128)S(1)} %get-tuple-element.70.second_ref), channel_id=1, source_target_pairs={{1,2},{17,18},{2,1},{18,17},{3,4},{19,20},{4,3},{20,19},{5,6},{21,... | collective-permute-start | bytes 393224 | tf_op jit(solution)/shard_map/ppermute | solution.py:444
  30.4 3.7 %collective-permute-start.13 = (f32[2,128,128]{2,1,0:T(8,128)S(1)}, f32[2,128,128]{2,1,0:T(8,128)S(1)}, u32[]{:S(2)}, u32[]{:S(2)}) collective-permute-start(f32[2,128,128]{2,1,0:T(8,128)S(1)} %get-tuple-element.69.first_ref), channel_id=1, source_target_pairs={{0,1},{16,17},{1,0},{17,16},{2,3},{18,19},{3,2},{19,18},{4,5},{20,... | collective-permute-start | bytes 393224 | tf_op jit(solution)/shard_map/ppermute | solution.py:444
  34.2 5.2 %collective-permute-start.15 = (f32[2,2,64,128]{3,2,1,0:T(8,128)S(1)}, f32[2,2,64,128]{3,2,1,0:T(8,128)S(1)}, u32[]{:S(2)}, u32[]{:S(2)}) collective-permute-start(f32[2,2,64,128]{3,2,1,0:T(8,128)S(1)} %pad_maximum_fusion.4), channel_id=1, source_target_pairs={{0,16},{16,0},{1,17},{17,1},{2,18},{18,2},{3,19},{19,3},{4,20},{20... | collective-permute-start | bytes 393224 | tf_op jit(solution)/shard_map/ppermute | solution.py:444
  35.5 5.9 %collective-permute-start.18 = (f32[1,136,128]{2,1,0:T(8,128)S(1)}, f32[1,136,128]{2,1,0:T(8,128)S(1)}, u32[]{:S(2)}, u32[]{:S(2)}) collective-permute-start(f32[1,136,128]{2,1,0:T(8,128)S(1)} %add_add_fusion.2), channel_id=1, source_target_pairs={{0,18},{1,13},{2,16},{3,15},{4,22},{5,9},{6,20},{7,11},{8,26},{9,5... | collective-permute-start | bytes 208904 | tf_op jit(solution)/shard_map/ppermute | solution.py:367
  37.7 4.4 %collective-permute-start.17 = (f32[1,136,128]{2,1,0:T(8,128)S(1)}, f32[1,136,128]{2,1,0:T(8,128)S(1)}, u32[]{:S(2)}, u32[]{:S(2)}) collective-permute-start(f32[1,136,128]{2,1,0:T(8,128)S(1)} %add_add_fusion.2), channel_id=1, source_target_pairs={{0,2},{1,5},{2,0},{3,7},{4,6},{5,1},{6,4},{7,3},{8,10},{9,13},{10,... | collective-permute-start | bytes 208904 | tf_op jit(solution)/shard_map/ppermute | solution.py:367
  37.7 4.4 %collective-permute-start.16 = (f32[1,136,128]{2,1,0:T(8,128)S(1)}, f32[1,136,128]{2,1,0:T(8,128)S(1)}, u32[]{:S(2)}, u32[]{:S(2)}) collective-permute-start(f32[1,136,128]{2,1,0:T(8,128)S(1)} %add_add_fusion.2), channel_id=1, source_target_pairs={{0,16},{1,9},{2,18},{3,11},{4,20},{5,13},{6,22},{7,15},{8,24},{9,1... | collective-permute-start | bytes 208904 | tf_op jit(solution)/shard_map/ppermute | solution.py:367
  42.3 1.6 %collective-permute-start.19 = (f32[4,136,128]{2,1,0:T(8,128)S(1)}, f32[4,136,128]{2,1,0:T(8,128)S(1)}, u32[]{:S(2)}, u32[]{:S(2)}) collective-permute-start(f32[4,136,128]{2,1,0:T(8,128)S(1)} %pad_maximum_fusion.1.own_ref), channel_id=1, source_target_pairs={{0,1},{1,0},{2,3},{3,2},{4,5},{5,4},{6,7},{7,6},{8,9},{9,8},{10,11... | collective-permute-start | bytes 835592 | tf_op jit(solution)/shard_map/ppermute | solution.py:57
  48.2 1.6 %collective-permute-start.20 = (f32[4,136,128]{2,1,0:T(8,128)S(1)}, f32[4,136,128]{2,1,0:T(8,128)S(1)}, u32[]{:S(2)}, u32[]{:S(2)}) collective-permute-start(f32[4,136,128]{2,1,0:T(8,128)S(1)} %get-tuple-element.78), channel_id=1, source_target_pairs={{0,1},{1,0},{2,3},{3,2},{4,5},{5,4},{6,7},{7,6},{8,9},{9,8},{10,11... | collective-permute-start | bytes 835592 | tf_op jit(solution)/shard_map/ppermute | solution.py:57
  48.4 5.8 %collective-permute-start.21 = (f32[2,2,64,128]{3,2,1,0:T(8,128)S(1)}, f32[2,2,64,128]{3,2,1,0:T(8,128)S(1)}, u32[]{:S(2)}, u32[]{:S(2)}) collective-permute-start(f32[2,2,64,128]{3,2,1,0:T(8,128)S(1)} %get-tuple-element.79), channel_id=1, source_target_pairs={{0,16},{16,0},{1,17},{17,1},{2,18},{18,2},{3,19},{19,3},{4,20},{20... | collective-permute-start | bytes 393224 | tf_op jit(solution)/shard_map/ppermute | solution.py:444
  49.9 5.0 %collective-permute-start.22 = (f32[1,136,128]{2,1,0:T(8,128)S(1)}, f32[1,136,128]{2,1,0:T(8,128)S(1)}, u32[]{:S(2)}, u32[]{:S(2)}) collective-permute-start(f32[1,136,128]{2,1,0:T(8,128)S(1)} %get-tuple-element.94), channel_id=1, source_target_pairs={{0,16},{1,9},{2,18},{3,11},{4,20},{5,13},{6,22},{7,15},{8,24},{9,1... | collective-permute-start | bytes 208904 | tf_op jit(solution)/shard_map/ppermute | solution.py:367
  51.1 5.9 %collective-permute-start.24 = (f32[1,136,128]{2,1,0:T(8,128)S(1)}, f32[1,136,128]{2,1,0:T(8,128)S(1)}, u32[]{:S(2)}, u32[]{:S(2)}) collective-permute-start(f32[1,136,128]{2,1,0:T(8,128)S(1)} %get-tuple-element.95), channel_id=1, source_target_pairs={{0,18},{1,13},{2,16},{3,15},{4,22},{5,9},{6,20},{7,11},{8,26},{9,5... | collective-permute-start | bytes 208904 | tf_op jit(solution)/shard_map/ppermute | solution.py:367
  53.3 4.4 %collective-permute-start.23 = (f32[1,136,128]{2,1,0:T(8,128)S(1)}, f32[1,136,128]{2,1,0:T(8,128)S(1)}, u32[]{:S(2)}, u32[]{:S(2)}) collective-permute-start(f32[1,136,128]{2,1,0:T(8,128)S(1)} %get-tuple-element.96), channel_id=1, source_target_pairs={{0,2},{1,5},{2,0},{3,7},{4,6},{5,1},{6,4},{7,3},{8,10},{9,13},{10,... | collective-permute-start | bytes 208904 | tf_op jit(solution)/shard_map/ppermute | solution.py:367
  57.8 6.2 %collective-permute-start.27 = (f32[1,136,128]{2,1,0:T(8,128)S(1)}, f32[1,136,128]{2,1,0:T(8,128)S(1)}, u32[]{:S(2)}, u32[]{:S(2)}) collective-permute-start(f32[1,136,128]{2,1,0:T(8,128)S(1)} %add_add_fusion.1), channel_id=1, source_target_pairs={{0,12},{1,19},{2,14},{3,17},{4,8},{5,23},{6,10},{7,21},{8,4},{9,27... | collective-permute-start | bytes 208904 | tf_op jit(solution)/shard_map/ppermute | solution.py:367
  60.5 4.3 %collective-permute-start.26 = (f32[1,136,128]{2,1,0:T(8,128)S(1)}, f32[1,136,128]{2,1,0:T(8,128)S(1)}, u32[]{:S(2)}, u32[]{:S(2)}) collective-permute-start(f32[1,136,128]{2,1,0:T(8,128)S(1)} %add_add_fusion.1), channel_id=1, source_target_pairs={{0,4},{1,3},{2,6},{3,1},{4,0},{5,7},{6,2},{7,5},{8,12},{9,11},{10,... | collective-permute-start | bytes 208904 | tf_op jit(solution)/shard_map/ppermute | solution.py:367
  60.5 5.3 %collective-permute-start.25 = (f32[1,136,128]{2,1,0:T(8,128)S(1)}, f32[1,136,128]{2,1,0:T(8,128)S(1)}, u32[]{:S(2)}, u32[]{:S(2)}) collective-permute-start(f32[1,136,128]{2,1,0:T(8,128)S(1)} %add_add_fusion.1), channel_id=1, source_target_pairs={{0,8},{1,17},{2,10},{3,19},{4,12},{5,21},{6,14},{7,23},{8,0},{9,25... | collective-permute-start | bytes 208904 | tf_op jit(solution)/shard_map/ppermute | solution.py:367
  62.3 7.1 %collective-permute-start.29 = (f32[2,128,128]{2,1,0:T(8,128)S(1)}, f32[2,128,128]{2,1,0:T(8,128)S(1)}, u32[]{:S(2)}, u32[]{:S(2)}) collective-permute-start(f32[2,128,128]{2,1,0:T(8,128)S(1)} %get-tuple-element.85.second_ref), channel_id=1, source_target_pairs={{1,2},{17,18},{2,1},{18,17},{3,4},{19,20},{4,3},{20,19},{5,6},{21,... | collective-permute-start | bytes 393224 | tf_op jit(solution)/shard_map/ppermute | solution.py:444
  63.3 6.1 %collective-permute-start.28 = (f32[2,128,128]{2,1,0:T(8,128)S(1)}, f32[2,128,128]{2,1,0:T(8,128)S(1)}, u32[]{:S(2)}, u32[]{:S(2)}) collective-permute-start(f32[2,128,128]{2,1,0:T(8,128)S(1)} %get-tuple-element.84.first_ref), channel_id=1, source_target_pairs={{0,1},{16,17},{1,0},{17,16},{2,3},{18,19},{3,2},{19,18},{4,5},{20,... | collective-permute-start | bytes 393224 | tf_op jit(solution)/shard_map/ppermute | solution.py:444
  65.8 5.3 %collective-permute-start.32 = (f32[1,136,128]{2,1,0:T(8,128)S(1)}, f32[1,136,128]{2,1,0:T(8,128)S(1)}, u32[]{:S(2)}, u32[]{:S(2)}) collective-permute-start(f32[1,136,128]{2,1,0:T(8,128)S(1)} %add_add_fusion), channel_id=1, source_target_pairs={{0,18},{1,13},{2,16},{3,15},{4,22},{5,9},{6,20},{7,11},{8,26},{9,5... | collective-permute-start | bytes 208904 | tf_op jit(solution)/shard_map/ppermute | solution.py:367
  67.2 4.7 %collective-permute-start.31 = (f32[1,136,128]{2,1,0:T(8,128)S(1)}, f32[1,136,128]{2,1,0:T(8,128)S(1)}, u32[]{:S(2)}, u32[]{:S(2)}) collective-permute-start(f32[1,136,128]{2,1,0:T(8,128)S(1)} %add_add_fusion), channel_id=1, source_target_pairs={{0,2},{1,5},{2,0},{3,7},{4,6},{5,1},{6,4},{7,3},{8,10},{9,13},{10,... | collective-permute-start | bytes 208904 | tf_op jit(solution)/shard_map/ppermute | solution.py:367
  68.3 4.3 %collective-permute-start.30 = (f32[1,136,128]{2,1,0:T(8,128)S(1)}, f32[1,136,128]{2,1,0:T(8,128)S(1)}, u32[]{:S(2)}, u32[]{:S(2)}) collective-permute-start(f32[1,136,128]{2,1,0:T(8,128)S(1)} %add_add_fusion), channel_id=1, source_target_pairs={{0,16},{1,9},{2,18},{3,11},{4,20},{5,13},{6,22},{7,15},{8,24},{9,1... | collective-permute-start | bytes 208904 | tf_op jit(solution)/shard_map/ppermute | solution.py:367
  72.7 1.6 %collective-permute-start.33 = (f32[4,136,128]{2,1,0:T(8,128)S(1)}, f32[4,136,128]{2,1,0:T(8,128)S(1)}, u32[]{:S(2)}, u32[]{:S(2)}) collective-permute-start(f32[4,136,128]{2,1,0:T(8,128)S(1)} %pad_maximum_fusion.3.own_ref), channel_id=1, source_target_pairs={{0,1},{1,0},{2,3},{3,2},{4,5},{5,4},{6,7},{7,6},{8,9},{9,8},{10,11... | collective-permute-start | bytes 835592 | tf_op jit(solution)/shard_map/ppermute | solution.py:57
